TPU v7x, 32 devices: a whole 2x2x4 slice. The times are simulated.
32 devices in a mesh: groups: 2 (over y), dp: 8 (over z, x), layer: 2 (over core).
Axes of the slice: x: 2, y: 2, z: 4, core: 2. Of those that a mesh axis runs over, the one named last changes fastest.
Arguments:
- train_grads: bfloat16 [4096, 2, 4096], P(('groups', 'dp'), 'layer'), parts along dimension 0, as said below
- query_grads: bfloat16 [128, 2, 4096], P(('groups', 'dp'), 'layer'), parts along dimension 0, as said below
- listed: int32 [16, 4], P(('groups', 'dp')), parts along dimension 0, may hold values from 0 to 7, all different within a row; in each aligned block of 8 rows (0 to 7, 8 to 15, ...) at most 6 rows name the same one
Outputs:
- tiles: float32 [64, 8, 256], P(('groups', 'dp'), None, 'layer'), parts along dimension 0
There are 2 independent parts, one for each index of `groups`. A program takes and returns all parts, laid end to end along the dimension named above; each array names one. Nothing has to cross between parts.
Inputs may be any that keep to these rules, and one draw needn't show every extreme that they name: `listed`: each row holds 4 different train shards; no train shard appears in more than 6 rows, and some train shard appears in exactly 6 rows. `train_grads`: draws of projected gradients: finite values of order 0.01 to 1. `query_grads`: draws of projected gradients: finite values of order 0.01 to 1.
All inputs are finite; a program needn't handle non-finite values.
Results may differ from a plain program's by a relative error of at most 0.0036.
Values may be sent and summed in bfloat16 or wider, within the bound.
No kernel may reach another device: no remote copies, remote signals or barrier semaphores. Data moves between devices by JAX's collectives and lax.ppermute only.
A program may use at most 64 MiB of HBM per device.

v0:
```python
import jax
import jax.numpy as jnp
from jax import lax
from jax.sharding import PartitionSpec as P

K_OUT = 64
K_IN = 64


def chol_solve(factor, right_side):
    lower_done = lax.linalg.triangular_solve(factor, right_side, left_side=True, lower=True)
    return lax.linalg.triangular_solve(
        factor, lower_done, left_side=True, lower=True, transpose_a=True
    )


def damped_factors(in_sum, out_sum, total_count):
    in_cov = in_sum / total_count
    out_cov = out_sum / total_count
    in_trace = jnp.trace(in_cov, axis1=1, axis2=2)
    out_trace = jnp.trace(out_cov, axis1=1, axis2=2)
    in_eye = jnp.eye(in_cov.shape[1], dtype=jnp.float32)
    out_eye = jnp.eye(out_cov.shape[1], dtype=jnp.float32)
    in_damped = in_cov / (in_trace / in_cov.shape[1])[:, None, None] + 0.1 * in_eye
    out_damped = out_cov + 0.1 * (out_trace / out_cov.shape[1])[:, None, None] * out_eye
    return (jnp.linalg.cholesky(in_damped), jnp.linalg.cholesky(out_damped))


def precondition(gradients, in_chol, out_chol):
    count = gradients.shape[0]
    layer_count = gradients.shape[1]
    rows_out = out_chol.shape[1]
    cols_in = in_chol.shape[1]
    field = gradients.astype(jnp.float32).reshape(count, layer_count, rows_out, cols_in)
    stacked = jnp.transpose(field, (1, 2, 0, 3)).reshape(layer_count, rows_out, count * cols_in)
    solved = jax.vmap(chol_solve)(out_chol, stacked)
    solved = jnp.transpose(solved.reshape(layer_count, rows_out, count, cols_in), (0, 3, 2, 1))
    solved = solved.reshape(layer_count, cols_in, count * rows_out)
    twice = jax.vmap(chol_solve)(in_chol, solved)
    twice = jnp.transpose(twice.reshape(layer_count, cols_in, count, rows_out), (2, 0, 3, 1))
    return twice.reshape(count, layer_count, rows_out * cols_in).astype(jnp.bfloat16)


def covariance_factors(train_grads, shard_count):
    examples = train_grads.shape[0]
    layer_count = train_grads.shape[1]
    field = train_grads.reshape(examples, layer_count, K_OUT, K_IN)
    in_part = jnp.einsum("nlij,nlik->ljk", field, field, preferred_element_type=jnp.float32)
    out_part = jnp.einsum("nlij,nlkj->lik", field, field, preferred_element_type=jnp.float32)
    in_sum, out_sum = lax.psum((in_part, out_part), "dp")
    return damped_factors(in_sum, out_sum, float(examples * shard_count))


def shards(train_grads, query_grads, listed):
    shard_count = lax.axis_size("dp")
    own_index = lax.axis_index("dp")
    per_query = query_grads.shape[0]
    examples = train_grads.shape[0]
    layer_count = train_grads.shape[1]
    width = train_grads.shape[2]
    listed_count = listed.shape[1]
    slot_count = min(3 * listed_count // 2, shard_count)
    in_chol, out_chol = covariance_factors(train_grads, shard_count)
    solved_own = precondition(query_grads, in_chol, out_chol)
    all_lists, all_queries = (
        lax.all_gather(listed, "dp", axis=0, tiled=True),
        lax.all_gather(solved_own, "dp", axis=0, tiled=True),
    )
    owner_ids = jnp.arange(shard_count, dtype=jnp.int32)
    hit = jnp.any(all_lists == own_index, axis=1).astype(jnp.int32)
    rank = jnp.cumsum(hit) - 1
    slot_ids = jnp.arange(slot_count, dtype=jnp.int32)
    one_hot = (hit[:, None] == 1) & (rank[:, None] == slot_ids[None, :])
    slot_used = jnp.any(one_hot, axis=0)
    slot_owner = jnp.sum(jnp.where(one_hot, owner_ids[:, None], 0), axis=0)
    gather_owner = jnp.where(slot_used, slot_owner, 0)
    place_owner = jnp.where(slot_used, slot_owner, shard_count)
    query_blocks = all_queries.reshape(shard_count, per_query, layer_count, width)
    chosen = jnp.take(query_blocks, gather_owner, axis=0)
    slot_scores = jnp.einsum(
        "sqlk,elk->sqe", chosen, train_grads, preferred_element_type=jnp.float32
    )
    outgoing = (
        jnp.zeros((shard_count, per_query, examples), jnp.float32)
        .at[place_owner]
        .set(slot_scores, mode="drop")
    )
    own_list = listed[0]
    received = lax.all_to_all(outgoing, "dp", split_axis=0, concat_axis=0, tiled=True)
    owned = jnp.take(received, own_list, axis=0)
    return lax.psum_scatter(owned, "layer", scatter_dimension=2, tiled=True)


def solution(mesh):
    in_specs = (
        P(("groups", "dp"), "layer", None),
        P(("groups", "dp"), "layer", None),
        P(("groups", "dp"), None),
    )
    out_specs = P(("groups", "dp"), None, "layer")
    return jax.shard_map(shards, mesh=mesh, in_specs=in_specs, out_specs=out_specs, check_vma=False)
```

profile of v0, /device:TPU:0, one launch (start us, length us, event | category | flops | bytes accessed | tf_op | source)
XLA Modules:
  0.0 158.4 jit_solution(14411445254311199654)
XLA Ops:
  6.5 3.3 %copy.32 = bf16[256,1,4096]{0,2,1:T(8,128)(2,1)S(1)} copy(bf16[256,1,4096]{2,0,1:T(8,128)(2,1)} %param.8) | data formatting | bytes 4194304 | tf_op args[0]
  9.8 0.7 convolution_bitcast_fusion.2
  10.5 0.0 copy-start.2
  10.5 0.0 copy-start.1
  10.5 3.3 %fusion.5 = f32[1,64,64]{1,2,0:T(8,128)S(1)} fusion(bf16[256,64,64]{0,2,1:T(8,128)(2,1)S(1)} %bitcast.97), kind=kOutput, calls=%fused_computation.10 | convolution fusion | flops 134217728 | bytes 2113536 | tf_op jit(solution)/shard_map/nlij,nlkj->lik/dot_general | solution.py:49
  13.9 22.1 %all-gather = s32[8,1,4]{2,1,0:T(1,128)S(1)} all-gather(s32[1,1,4]{2,1,0:T(1,128)S(1)} %bitcast.102), channel_id=1, replica_groups=mesh['groups'=2,'dp'=8,'layer'=2] {'dp'}, dimensions={0}, use_global_device_ids=true | all-gather | bytes 144 | tf_op jit(solution)/shard_map/all_gather | solution.py:66
  36.0 0.2 compare_reduce_fusion
  36.2 0.2 reduce-window.8
  36.4 0.1 fusion.22
  36.5 0.1 select_reduce_fusion.4
  36.6 33.4 %all-reduce = (f32[1,64,64]{1,2,0:T(8,128)S(1)}, f32[1,64,64]{1,2,0:T(8,128)S(1)}) all-reduce(f32[1,64,64]{1,2,0:T(8,128)S(1)} %fusion.5, f32[1,64,64]{1,2,0:T(8,128)S(1)} %convolution_bitcast_fusion.2), channel_id=1, replica_groups=mesh['groups'=2,'dp'=8,'layer'=2] {'dp'}, use_global_device_ids=true, to_apply=%region_8.10 | all-reduce | flops 8192 | bytes 65536 | tf_op jit(solution)/shard_map/psum | solution.py:50
  70.0 0.7 select_reduce_fusion.3
  70.7 0.6 select_reduce_fusion.2
  72.7 0.1 copy.38
  72.8 5.8 %custom-call.13 = f32[1,64,64]{2,1,0:T(8,128)S(1)} custom-call(f32[1,64,64]{2,1,0:T(8,128)S(1)} %fusion.16), custom_call_target="Cholesky" | custom-call | tf_op jit(solution)/shard_map/jit(cholesky)/cholesky | solution.py:26
  78.7 0.6 compare_reduce_fusion.1
  79.3 0.7 fusion.12
  80.0 4.9 %custom-call.15 = f32[1,1,64,64]{2,3,1,0:T(8,128)S(1)} custom-call(f32[1,1,64,64]{3,2,1,0:T(8,128)S(1)} %fusion.12), custom_call_target="InvertDiagBlocksLowerTriangular" | custom-call | tf_op jit(solution)/shard_map/vmap()/triangular_solve/custom-call.2 | solution.py:12
  84.9 0.0 copy-done.1
  84.9 0.2 reshape.336
  85.1 0.2 copy.52
  85.2 0.1 reshape.370
  85.4 0.3 fusion.13
  85.7 0.3 convolution_bitcast_fusion.1
  86.0 0.1 reshape.319
  86.1 0.2 copy.40
  86.2 0.1 reshape.378
  86.4 0.1 copy.34
  86.5 5.8 %custom-call.12 = f32[1,64,64]{2,1,0:T(8,128)S(1)} custom-call(f32[1,64,64]{2,1,0:T(8,128)S(1)} %fusion.20), custom_call_target="Cholesky" | custom-call | tf_op jit(solution)/shard_map/jit(cholesky)/cholesky | solution.py:26
  92.3 0.6 compare_reduce_fusion.2
  93.0 0.7 fusion.11
  93.6 4.9 %custom-call.17 = f32[1,1,64,64]{2,3,1,0:T(8,128)S(1)} custom-call(f32[1,1,64,64]{3,2,1,0:T(8,128)S(1)} %fusion.11), custom_call_target="InvertDiagBlocksLowerTriangular" | custom-call | tf_op jit(solution)/shard_map/vmap()/triangular_solve/custom-call.2 | solution.py:12
  98.5 0.3 fusion.17
  98.9 0.3 fusion.4
  99.2 0.1 copy.46
  99.3 0.2 convert_element_type.48
  99.5 31.6 %all_gather.7 = bf16[64,1,4096]{2,0,1:T(8,128)(2,1)S(1)} all-gather(bf16[8,1,4096]{2,0,1:T(8,128)(2,1)S(1)} %convert_element_type.48), channel_id=1, replica_groups=mesh['groups'=2,'dp'=8,'layer'=2] {'dp'}, dimensions={0}, use_global_device_ids=true | all-gather | bytes 589824 | tf_op jit(solution)/shard_map/all_gather | solution.py:67
  131.1 0.6 gather_fusion
  131.7 0.8 fusion
  132.4 0.6 broadcast_in_dim.63
  133.0 2.0 %scatter_fusion = f32[8,8,256]{2,1,0:T(8,128)} fusion(f32[8,8,256]{2,1,0:T(8,128)} %broadcast_in_dim.63, s32[6]{0:T(128)S(1)} %get-tuple-element.11, f32[6,8,256]{2,1,0:T(8,128)S(1)} %fusion), kind=kCustom, calls=%fused_computation.2 | custom fusion | bytes 147480 | tf_op jit(solution)/shard_map/scatter | solution.py:86
  135.1 3.3 %all-to-all-start = ((f32[8,8,256]{2,1,0:T(8,128)}), f32[8,8,256]{2,1,0:T(8,128)S(1)}, u32[]{:S(2)}, u32[]{:S(2)}) async-start(f32[8,8,256]{2,1,0:T(8,128)} %scatter_fusion), calls=%async_computation | async-start | bytes 131072 | tf_op jit(solution)/shard_map/all_to_all | solution.py:89
  138.4 0.0 reduce-scatter.2.cloned.1.call-start
  138.5 6.8 %all-to-all-done = f32[8,8,256]{2,1,0:T(8,128)S(1)} async-done(((f32[8,8,256]{2,1,0:T(8,128)}), f32[8,8,256]{2,1,0:T(8,128)S(1)}, u32[]{:S(2)}, u32[]{:S(2)}) %all-to-all-start) | async-done | bytes 65568 | tf_op jit(solution)/shard_map/all_to_all | solution.py:89
  145.3 0.5 gather_fusion.1
  145.8 0.7 broadcast_select_fusion
  146.5 0.0 reduce-scatter.2.cloned.1.call-update
  146.5 5.1 %reduce-scatter.2.cloned.1.call-done = f32[4,8,128]{2,1,0:T(8,128)} async-done(((f32[4,8,256]{2,1,0:T(8,128)}), f32[4,8,128]{2,1,0:T(8,128)}) %reduce-scatter.2.cloned.1.call-update) | async-done | bytes 16400 | tf_op jit(solution)/shard_map/reduce_scatter | solution.py:91
  (16 shorter events, 0.2 us)
Async XLA Ops:
  10.5 3.4 %copy-start.2 = (s32[1,4]{1,0:T(1,128)S(1)}, s32[1,4]{1,0:T(1,128)}, u32[]{:S(2)}) copy-start(s32[1,4]{1,0:T(1,128)} %param.10) | copy-start | bytes 52
  10.5 74.4 %copy-start.1 = (bf16[8,1,4096]{2,0,1:T(8,128)(2,1)S(1)}, bf16[8,1,4096]{2,0,1:T(8,128)(2,1)}, u32[]{:S(2)}) copy-start(bf16[8,1,4096]{2,0,1:T(8,128)(2,1)} %param.9) | copy-start | bytes 196612
  85.7 46.0 %copy-start = (bf16[256,1,4096]{2,0,1:T(8,128)(2,1)S(1)}, bf16[256,1,4096]{2,0,1:T(8,128)(2,1)}, u32[]{:S(2)}) copy-start(bf16[256,1,4096]{2,0,1:T(8,128)(2,1)} %param.8) | copy-start | bytes 6291460
  135.1 10.2 %all-to-all-start = ((f32[8,8,256]{2,1,0:T(8,128)}), f32[8,8,256]{2,1,0:T(8,128)S(1)}, u32[]{:S(2)}, u32[]{:S(2)}) async-start(f32[8,8,256]{2,1,0:T(8,128)} %scatter_fusion), calls=%async_computation | async-start | bytes 131072 | tf_op jit(solution)/shard_map/all_to_all | solution.py:89
  138.4 13.2 %reduce-scatter.2.cloned.1.call-start = ((), (), s32[]{:S(2)}) async-start(), calls=%async_computation.2 | async-start | bytes 49152 | tf_op jit(solution)/shard_map/reduce_scatter | solution.py:91
Sparse Core Ops, SparseCore 0:
  146.6 4.9 reduce-scatter.1
where the time goes:
time: 159 us; the launch traced here: 158 us
  blocking collectives  87.1 us (55%)
  other arithmetic  26.8 us (17%)
  between operations  15 us (9%)
  waiting for transfers between devices  11.8 us (7%)
  local copies, waits for them, and re-layouts  8.32 us (5%)
  matrix products  5.95 us (4%)
  starting transfers between devices  3.39 us (2%)
    psum x1, blocking collectives, covariance_factors(): in_sum, out_sum = lax.psum((in_part, out_part), 'dp')  33.4 us
    all_gather x1, blocking collectives, shards(): lax.all_gather(solved_own, 'dp', axis=0, tiled=True)  31.6 us
    all_gather x1, blocking collectives, shards(): lax.all_gather(listed, 'dp', axis=0, tiled=True)  22.1 us
    another operation x6, other arithmetic, damped_factors(): return (jnp.linalg.cholesky(in_damped), jnp.linalg.cholesky(out_damped))  13 us
    another operation x4, other arithmetic, chol_solve(): lax.linalg.triangular_solve(factor, lower_done, left_side=True, lower=Tru...  11.1 us
    all_to_all x1, waiting for transfers between devices, shards(): lax.all_to_all(outgoing, 'dp', split_axis=0, concat_axis=0, tiled=True)  6.75 us
    reduce_scatter x1, waiting for transfers between devices, shards(): return lax.psum_scatter(owned, 'layer', scatter_dimension=2, tiled=True)  5.07 us
    all_to_all x1, starting transfers between devices, shards(): lax.all_to_all(outgoing, 'dp', split_axis=0, concat_axis=0, tiled=True)  3.35 us
  transfers between devices with their start and end apart: 2, of which 2 were waited for; matrix products, arithmetic and copies ran while one was open for 0% of the time, Pallas kernels for 0%

commit v1 on v0

v1 whole, which is shorter than its diff:
```python
import functools
import jax
import jax.numpy as jnp
from jax import lax
from jax.experimental import pallas as pl
from jax.experimental.pallas import tpu as pltpu
from jax.sharding import PartitionSpec as P

K_OUT = 64
K_IN = 64
LANES = 128
CHUNK = 64
PIVOT = 4
F32 = jnp.float32
BF16 = jnp.bfloat16
VMEM_LIMIT = 48 * 1024 * 1024

NT = (((1,), (1,)), ((), ()))


def low_half(rows):
    return lax.broadcasted_iota(jnp.int32, (rows, LANES), 1) < LANES // 2


def swap_pair(first, second):
    low = low_half(first.shape[0])
    even = jnp.where(low, first, pltpu.roll(second, LANES // 2, 1))
    odd = jnp.where(low, pltpu.roll(first, LANES // 2, 1), second)
    return even, odd


def covariance_kernel(train_ref, cov_ref, turned, by_in, by_out):
    examples, width = train_ref.shape
    blocks = width // LANES
    parts = examples // LANES
    for c in range(blocks):
        block = train_ref[:, c * LANES:(c + 1) * LANES].astype(F32).T
        for part in range(parts):
            piece = block[:, part * LANES:(part + 1) * LANES]
            turned[part, c * LANES:(c + 1) * LANES, :] = piece
        small = block.astype(BF16)
        for half in range(2):
            start = (2 * c + half) * examples
            by_in[:, start:start + examples] = small[half * K_IN:(half + 1) * K_IN, :]
    for j in range(K_IN):
        for part in range(parts):
            start = j * examples + part * LANES
            for half in range(2):
                rows = turned[part, pl.ds(half * K_IN + j, blocks, stride=LANES), :]
                by_out[half * blocks:(half + 1) * blocks, start:start + LANES] = rows.astype(BF16)
    in_sum = lax.dot_general(by_in[...], by_in[...], NT, preferred_element_type=F32)
    out_sum = lax.dot_general(by_out[...], by_out[...], NT, preferred_element_type=F32)
    cov_ref[...] = jnp.concatenate([in_sum, out_sum], axis=1)


def covariance_sums(train):
    examples, width = train.shape
    return pl.pallas_call(
        covariance_kernel,
        out_shape=jax.ShapeDtypeStruct((K_OUT, 2 * K_IN), F32),
        in_specs=[pl.BlockSpec(memory_space=pltpu.VMEM)],
        out_specs=pl.BlockSpec(memory_space=pltpu.VMEM),
        scratch_shapes=[
            pltpu.VMEM((examples // LANES, width, LANES), F32),
            pltpu.VMEM((K_IN, K_OUT * examples), BF16),
            pltpu.VMEM((K_OUT, K_IN * examples), BF16),
        ],
        compiler_params=pltpu.CompilerParams(vmem_limit_bytes=VMEM_LIMIT),
        cost_estimate=pl.CostEstimate(flops=4 * examples * 64**3, bytes_accessed=2 * examples * width, transcendentals=0),
        name="covariance",
    )(train)


def turn_kernel(*refs):
    query_refs, out_ref, spread = refs[:-2], refs[-2], refs[-1]
    blocks = out_ref.shape[0] // 2
    half = CHUNK // 2
    for c in range(blocks):
        at = c * CHUNK
        for ref in query_refs:
            count = ref.shape[0]
            spread[at:at + count, :] = ref[:, c * LANES:(c + 1) * LANES].astype(F32)
            at = at + count
    for p in range(half):
        first = spread[pl.ds(p, blocks, stride=CHUNK), :]
        second = spread[pl.ds(p + half, blocks, stride=CHUNK), :]
        even, odd = swap_pair(first, second)
        out_ref[:blocks, p * LANES:(p + 1) * LANES] = even.astype(BF16)
        out_ref[blocks:, p * LANES:(p + 1) * LANES] = odd.astype(BF16)


def turned_queries(queries):
    width = queries[0].shape[1]
    total = sum(part.shape[0] for part in queries)
    steps = total // CHUNK
    if steps == 1:
        in_specs = [pl.BlockSpec(part.shape, lambda step: (0, 0)) for part in queries]
    else:
        in_specs = [pl.BlockSpec((CHUNK, width), lambda step: (step, 0))]
    return pl.pallas_call(
        turn_kernel,
        out_shape=jax.ShapeDtypeStruct((K_OUT, total * K_IN), BF16),
        grid=(steps,),
        in_specs=in_specs,
        out_specs=pl.BlockSpec((K_OUT, CHUNK * K_IN), lambda step: (0, step)),
        scratch_shapes=[pltpu.VMEM((width // LANES * CHUNK, LANES), F32)],
        compiler_params=pltpu.CompilerParams(vmem_limit_bytes=VMEM_LIMIT),
        cost_estimate=pl.CostEstimate(flops=total * width, bytes_accessed=4 * total * width, transcendentals=0),
        name="turn_queries",
    )(*queries)


def damped(cov, total_count):
    rows = lax.broadcasted_iota(jnp.int32, (K_OUT, LANES), 0)
    lanes = lax.broadcasted_iota(jnp.int32, (K_OUT, LANES), 1)
    low = lanes < K_IN
    diagonal = rows == jnp.where(low, lanes, lanes - K_IN)
    cov = cov * (1.0 / total_count)
    on_diagonal = jnp.sum(jnp.where(diagonal, cov, 0.0), axis=0, keepdims=True)
    low_row = low_half(1)
    in_mean = jnp.sum(jnp.where(low_row, on_diagonal, 0.0), axis=1, keepdims=True) / K_IN
    out_mean = jnp.sum(jnp.where(low_row, 0.0, on_diagonal), axis=1, keepdims=True) / K_OUT
    scale = jnp.where(low_row, 1.0 / in_mean, 1.0)
    added = jnp.where(low_row, 0.1, 0.1 * out_mean)
    return cov * scale + jnp.where(diagonal, added, 0.0)


def inverses(matrix):
    size = matrix.shape[0]
    lanes = lax.broadcasted_iota(jnp.int32, (size, LANES), 1)
    offset = jnp.where(lanes < size, 0, size)
    rows = lax.broadcasted_iota(jnp.int32, (size, LANES), 0)
    row_lanes = lax.broadcasted_iota(jnp.int32, (8, LANES), 1)
    row_place = jnp.where(row_lanes < size, row_lanes, row_lanes - size)
    place = lanes - offset

    def spread_row(values, row):
        return jnp.broadcast_to(values[row:row + 1, :], (8, LANES))

    for begin in range(0, size, PIVOT):
        columns = [jnp.take_along_axis(matrix, offset + begin + a, axis=1) for a in range(PIVOT)]
        p = [[spread_row(columns[b], begin + a) for b in range(PIVOT)] for a in range(PIVOT)]
        r = []
        for a in range(PIVOT):
            row = spread_row(matrix, begin + a)
            inside = (row_place >= begin) & (row_place < begin + PIVOT)
            unit = jnp.where(row_place == begin + a, 1.0, 0.0)
            r.append(jnp.where(inside, unit, row))
        det = 1.0 / (p[0][0] * p[1][1] - p[0][1] * p[1][0])
        e = [[p[1][1] * det, -p[0][1] * det], [-p[1][0] * det, p[0][0] * det]]
        u = [[e[a][0] * p[0][b] + e[a][1] * p[1][b] for b in (2, 3)] for a in (0, 1)]
        s = [[p[a][b + 2] - (p[a][0] * u[0][b] + p[a][1] * u[1][b]) for b in (0, 1)] for a in (2, 3)]
        det = 1.0 / (s[0][0] * s[1][1] - s[0][1] * s[1][0])
        f = [[s[1][1] * det, -s[0][1] * det], [-s[1][0] * det, s[0][0] * det]]
        w = [e[a][0] * r[0] + e[a][1] * r[1] for a in (0, 1)]
        t = [r[a] - (p[a][0] * w[0] + p[a][1] * w[1]) for a in (2, 3)]
        last = [f[a][0] * t[0] + f[a][1] * t[1] for a in (0, 1)]
        first = [w[a] - (u[a][0] * last[0] + u[a][1] * last[1]) for a in (0, 1)]
        solved = first + last
        inside = (place >= begin) & (place < begin + PIVOT)
        rest = jnp.where(inside, 0.0, matrix)
        tall = [jnp.concatenate([row] * (size // 8), axis=0) for row in solved]
        for a in range(PIVOT):
            rest = rest - columns[a] * tall[a]
        for a in range(PIVOT):
            rest = jnp.where(rows == begin + a, tall[a], rest)
        matrix = rest
    return matrix


def split(values, terms):
    parts = []
    for _ in range(terms):
        part = values.astype(BF16)
        parts.append(part)
        values = values - part.astype(F32)
    return parts


def score_kernel(total_count, route_ref, cov_ref, turned_ref, train_ref, out_ref, left, right, solved, ready):
    blocks = K_OUT // 2
    half = CHUNK // 2
    step = pl.program_id(0)

    @pl.when(step == 0)
    def _():
        inverse = inverses(damped(cov_ref[...], total_count))
        turned = pltpu.roll(inverse, LANES // 2, 1)
        low = low_half(K_OUT)
        left[...] = jnp.concatenate(split(turned[:, :K_OUT], 3), axis=1)
        double = jnp.concatenate([jnp.where(low, inverse, 0.0), jnp.where(low, 0.0, turned)], axis=0)
        high, small = split(double, 2)
        right[:LANES, :LANES] = high
        right[:LANES, LANES:] = small
        right[LANES:, :LANES] = high
        right[LANES:, LANES:] = jnp.zeros_like(small)

    group = 4
    for g in range(half // group):
        block = turned_ref[:, g * group * LANES:(g + 1) * group * LANES]
        tall = jnp.concatenate([block, block, block], axis=0)
        once = jnp.dot(left[...], tall, preferred_element_type=F32)
        once = jnp.concatenate([once[:, k * LANES:(k + 1) * LANES] for k in range(group)], axis=0)
        wide = jnp.concatenate(split(once, 2), axis=1)
        twice = jnp.dot(wide, right[...], preferred_element_type=F32)
        solved[g * group * K_OUT:(g + 1) * group * K_OUT, :] = twice[:, :LANES] + twice[:, LANES:]
    for c in range(blocks):
        first = solved[pl.ds(c, half, stride=K_OUT), :]
        second = solved[pl.ds(c + blocks, half, stride=K_OUT), :]
        even, odd = swap_pair(first, second)
        ready[:half, c * LANES:(c + 1) * LANES] = even.astype(BF16)
        ready[half:, c * LANES:(c + 1) * LANES] = odd.astype(BF16)
    scores = lax.dot_general(ready[...], train_ref[...], NT, preferred_element_type=F32)
    per_query = out_ref.shape[2]
    parts = out_ref.shape[1]
    for s in range(CHUNK // per_query):
        owner = route_ref[step * (CHUNK // per_query) + s]
        for part in range(parts):
            piece = scores[s * per_query:(s + 1) * per_query, part * LANES:(part + 1) * LANES]
            out_ref[owner, part, :, :] = piece


def all_scores(route, cov, turned, train, per_query, total_count):
    shard_count = route.shape[0]
    examples, width = train.shape
    steps = shard_count * per_query // CHUNK
    parts = examples // LANES
    return pl.pallas_call(
        functools.partial(score_kernel, total_count),
        out_shape=jax.ShapeDtypeStruct((shard_count, parts, per_query, LANES), F32),
        grid=(steps,),
        in_specs=[
            pl.BlockSpec(memory_space=pltpu.SMEM),
            pl.BlockSpec((K_OUT, 2 * K_IN), lambda step: (0, 0)),
            pl.BlockSpec((K_OUT, CHUNK * K_IN), lambda step: (0, step)),
            pl.BlockSpec((examples, width), lambda step: (0, 0)),
        ],
        out_specs=pl.BlockSpec((shard_count, parts, per_query, LANES), lambda step: (0, 0, 0, 0)),
        scratch_shapes=[
            pltpu.VMEM((K_OUT, 3 * K_OUT), BF16),
            pltpu.VMEM((2 * LANES, 2 * LANES), BF16),
            pltpu.VMEM((CHUNK // 2 * K_OUT, LANES), F32),
            pltpu.VMEM((CHUNK, width), BF16),
        ],
        compiler_params=pltpu.CompilerParams(vmem_limit_bytes=VMEM_LIMIT),
        cost_estimate=pl.CostEstimate(
            flops=2 * shard_count * per_query * width * (examples + 128), bytes_accessed=2 * examples * width, transcendentals=0
        ),
        name="solve_and_score",
    )(route, cov, turned, train)


def pick_kernel(listed_ref, received_ref, out_ref):
    for r in range(out_ref.shape[0]):
        shard = listed_ref[0, r]
        total = received_ref[shard, 0]
        for layer in range(1, received_ref.shape[1]):
            total = total + received_ref[shard, layer]
        out_ref[r] = total


def picked(listed, received):
    return pl.pallas_call(
        pick_kernel,
        out_shape=jax.ShapeDtypeStruct((listed.shape[1],) + received.shape[2:], F32),
        in_specs=[pl.BlockSpec(memory_space=pltpu.SMEM), pl.BlockSpec(memory_space=pltpu.VMEM)],
        out_specs=pl.BlockSpec(memory_space=pltpu.VMEM),
        compiler_params=pltpu.CompilerParams(vmem_limit_bytes=VMEM_LIMIT),
        name="pick_tiles",
    )(listed, received)


def exchange(values, distance, count):
    return lax.ppermute(values, "dp", [(k, k ^ distance) for k in range(count)])


def shards(train_grads, query_grads, listed):
    shard_count = lax.axis_size("dp")
    layers = lax.axis_size("layer")
    own_index = lax.axis_index("dp").astype(jnp.int32)
    examples = train_grads.shape[0]
    per_query = query_grads.shape[0]
    train = train_grads.reshape(examples, train_grads.shape[2])
    own_queries = query_grads.reshape(per_query, query_grads.shape[2])
    total_count = float(examples * shard_count)
    order = jnp.arange(shard_count, dtype=jnp.int32)
    if shard_count <= 8:
        queries = [own_queries] + [exchange(own_queries, d, shard_count) for d in range(1, shard_count)]
        cov = covariance_sums(train)
        distance = 1
        while distance < shard_count:
            cov = cov + exchange(cov, distance, shard_count)
            distance = 2 * distance
        route = own_index ^ order
    else:
        queries = [lax.all_gather(own_queries, "dp", axis=0, tiled=True)]
        cov = lax.psum(covariance_sums(train), "dp")
        route = order
    turned = turned_queries(queries)
    scores = all_scores(route, cov, turned, train, per_query, total_count)
    outgoing = scores.reshape(shard_count * layers, per_query, examples // layers)
    received = lax.all_to_all(outgoing, ("dp", "layer"), split_axis=0, concat_axis=0, tiled=True)
    received = received.reshape(shard_count, layers, per_query, examples // layers)
    return picked(listed, received)


def solution(mesh):
    in_specs = (
        P(("groups", "dp"), "layer", None),
        P(("groups", "dp"), "layer", None),
        P(("groups", "dp"), None),
    )
    out_specs = P(("groups", "dp"), None, "layer")
    return jax.shard_map(shards, mesh=mesh, in_specs=in_specs, out_specs=out_specs, check_vma=False)
```

time: 159 us -> 49.2 us (0.31)
  blocking collectives: 87.1 us -> 11.3 us
  other arithmetic: 26.8 us -> 0.02 us
  between operations: 15 us -> 0.05 us
  starting transfers between devices: 3.39 us -> 17.4 us
  Pallas kernels: 0 us -> 13.3 us
  local copies, waits for them, and re-layouts: 8.32 us -> 1.6 us
  waiting for transfers between devices: 11.8 us -> 5.37 us
  matrix products: 5.95 us -> 0 us
    all_gather x2 -> x0, blocking collectives: 53.7 us -> none  [the longest x1 31.6 us: shards(): lax.all_gather(solved_own, 'dp', axis=0, tiled=True)]
    psum x1 -> x0, blocking collectives: 33.4 us -> none  [covariance_factors(): in_sum, out_sum = lax.psum((in_part, out_part), 'dp')]
    another operation x11 -> x0, other arithmetic: 24.3 us -> none  [the longest x6 13 us: damped_factors(): return (jnp.linalg.cholesky(in_damped), jnp.linalg.cholesky(out_damped))]
    ppermute x0 -> x10, starting transfers between devices: none -> 17.4 us  [exchange(): return lax.ppermute(values, 'dp', [(k, k ^ distance) for k in range(count)])]
    pallas_call x0 -> x4, Pallas kernels: none -> 13.3 us  [the longest x1 5.61 us: all_scores(): pl.pallas_call(functools.partial(score_kernel, total_count), out_shape=ja...]
    all_to_all x0 -> x1, blocking collectives: none -> 11.3 us  [shards(): lax.all_to_all(outgoing, ('dp', 'layer'), split_axis=0, concat_axis=0, ti...]
    all_to_all x1 -> x0, waiting for transfers between devices: 6.75 us -> none  [shards(): lax.all_to_all(outgoing, 'dp', split_axis=0, concat_axis=0, tiled=True)]
    ppermute x0 -> x10, waiting for transfers between devices: none -> 5.37 us  [exchange(): return lax.ppermute(values, 'dp', [(k, k ^ distance) for k in range(count)])]
  transfers between devices with their start and end apart: 2 -> 10, of which waited for: 2 -> 4; matrix products, arithmetic and copies ran while one was open for 0% -> 0% of each run, Pallas kernels for 0% -> 2%
where the time goes in v1:
time: 49.2 us; the launch traced here: 49 us
  starting transfers between devices  17.4 us (35%)
  Pallas kernels  13.3 us (27%)
  blocking collectives  11.3 us (23%)
  waiting for transfers between devices  5.37 us (11%)
  local copies, waits for them, and re-layouts  1.6 us (3%)
    ppermute x10, starting transfers between devices, exchange(): return lax.ppermute(values, 'dp', [(k, k ^ distance) for k in range(count)])  17.4 us
    all_to_all x1, blocking collectives, shards(): lax.all_to_all(outgoing, ('dp', 'layer'), split_axis=0, concat_axis=0, ti...  11.3 us
    pallas_call x1, Pallas kernels, all_scores(): pl.pallas_call(functools.partial(score_kernel, total_count), out_shape=ja...  5.61 us
    pallas_call x1, Pallas kernels, covariance_sums(): pl.pallas_call(covariance_kernel, out_shape=jax.ShapeDtypeStruct((K_OUT,...  5.51 us
    ppermute x10, waiting for transfers between devices, exchange(): return lax.ppermute(values, 'dp', [(k, k ^ distance) for k in range(count)])  5.37 us
    unnamed x8, local copies, waits for them, and re-layouts  1.6 us
    pallas_call x1, Pallas kernels, picked(): pl.pallas_call(pick_kernel, out_shape=jax.ShapeDtypeStruct((listed.shape[...  1.15 us
    pallas_call x1, Pallas kernels, turned_queries(): pl.pallas_call(turn_kernel, out_shape=jax.ShapeDtypeStruct((K_OUT, total...  1.04 us
  transfers between devices with their start and end apart: 10, of which 4 were waited for; matrix products, arithmetic and copies ran while one was open for 0% of the time, Pallas kernels for 2%

profile of v1, /device:TPU:0, one launch (start us, length us, event | category | flops | bytes accessed | tf_op | source)
XLA Modules:
  0.0 49.0 jit_solution(15465215272234893406)
XLA Ops:
  0.0 0.0 copy-start
  0.0 1.6 %copy-done = bf16[256,1,4096]{2,0,1:T(8,128)(2,1)S(1)} copy-done((bf16[256,1,4096]{2,0,1:T(8,128)(2,1)S(1)}, bf16[256,1,4096]{2,0,1:T(8,128)(2,1)}, u32[]{:S(2)}) %copy-start) | copy-done | bytes 2097176
  1.6 0.0 copy-start.2
  1.6 0.0 copy-start.1
  1.6 5.5 %covariance.1 = f32[64,128]{1,0:T(8,128)S(1)} custom-call(bf16[256,4096]{1,0:T(8,128)(2,1)S(1)} %bitcast.4), custom_call_target="tpu_custom_call" | custom-call | flops 268435456 | bytes 2097152 | tf_op jit(solution)/shard_map/covariance/pallas_call | solution.py:58
  7.1 3.0 %collective-permute-start = (f32[64,128]{1,0:T(8,128)S(1)}, f32[64,128]{1,0:T(8,128)S(1)}, u32[]{:S(2)}, u32[]{:S(2)}) collective-permute-start(f32[64,128]{1,0:T(8,128)S(1)} %covariance.1), channel_id=1, source_target_pairs={{0,2},{2,0},{4,6},{6,4},{8,10},{10,8},{12,14},{14,12},{1,3},{3,1},... | collective-permute-start | bytes 98312 | tf_op jit(solution)/shard_map/ppermute | solution.py:274
  10.1 0.0 copy-start.3
  10.1 0.1 collective-permute-start.3
  10.2 2.0 %collective-permute-start.4 = (bf16[8,4096]{1,0:T(8,128)(2,1)}, bf16[8,4096]{1,0:T(8,128)(2,1)S(1)}, u32[]{:S(2)}, u32[]{:S(2)}) collective-permute-start(bf16[8,4096]{1,0:T(8,128)(2,1)} %bitcast.9), channel_id=1, source_target_pairs={{0,4},{2,6},{4,0},{6,2},{8,12},{10,14},{12,8},{14,10},{1,5},{3,7},... | collective-permute-start | bytes 196616 | tf_op jit(solution)/shard_map/ppermute | solution.py:274
  12.2 1.4 %collective-permute-start.5 = (bf16[8,4096]{1,0:T(8,128)(2,1)}, bf16[8,4096]{1,0:T(8,128)(2,1)S(1)}, u32[]{:S(2)}, u32[]{:S(2)}) collective-permute-start(bf16[8,4096]{1,0:T(8,128)(2,1)} %bitcast.10), channel_id=1, source_target_pairs={{0,6},{2,4},{4,2},{6,0},{8,14},{10,12},{12,10},{14,8},{1,7},{3,5},... | collective-permute-start | bytes 196616 | tf_op jit(solution)/shard_map/ppermute | solution.py:274
  13.6 0.0 collective-permute-done
  13.6 1.6 %collective-permute-start.1 = (f32[64,128]{1,0:T(8,128)S(1)}, f32[64,128]{1,0:T(8,128)S(1)}, u32[]{:S(2)}, u32[]{:S(2)}) collective-permute-start(f32[64,128]{1,0:T(8,128)S(1)} %add.9), channel_id=1, source_target_pairs={{0,4},{2,6},{4,0},{6,2},{8,12},{10,14},{12,8},{14,10},{1,5},{3,7},... | collective-permute-start | bytes 98312 | tf_op jit(solution)/shard_map/ppermute | solution.py:274
  15.3 0.0 copy-done.2
  15.3 2.6 %collective-permute-start.6 = (bf16[8,4096]{1,0:T(8,128)(2,1)S(1)}, bf16[8,4096]{1,0:T(8,128)(2,1)S(1)}, u32[]{:S(2)}, u32[]{:S(2)}) collective-permute-start(bf16[8,4096]{1,0:T(8,128)(2,1)S(1)} %bitcast.11), channel_id=1, source_target_pairs={{0,8},{2,10},{4,12},{6,14},{8,0},{10,2},{12,4},{14,6},{1,9},{3,11}... | collective-permute-start | bytes 196616 | tf_op jit(solution)/shard_map/ppermute | solution.py:274
  17.9 0.8 %collective-permute-done.1 = f32[64,128]{1,0:T(8,128)S(1)} collective-permute-done((f32[64,128]{1,0:T(8,128)S(1)}, f32[64,128]{1,0:T(8,128)S(1)}, u32[]{:S(2)}, u32[]{:S(2)}) %collective-permute-start.1) | collective-permute-done | bytes 32800 | tf_op jit(solution)/shard_map/ppermute | solution.py:274
  18.7 2.3 %collective-permute-start.7 = (bf16[8,4096]{1,0:T(8,128)(2,1)S(1)}, bf16[8,4096]{1,0:T(8,128)(2,1)S(1)}, u32[]{:S(2)}, u32[]{:S(2)}) collective-permute-start(bf16[8,4096]{1,0:T(8,128)(2,1)S(1)} %bitcast.12), channel_id=1, source_target_pairs={{0,10},{2,8},{4,14},{6,12},{8,2},{10,0},{12,6},{14,4},{1,11},{3,9}... | collective-permute-start | bytes 196616 | tf_op jit(solution)/shard_map/ppermute | solution.py:274
  21.0 0.0 collective-permute-done.3.refs_1_
  21.0 0.8 %collective-permute-start.8 = (bf16[8,4096]{1,0:T(8,128)(2,1)S(1)}, bf16[8,4096]{1,0:T(8,128)(2,1)S(1)}, u32[]{:S(2)}, u32[]{:S(2)}) collective-permute-start(bf16[8,4096]{1,0:T(8,128)(2,1)S(1)} %bitcast.13), channel_id=1, source_target_pairs={{0,12},{2,14},{4,8},{6,10},{8,4},{10,6},{12,0},{14,2},{1,13},{3,15... | collective-permute-start | bytes 196616 | tf_op jit(solution)/shard_map/ppermute | solution.py:274
  21.9 0.0 collective-permute-done.4.refs_2_
  21.9 3.5 %collective-permute-start.9 = (bf16[8,4096]{1,0:T(8,128)(2,1)S(1)}, bf16[8,4096]{1,0:T(8,128)(2,1)S(1)}, u32[]{:S(2)}, u32[]{:S(2)}) collective-permute-start(bf16[8,4096]{1,0:T(8,128)(2,1)S(1)} %bitcast.14), channel_id=1, source_target_pairs={{0,14},{2,12},{4,10},{6,8},{8,6},{10,4},{12,2},{14,0},{1,15},{3,13... | collective-permute-start | bytes 196616 | tf_op jit(solution)/shard_map/ppermute | solution.py:274
  25.4 0.0 collective-permute-done.5.refs_3_
  25.4 0.0 collective-permute-start.2
  25.4 0.0 collective-permute-done.6.refs_4_
  25.4 2.7 %collective-permute-done.7.refs_5_ = bf16[8,4096]{1,0:T(8,128)(2,1)S(1)} collective-permute-done((bf16[8,4096]{1,0:T(8,128)(2,1)S(1)}, bf16[8,4096]{1,0:T(8,128)(2,1)S(1)}, u32[]{:S(2)}, u32[]{:S(2)}) %collective-permute-start.7) | collective-permute-done | bytes 65568 | tf_op jit(solution)/shard_map/ppermute | solution.py:274
  28.1 0.0 collective-permute-done.8.refs_6_
  28.1 0.8 %collective-permute-done.9.refs_7_ = bf16[8,4096]{1,0:T(8,128)(2,1)S(1)} collective-permute-done((bf16[8,4096]{1,0:T(8,128)(2,1)S(1)}, bf16[8,4096]{1,0:T(8,128)(2,1)S(1)}, u32[]{:S(2)}, u32[]{:S(2)}) %collective-permute-start.9) | collective-permute-done | bytes 65568 | tf_op jit(solution)/shard_map/ppermute | solution.py:274
  28.8 1.0 %turn_queries.1.turned_ref = bf16[64,4096]{1,0:T(8,128)(2,1)S(1)} custom-call(bf16[8,4096]{1,0:T(8,128)(2,1)S(1)} %bitcast.15, bf16[8,4096]{1,0:T(8,128)(2,1)S(1)} %collective-permute-done.3.refs_1_, bf16[8,4096]{1,0:T(8,128)(2,1)S(1)} %collective-permute-done.4.refs_2_, bf16[8,4096]{1,0:T(8,128)(2,1)S(1)} %collective-permute-done.5.refs_3_, ...), custom_call_target="tpu_custom_call" | custom-call | flops 262144 | bytes 1048576 | tf_op jit(solution)/shard_map/turn_queries/pallas_call | solution.py:100
  29.9 1.1 %collective-permute-done.2 = f32[64,128]{1,0:T(8,128)S(1)} collective-permute-done((f32[64,128]{1,0:T(8,128)S(1)}, f32[64,128]{1,0:T(8,128)S(1)}, u32[]{:S(2)}, u32[]{:S(2)}) %collective-permute-start.2) | collective-permute-done | bytes 32800 | tf_op jit(solution)/shard_map/ppermute | solution.py:274
  31.0 0.0 copy-done.1
  31.0 5.6 %solve_and_score.1 = f32[8,2,8,128]{3,2,1,0:T(8,128)S(1)} custom-call(s32[8]{0:T(128)S(1)} %iota_xor_fusion.route_ref, f32[64,128]{1,0:T(8,128)S(1)} %add.11.cov_ref, bf16[64,4096]{1,0:T(8,128)(2,1)S(1)} %turn_queries.1.turned_ref, bf16[256,4096]{1,0:T(8,128)(2,1)S(1)} %bitcast.5), custom_call_target="tpu_custom_call" | custom-call | flops 201326592 | bytes 2097152 | tf_op jit(solution)/shard_map/solve_and_score/pallas_call | solution.py:228
  36.6 11.3 %all_to_all.5 = f32[16,8,128]{2,1,0:T(8,128)S(1)} all-to-all(f32[16,8,128]{2,1,0:T(8,128)S(1)} %bitcast.6), channel_id=1, replica_groups=mesh['groups'=2,'dp'=8,'layer'=2] {'dp','layer'}, dimensions={0} | all-to-all | bytes 131072 | tf_op jit(solution)/shard_map/all_to_all | solution.py:302
  47.9 0.0 copy-done.3
  47.9 1.2 %pick_tiles.1 = f32[4,8,128]{2,1,0:T(8,128)} custom-call(s32[1,4]{1,0:T(1,128)S(1)} %copy-done.3, f32[8,2,8,128]{3,2,1,0:T(8,128)S(1)} %bitcast.7), custom_call_target="tpu_custom_call" | custom-call | tf_op jit(solution)/shard_map/pick_tiles/pallas_call | solution.py:263
  (4 shorter events, 0.0 us)
Async XLA Ops:
  0.0 1.6 %copy-start = (bf16[256,1,4096]{2,0,1:T(8,128)(2,1)S(1)}, bf16[256,1,4096]{2,0,1:T(8,128)(2,1)}, u32[]{:S(2)}) copy-start(bf16[256,1,4096]{2,0,1:T(8,128)(2,1)} %param.3) | copy-start | bytes 6291460
  1.6 13.7 %copy-start.2 = (bf16[8,1,4096]{2,0,1:T(8,128)(2,1)S(1)}, bf16[8,1,4096]{2,0,1:T(8,128)(2,1)}, u32[]{:S(2)}) copy-start(bf16[8,1,4096]{2,0,1:T(8,128)(2,1)} %param.4) | copy-start | bytes 196612
  1.6 29.4 %copy-start.1 = (bf16[256,1,4096]{2,0,1:T(8,128)(2,1)S(1)}, bf16[256,1,4096]{2,0,1:T(8,128)(2,1)}, u32[]{:S(2)}) copy-start(bf16[256,1,4096]{2,0,1:T(8,128)(2,1)} %param.3) | copy-start | bytes 6291460
  7.1 6.5 %collective-permute-start = (f32[64,128]{1,0:T(8,128)S(1)}, f32[64,128]{1,0:T(8,128)S(1)}, u32[]{:S(2)}, u32[]{:S(2)}) collective-permute-start(f32[64,128]{1,0:T(8,128)S(1)} %covariance.1), channel_id=1, source_target_pairs={{0,2},{2,0},{4,6},{6,4},{8,10},{10,8},{12,14},{14,12},{1,3},{3,1},... | collective-permute-start | bytes 98312 | tf_op jit(solution)/shard_map/ppermute | solution.py:274
  10.1 37.7 %copy-start.3 = (s32[1,4]{1,0:T(1,128)S(1)}, s32[1,4]{1,0:T(1,128)}, u32[]{:S(2)}) copy-start(s32[1,4]{1,0:T(1,128)} %listed_ref.1) | copy-start | bytes 52
  10.1 10.9 %collective-permute-start.3 = (bf16[8,4096]{1,0:T(8,128)(2,1)}, bf16[8,4096]{1,0:T(8,128)(2,1)S(1)}, u32[]{:S(2)}, u32[]{:S(2)}) collective-permute-start(bf16[8,4096]{1,0:T(8,128)(2,1)} %bitcast.8), channel_id=1, source_target_pairs={{0,2},{2,0},{4,6},{6,4},{8,10},{10,8},{12,14},{14,12},{1,3},{3,1},... | collective-permute-start | bytes 196616 | tf_op jit(solution)/shard_map/ppermute | solution.py:274
  10.2 11.7 %collective-permute-start.4 = (bf16[8,4096]{1,0:T(8,128)(2,1)}, bf16[8,4096]{1,0:T(8,128)(2,1)S(1)}, u32[]{:S(2)}, u32[]{:S(2)}) collective-permute-start(bf16[8,4096]{1,0:T(8,128)(2,1)} %bitcast.9), channel_id=1, source_target_pairs={{0,4},{2,6},{4,0},{6,2},{8,12},{10,14},{12,8},{14,10},{1,5},{3,7},... | collective-permute-start | bytes 196616 | tf_op jit(solution)/shard_map/ppermute | solution.py:274
  12.2 13.2 %collective-permute-start.5 = (bf16[8,4096]{1,0:T(8,128)(2,1)}, bf16[8,4096]{1,0:T(8,128)(2,1)S(1)}, u32[]{:S(2)}, u32[]{:S(2)}) collective-permute-start(bf16[8,4096]{1,0:T(8,128)(2,1)} %bitcast.10), channel_id=1, source_target_pairs={{0,6},{2,4},{4,2},{6,0},{8,14},{10,12},{12,10},{14,8},{1,7},{3,5},... | collective-permute-start | bytes 196616 | tf_op jit(solution)/shard_map/ppermute | solution.py:274
  13.6 5.1 %collective-permute-start.1 = (f32[64,128]{1,0:T(8,128)S(1)}, f32[64,128]{1,0:T(8,128)S(1)}, u32[]{:S(2)}, u32[]{:S(2)}) collective-permute-start(f32[64,128]{1,0:T(8,128)S(1)} %add.9), channel_id=1, source_target_pairs={{0,4},{2,6},{4,0},{6,2},{8,12},{10,14},{12,8},{14,10},{1,5},{3,7},... | collective-permute-start | bytes 98312 | tf_op jit(solution)/shard_map/ppermute | solution.py:274
  15.3 10.1 %collective-permute-start.6 = (bf16[8,4096]{1,0:T(8,128)(2,1)S(1)}, bf16[8,4096]{1,0:T(8,128)(2,1)S(1)}, u32[]{:S(2)}, u32[]{:S(2)}) collective-permute-start(bf16[8,4096]{1,0:T(8,128)(2,1)S(1)} %bitcast.11), channel_id=1, source_target_pairs={{0,8},{2,10},{4,12},{6,14},{8,0},{10,2},{12,4},{14,6},{1,9},{3,11}... | collective-permute-start | bytes 196616 | tf_op jit(solution)/shard_map/ppermute | solution.py:274
  18.7 9.4 %collective-permute-start.7 = (bf16[8,4096]{1,0:T(8,128)(2,1)S(1)}, bf16[8,4096]{1,0:T(8,128)(2,1)S(1)}, u32[]{:S(2)}, u32[]{:S(2)}) collective-permute-start(bf16[8,4096]{1,0:T(8,128)(2,1)S(1)} %bitcast.12), channel_id=1, source_target_pairs={{0,10},{2,8},{4,14},{6,12},{8,2},{10,0},{12,6},{14,4},{1,11},{3,9}... | collective-permute-start | bytes 196616 | tf_op jit(solution)/shard_map/ppermute | solution.py:274
  21.0 7.0 %collective-permute-start.8 = (bf16[8,4096]{1,0:T(8,128)(2,1)S(1)}, bf16[8,4096]{1,0:T(8,128)(2,1)S(1)}, u32[]{:S(2)}, u32[]{:S(2)}) collective-permute-start(bf16[8,4096]{1,0:T(8,128)(2,1)S(1)} %bitcast.13), channel_id=1, source_target_pairs={{0,12},{2,14},{4,8},{6,10},{8,4},{10,6},{12,0},{14,2},{1,13},{3,15... | collective-permute-start | bytes 196616 | tf_op jit(solution)/shard_map/ppermute | solution.py:274
  21.9 7.0 %collective-permute-start.9 = (bf16[8,4096]{1,0:T(8,128)(2,1)S(1)}, bf16[8,4096]{1,0:T(8,128)(2,1)S(1)}, u32[]{:S(2)}, u32[]{:S(2)}) collective-permute-start(bf16[8,4096]{1,0:T(8,128)(2,1)S(1)} %bitcast.14), channel_id=1, source_target_pairs={{0,14},{2,12},{4,10},{6,8},{8,6},{10,4},{12,2},{14,0},{1,15},{3,13... | collective-permute-start | bytes 196616 | tf_op jit(solution)/shard_map/ppermute | solution.py:274
  25.4 5.6 %collective-permute-start.2 = (f32[64,128]{1,0:T(8,128)S(1)}, f32[64,128]{1,0:T(8,128)S(1)}, u32[]{:S(2)}, u32[]{:S(2)}) collective-permute-start(f32[64,128]{1,0:T(8,128)S(1)} %add.10), channel_id=1, source_target_pairs={{0,8},{2,10},{4,12},{6,14},{8,0},{10,2},{12,4},{14,6},{1,9},{3,11}... | collective-permute-start | bytes 98312 | tf_op jit(solution)/shard_map/ppermute | solution.py:274

commit v2 on v1

--- a/solution.py
+++ b/solution.py
@@ -29,46 +29,87 @@
     return even, odd
 
 
-def covariance_kernel(train_ref, cov_ref, turned, by_in, by_out):
+def split(values, terms):
+    parts = []
+    for _ in range(terms):
+        part = values.astype(BF16)
+        parts.append(part)
+        values = values - part.astype(F32)
+    return parts
+
+
+def stage_kernel(train_ref, in_ref, rows_ref, held, by_in, arrived):
     examples, width = train_ref.shape
-    blocks = width // LANES
-    parts = examples // LANES
-    for c in range(blocks):
-        block = train_ref[:, c * LANES:(c + 1) * LANES].astype(F32).T
-        for part in range(parts):
-            piece = block[:, part * LANES:(part + 1) * LANES]
-            turned[part, c * LANES:(c + 1) * LANES, :] = piece
-        small = block.astype(BF16)
+    pair = 2 * LANES
+    chunks, _, chunk = held.shape
+    copies = []
+    for g in range(chunks):
+        source = train_ref.at[:, pl.ds(g * chunk, chunk)]
+        copies.append(pltpu.make_async_copy(source, held.at[g], arrived.at[g]))
+        copies[-1].start()
+    for m in range(width // pair):
+        if m * pair % chunk == 0:
+            copies[m * pair // chunk].wait()
+        begin = m * pair % chunk
+        block = held[m * pair // chunk, :, begin:begin + pair].astype(F32).T
+        for k in range(4):
+            start = (4 * m + k) * examples
+            by_in[:, start:start + examples] = block[k * K_IN:(k + 1) * K_IN, :].astype(BF16)
         for half in range(2):
-            start = (2 * c + half) * examples
-            by_in[:, start:start + examples] = small[half * K_IN:(half + 1) * K_IN, :]
-    for j in range(K_IN):
-        for part in range(parts):
-            start = j * examples + part * LANES
-            for half in range(2):
-                rows = turned[part, pl.ds(half * K_IN + j, blocks, stride=LANES), :]
-                by_out[half * blocks:(half + 1) * blocks, start:start + LANES] = rows.astype(BF16)
-    in_sum = lax.dot_general(by_in[...], by_in[...], NT, preferred_element_type=F32)
-    out_sum = lax.dot_general(by_out[...], by_out[...], NT, preferred_element_type=F32)
-    cov_ref[...] = jnp.concatenate([in_sum, out_sum], axis=1)
-
-
-def covariance_sums(train):
+            for j in range(K_IN // 8):
+                first = half * K_IN + j * 8
+                both = jnp.concatenate([block[first:first + 8, :], block[first + LANES:first + LANES + 8, :]], axis=0)
+                at = half * K_OUT // 2 * 8 + m * 16
+                rows_ref[at:at + 16, j * examples:(j + 1) * examples] = both.astype(BF16)
+    in_ref[...] = lax.dot_general(by_in[...], by_in[...], NT, preferred_element_type=F32)
+
+
+def gram_kernel(in_ref, rows_ref, cov_ref):
+    count = rows_ref.shape[0]
+    every = lax.dot_general(rows_ref[...], rows_ref[...], NT, preferred_element_type=F32)
+    row = lax.broadcasted_iota(jnp.int32, (count, count), 0)
+    lane = lax.broadcasted_iota(jnp.int32, (count, count), 1)
+    every = jnp.where((row & 7) == (lane & 7), every, 0.0)
+    summed = jnp.sum(every.reshape(count // 8, 8, count), axis=1)
+    lane = lax.broadcasted_iota(jnp.int32, (count, count // 8), 0)
+    column = lax.broadcasted_iota(jnp.int32, (count, count // 8), 1)
+    merge = jnp.where(lane // 8 == column, 1.0, 0.0).astype(BF16)
+    out_sum = sum(jnp.dot(part, merge, preferred_element_type=F32) for part in reversed(split(summed, 3)))
+    cov_ref[...] = jnp.concatenate([in_ref[...], out_sum], axis=1)
+
+
+def staged_rows(train):
     examples, width = train.shape
-    return pl.pallas_call(
-        covariance_kernel,
+    chunks = 8 if width % (8 * 2 * LANES) == 0 else 1
+    return pl.pallas_call(
+        stage_kernel,
+        out_shape=(
+            jax.ShapeDtypeStruct((K_IN, K_IN), F32),
+            jax.ShapeDtypeStruct((8 * K_OUT, K_IN // 8 * examples), BF16),
+        ),
+        in_specs=[pl.BlockSpec(memory_space=pltpu.HBM)],
+        out_specs=(pl.BlockSpec(memory_space=pltpu.VMEM), pl.BlockSpec(memory_space=pltpu.VMEM)),
+        scratch_shapes=[
+            pltpu.VMEM((chunks, examples, width // chunks), BF16),
+            pltpu.VMEM((K_IN, K_OUT * examples), BF16),
+            pltpu.SemaphoreType.DMA((chunks,)),
+        ],
+        compiler_params=pltpu.CompilerParams(vmem_limit_bytes=VMEM_LIMIT),
+        cost_estimate=pl.CostEstimate(flops=32 * examples * 64**3, bytes_accessed=2 * examples * width, transcendentals=0),
+        name="stage_rows",
+    )(train)
+
+
+def covariance_sums(in_sum, rows):
+    return pl.pallas_call(
+        gram_kernel,
         out_shape=jax.ShapeDtypeStruct((K_OUT, 2 * K_IN), F32),
-        in_specs=[pl.BlockSpec(memory_space=pltpu.VMEM)],
+        in_specs=[pl.BlockSpec(memory_space=pltpu.VMEM), pl.BlockSpec(memory_space=pltpu.VMEM)],
         out_specs=pl.BlockSpec(memory_space=pltpu.VMEM),
-        scratch_shapes=[
-            pltpu.VMEM((examples // LANES, width, LANES), F32),
-            pltpu.VMEM((K_IN, K_OUT * examples), BF16),
-            pltpu.VMEM((K_OUT, K_IN * examples), BF16),
-        ],
-        compiler_params=pltpu.CompilerParams(vmem_limit_bytes=VMEM_LIMIT),
-        cost_estimate=pl.CostEstimate(flops=4 * examples * 64**3, bytes_accessed=2 * examples * width, transcendentals=0),
+        compiler_params=pltpu.CompilerParams(vmem_limit_bytes=VMEM_LIMIT),
+        cost_estimate=pl.CostEstimate(flops=2 * rows.shape[0] * rows.size, bytes_accessed=2 * rows.size, transcendentals=0),
         name="covariance",
-    )(train)
+    )(in_sum, rows)
 
 
 def turn_kernel(*refs):
@@ -168,15 +209,6 @@
     return matrix
 
 
-def split(values, terms):
-    parts = []
-    for _ in range(terms):
-        part = values.astype(BF16)
-        parts.append(part)
-        values = values - part.astype(F32)
-    return parts
-
-
 def score_kernel(total_count, route_ref, cov_ref, turned_ref, train_ref, out_ref, left, right, solved, ready):
     blocks = K_OUT // 2
     half = CHUNK // 2
@@ -284,17 +316,26 @@
     own_queries = query_grads.reshape(per_query, query_grads.shape[2])
     total_count = float(examples * shard_count)
     order = jnp.arange(shard_count, dtype=jnp.int32)
-    if shard_count <= 8:
-        queries = [own_queries] + [exchange(own_queries, d, shard_count) for d in range(1, shard_count)]
-        cov = covariance_sums(train)
-        distance = 1
-        while distance < shard_count:
+    if shard_count == 8:
+        queries = {0: own_queries}
+        queries[4] = exchange(queries[0], 4, shard_count)
+        queries[1] = exchange(queries[0], 1, shard_count)
+        in_sum, rows = staged_rows(train)
+        queries[4], queries[1], in_sum = lax.optimization_barrier((queries[4], queries[1], in_sum))
+        queries[2] = exchange(queries[0], 2, shard_count)
+        queries[6] = exchange(queries[4], 2, shard_count)
+        queries[5] = exchange(queries[4], 1, shard_count)
+        cov = covariance_sums(in_sum, rows)
+        queries[2], queries[6], cov = lax.optimization_barrier((queries[2], queries[6], cov))
+        queries[3] = exchange(queries[2], 1, shard_count)
+        queries[7] = exchange(queries[6], 1, shard_count)
+        for distance in (4, 2, 1):
             cov = cov + exchange(cov, distance, shard_count)
-            distance = 2 * distance
+        queries = [queries[d] for d in range(shard_count)]
         route = own_index ^ order
     else:
         queries = [lax.all_gather(own_queries, "dp", axis=0, tiled=True)]
-        cov = lax.psum(covariance_sums(train), "dp")
+        cov = lax.psum(covariance_sums(*staged_rows(train)), "dp")
         route = order
     turned = turned_queries(queries)
     scores = all_scores(route, cov, turned, train, per_query, total_count)

time: 49.2 us -> 44.7 us (0.909)
  starting transfers between devices: 17.4 us -> 11.4 us
  waiting for transfers between devices: 5.37 us -> 9.75 us
  blocking collectives: 11.3 us -> 9.76 us
  Pallas kernels: 13.3 us -> 11.9 us
    ppermute x10, starting transfers between devices: 17.4 us -> 11.4 us  [exchange(): return lax.ppermute(values, 'dp', [(k, k ^ distance) for k in range(count)])]
    ppermute x10, waiting for transfers between devices: 5.37 us -> 9.75 us  [exchange(): return lax.ppermute(values, 'dp', [(k, k ^ distance) for k in range(count)])]
    all_to_all x1, blocking collectives: 11.3 us -> 9.76 us  [shards(): lax.all_to_all(outgoing, ('dp', 'layer'), split_axis=0, concat_axis=0, ti...]
    pallas_call x1 -> x2, Pallas kernels: 5.51 us -> 4.07 us  [the longest x1 2.16 us: covariance_sums(): pl.pallas_call(gram_kernel, out_shape=jax.ShapeDtypeStruct((K_OUT, 2 * K_...]
  transfers between devices with their start and end apart: 10 -> 10, of which waited for: 4 -> 6; matrix products, arithmetic and copies ran while one was open for 0% -> 0% of each run, Pallas kernels for 2% -> 11%
where the time goes in v2:
time: 44.7 us; the launch traced here: 44.5 us
  Pallas kernels  11.9 us (27%)
  starting transfers between devices  11.4 us (26%)
  blocking collectives  9.76 us (22%)
  waiting for transfers between devices  9.75 us (22%)
  local copies, waits for them, and re-layouts  1.6 us (4%)
    ppermute x10, starting transfers between devices, exchange(): return lax.ppermute(values, 'dp', [(k, k ^ distance) for k in range(count)])  11.4 us
    all_to_all x1, blocking collectives, shards(): lax.all_to_all(outgoing, ('dp', 'layer'), split_axis=0, concat_axis=0, ti...  9.76 us
    ppermute x10, waiting for transfers between devices, exchange(): return lax.ppermute(values, 'dp', [(k, k ^ distance) for k in range(count)])  9.75 us
    pallas_call x1, Pallas kernels, all_scores(): pl.pallas_call(functools.partial(score_kernel, total_count), out_shape=ja...  5.6 us
    pallas_call x1, Pallas kernels, covariance_sums(): pl.pallas_call(gram_kernel, out_shape=jax.ShapeDtypeStruct((K_OUT, 2 * K_...  2.16 us
    pallas_call x1, Pallas kernels, staged_rows(): pl.pallas_call(stage_kernel, out_shape=(jax.ShapeDtypeStruct((K_IN, K_IN)...  1.91 us
    unnamed x8, local copies, waits for them, and re-layouts  1.6 us
    pallas_call x1, Pallas kernels, picked(): pl.pallas_call(pick_kernel, out_shape=jax.ShapeDtypeStruct((listed.shape[...  1.15 us
  transfers between devices with their start and end apart: 10, of which 6 were waited for; matrix products, arithmetic and copies ran while one was open for 0% of the time, Pallas kernels for 11%

profile of v2, /device:TPU:0, one launch (start us, length us, event | category | flops | bytes accessed | tf_op | source)
XLA Modules:
  0.0 44.5 jit_solution(13061873341655129198)
XLA Ops:
  0.0 4.0 %collective-permute-start.1 = (bf16[8,4096]{1,0:T(8,128)(2,1)}, bf16[8,4096]{1,0:T(8,128)(2,1)S(1)}, u32[]{:S(2)}, u32[]{:S(2)}) collective-permute-start(bf16[8,4096]{1,0:T(8,128)(2,1)} %bitcast.8), channel_id=1, source_target_pairs={{0,8},{2,10},{4,12},{6,14},{8,0},{10,2},{12,4},{14,6},{1,9},{3,11}... | collective-permute-start | bytes 196616 | tf_op jit(solution)/shard_map/ppermute | solution.py:306
  4.0 1.5 %collective-permute-start.2 = (bf16[8,4096]{1,0:T(8,128)(2,1)}, bf16[8,4096]{1,0:T(8,128)(2,1)S(1)}, u32[]{:S(2)}, u32[]{:S(2)}) collective-permute-start(bf16[8,4096]{1,0:T(8,128)(2,1)} %bitcast.9), channel_id=1, source_target_pairs={{0,2},{2,0},{4,6},{6,4},{8,10},{10,8},{12,14},{14,12},{1,3},{3,1},... | collective-permute-start | bytes 196616 | tf_op jit(solution)/shard_map/ppermute | solution.py:306
  5.5 1.6 %collective-permute-start = (bf16[8,4096]{1,0:T(8,128)(2,1)}, bf16[8,4096]{1,0:T(8,128)(2,1)S(1)}, u32[]{:S(2)}, u32[]{:S(2)}) collective-permute-start(bf16[8,4096]{1,0:T(8,128)(2,1)} %bitcast.10), channel_id=1, source_target_pairs={{0,4},{2,6},{4,0},{6,2},{8,12},{10,14},{12,8},{14,10},{1,5},{3,7},... | collective-permute-start | bytes 196616 | tf_op jit(solution)/shard_map/ppermute | solution.py:306
  7.1 0.0 copy-start
  7.1 1.6 %copy-done = bf16[256,1,4096]{2,0,1:T(8,128)(2,1)S(1)} copy-done((bf16[256,1,4096]{2,0,1:T(8,128)(2,1)S(1)}, bf16[256,1,4096]{2,0,1:T(8,128)(2,1)}, u32[]{:S(2)}) %copy-start) | copy-done | bytes 2097176
  8.7 1.9 %stage_rows.1 = (f32[64,64]{1,0:T(8,128)S(1)}, bf16[512,2048]{1,0:T(8,128)(2,1)S(1)}) custom-call(bf16[256,4096]{1,0:T(8,128)(2,1)S(1)} %bitcast.4), custom_call_target="tpu_custom_call" | custom-call | flops 2147483648 | bytes 2097152 | tf_op jit(solution)/shard_map/stage_rows/pallas_call | solution.py:84
  10.6 0.0 copy-start.2
  10.6 0.0 collective-permute-done.1.refs_4_
  10.6 0.0 collective-permute-done.2.refs_1_
  10.6 0.5 %collective-permute-start.3 = (bf16[8,4096]{1,0:T(8,128)(2,1)S(1)}, bf16[8,4096]{1,0:T(8,128)(2,1)S(1)}, u32[]{:S(2)}, u32[]{:S(2)}) collective-permute-start(bf16[8,4096]{1,0:T(8,128)(2,1)S(1)} %collective-permute-done.1.refs_4_), channel_id=1, source_target_pairs={{0,4},{2,6},{4,0},{6,2},{8,12},{10,14},{12,8},{14,10},{1,5},{3,7},... | collective-permute-start | bytes 196616 | tf_op jit(solution)/shard_map/ppermute | solution.py:306
  11.2 0.0 copy-start.1
  11.2 2.2 %covariance.1 = f32[64,128]{1,0:T(8,128)S(1)} custom-call(f32[64,64]{1,0:T(8,128)S(1)} %get-tuple-element.15.in_ref, bf16[512,2048]{1,0:T(8,128)(2,1)S(1)} %get-tuple-element.16.rows_ref), custom_call_target="tpu_custom_call" | custom-call | flops 1073741824 | bytes 2097152 | tf_op jit(solution)/shard_map/covariance/pallas_call | solution.py:104
  13.3 0.0 copy-start.3
  13.3 0.0 collective-permute-done.refs_2_
  13.3 1.6 %collective-permute-done.3.refs_6_ = bf16[8,4096]{1,0:T(8,128)(2,1)S(1)} collective-permute-done((bf16[8,4096]{1,0:T(8,128)(2,1)S(1)}, bf16[8,4096]{1,0:T(8,128)(2,1)S(1)}, u32[]{:S(2)}, u32[]{:S(2)}) %collective-permute-start.3) | collective-permute-done | bytes 65568 | tf_op jit(solution)/shard_map/ppermute | solution.py:306
  15.0 0.3 collective-permute-start.4
  15.3 4.8 %collective-permute-done.4 = f32[64,128]{1,0:T(8,128)S(1)} collective-permute-done((f32[64,128]{1,0:T(8,128)S(1)}, f32[64,128]{1,0:T(8,128)S(1)}, u32[]{:S(2)}, u32[]{:S(2)}) %collective-permute-start.4) | collective-permute-done | bytes 32800 | tf_op jit(solution)/shard_map/ppermute | solution.py:306
  20.1 0.5 %collective-permute-start.5 = (f32[64,128]{1,0:T(8,128)S(1)}, f32[64,128]{1,0:T(8,128)S(1)}, u32[]{:S(2)}, u32[]{:S(2)}) collective-permute-start(f32[64,128]{1,0:T(8,128)S(1)} %add.9), channel_id=1, source_target_pairs={{0,4},{2,6},{4,0},{6,2},{8,12},{10,14},{12,8},{14,10},{1,5},{3,7},... | collective-permute-start | bytes 98312 | tf_op jit(solution)/shard_map/ppermute | solution.py:306
  20.6 0.2 collective-permute-start.8
  20.8 1.8 %collective-permute-start.7 = (bf16[8,4096]{1,0:T(8,128)(2,1)S(1)}, bf16[8,4096]{1,0:T(8,128)(2,1)S(1)}, u32[]{:S(2)}, u32[]{:S(2)}) collective-permute-start(bf16[8,4096]{1,0:T(8,128)(2,1)S(1)} %collective-permute-done.refs_2_), channel_id=1, source_target_pairs={{0,2},{2,0},{4,6},{6,4},{8,10},{10,8},{12,14},{14,12},{1,3},{3,1},... | collective-permute-start | bytes 196616 | tf_op jit(solution)/shard_map/ppermute | solution.py:306
  22.6 0.2 collective-permute-start.9
  22.8 1.2 %collective-permute-done.5 = f32[64,128]{1,0:T(8,128)S(1)} collective-permute-done((f32[64,128]{1,0:T(8,128)S(1)}, f32[64,128]{1,0:T(8,128)S(1)}, u32[]{:S(2)}, u32[]{:S(2)}) %collective-permute-start.5) | collective-permute-done | bytes 32800 | tf_op jit(solution)/shard_map/ppermute | solution.py:306
  24.0 0.7 %collective-permute-start.6 = (f32[64,128]{1,0:T(8,128)S(1)}, f32[64,128]{1,0:T(8,128)S(1)}, u32[]{:S(2)}, u32[]{:S(2)}) collective-permute-start(f32[64,128]{1,0:T(8,128)S(1)} %add.10), channel_id=1, source_target_pairs={{0,2},{2,0},{4,6},{6,4},{8,10},{10,8},{12,14},{14,12},{1,3},{3,1},... | collective-permute-start | bytes 98312 | tf_op jit(solution)/shard_map/ppermute | solution.py:306
  24.7 0.1 collective-permute-done.8.refs_5_
  24.9 0.7 %collective-permute-done.7.refs_3_ = bf16[8,4096]{1,0:T(8,128)(2,1)S(1)} collective-permute-done((bf16[8,4096]{1,0:T(8,128)(2,1)S(1)}, bf16[8,4096]{1,0:T(8,128)(2,1)S(1)}, u32[]{:S(2)}, u32[]{:S(2)}) %collective-permute-start.7) | collective-permute-done | bytes 65568 | tf_op jit(solution)/shard_map/ppermute | solution.py:306
  25.6 1.3 %collective-permute-done.9.refs_7_ = bf16[8,4096]{1,0:T(8,128)(2,1)S(1)} collective-permute-done((bf16[8,4096]{1,0:T(8,128)(2,1)S(1)}, bf16[8,4096]{1,0:T(8,128)(2,1)S(1)}, u32[]{:S(2)}, u32[]{:S(2)}) %collective-permute-start.9) | collective-permute-done | bytes 65568 | tf_op jit(solution)/shard_map/ppermute | solution.py:306
  26.9 0.0 copy-done.2
  26.9 1.0 %turn_queries.1.turned_ref = bf16[64,4096]{1,0:T(8,128)(2,1)S(1)} custom-call(bf16[8,4096]{1,0:T(8,128)(2,1)S(1)} %bitcast.11, bf16[8,4096]{1,0:T(8,128)(2,1)S(1)} %collective-permute-done.2.refs_1_, bf16[8,4096]{1,0:T(8,128)(2,1)S(1)} %collective-permute-done.refs_2_, bf16[8,4096]{1,0:T(8,128)(2,1)S(1)} %collective-permute-done.7.refs_3_, ...), custom_call_target="tpu_custom_call" | custom-call | flops 262144 | bytes 1048576 | tf_op jit(solution)/shard_map/turn_queries/pallas_call | solution.py:141
  27.9 0.0 collective-permute-done.6
  27.9 0.0 copy-done.1
  28.0 5.6 %solve_and_score.1 = f32[8,2,8,128]{3,2,1,0:T(8,128)S(1)} custom-call(s32[8]{0:T(128)S(1)} %iota_xor_fusion.route_ref, f32[64,128]{1,0:T(8,128)S(1)} %add.11.cov_ref, bf16[64,4096]{1,0:T(8,128)(2,1)S(1)} %turn_queries.1.turned_ref, bf16[256,4096]{1,0:T(8,128)(2,1)S(1)} %bitcast.5), custom_call_target="tpu_custom_call" | custom-call | flops 201326592 | bytes 2097152 | tf_op jit(solution)/shard_map/solve_and_score/pallas_call | solution.py:260
  33.6 9.8 %all_to_all.5 = f32[16,8,128]{2,1,0:T(8,128)S(1)} all-to-all(f32[16,8,128]{2,1,0:T(8,128)S(1)} %bitcast.6), channel_id=1, replica_groups=mesh['groups'=2,'dp'=8,'layer'=2] {'dp','layer'}, dimensions={0} | all-to-all | bytes 131072 | tf_op jit(solution)/shard_map/all_to_all | solution.py:343
  43.3 0.0 copy-done.3
  43.3 1.2 %pick_tiles.1 = f32[4,8,128]{2,1,0:T(8,128)} custom-call(s32[1,4]{1,0:T(1,128)S(1)} %copy-done.3, f32[8,2,8,128]{3,2,1,0:T(8,128)S(1)} %bitcast.7), custom_call_target="tpu_custom_call" | custom-call | tf_op jit(solution)/shard_map/pick_tiles/pallas_call | solution.py:295
  (4 shorter events, 0.0 us)
Async XLA Ops:
  0.0 10.6 %collective-permute-start.1 = (bf16[8,4096]{1,0:T(8,128)(2,1)}, bf16[8,4096]{1,0:T(8,128)(2,1)S(1)}, u32[]{:S(2)}, u32[]{:S(2)}) collective-permute-start(bf16[8,4096]{1,0:T(8,128)(2,1)} %bitcast.8), channel_id=1, source_target_pairs={{0,8},{2,10},{4,12},{6,14},{8,0},{10,2},{12,4},{14,6},{1,9},{3,11}... | collective-permute-start | bytes 196616 | tf_op jit(solution)/shard_map/ppermute | solution.py:306
  4.0 6.6 %collective-permute-start.2 = (bf16[8,4096]{1,0:T(8,128)(2,1)}, bf16[8,4096]{1,0:T(8,128)(2,1)S(1)}, u32[]{:S(2)}, u32[]{:S(2)}) collective-permute-start(bf16[8,4096]{1,0:T(8,128)(2,1)} %bitcast.9), channel_id=1, source_target_pairs={{0,2},{2,0},{4,6},{6,4},{8,10},{10,8},{12,14},{14,12},{1,3},{3,1},... | collective-permute-start | bytes 196616 | tf_op jit(solution)/shard_map/ppermute | solution.py:306
  5.5 7.8 %collective-permute-start = (bf16[8,4096]{1,0:T(8,128)(2,1)}, bf16[8,4096]{1,0:T(8,128)(2,1)S(1)}, u32[]{:S(2)}, u32[]{:S(2)}) collective-permute-start(bf16[8,4096]{1,0:T(8,128)(2,1)} %bitcast.10), channel_id=1, source_target_pairs={{0,4},{2,6},{4,0},{6,2},{8,12},{10,14},{12,8},{14,10},{1,5},{3,7},... | collective-permute-start | bytes 196616 | tf_op jit(solution)/shard_map/ppermute | solution.py:306
  7.1 1.6 %copy-start = (bf16[256,1,4096]{2,0,1:T(8,128)(2,1)S(1)}, bf16[256,1,4096]{2,0,1:T(8,128)(2,1)}, u32[]{:S(2)}) copy-start(bf16[256,1,4096]{2,0,1:T(8,128)(2,1)} %param.3) | copy-start | bytes 6291460
  10.6 16.3 %copy-start.2 = (bf16[8,1,4096]{2,0,1:T(8,128)(2,1)S(1)}, bf16[8,1,4096]{2,0,1:T(8,128)(2,1)}, u32[]{:S(2)}) copy-start(bf16[8,1,4096]{2,0,1:T(8,128)(2,1)} %param.4) | copy-start | bytes 196612
  10.6 4.3 %collective-permute-start.3 = (bf16[8,4096]{1,0:T(8,128)(2,1)S(1)}, bf16[8,4096]{1,0:T(8,128)(2,1)S(1)}, u32[]{:S(2)}, u32[]{:S(2)}) collective-permute-start(bf16[8,4096]{1,0:T(8,128)(2,1)S(1)} %collective-permute-done.1.refs_4_), channel_id=1, source_target_pairs={{0,4},{2,6},{4,0},{6,2},{8,12},{10,14},{12,8},{14,10},{1,5},{3,7},... | collective-permute-start | bytes 196616 | tf_op jit(solution)/shard_map/ppermute | solution.py:306
  11.2 16.8 %copy-start.1 = (bf16[256,1,4096]{2,0,1:T(8,128)(2,1)S(1)}, bf16[256,1,4096]{2,0,1:T(8,128)(2,1)}, u32[]{:S(2)}) copy-start(bf16[256,1,4096]{2,0,1:T(8,128)(2,1)} %param.3) | copy-start | bytes 6291460
  13.3 30.0 %copy-start.3 = (s32[1,4]{1,0:T(1,128)S(1)}, s32[1,4]{1,0:T(1,128)}, u32[]{:S(2)}) copy-start(s32[1,4]{1,0:T(1,128)} %listed_ref.1) | copy-start | bytes 52
  15.0 5.1 %collective-permute-start.4 = (f32[64,128]{1,0:T(8,128)S(1)}, f32[64,128]{1,0:T(8,128)S(1)}, u32[]{:S(2)}, u32[]{:S(2)}) collective-permute-start(f32[64,128]{1,0:T(8,128)S(1)} %covariance.1), channel_id=1, source_target_pairs={{0,8},{2,10},{4,12},{6,14},{8,0},{10,2},{12,4},{14,6},{1,9},{3,11}... | collective-permute-start | bytes 98312 | tf_op jit(solution)/shard_map/ppermute | solution.py:306
  20.1 3.9 %collective-permute-start.5 = (f32[64,128]{1,0:T(8,128)S(1)}, f32[64,128]{1,0:T(8,128)S(1)}, u32[]{:S(2)}, u32[]{:S(2)}) collective-permute-start(f32[64,128]{1,0:T(8,128)S(1)} %add.9), channel_id=1, source_target_pairs={{0,4},{2,6},{4,0},{6,2},{8,12},{10,14},{12,8},{14,10},{1,5},{3,7},... | collective-permute-start | bytes 98312 | tf_op jit(solution)/shard_map/ppermute | solution.py:306
  20.6 4.3 %collective-permute-start.8 = (bf16[8,4096]{1,0:T(8,128)(2,1)S(1)}, bf16[8,4096]{1,0:T(8,128)(2,1)S(1)}, u32[]{:S(2)}, u32[]{:S(2)}) collective-permute-start(bf16[8,4096]{1,0:T(8,128)(2,1)S(1)} %collective-permute-done.1.refs_4_), channel_id=1, source_target_pairs={{0,2},{2,0},{4,6},{6,4},{8,10},{10,8},{12,14},{14,12},{1,3},{3,1},... | collective-permute-start | bytes 196616 | tf_op jit(solution)/shard_map/ppermute | solution.py:306
  20.8 4.7 %collective-permute-start.7 = (bf16[8,4096]{1,0:T(8,128)(2,1)S(1)}, bf16[8,4096]{1,0:T(8,128)(2,1)S(1)}, u32[]{:S(2)}, u32[]{:S(2)}) collective-permute-start(bf16[8,4096]{1,0:T(8,128)(2,1)S(1)} %collective-permute-done.refs_2_), channel_id=1, source_target_pairs={{0,2},{2,0},{4,6},{6,4},{8,10},{10,8},{12,14},{14,12},{1,3},{3,1},... | collective-permute-start | bytes 196616 | tf_op jit(solution)/shard_map/ppermute | solution.py:306
  22.6 4.3 %collective-permute-start.9 = (bf16[8,4096]{1,0:T(8,128)(2,1)S(1)}, bf16[8,4096]{1,0:T(8,128)(2,1)S(1)}, u32[]{:S(2)}, u32[]{:S(2)}) collective-permute-start(bf16[8,4096]{1,0:T(8,128)(2,1)S(1)} %collective-permute-done.3.refs_6_), channel_id=1, source_target_pairs={{0,2},{2,0},{4,6},{6,4},{8,10},{10,8},{12,14},{14,12},{1,3},{3,1},... | collective-permute-start | bytes 196616 | tf_op jit(solution)/shard_map/ppermute | solution.py:306
  24.0 3.9 %collective-permute-start.6 = (f32[64,128]{1,0:T(8,128)S(1)}, f32[64,128]{1,0:T(8,128)S(1)}, u32[]{:S(2)}, u32[]{:S(2)}) collective-permute-start(f32[64,128]{1,0:T(8,128)S(1)} %add.10), channel_id=1, source_target_pairs={{0,2},{2,0},{4,6},{6,4},{8,10},{10,8},{12,14},{14,12},{1,3},{3,1},... | collective-permute-start | bytes 98312 | tf_op jit(solution)/shard_map/ppermute | solution.py:306

commit v3 on v2

--- a/solution.py
+++ b/solution.py
@@ -14,6 +14,7 @@
 F32 = jnp.float32
 BF16 = jnp.bfloat16
 VMEM_LIMIT = 48 * 1024 * 1024
+STAGE_VMEM_LIMIT = 50 * 1024 * 1024
 
 NT = (((1,), (1,)), ((), ()))
 
@@ -94,7 +95,7 @@
             pltpu.VMEM((K_IN, K_OUT * examples), BF16),
             pltpu.SemaphoreType.DMA((chunks,)),
         ],
-        compiler_params=pltpu.CompilerParams(vmem_limit_bytes=VMEM_LIMIT),
+        compiler_params=pltpu.CompilerParams(vmem_limit_bytes=STAGE_VMEM_LIMIT),
         cost_estimate=pl.CostEstimate(flops=32 * examples * 64**3, bytes_accessed=2 * examples * width, transcendentals=0),
         name="stage_rows",
     )(train)
@@ -146,7 +147,7 @@
         out_specs=pl.BlockSpec((K_OUT, CHUNK * K_IN), lambda step: (0, step)),
         scratch_shapes=[pltpu.VMEM((width // LANES * CHUNK, LANES), F32)],
         compiler_params=pltpu.CompilerParams(vmem_limit_bytes=VMEM_LIMIT),
-        cost_estimate=pl.CostEstimate(flops=total * width, bytes_accessed=4 * total * width, transcendentals=0),
+        cost_estimate=pl.CostEstimate(flops=4096 * total * width, bytes_accessed=4 * total * width, transcendentals=0),
         name="turn_queries",
     )(*queries)
 
@@ -317,27 +318,26 @@
     total_count = float(examples * shard_count)
     order = jnp.arange(shard_count, dtype=jnp.int32)
     if shard_count == 8:
-        queries = {0: own_queries}
-        queries[4] = exchange(queries[0], 4, shard_count)
-        queries[1] = exchange(queries[0], 1, shard_count)
+        quarter = exchange(own_queries, 4, shard_count)
         in_sum, rows = staged_rows(train)
-        queries[4], queries[1], in_sum = lax.optimization_barrier((queries[4], queries[1], in_sum))
-        queries[2] = exchange(queries[0], 2, shard_count)
-        queries[6] = exchange(queries[4], 2, shard_count)
-        queries[5] = exchange(queries[4], 1, shard_count)
+        quarter, in_sum = lax.optimization_barrier((quarter, in_sum))
+        column = jnp.concatenate([own_queries, quarter], axis=0)
+        other = exchange(column, 2, shard_count)
         cov = covariance_sums(in_sum, rows)
-        queries[2], queries[6], cov = lax.optimization_barrier((queries[2], queries[6], cov))
-        queries[3] = exchange(queries[2], 1, shard_count)
-        queries[7] = exchange(queries[6], 1, shard_count)
-        for distance in (4, 2, 1):
+        other, cov = lax.optimization_barrier((other, cov))
+        column = jnp.concatenate([column, other], axis=0)
+        queries = [column, exchange(column, 1, shard_count)]
+        for distance in (1, 4):
             cov = cov + exchange(cov, distance, shard_count)
-        queries = [queries[d] for d in range(shard_count)]
+        last = exchange(cov, 2, shard_count)
+        turned, cov = lax.optimization_barrier((turned_queries(queries), cov))
+        cov = cov + last
+        order = jnp.array([0, 4, 2, 6, 1, 5, 3, 7], jnp.int32)
         route = own_index ^ order
     else:
-        queries = [lax.all_gather(own_queries, "dp", axis=0, tiled=True)]
+        turned = turned_queries([lax.all_gather(own_queries, "dp", axis=0, tiled=True)])
         cov = lax.psum(covariance_sums(*staged_rows(train)), "dp")
         route = order
-    turned = turned_queries(queries)
     scores = all_scores(route, cov, turned, train, per_query, total_count)
     outgoing = scores.reshape(shard_count * layers, per_query, examples // layers)
     received = lax.all_to_all(outgoing, ("dp", "layer"), split_axis=0, concat_axis=0, tiled=True)

time: 44.7 us -> 49.4 us (1.11)
  blocking collectives: 9.76 us -> 13.1 us
  local copies, waits for them, and re-layouts: 1.6 us -> 0.01 us
  waiting for transfers between devices: 9.75 us -> 11.3 us
  Pallas kernels: 11.9 us -> 12.7 us
  starting transfers between devices: 11.4 us -> 11.9 us
    all_to_all x1, blocking collectives: 9.76 us -> 13.1 us  [shards(): lax.all_to_all(outgoing, ('dp', 'layer'), split_axis=0, concat_axis=0, ti...]
    unnamed x8, local copies, waits for them, and re-layouts: 1.6 us -> 0.01 us
    ppermute x10 -> x6, waiting for transfers between devices: 9.75 us -> 11.3 us  [exchange(): return lax.ppermute(values, 'dp', [(k, k ^ distance) for k in range(count)])]
    pallas_call x1, Pallas kernels: 1.91 us -> 2.73 us  [staged_rows(): pl.pallas_call(stage_kernel, out_shape=(jax.ShapeDtypeStruct((K_IN, K_IN)...]
    ppermute x10 -> x6, starting transfers between devices: 11.4 us -> 11.9 us  [exchange(): return lax.ppermute(values, 'dp', [(k, k ^ distance) for k in range(count)])]
  transfers between devices with their start and end apart: 10 -> 6, of which waited for: 6 -> 5; matrix products, arithmetic and copies ran while one was open for 0% -> 0% of each run, Pallas kernels for 11% -> 12%
where the time goes in v3:
time: 49.4 us; the launch traced here: 49.2 us
  blocking collectives  13.1 us (27%)
  Pallas kernels  12.7 us (26%)
  starting transfers between devices  11.9 us (24%)
  waiting for transfers between devices  11.3 us (23%)
    all_to_all x1, blocking collectives, shards(): lax.all_to_all(outgoing, ('dp', 'layer'), split_axis=0, concat_axis=0, ti...  13.1 us
    ppermute x6, starting transfers between devices, exchange(): return lax.ppermute(values, 'dp', [(k, k ^ distance) for k in range(count)])  11.9 us
    ppermute x6, waiting for transfers between devices, exchange(): return lax.ppermute(values, 'dp', [(k, k ^ distance) for k in range(count)])  11.3 us
    pallas_call x1, Pallas kernels, all_scores(): pl.pallas_call(functools.partial(score_kernel, total_count), out_shape=ja...  5.65 us
    pallas_call x1, Pallas kernels, staged_rows(): pl.pallas_call(stage_kernel, out_shape=(jax.ShapeDtypeStruct((K_IN, K_IN)...  2.73 us
    pallas_call x1, Pallas kernels, covariance_sums(): pl.pallas_call(gram_kernel, out_shape=jax.ShapeDtypeStruct((K_OUT, 2 * K_...  2.16 us
    pallas_call x1, Pallas kernels, picked(): pl.pallas_call(pick_kernel, out_shape=jax.ShapeDtypeStruct((listed.shape[...  1.15 us
    pallas_call x1, Pallas kernels, turned_queries(): pl.pallas_call(turn_kernel, out_shape=jax.ShapeDtypeStruct((K_OUT, total...  1.04 us
  transfers between devices with their start and end apart: 6, of which 5 were waited for; matrix products, arithmetic and copies ran while one was open for 0% of the time, Pallas kernels for 12%

profile of v3, /device:TPU:0, one launch (start us, length us, event | category | flops | bytes accessed | tf_op | source)
XLA Modules:
  0.0 49.2 jit_solution(12798770842900191883)
XLA Ops:
  0.0 4.0 %collective-permute-start = (bf16[8,4096]{1,0:T(8,128)(2,1)}, bf16[8,4096]{1,0:T(8,128)(2,1)S(1)}, u32[]{:S(2)}, u32[]{:S(2)}) collective-permute-start(bf16[8,4096]{1,0:T(8,128)(2,1)} %bitcast.8), channel_id=1, source_target_pairs={{0,8},{2,10},{4,12},{6,14},{8,0},{10,2},{12,4},{14,6},{1,9},{3,11}... | collective-permute-start | bytes 196616 | tf_op jit(solution)/shard_map/ppermute | solution.py:307
  4.0 0.0 copy-start.2
  4.0 2.7 %stage_rows.1 = (f32[64,64]{1,0:T(8,128)S(1)}, bf16[512,2048]{1,0:T(8,128)(2,1)S(1)}) custom-call(bf16[256,4096]{1,0:T(8,128)(2,1)} %bitcast.4), custom_call_target="tpu_custom_call" | custom-call | flops 2147483648 | bytes 2097152 | tf_op jit(solution)/shard_map/stage_rows/pallas_call | solution.py:85
  6.8 1.1 %collective-permute-done = bf16[8,4096]{1,0:T(8,128)(2,1)S(1)} collective-permute-done((bf16[8,4096]{1,0:T(8,128)(2,1)}, bf16[8,4096]{1,0:T(8,128)(2,1)S(1)}, u32[]{:S(2)}, u32[]{:S(2)}) %collective-permute-start) | collective-permute-done | bytes 65568 | tf_op jit(solution)/shard_map/ppermute | solution.py:307
  7.9 0.0 copy-done.2
  7.9 0.7 %collective-permute-start.1 = (bf16[16,4096]{1,0:T(8,128)(2,1)S(1)}, bf16[16,4096]{1,0:T(8,128)(2,1)S(1)}, u32[]{:S(2)}, u32[]{:S(2)}) collective-permute-start(bf16[16,4096]{1,0:T(8,128)(2,1)S(1)} %pad_maximum_fusion.1), channel_id=1, source_target_pairs={{0,4},{2,6},{4,0},{6,2},{8,12},{10,14},{12,8},{14,10},{1,5},{3,7},... | collective-permute-start | bytes 393224 | tf_op jit(solution)/shard_map/ppermute | solution.py:307
  8.7 0.0 copy-start.3
  8.7 2.2 %covariance.1 = f32[64,128]{1,0:T(8,128)S(1)} custom-call(f32[64,64]{1,0:T(8,128)S(1)} %get-tuple-element.15.in_ref, bf16[512,2048]{1,0:T(8,128)(2,1)S(1)} %get-tuple-element.16.rows_ref), custom_call_target="tpu_custom_call" | custom-call | flops 1073741824 | bytes 2097152 | tf_op jit(solution)/shard_map/covariance/pallas_call | solution.py:105
  10.8 2.1 %collective-permute-done.1 = bf16[16,4096]{1,0:T(8,128)(2,1)S(1)} collective-permute-done((bf16[16,4096]{1,0:T(8,128)(2,1)S(1)}, bf16[16,4096]{1,0:T(8,128)(2,1)S(1)}, u32[]{:S(2)}, u32[]{:S(2)}) %collective-permute-start.1) | collective-permute-done | bytes 131104 | tf_op jit(solution)/shard_map/ppermute | solution.py:307
  13.0 1.8 %collective-permute-start.2 = (bf16[32,4096]{1,0:T(8,128)(2,1)S(1)}, bf16[32,4096]{1,0:T(8,128)(2,1)S(1)}, u32[]{:S(2)}, u32[]{:S(2)}) collective-permute-start(bf16[32,4096]{1,0:T(8,128)(2,1)S(1)} %pad_maximum_fusion.refs_0_), channel_id=1, source_target_pairs={{0,2},{2,0},{4,6},{6,4},{8,10},{10,8},{12,14},{14,12},{1,3},{3,1},... | collective-permute-start | bytes 786440 | tf_op jit(solution)/shard_map/ppermute | solution.py:307
  14.7 0.3 collective-permute-start.3
  15.1 4.7 %collective-permute-done.3 = f32[64,128]{1,0:T(8,128)S(1)} collective-permute-done((f32[64,128]{1,0:T(8,128)S(1)}, f32[64,128]{1,0:T(8,128)S(1)}, u32[]{:S(2)}, u32[]{:S(2)}) %collective-permute-start.3) | collective-permute-done | bytes 32800 | tf_op jit(solution)/shard_map/ppermute | solution.py:307
  19.8 0.0 copy-start
  19.8 3.7 %collective-permute-start.4 = (f32[64,128]{1,0:T(8,128)S(1)}, f32[64,128]{1,0:T(8,128)S(1)}, u32[]{:S(2)}, u32[]{:S(2)}) collective-permute-start(f32[64,128]{1,0:T(8,128)S(1)} %add.9), channel_id=1, source_target_pairs={{0,8},{2,10},{4,12},{6,14},{8,0},{10,2},{12,4},{14,6},{1,9},{3,11}... | collective-permute-start | bytes 98312 | tf_op jit(solution)/shard_map/ppermute | solution.py:307
  23.4 0.0 copy-done.3
  23.4 1.9 %collective-permute-done.4 = f32[64,128]{1,0:T(8,128)S(1)} collective-permute-done((f32[64,128]{1,0:T(8,128)S(1)}, f32[64,128]{1,0:T(8,128)S(1)}, u32[]{:S(2)}, u32[]{:S(2)}) %collective-permute-start.4) | collective-permute-done | bytes 32800 | tf_op jit(solution)/shard_map/ppermute | solution.py:307
  25.3 1.4 %collective-permute-start.5 = (f32[64,128]{1,0:T(8,128)S(1)}, f32[64,128]{1,0:T(8,128)S(1)}, u32[]{:S(2)}, u32[]{:S(2)}) collective-permute-start(f32[64,128]{1,0:T(8,128)S(1)} %add.10), channel_id=1, source_target_pairs={{0,4},{2,6},{4,0},{6,2},{8,12},{10,14},{12,8},{14,10},{1,5},{3,7},... | collective-permute-start | bytes 98312 | tf_op jit(solution)/shard_map/ppermute | solution.py:307
  26.7 0.0 collective-permute-done.2.refs_1_
  26.7 1.0 %turn_queries.1.turned_ref = bf16[64,4096]{1,0:T(8,128)(2,1)S(1)} custom-call(bf16[32,4096]{1,0:T(8,128)(2,1)S(1)} %pad_maximum_fusion.refs_0_, bf16[32,4096]{1,0:T(8,128)(2,1)S(1)} %collective-permute-done.2.refs_1_), custom_call_target="tpu_custom_call" | custom-call | flops 1073741824 | bytes 1048576 | tf_op jit(solution)/shard_map/turn_queries/pallas_call | solution.py:142
  27.8 0.0 copy-start.1
  27.8 1.4 %collective-permute-done.5 = f32[64,128]{1,0:T(8,128)S(1)} collective-permute-done((f32[64,128]{1,0:T(8,128)S(1)}, f32[64,128]{1,0:T(8,128)S(1)}, u32[]{:S(2)}, u32[]{:S(2)}) %collective-permute-start.5) | collective-permute-done | bytes 32800 | tf_op jit(solution)/shard_map/ppermute | solution.py:307
  29.2 0.0 copy-done
  29.3 5.6 %solve_and_score.1 = f32[8,2,8,128]{3,2,1,0:T(8,128)S(1)} custom-call(s32[8]{0:T(128)S(1)} %broadcast_xor_fusion.route_ref, f32[64,128]{1,0:T(8,128)S(1)} %add.11.cov_ref, bf16[64,4096]{1,0:T(8,128)(2,1)S(1)} %turn_queries.1.turned_ref, bf16[256,4096]{1,0:T(8,128)(2,1)S(1)} %bitcast.5), custom_call_target="tpu_custom_call" | custom-call | flops 201326592 | bytes 2097152 | tf_op jit(solution)/shard_map/solve_and_score/pallas_call | solution.py:261
  34.9 13.1 %all_to_all.5 = f32[16,8,128]{2,1,0:T(8,128)S(1)} all-to-all(f32[16,8,128]{2,1,0:T(8,128)S(1)} %bitcast.6), channel_id=1, replica_groups=mesh['groups'=2,'dp'=8,'layer'=2] {'dp','layer'}, dimensions={0} | all-to-all | bytes 131072 | tf_op jit(solution)/shard_map/all_to_all | solution.py:343
  48.0 0.0 copy-done.1
  48.0 1.2 %pick_tiles.1 = f32[4,8,128]{2,1,0:T(8,128)} custom-call(s32[1,4]{1,0:T(1,128)S(1)} %copy-done.1, f32[8,2,8,128]{3,2,1,0:T(8,128)S(1)} %bitcast.7), custom_call_target="tpu_custom_call" | custom-call | tf_op jit(solution)/shard_map/pick_tiles/pallas_call | solution.py:296
  (6 shorter events, 0.0 us)
Async XLA Ops:
  0.0 7.9 %collective-permute-start = (bf16[8,4096]{1,0:T(8,128)(2,1)}, bf16[8,4096]{1,0:T(8,128)(2,1)S(1)}, u32[]{:S(2)}, u32[]{:S(2)}) collective-permute-start(bf16[8,4096]{1,0:T(8,128)(2,1)} %bitcast.8), channel_id=1, source_target_pairs={{0,8},{2,10},{4,12},{6,14},{8,0},{10,2},{12,4},{14,6},{1,9},{3,11}... | collective-permute-start | bytes 196616 | tf_op jit(solution)/shard_map/ppermute | solution.py:307
  4.0 3.9 %copy-start.2 = (bf16[8,1,4096]{2,0,1:T(8,128)(2,1)S(1)}, bf16[8,1,4096]{2,0,1:T(8,128)(2,1)}, u32[]{:S(2)}) copy-start(bf16[8,1,4096]{2,0,1:T(8,128)(2,1)} %param.5) | copy-start | bytes 196612
  7.9 5.0 %collective-permute-start.1 = (bf16[16,4096]{1,0:T(8,128)(2,1)S(1)}, bf16[16,4096]{1,0:T(8,128)(2,1)S(1)}, u32[]{:S(2)}, u32[]{:S(2)}) collective-permute-start(bf16[16,4096]{1,0:T(8,128)(2,1)S(1)} %pad_maximum_fusion.1), channel_id=1, source_target_pairs={{0,4},{2,6},{4,0},{6,2},{8,12},{10,14},{12,8},{14,10},{1,5},{3,7},... | collective-permute-start | bytes 393224 | tf_op jit(solution)/shard_map/ppermute | solution.py:307
  8.7 14.8 %copy-start.3 = (s32[8]{0:T(128)S(1)}, s32[8]{0:T(128)}, u32[]{:S(2)}) copy-start(s32[8]{0:T(128)} %constant.8.clone) | copy-start | bytes 100
  13.0 13.8 %collective-permute-start.2 = (bf16[32,4096]{1,0:T(8,128)(2,1)S(1)}, bf16[32,4096]{1,0:T(8,128)(2,1)S(1)}, u32[]{:S(2)}, u32[]{:S(2)}) collective-permute-start(bf16[32,4096]{1,0:T(8,128)(2,1)S(1)} %pad_maximum_fusion.refs_0_), channel_id=1, source_target_pairs={{0,2},{2,0},{4,6},{6,4},{8,10},{10,8},{12,14},{14,12},{1,3},{3,1},... | collective-permute-start | bytes 786440 | tf_op jit(solution)/shard_map/ppermute | solution.py:307
  14.7 5.0 %collective-permute-start.3 = (f32[64,128]{1,0:T(8,128)S(1)}, f32[64,128]{1,0:T(8,128)S(1)}, u32[]{:S(2)}, u32[]{:S(2)}) collective-permute-start(f32[64,128]{1,0:T(8,128)S(1)} %covariance.1), channel_id=1, source_target_pairs={{0,2},{2,0},{4,6},{6,4},{8,10},{10,8},{12,14},{14,12},{1,3},{3,1},... | collective-permute-start | bytes 98312 | tf_op jit(solution)/shard_map/ppermute | solution.py:307
  19.8 9.5 %copy-start = (bf16[256,1,4096]{2,0,1:T(8,128)(2,1)S(1)}, bf16[256,1,4096]{2,0,1:T(8,128)(2,1)}, u32[]{:S(2)}) copy-start(bf16[256,1,4096]{2,0,1:T(8,128)(2,1)} %param.4) | copy-start | bytes 6291460
  19.8 5.6 %collective-permute-start.4 = (f32[64,128]{1,0:T(8,128)S(1)}, f32[64,128]{1,0:T(8,128)S(1)}, u32[]{:S(2)}, u32[]{:S(2)}) collective-permute-start(f32[64,128]{1,0:T(8,128)S(1)} %add.9), channel_id=1, source_target_pairs={{0,8},{2,10},{4,12},{6,14},{8,0},{10,2},{12,4},{14,6},{1,9},{3,11}... | collective-permute-start | bytes 98312 | tf_op jit(solution)/shard_map/ppermute | solution.py:307
  25.3 3.9 %collective-permute-start.5 = (f32[64,128]{1,0:T(8,128)S(1)}, f32[64,128]{1,0:T(8,128)S(1)}, u32[]{:S(2)}, u32[]{:S(2)}) collective-permute-start(f32[64,128]{1,0:T(8,128)S(1)} %add.10), channel_id=1, source_target_pairs={{0,4},{2,6},{4,0},{6,2},{8,12},{10,14},{12,8},{14,10},{1,5},{3,7},... | collective-permute-start | bytes 98312 | tf_op jit(solution)/shard_map/ppermute | solution.py:307
  27.8 20.2 %copy-start.1 = (s32[1,4]{1,0:T(1,128)S(1)}, s32[1,4]{1,0:T(1,128)}, u32[]{:S(2)}) copy-start(s32[1,4]{1,0:T(1,128)} %listed_ref.1) | copy-start | bytes 52

commit v4 on v3

--- a/solution.py
+++ b/solution.py
@@ -318,18 +318,19 @@
     total_count = float(examples * shard_count)
     order = jnp.arange(shard_count, dtype=jnp.int32)
     if shard_count == 8:
-        quarter = exchange(own_queries, 4, shard_count)
+        far = exchange(own_queries, 4, shard_count)
+        beside = exchange(own_queries, 1, shard_count)
         in_sum, rows = staged_rows(train)
-        quarter, in_sum = lax.optimization_barrier((quarter, in_sum))
-        column = jnp.concatenate([own_queries, quarter], axis=0)
-        other = exchange(column, 2, shard_count)
+        far, beside, in_sum = lax.optimization_barrier((far, beside, in_sum))
+        near = exchange(jnp.concatenate([own_queries, far], axis=0), 2, shard_count)
+        far_beside = exchange(far, 1, shard_count)
         cov = covariance_sums(in_sum, rows)
-        other, cov = lax.optimization_barrier((other, cov))
-        column = jnp.concatenate([column, other], axis=0)
-        queries = [column, exchange(column, 1, shard_count)]
-        for distance in (1, 4):
+        near, cov = lax.optimization_barrier((near, cov))
+        near_beside = exchange(near, 1, shard_count)
+        queries = [own_queries, far, near, beside, far_beside, near_beside]
+        for distance in (4, 2):
             cov = cov + exchange(cov, distance, shard_count)
-        last = exchange(cov, 2, shard_count)
+        last = exchange(cov, 1, shard_count)
         turned, cov = lax.optimization_barrier((turned_queries(queries), cov))
         cov = cov + last
         order = jnp.array([0, 4, 2, 6, 1, 5, 3, 7], jnp.int32)

time: 49.4 us -> 45.4 us (0.919)
  waiting for transfers between devices: 11.3 us -> 6.9 us
  starting transfers between devices: 11.9 us -> 13.5 us
  blocking collectives: 13.1 us -> 11.9 us
    ppermute x6 -> x8, waiting for transfers between devices: 11.3 us -> 6.9 us  [exchange(): return lax.ppermute(values, 'dp', [(k, k ^ distance) for k in range(count)])]
    ppermute x6 -> x8, starting transfers between devices: 11.9 us -> 13.5 us  [exchange(): return lax.ppermute(values, 'dp', [(k, k ^ distance) for k in range(count)])]
    all_to_all x1, blocking collectives: 13.1 us -> 11.9 us  [shards(): lax.all_to_all(outgoing, ('dp', 'layer'), split_axis=0, concat_axis=0, ti...]
  transfers between devices with their start and end apart: 6 -> 8, of which waited for: 5 -> 5; matrix products, arithmetic and copies ran while one was open for 0% -> 0% of each run, Pallas kernels for 12% -> 13%
where the time goes in v4:
time: 45.4 us; the launch traced here: 45.2 us
  starting transfers between devices  13.5 us (30%)
  Pallas kernels  12.7 us (28%)
  blocking collectives  11.9 us (26%)
  waiting for transfers between devices  6.9 us (15%)
    ppermute x8, starting transfers between devices, exchange(): return lax.ppermute(values, 'dp', [(k, k ^ distance) for k in range(count)])  13.5 us
    all_to_all x1, blocking collectives, shards(): lax.all_to_all(outgoing, ('dp', 'layer'), split_axis=0, concat_axis=0, ti...  11.9 us
    ppermute x8, waiting for transfers between devices, exchange(): return lax.ppermute(values, 'dp', [(k, k ^ distance) for k in range(count)])  6.9 us
    pallas_call x1, Pallas kernels, all_scores(): pl.pallas_call(functools.partial(score_kernel, total_count), out_shape=ja...  5.65 us
    pallas_call x1, Pallas kernels, staged_rows(): pl.pallas_call(stage_kernel, out_shape=(jax.ShapeDtypeStruct((K_IN, K_IN)...  2.74 us
    pallas_call x1, Pallas kernels, covariance_sums(): pl.pallas_call(gram_kernel, out_shape=jax.ShapeDtypeStruct((K_OUT, 2 * K_...  2.16 us
    pallas_call x1, Pallas kernels, picked(): pl.pallas_call(pick_kernel, out_shape=jax.ShapeDtypeStruct((listed.shape[...  1.15 us
    pallas_call x1, Pallas kernels, turned_queries(): pl.pallas_call(turn_kernel, out_shape=jax.ShapeDtypeStruct((K_OUT, total...  1.05 us
  transfers between devices with their start and end apart: 8, of which 5 were waited for; matrix products, arithmetic and copies ran while one was open for 0% of the time, Pallas kernels for 13%

profile of v4, /device:TPU:0, one launch (start us, length us, event | category | flops | bytes accessed | tf_op | source)
XLA Modules:
  0.0 45.2 jit_solution(14299776757937788098)
XLA Ops:
  0.0 2.9 %collective-permute-start.1 = (bf16[8,4096]{1,0:T(8,128)(2,1)}, bf16[8,4096]{1,0:T(8,128)(2,1)S(1)}, u32[]{:S(2)}, u32[]{:S(2)}) collective-permute-start(bf16[8,4096]{1,0:T(8,128)(2,1)} %bitcast.8), channel_id=1, source_target_pairs={{0,2},{2,0},{4,6},{6,4},{8,10},{10,8},{12,14},{14,12},{1,3},{3,1},... | collective-permute-start | bytes 196616 | tf_op jit(solution)/shard_map/ppermute | solution.py:307
  2.9 2.6 %collective-permute-start = (bf16[8,4096]{1,0:T(8,128)(2,1)}, bf16[8,4096]{1,0:T(8,128)(2,1)S(1)}, u32[]{:S(2)}, u32[]{:S(2)}) collective-permute-start(bf16[8,4096]{1,0:T(8,128)(2,1)} %bitcast.9), channel_id=1, source_target_pairs={{0,8},{2,10},{4,12},{6,14},{8,0},{10,2},{12,4},{14,6},{1,9},{3,11}... | collective-permute-start | bytes 196616 | tf_op jit(solution)/shard_map/ppermute | solution.py:307
  5.5 0.0 copy-start.1
  5.5 2.7 %stage_rows.1 = (f32[64,64]{1,0:T(8,128)S(1)}, bf16[512,2048]{1,0:T(8,128)(2,1)S(1)}) custom-call(bf16[256,4096]{1,0:T(8,128)(2,1)} %bitcast.4), custom_call_target="tpu_custom_call" | custom-call | flops 2147483648 | bytes 2097152 | tf_op jit(solution)/shard_map/stage_rows/pallas_call | solution.py:85
  8.3 0.0 collective-permute-done.1.refs_3_
  8.3 0.4 collective-permute-done.refs_1_
  8.6 0.0 copy-done.1
  8.7 0.0 copy-start.3
  8.7 1.3 %collective-permute-start.2 = (bf16[16,4096]{1,0:T(8,128)(2,1)S(1)}, bf16[16,4096]{1,0:T(8,128)(2,1)S(1)}, u32[]{:S(2)}, u32[]{:S(2)}) collective-permute-start(bf16[16,4096]{1,0:T(8,128)(2,1)S(1)} %pad_maximum_fusion), channel_id=1, source_target_pairs={{0,4},{2,6},{4,0},{6,2},{8,12},{10,14},{12,8},{14,10},{1,5},{3,7},... | collective-permute-start | bytes 393224 | tf_op jit(solution)/shard_map/ppermute | solution.py:307
  10.0 2.2 %covariance.1 = f32[64,128]{1,0:T(8,128)S(1)} custom-call(f32[64,64]{1,0:T(8,128)S(1)} %get-tuple-element.16.in_ref, bf16[512,2048]{1,0:T(8,128)(2,1)S(1)} %get-tuple-element.17.rows_ref), custom_call_target="tpu_custom_call" | custom-call | flops 1073741824 | bytes 2097152 | tf_op jit(solution)/shard_map/covariance/pallas_call | solution.py:105
  12.2 1.6 %collective-permute-done.2.refs_2_ = bf16[16,4096]{1,0:T(8,128)(2,1)S(1)} collective-permute-done((bf16[16,4096]{1,0:T(8,128)(2,1)S(1)}, bf16[16,4096]{1,0:T(8,128)(2,1)S(1)}, u32[]{:S(2)}, u32[]{:S(2)}) %collective-permute-start.2) | collective-permute-done | bytes 131104 | tf_op jit(solution)/shard_map/ppermute | solution.py:307
  13.7 2.4 %collective-permute-start.5 = (f32[64,128]{1,0:T(8,128)S(1)}, f32[64,128]{1,0:T(8,128)S(1)}, u32[]{:S(2)}, u32[]{:S(2)}) collective-permute-start(f32[64,128]{1,0:T(8,128)S(1)} %covariance.1), channel_id=1, source_target_pairs={{0,8},{2,10},{4,12},{6,14},{8,0},{10,2},{12,4},{14,6},{1,9},{3,11}... | collective-permute-start | bytes 98312 | tf_op jit(solution)/shard_map/ppermute | solution.py:307
  16.1 0.5 %collective-permute-start.3 = (bf16[8,4096]{1,0:T(8,128)(2,1)S(1)}, bf16[8,4096]{1,0:T(8,128)(2,1)S(1)}, u32[]{:S(2)}, u32[]{:S(2)}) collective-permute-start(bf16[8,4096]{1,0:T(8,128)(2,1)S(1)} %collective-permute-done.refs_1_), channel_id=1, source_target_pairs={{0,2},{2,0},{4,6},{6,4},{8,10},{10,8},{12,14},{14,12},{1,3},{3,1},... | collective-permute-start | bytes 196616 | tf_op jit(solution)/shard_map/ppermute | solution.py:307
  16.6 1.5 %collective-permute-start.4 = (bf16[16,4096]{1,0:T(8,128)(2,1)S(1)}, bf16[16,4096]{1,0:T(8,128)(2,1)S(1)}, u32[]{:S(2)}, u32[]{:S(2)}) collective-permute-start(bf16[16,4096]{1,0:T(8,128)(2,1)S(1)} %collective-permute-done.2.refs_2_), channel_id=1, source_target_pairs={{0,2},{2,0},{4,6},{6,4},{8,10},{10,8},{12,14},{14,12},{1,3},{3,1},... | collective-permute-start | bytes 393224 | tf_op jit(solution)/shard_map/ppermute | solution.py:307
  18.1 0.4 collective-permute-done.5
  18.5 0.0 copy-start
  18.5 1.7 %collective-permute-start.6 = (f32[64,128]{1,0:T(8,128)S(1)}, f32[64,128]{1,0:T(8,128)S(1)}, u32[]{:S(2)}, u32[]{:S(2)}) collective-permute-start(f32[64,128]{1,0:T(8,128)S(1)} %add.9), channel_id=1, source_target_pairs={{0,4},{2,6},{4,0},{6,2},{8,12},{10,14},{12,8},{14,10},{1,5},{3,7},... | collective-permute-start | bytes 98312 | tf_op jit(solution)/shard_map/ppermute | solution.py:307
  20.2 0.0 copy-done.3
  20.3 2.3 %collective-permute-done.6 = f32[64,128]{1,0:T(8,128)S(1)} collective-permute-done((f32[64,128]{1,0:T(8,128)S(1)}, f32[64,128]{1,0:T(8,128)S(1)}, u32[]{:S(2)}, u32[]{:S(2)}) %collective-permute-start.6) | collective-permute-done | bytes 32800 | tf_op jit(solution)/shard_map/ppermute | solution.py:307
  22.5 0.5 %collective-permute-start.7 = (f32[64,128]{1,0:T(8,128)S(1)}, f32[64,128]{1,0:T(8,128)S(1)}, u32[]{:S(2)}, u32[]{:S(2)}) collective-permute-start(f32[64,128]{1,0:T(8,128)S(1)} %add.10), channel_id=1, source_target_pairs={{0,2},{2,0},{4,6},{6,4},{8,10},{10,8},{12,14},{14,12},{1,3},{3,1},... | collective-permute-start | bytes 98312 | tf_op jit(solution)/shard_map/ppermute | solution.py:307
  23.1 0.0 collective-permute-done.3.refs_4_
  23.1 0.0 collective-permute-done.4.refs_5_
  23.1 1.0 %turn_queries.1.turned_ref = bf16[64,4096]{1,0:T(8,128)(2,1)S(1)} custom-call(bf16[8,4096]{1,0:T(8,128)(2,1)S(1)} %bitcast.11, bf16[8,4096]{1,0:T(8,128)(2,1)S(1)} %collective-permute-done.refs_1_, bf16[16,4096]{1,0:T(8,128)(2,1)S(1)} %collective-permute-done.2.refs_2_, bf16[8,4096]{1,0:T(8,128)(2,1)S(1)} %collective-permute-done.1.refs_3_, ...), custom_call_target="tpu_custom_call" | custom-call | flops 1073741824 | bytes 1048576 | tf_op jit(solution)/shard_map/turn_queries/pallas_call | solution.py:142
  24.1 0.0 copy-start.2
  24.1 2.3 %collective-permute-done.7 = f32[64,128]{1,0:T(8,128)S(1)} collective-permute-done((f32[64,128]{1,0:T(8,128)S(1)}, f32[64,128]{1,0:T(8,128)S(1)}, u32[]{:S(2)}, u32[]{:S(2)}) %collective-permute-start.7) | collective-permute-done | bytes 32800 | tf_op jit(solution)/shard_map/ppermute | solution.py:307
  26.4 0.0 copy-done
  26.5 5.6 %solve_and_score.1 = f32[8,2,8,128]{3,2,1,0:T(8,128)S(1)} custom-call(s32[8]{0:T(128)S(1)} %broadcast_xor_fusion.route_ref, f32[64,128]{1,0:T(8,128)S(1)} %add.11.cov_ref, bf16[64,4096]{1,0:T(8,128)(2,1)S(1)} %turn_queries.1.turned_ref, bf16[256,4096]{1,0:T(8,128)(2,1)S(1)} %bitcast.5), custom_call_target="tpu_custom_call" | custom-call | flops 201326592 | bytes 2097152 | tf_op jit(solution)/shard_map/solve_and_score/pallas_call | solution.py:261
  32.1 11.9 %all_to_all.5 = f32[16,8,128]{2,1,0:T(8,128)S(1)} all-to-all(f32[16,8,128]{2,1,0:T(8,128)S(1)} %bitcast.6), channel_id=1, replica_groups=mesh['groups'=2,'dp'=8,'layer'=2] {'dp','layer'}, dimensions={0} | all-to-all | bytes 131072 | tf_op jit(solution)/shard_map/all_to_all | solution.py:344
  44.0 0.0 copy-done.2
  44.0 1.2 %pick_tiles.1 = f32[4,8,128]{2,1,0:T(8,128)} custom-call(s32[1,4]{1,0:T(1,128)S(1)} %copy-done.2, f32[8,2,8,128]{3,2,1,0:T(8,128)S(1)} %bitcast.7), custom_call_target="tpu_custom_call" | custom-call | tf_op jit(solution)/shard_map/pick_tiles/pallas_call | solution.py:296
  (5 shorter events, 0.0 us)
Async XLA Ops:
  0.0 8.3 %collective-permute-start.1 = (bf16[8,4096]{1,0:T(8,128)(2,1)}, bf16[8,4096]{1,0:T(8,128)(2,1)S(1)}, u32[]{:S(2)}, u32[]{:S(2)}) collective-permute-start(bf16[8,4096]{1,0:T(8,128)(2,1)} %bitcast.8), channel_id=1, source_target_pairs={{0,2},{2,0},{4,6},{6,4},{8,10},{10,8},{12,14},{14,12},{1,3},{3,1},... | collective-permute-start | bytes 196616 | tf_op jit(solution)/shard_map/ppermute | solution.py:307
  2.9 5.7 %collective-permute-start = (bf16[8,4096]{1,0:T(8,128)(2,1)}, bf16[8,4096]{1,0:T(8,128)(2,1)S(1)}, u32[]{:S(2)}, u32[]{:S(2)}) collective-permute-start(bf16[8,4096]{1,0:T(8,128)(2,1)} %bitcast.9), channel_id=1, source_target_pairs={{0,8},{2,10},{4,12},{6,14},{8,0},{10,2},{12,4},{14,6},{1,9},{3,11}... | collective-permute-start | bytes 196616 | tf_op jit(solution)/shard_map/ppermute | solution.py:307
  5.5 3.1 %copy-start.1 = (bf16[8,1,4096]{2,0,1:T(8,128)(2,1)S(1)}, bf16[8,1,4096]{2,0,1:T(8,128)(2,1)}, u32[]{:S(2)}) copy-start(bf16[8,1,4096]{2,0,1:T(8,128)(2,1)} %param.5) | copy-start | bytes 196612
  8.7 11.6 %copy-start.3 = (s32[8]{0:T(128)S(1)}, s32[8]{0:T(128)}, u32[]{:S(2)}) copy-start(s32[8]{0:T(128)} %constant.8.clone) | copy-start | bytes 100
  8.7 5.0 %collective-permute-start.2 = (bf16[16,4096]{1,0:T(8,128)(2,1)S(1)}, bf16[16,4096]{1,0:T(8,128)(2,1)S(1)}, u32[]{:S(2)}, u32[]{:S(2)}) collective-permute-start(bf16[16,4096]{1,0:T(8,128)(2,1)S(1)} %pad_maximum_fusion), channel_id=1, source_target_pairs={{0,4},{2,6},{4,0},{6,2},{8,12},{10,14},{12,8},{14,10},{1,5},{3,7},... | collective-permute-start | bytes 393224 | tf_op jit(solution)/shard_map/ppermute | solution.py:307
  13.7 4.8 %collective-permute-start.5 = (f32[64,128]{1,0:T(8,128)S(1)}, f32[64,128]{1,0:T(8,128)S(1)}, u32[]{:S(2)}, u32[]{:S(2)}) collective-permute-start(f32[64,128]{1,0:T(8,128)S(1)} %covariance.1), channel_id=1, source_target_pairs={{0,8},{2,10},{4,12},{6,14},{8,0},{10,2},{12,4},{14,6},{1,9},{3,11}... | collective-permute-start | bytes 98312 | tf_op jit(solution)/shard_map/ppermute | solution.py:307
  16.1 7.0 %collective-permute-start.3 = (bf16[8,4096]{1,0:T(8,128)(2,1)S(1)}, bf16[8,4096]{1,0:T(8,128)(2,1)S(1)}, u32[]{:S(2)}, u32[]{:S(2)}) collective-permute-start(bf16[8,4096]{1,0:T(8,128)(2,1)S(1)} %collective-permute-done.refs_1_), channel_id=1, source_target_pairs={{0,2},{2,0},{4,6},{6,4},{8,10},{10,8},{12,14},{14,12},{1,3},{3,1},... | collective-permute-start | bytes 196616 | tf_op jit(solution)/shard_map/ppermute | solution.py:307
  16.6 6.4 %collective-permute-start.4 = (bf16[16,4096]{1,0:T(8,128)(2,1)S(1)}, bf16[16,4096]{1,0:T(8,128)(2,1)S(1)}, u32[]{:S(2)}, u32[]{:S(2)}) collective-permute-start(bf16[16,4096]{1,0:T(8,128)(2,1)S(1)} %collective-permute-done.2.refs_2_), channel_id=1, source_target_pairs={{0,2},{2,0},{4,6},{6,4},{8,10},{10,8},{12,14},{14,12},{1,3},{3,1},... | collective-permute-start | bytes 393224 | tf_op jit(solution)/shard_map/ppermute | solution.py:307
  18.5 7.9 %copy-start = (bf16[256,1,4096]{2,0,1:T(8,128)(2,1)S(1)}, bf16[256,1,4096]{2,0,1:T(8,128)(2,1)}, u32[]{:S(2)}) copy-start(bf16[256,1,4096]{2,0,1:T(8,128)(2,1)} %param.4) | copy-start | bytes 6291460
  18.5 4.0 %collective-permute-start.6 = (f32[64,128]{1,0:T(8,128)S(1)}, f32[64,128]{1,0:T(8,128)S(1)}, u32[]{:S(2)}, u32[]{:S(2)}) collective-permute-start(f32[64,128]{1,0:T(8,128)S(1)} %add.9), channel_id=1, source_target_pairs={{0,4},{2,6},{4,0},{6,2},{8,12},{10,14},{12,8},{14,10},{1,5},{3,7},... | collective-permute-start | bytes 98312 | tf_op jit(solution)/shard_map/ppermute | solution.py:307
  22.5 3.9 %collective-permute-start.7 = (f32[64,128]{1,0:T(8,128)S(1)}, f32[64,128]{1,0:T(8,128)S(1)}, u32[]{:S(2)}, u32[]{:S(2)}) collective-permute-start(f32[64,128]{1,0:T(8,128)S(1)} %add.10), channel_id=1, source_target_pairs={{0,2},{2,0},{4,6},{6,4},{8,10},{10,8},{12,14},{14,12},{1,3},{3,1},... | collective-permute-start | bytes 98312 | tf_op jit(solution)/shard_map/ppermute | solution.py:307
  24.1 19.9 %copy-start.2 = (s32[1,4]{1,0:T(1,128)S(1)}, s32[1,4]{1,0:T(1,128)}, u32[]{:S(2)}) copy-start(s32[1,4]{1,0:T(1,128)} %listed_ref.1) | copy-start | bytes 52

commit v5 on v4

--- a/solution.py
+++ b/solution.py
@@ -318,22 +318,18 @@
     total_count = float(examples * shard_count)
     order = jnp.arange(shard_count, dtype=jnp.int32)
     if shard_count == 8:
-        far = exchange(own_queries, 4, shard_count)
         beside = exchange(own_queries, 1, shard_count)
-        in_sum, rows = staged_rows(train)
-        far, beside, in_sum = lax.optimization_barrier((far, beside, in_sum))
-        near = exchange(jnp.concatenate([own_queries, far], axis=0), 2, shard_count)
-        far_beside = exchange(far, 1, shard_count)
-        cov = covariance_sums(in_sum, rows)
-        near, cov = lax.optimization_barrier((near, cov))
-        near_beside = exchange(near, 1, shard_count)
-        queries = [own_queries, far, near, beside, far_beside, near_beside]
+        column = [exchange(own_queries, distance, shard_count) for distance in (4, 6, 2)]
+        cov = covariance_sums(*staged_rows(train))
+        beside, column, cov = lax.optimization_barrier((beside, column, cov))
+        column = jnp.concatenate(column, axis=0)
+        queries = [own_queries, column, beside, exchange(column, 1, shard_count)]
         for distance in (4, 2):
             cov = cov + exchange(cov, distance, shard_count)
         last = exchange(cov, 1, shard_count)
         turned, cov = lax.optimization_barrier((turned_queries(queries), cov))
         cov = cov + last
-        order = jnp.array([0, 4, 2, 6, 1, 5, 3, 7], jnp.int32)
+        order = jnp.array([0, 4, 6, 2, 1, 5, 7, 3], jnp.int32)
         route = own_index ^ order
     else:
         turned = turned_queries([lax.all_gather(own_queries, "dp", axis=0, tiled=True)])

time: 45.4 us -> 42.8 us (0.943)
  waiting for transfers between devices: 6.9 us -> 5.83 us
  blocking collectives: 11.9 us -> 11 us
  starting transfers between devices: 13.5 us -> 13 us
    ppermute x8, waiting for transfers between devices: 6.9 us -> 5.83 us  [exchange(): return lax.ppermute(values, 'dp', [(k, k ^ distance) for k in range(count)])]
    all_to_all x1, blocking collectives: 11.9 us -> 11 us  [shards(): lax.all_to_all(outgoing, ('dp', 'layer'), split_axis=0, concat_axis=0, ti...]
    ppermute x8, starting transfers between devices: 13.5 us -> 13 us  [exchange(): return lax.ppermute(values, 'dp', [(k, k ^ distance) for k in range(count)])]
  transfers between devices with their start and end apart: 8 -> 8, of which waited for: 5 -> 3; matrix products, arithmetic and copies ran while one was open for 0% -> 0% of each run, Pallas kernels for 13% -> 14%
where the time goes in v5:
time: 42.8 us; the launch traced here: 42.7 us
  starting transfers between devices  13 us (30%)
  Pallas kernels  12.7 us (30%)
  blocking collectives  11 us (26%)
  waiting for transfers between devices  5.83 us (14%)
    ppermute x8, starting transfers between devices, exchange(): return lax.ppermute(values, 'dp', [(k, k ^ distance) for k in range(count)])  13 us
    all_to_all x1, blocking collectives, shards(): lax.all_to_all(outgoing, ('dp', 'layer'), split_axis=0, concat_axis=0, ti...  11 us
    ppermute x8, waiting for transfers between devices, exchange(): return lax.ppermute(values, 'dp', [(k, k ^ distance) for k in range(count)])  5.83 us
    pallas_call x1, Pallas kernels, all_scores(): pl.pallas_call(functools.partial(score_kernel, total_count), out_shape=ja...  5.64 us
    pallas_call x1, Pallas kernels, staged_rows(): pl.pallas_call(stage_kernel, out_shape=(jax.ShapeDtypeStruct((K_IN, K_IN)...  2.69 us
    pallas_call x1, Pallas kernels, covariance_sums(): pl.pallas_call(gram_kernel, out_shape=jax.ShapeDtypeStruct((K_OUT, 2 * K_...  2.16 us
    pallas_call x1, Pallas kernels, picked(): pl.pallas_call(pick_kernel, out_shape=jax.ShapeDtypeStruct((listed.shape[...  1.15 us
    pallas_call x1, Pallas kernels, turned_queries(): pl.pallas_call(turn_kernel, out_shape=jax.ShapeDtypeStruct((K_OUT, total...  1.04 us
  transfers between devices with their start and end apart: 8, of which 3 were waited for; matrix products, arithmetic and copies ran while one was open for 0% of the time, Pallas kernels for 14%

profile of v5, /device:TPU:0, one launch (start us, length us, event | category | flops | bytes accessed | tf_op | source)
XLA Modules:
  0.0 42.7 jit_solution(1502203223932633628)
XLA Ops:
  0.0 2.9 %collective-permute-start = (bf16[8,4096]{1,0:T(8,128)(2,1)}, bf16[8,4096]{1,0:T(8,128)(2,1)S(1)}, u32[]{:S(2)}, u32[]{:S(2)}) collective-permute-start(bf16[8,4096]{1,0:T(8,128)(2,1)} %bitcast.8), channel_id=1, source_target_pairs={{0,2},{2,0},{4,6},{6,4},{8,10},{10,8},{12,14},{14,12},{1,3},{3,1},... | collective-permute-start | bytes 196616 | tf_op jit(solution)/shard_map/ppermute | solution.py:307
  2.9 2.6 %collective-permute-start.1 = (bf16[8,4096]{1,0:T(8,128)(2,1)}, bf16[8,4096]{1,0:T(8,128)(2,1)S(1)}, u32[]{:S(2)}, u32[]{:S(2)}) collective-permute-start(bf16[8,4096]{1,0:T(8,128)(2,1)} %bitcast.9), channel_id=1, source_target_pairs={{0,8},{2,10},{4,12},{6,14},{8,0},{10,2},{12,4},{14,6},{1,9},{3,11}... | collective-permute-start | bytes 196616 | tf_op jit(solution)/shard_map/ppermute | solution.py:307
  5.5 1.3 %collective-permute-start.2 = (bf16[8,4096]{1,0:T(8,128)(2,1)}, bf16[8,4096]{1,0:T(8,128)(2,1)S(1)}, u32[]{:S(2)}, u32[]{:S(2)}) collective-permute-start(bf16[8,4096]{1,0:T(8,128)(2,1)} %bitcast.10), channel_id=1, source_target_pairs={{0,12},{2,14},{4,8},{6,10},{8,4},{10,6},{12,0},{14,2},{1,13},{3,15... | collective-permute-start | bytes 196616 | tf_op jit(solution)/shard_map/ppermute | solution.py:307
  6.9 0.2 collective-permute-start.3
  7.1 2.7 %stage_rows.1 = (f32[64,64]{1,0:T(8,128)S(1)}, bf16[512,2048]{1,0:T(8,128)(2,1)S(1)}) custom-call(bf16[256,4096]{1,0:T(8,128)(2,1)} %bitcast.4), custom_call_target="tpu_custom_call" | custom-call | flops 2147483648 | bytes 2097152 | tf_op jit(solution)/shard_map/stage_rows/pallas_call | solution.py:85
  9.8 0.0 copy-start.3
  9.8 0.0 copy-start.2
  9.8 2.2 %covariance.1 = f32[64,128]{1,0:T(8,128)S(1)} custom-call(f32[64,64]{1,0:T(8,128)S(1)} %get-tuple-element.14.in_ref, bf16[512,2048]{1,0:T(8,128)(2,1)S(1)} %get-tuple-element.15.rows_ref), custom_call_target="tpu_custom_call" | custom-call | flops 1073741824 | bytes 2097152 | tf_op jit(solution)/shard_map/covariance/pallas_call | solution.py:105
  12.0 0.0 collective-permute-done.refs_2_
  12.0 0.0 collective-permute-done.1
  12.0 0.0 collective-permute-done.2
  12.0 0.0 collective-permute-done.3
  12.1 2.9 %collective-permute-start.5 = (f32[64,128]{1,0:T(8,128)S(1)}, f32[64,128]{1,0:T(8,128)S(1)}, u32[]{:S(2)}, u32[]{:S(2)}) collective-permute-start(f32[64,128]{1,0:T(8,128)S(1)} %covariance.1), channel_id=1, source_target_pairs={{0,8},{2,10},{4,12},{6,14},{8,0},{10,2},{12,4},{14,6},{1,9},{3,11}... | collective-permute-start | bytes 98312 | tf_op jit(solution)/shard_map/ppermute | solution.py:307
  15.0 0.6 %collective-permute-start.4 = (bf16[24,4096]{1,0:T(8,128)(2,1)S(1)}, bf16[24,4096]{1,0:T(8,128)(2,1)S(1)}, u32[]{:S(2)}, u32[]{:S(2)}) collective-permute-start(bf16[24,4096]{1,0:T(8,128)(2,1)S(1)} %constant_dynamic-update-slice_fusion.refs_1_), channel_id=1, source_target_pairs={{0,2},{2,0},{4,6},{6,4},{8,10},{10,8},{12,14},{14,12},{1,3},{3,1},... | collective-permute-start | bytes 589832 | tf_op jit(solution)/shard_map/ppermute | solution.py:307
  15.6 1.4 %collective-permute-done.5 = f32[64,128]{1,0:T(8,128)S(1)} collective-permute-done((f32[64,128]{1,0:T(8,128)S(1)}, f32[64,128]{1,0:T(8,128)S(1)}, u32[]{:S(2)}, u32[]{:S(2)}) %collective-permute-start.5) | collective-permute-done | bytes 32800 | tf_op jit(solution)/shard_map/ppermute | solution.py:307
  16.9 0.0 copy-start
  16.9 1.9 %collective-permute-start.6 = (f32[64,128]{1,0:T(8,128)S(1)}, f32[64,128]{1,0:T(8,128)S(1)}, u32[]{:S(2)}, u32[]{:S(2)}) collective-permute-start(f32[64,128]{1,0:T(8,128)S(1)} %add.9), channel_id=1, source_target_pairs={{0,4},{2,6},{4,0},{6,2},{8,12},{10,14},{12,8},{14,10},{1,5},{3,7},... | collective-permute-start | bytes 98312 | tf_op jit(solution)/shard_map/ppermute | solution.py:307
  18.8 0.0 copy-done.3
  18.8 2.1 %collective-permute-done.6 = f32[64,128]{1,0:T(8,128)S(1)} collective-permute-done((f32[64,128]{1,0:T(8,128)S(1)}, f32[64,128]{1,0:T(8,128)S(1)}, u32[]{:S(2)}, u32[]{:S(2)}) %collective-permute-start.6) | collective-permute-done | bytes 32800 | tf_op jit(solution)/shard_map/ppermute | solution.py:307
  20.9 0.5 %collective-permute-start.7 = (f32[64,128]{1,0:T(8,128)S(1)}, f32[64,128]{1,0:T(8,128)S(1)}, u32[]{:S(2)}, u32[]{:S(2)}) collective-permute-start(f32[64,128]{1,0:T(8,128)S(1)} %add.10), channel_id=1, source_target_pairs={{0,2},{2,0},{4,6},{6,4},{8,10},{10,8},{12,14},{14,12},{1,3},{3,1},... | collective-permute-start | bytes 98312 | tf_op jit(solution)/shard_map/ppermute | solution.py:307
  21.5 0.0 collective-permute-done.4.refs_3_
  21.5 0.0 copy-done.2
  21.5 1.0 %turn_queries.1.turned_ref = bf16[64,4096]{1,0:T(8,128)(2,1)S(1)} custom-call(bf16[8,4096]{1,0:T(8,128)(2,1)S(1)} %bitcast.12, bf16[24,4096]{1,0:T(8,128)(2,1)S(1)} %constant_dynamic-update-slice_fusion.refs_1_, bf16[8,4096]{1,0:T(8,128)(2,1)S(1)} %collective-permute-done.refs_2_, bf16[24,4096]{1,0:T(8,128)(2,1)S(1)} %collective-permute-done.4.refs_3_), custom_call_target="tpu_custom_call" | custom-call | flops 1073741824 | bytes 1048576 | tf_op jit(solution)/shard_map/turn_queries/pallas_call | solution.py:142
  22.5 0.0 copy-start.1
  22.5 2.3 %collective-permute-done.7 = f32[64,128]{1,0:T(8,128)S(1)} collective-permute-done((f32[64,128]{1,0:T(8,128)S(1)}, f32[64,128]{1,0:T(8,128)S(1)}, u32[]{:S(2)}, u32[]{:S(2)}) %collective-permute-start.7) | collective-permute-done | bytes 32800 | tf_op jit(solution)/shard_map/ppermute | solution.py:307
  24.8 0.0 copy-done
  24.8 5.6 %solve_and_score.1 = f32[8,2,8,128]{3,2,1,0:T(8,128)S(1)} custom-call(s32[8]{0:T(128)S(1)} %broadcast_xor_fusion.route_ref, f32[64,128]{1,0:T(8,128)S(1)} %add.11.cov_ref, bf16[64,4096]{1,0:T(8,128)(2,1)S(1)} %turn_queries.1.turned_ref, bf16[256,4096]{1,0:T(8,128)(2,1)S(1)} %bitcast.5), custom_call_target="tpu_custom_call" | custom-call | flops 201326592 | bytes 2097152 | tf_op jit(solution)/shard_map/solve_and_score/pallas_call | solution.py:261
  30.5 11.0 %all_to_all.5 = f32[16,8,128]{2,1,0:T(8,128)S(1)} all-to-all(f32[16,8,128]{2,1,0:T(8,128)S(1)} %bitcast.6), channel_id=1, replica_groups=mesh['groups'=2,'dp'=8,'layer'=2] {'dp','layer'}, dimensions={0} | all-to-all | bytes 131072 | tf_op jit(solution)/shard_map/all_to_all | solution.py:340
  41.5 0.0 copy-done.1
  41.5 1.2 %pick_tiles.1 = f32[4,8,128]{2,1,0:T(8,128)} custom-call(s32[1,4]{1,0:T(1,128)S(1)} %copy-done.1, f32[8,2,8,128]{3,2,1,0:T(8,128)S(1)} %bitcast.7), custom_call_target="tpu_custom_call" | custom-call | tf_op jit(solution)/shard_map/pick_tiles/pallas_call | solution.py:296
  (7 shorter events, 0.0 us)
Async XLA Ops:
  0.0 12.0 %collective-permute-start = (bf16[8,4096]{1,0:T(8,128)(2,1)}, bf16[8,4096]{1,0:T(8,128)(2,1)S(1)}, u32[]{:S(2)}, u32[]{:S(2)}) collective-permute-start(bf16[8,4096]{1,0:T(8,128)(2,1)} %bitcast.8), channel_id=1, source_target_pairs={{0,2},{2,0},{4,6},{6,4},{8,10},{10,8},{12,14},{14,12},{1,3},{3,1},... | collective-permute-start | bytes 196616 | tf_op jit(solution)/shard_map/ppermute | solution.py:307
  2.9 9.1 %collective-permute-start.1 = (bf16[8,4096]{1,0:T(8,128)(2,1)}, bf16[8,4096]{1,0:T(8,128)(2,1)S(1)}, u32[]{:S(2)}, u32[]{:S(2)}) collective-permute-start(bf16[8,4096]{1,0:T(8,128)(2,1)} %bitcast.9), channel_id=1, source_target_pairs={{0,8},{2,10},{4,12},{6,14},{8,0},{10,2},{12,4},{14,6},{1,9},{3,11}... | collective-permute-start | bytes 196616 | tf_op jit(solution)/shard_map/ppermute | solution.py:307
  5.5 6.5 %collective-permute-start.2 = (bf16[8,4096]{1,0:T(8,128)(2,1)}, bf16[8,4096]{1,0:T(8,128)(2,1)S(1)}, u32[]{:S(2)}, u32[]{:S(2)}) collective-permute-start(bf16[8,4096]{1,0:T(8,128)(2,1)} %bitcast.10), channel_id=1, source_target_pairs={{0,12},{2,14},{4,8},{6,10},{8,4},{10,6},{12,0},{14,2},{1,13},{3,15... | collective-permute-start | bytes 196616 | tf_op jit(solution)/shard_map/ppermute | solution.py:307
  6.9 5.2 %collective-permute-start.3 = (bf16[8,4096]{1,0:T(8,128)(2,1)}, bf16[8,4096]{1,0:T(8,128)(2,1)S(1)}, u32[]{:S(2)}, u32[]{:S(2)}) collective-permute-start(bf16[8,4096]{1,0:T(8,128)(2,1)} %bitcast.11), channel_id=1, source_target_pairs={{0,4},{2,6},{4,0},{6,2},{8,12},{10,14},{12,8},{14,10},{1,5},{3,7},... | collective-permute-start | bytes 196616 | tf_op jit(solution)/shard_map/ppermute | solution.py:307
  9.8 9.0 %copy-start.3 = (s32[8]{0:T(128)S(1)}, s32[8]{0:T(128)}, u32[]{:S(2)}) copy-start(s32[8]{0:T(128)} %constant.8.clone) | copy-start | bytes 100
  9.8 11.6 %copy-start.2 = (bf16[8,1,4096]{2,0,1:T(8,128)(2,1)S(1)}, bf16[8,1,4096]{2,0,1:T(8,128)(2,1)}, u32[]{:S(2)}) copy-start(bf16[8,1,4096]{2,0,1:T(8,128)(2,1)} %param.5) | copy-start | bytes 196612
  12.1 4.9 %collective-permute-start.5 = (f32[64,128]{1,0:T(8,128)S(1)}, f32[64,128]{1,0:T(8,128)S(1)}, u32[]{:S(2)}, u32[]{:S(2)}) collective-permute-start(f32[64,128]{1,0:T(8,128)S(1)} %covariance.1), channel_id=1, source_target_pairs={{0,8},{2,10},{4,12},{6,14},{8,0},{10,2},{12,4},{14,6},{1,9},{3,11}... | collective-permute-start | bytes 98312 | tf_op jit(solution)/shard_map/ppermute | solution.py:307
  15.0 6.5 %collective-permute-start.4 = (bf16[24,4096]{1,0:T(8,128)(2,1)S(1)}, bf16[24,4096]{1,0:T(8,128)(2,1)S(1)}, u32[]{:S(2)}, u32[]{:S(2)}) collective-permute-start(bf16[24,4096]{1,0:T(8,128)(2,1)S(1)} %constant_dynamic-update-slice_fusion.refs_1_), channel_id=1, source_target_pairs={{0,2},{2,0},{4,6},{6,4},{8,10},{10,8},{12,14},{14,12},{1,3},{3,1},... | collective-permute-start | bytes 589832 | tf_op jit(solution)/shard_map/ppermute | solution.py:307
  16.9 7.9 %copy-start = (bf16[256,1,4096]{2,0,1:T(8,128)(2,1)S(1)}, bf16[256,1,4096]{2,0,1:T(8,128)(2,1)}, u32[]{:S(2)}) copy-start(bf16[256,1,4096]{2,0,1:T(8,128)(2,1)} %param.4) | copy-start | bytes 6291460
  16.9 4.0 %collective-permute-start.6 = (f32[64,128]{1,0:T(8,128)S(1)}, f32[64,128]{1,0:T(8,128)S(1)}, u32[]{:S(2)}, u32[]{:S(2)}) collective-permute-start(f32[64,128]{1,0:T(8,128)S(1)} %add.9), channel_id=1, source_target_pairs={{0,4},{2,6},{4,0},{6,2},{8,12},{10,14},{12,8},{14,10},{1,5},{3,7},... | collective-permute-start | bytes 98312 | tf_op jit(solution)/shard_map/ppermute | solution.py:307
  20.9 3.9 %collective-permute-start.7 = (f32[64,128]{1,0:T(8,128)S(1)}, f32[64,128]{1,0:T(8,128)S(1)}, u32[]{:S(2)}, u32[]{:S(2)}) collective-permute-start(f32[64,128]{1,0:T(8,128)S(1)} %add.10), channel_id=1, source_target_pairs={{0,2},{2,0},{4,6},{6,4},{8,10},{10,8},{12,14},{14,12},{1,3},{3,1},... | collective-permute-start | bytes 98312 | tf_op jit(solution)/shard_map/ppermute | solution.py:307
  22.5 19.0 %copy-start.1 = (s32[1,4]{1,0:T(1,128)S(1)}, s32[1,4]{1,0:T(1,128)}, u32[]{:S(2)}) copy-start(s32[1,4]{1,0:T(1,128)} %listed_ref.1) | copy-start | bytes 52

commit v6 on v3

--- a/solution.py
+++ b/solution.py
@@ -318,17 +318,16 @@
     total_count = float(examples * shard_count)
     order = jnp.arange(shard_count, dtype=jnp.int32)
     if shard_count == 8:
-        quarter = exchange(own_queries, 4, shard_count)
-        in_sum, rows = staged_rows(train)
-        quarter, in_sum = lax.optimization_barrier((quarter, in_sum))
-        column = jnp.concatenate([own_queries, quarter], axis=0)
-        other = exchange(column, 2, shard_count)
-        cov = covariance_sums(in_sum, rows)
-        other, cov = lax.optimization_barrier((other, cov))
-        column = jnp.concatenate([column, other], axis=0)
+        far = exchange(own_queries, 4, shard_count)
+        cov = covariance_sums(*staged_rows(train))
+        far, cov = lax.optimization_barrier((far, cov))
+        column = jnp.concatenate([own_queries, far], axis=0)
+        cov = cov + exchange(cov, 1, shard_count)
+        near = exchange(column, 2, shard_count)
+        near, cov = lax.optimization_barrier((near, cov))
+        cov = cov + exchange(cov, 4, shard_count)
+        column = jnp.concatenate([column, near], axis=0)
         queries = [column, exchange(column, 1, shard_count)]
-        for distance in (1, 4):
-            cov = cov + exchange(cov, distance, shard_count)
         last = exchange(cov, 2, shard_count)
         turned, cov = lax.optimization_barrier((turned_queries(queries), cov))
         cov = cov + last

time: 49.4 us -> 41.8 us (0.85)
  waiting for transfers between devices: 11.3 us -> 7.96 us
  blocking collectives: 13.1 us -> 9.87 us
  starting transfers between devices: 11.9 us -> 11 us
    ppermute x6, waiting for transfers between devices: 11.3 us -> 7.96 us  [exchange(): return lax.ppermute(values, 'dp', [(k, k ^ distance) for k in range(count)])]
    all_to_all x1, blocking collectives: 13.1 us -> 9.87 us  [shards(): lax.all_to_all(outgoing, ('dp', 'layer'), split_axis=0, concat_axis=0, ti...]
    ppermute x6, starting transfers between devices: 11.9 us -> 11 us  [exchange(): return lax.ppermute(values, 'dp', [(k, k ^ distance) for k in range(count)])]
  transfers between devices with their start and end apart: 6 -> 6, of which waited for: 5 -> 3; matrix products, arithmetic and copies ran while one was open for 0% -> 0% of each run, Pallas kernels for 12% -> 14%
where the time goes in v6:
time: 41.8 us; the launch traced here: 41.6 us
  Pallas kernels  12.7 us (30%)
  starting transfers between devices  11 us (26%)
  blocking collectives  9.87 us (24%)
  waiting for transfers between devices  7.96 us (19%)
    ppermute x6, starting transfers between devices, exchange(): return lax.ppermute(values, 'dp', [(k, k ^ distance) for k in range(count)])  11 us
    all_to_all x1, blocking collectives, shards(): lax.all_to_all(outgoing, ('dp', 'layer'), split_axis=0, concat_axis=0, ti...  9.87 us
    ppermute x6, waiting for transfers between devices, exchange(): return lax.ppermute(values, 'dp', [(k, k ^ distance) for k in range(count)])  7.96 us
    pallas_call x1, Pallas kernels, all_scores(): pl.pallas_call(functools.partial(score_kernel, total_count), out_shape=ja...  5.6 us
    pallas_call x1, Pallas kernels, staged_rows(): pl.pallas_call(stage_kernel, out_shape=(jax.ShapeDtypeStruct((K_IN, K_IN)...  2.7 us
    pallas_call x1, Pallas kernels, covariance_sums(): pl.pallas_call(gram_kernel, out_shape=jax.ShapeDtypeStruct((K_OUT, 2 * K_...  2.16 us
    pallas_call x1, Pallas kernels, picked(): pl.pallas_call(pick_kernel, out_shape=jax.ShapeDtypeStruct((listed.shape[...  1.15 us
    pallas_call x1, Pallas kernels, turned_queries(): pl.pallas_call(turn_kernel, out_shape=jax.ShapeDtypeStruct((K_OUT, total...  1.04 us
  transfers between devices with their start and end apart: 6, of which 3 were waited for; matrix products, arithmetic and copies ran while one was open for 0% of the time, Pallas kernels for 14%

profile of v6, /device:TPU:0, one launch (start us, length us, event | category | flops | bytes accessed | tf_op | source)
XLA Modules:
  0.0 41.6 jit_solution(10686927725365819402)
XLA Ops:
  0.0 4.0 %collective-permute-start = (bf16[8,4096]{1,0:T(8,128)(2,1)}, bf16[8,4096]{1,0:T(8,128)(2,1)S(1)}, u32[]{:S(2)}, u32[]{:S(2)}) collective-permute-start(bf16[8,4096]{1,0:T(8,128)(2,1)} %bitcast.8), channel_id=1, source_target_pairs={{0,8},{2,10},{4,12},{6,14},{8,0},{10,2},{12,4},{14,6},{1,9},{3,11}... | collective-permute-start | bytes 196616 | tf_op jit(solution)/shard_map/ppermute | solution.py:307
  4.0 2.7 %stage_rows.1 = (f32[64,64]{1,0:T(8,128)S(1)}, bf16[512,2048]{1,0:T(8,128)(2,1)S(1)}) custom-call(bf16[256,4096]{1,0:T(8,128)(2,1)} %bitcast.4), custom_call_target="tpu_custom_call" | custom-call | flops 2147483648 | bytes 2097152 | tf_op jit(solution)/shard_map/stage_rows/pallas_call | solution.py:85
  6.7 0.0 copy-start.2
  6.8 0.0 copy-start.3
  6.8 2.2 %covariance.1 = f32[64,128]{1,0:T(8,128)S(1)} custom-call(f32[64,64]{1,0:T(8,128)S(1)} %get-tuple-element.13.in_ref, bf16[512,2048]{1,0:T(8,128)(2,1)S(1)} %get-tuple-element.14.rows_ref), custom_call_target="tpu_custom_call" | custom-call | flops 1073741824 | bytes 2097152 | tf_op jit(solution)/shard_map/covariance/pallas_call | solution.py:105
  8.9 0.0 collective-permute-done
  8.9 0.0 copy-done.2
  9.0 1.6 %collective-permute-start.1 = (bf16[16,4096]{1,0:T(8,128)(2,1)S(1)}, bf16[16,4096]{1,0:T(8,128)(2,1)S(1)}, u32[]{:S(2)}, u32[]{:S(2)}) collective-permute-start(bf16[16,4096]{1,0:T(8,128)(2,1)S(1)} %pad_maximum_fusion.1), channel_id=1, source_target_pairs={{0,4},{2,6},{4,0},{6,2},{8,12},{10,14},{12,8},{14,10},{1,5},{3,7},... | collective-permute-start | bytes 393224 | tf_op jit(solution)/shard_map/ppermute | solution.py:307
  10.6 1.5 %collective-permute-start.2 = (f32[64,128]{1,0:T(8,128)S(1)}, f32[64,128]{1,0:T(8,128)S(1)}, u32[]{:S(2)}, u32[]{:S(2)}) collective-permute-start(f32[64,128]{1,0:T(8,128)S(1)} %covariance.1), channel_id=1, source_target_pairs={{0,2},{2,0},{4,6},{6,4},{8,10},{10,8},{12,14},{14,12},{1,3},{3,1},... | collective-permute-start | bytes 98312 | tf_op jit(solution)/shard_map/ppermute | solution.py:307
  12.1 2.4 %collective-permute-done.2 = f32[64,128]{1,0:T(8,128)S(1)} collective-permute-done((f32[64,128]{1,0:T(8,128)S(1)}, f32[64,128]{1,0:T(8,128)S(1)}, u32[]{:S(2)}, u32[]{:S(2)}) %collective-permute-start.2) | collective-permute-done | bytes 32800 | tf_op jit(solution)/shard_map/ppermute | solution.py:307
  14.5 0.0 collective-permute-done.1
  14.6 0.0 copy-start
  14.6 1.6 %collective-permute-start.3 = (bf16[32,4096]{1,0:T(8,128)(2,1)S(1)}, bf16[32,4096]{1,0:T(8,128)(2,1)S(1)}, u32[]{:S(2)}, u32[]{:S(2)}) collective-permute-start(bf16[32,4096]{1,0:T(8,128)(2,1)S(1)} %pad_maximum_fusion.refs_0_), channel_id=1, source_target_pairs={{0,2},{2,0},{4,6},{6,4},{8,10},{10,8},{12,14},{14,12},{1,3},{3,1},... | collective-permute-start | bytes 786440 | tf_op jit(solution)/shard_map/ppermute | solution.py:307
  16.1 1.3 %collective-permute-start.4 = (f32[64,128]{1,0:T(8,128)S(1)}, f32[64,128]{1,0:T(8,128)S(1)}, u32[]{:S(2)}, u32[]{:S(2)}) collective-permute-start(f32[64,128]{1,0:T(8,128)S(1)} %add.9), channel_id=1, source_target_pairs={{0,8},{2,10},{4,12},{6,14},{8,0},{10,2},{12,4},{14,6},{1,9},{3,11}... | collective-permute-start | bytes 98312 | tf_op jit(solution)/shard_map/ppermute | solution.py:307
  17.5 0.0 copy-done.3
  17.5 3.6 %collective-permute-done.4 = f32[64,128]{1,0:T(8,128)S(1)} collective-permute-done((f32[64,128]{1,0:T(8,128)S(1)}, f32[64,128]{1,0:T(8,128)S(1)}, u32[]{:S(2)}, u32[]{:S(2)}) %collective-permute-start.4) | collective-permute-done | bytes 32800 | tf_op jit(solution)/shard_map/ppermute | solution.py:307
  21.1 0.9 %collective-permute-start.5 = (f32[64,128]{1,0:T(8,128)S(1)}, f32[64,128]{1,0:T(8,128)S(1)}, u32[]{:S(2)}, u32[]{:S(2)}) collective-permute-start(f32[64,128]{1,0:T(8,128)S(1)} %add.10), channel_id=1, source_target_pairs={{0,4},{2,6},{4,0},{6,2},{8,12},{10,14},{12,8},{14,10},{1,5},{3,7},... | collective-permute-start | bytes 98312 | tf_op jit(solution)/shard_map/ppermute | solution.py:307
  22.0 0.0 collective-permute-done.3.refs_1_
  22.0 1.0 %turn_queries.1.turned_ref = bf16[64,4096]{1,0:T(8,128)(2,1)S(1)} custom-call(bf16[32,4096]{1,0:T(8,128)(2,1)S(1)} %pad_maximum_fusion.refs_0_, bf16[32,4096]{1,0:T(8,128)(2,1)S(1)} %collective-permute-done.3.refs_1_), custom_call_target="tpu_custom_call" | custom-call | flops 1073741824 | bytes 1048576 | tf_op jit(solution)/shard_map/turn_queries/pallas_call | solution.py:142
  23.0 0.0 copy-start.1
  23.0 1.9 %collective-permute-done.5 = f32[64,128]{1,0:T(8,128)S(1)} collective-permute-done((f32[64,128]{1,0:T(8,128)S(1)}, f32[64,128]{1,0:T(8,128)S(1)}, u32[]{:S(2)}, u32[]{:S(2)}) %collective-permute-start.5) | collective-permute-done | bytes 32800 | tf_op jit(solution)/shard_map/ppermute | solution.py:307
  25.0 0.0 copy-done
  25.0 5.6 %solve_and_score.1 = f32[8,2,8,128]{3,2,1,0:T(8,128)S(1)} custom-call(s32[8]{0:T(128)S(1)} %broadcast_xor_fusion.route_ref, f32[64,128]{1,0:T(8,128)S(1)} %add.11.cov_ref, bf16[64,4096]{1,0:T(8,128)(2,1)S(1)} %turn_queries.1.turned_ref, bf16[256,4096]{1,0:T(8,128)(2,1)S(1)} %bitcast.5), custom_call_target="tpu_custom_call" | custom-call | flops 201326592 | bytes 2097152 | tf_op jit(solution)/shard_map/solve_and_score/pallas_call | solution.py:261
  30.6 9.9 %all_to_all.5 = f32[16,8,128]{2,1,0:T(8,128)S(1)} all-to-all(f32[16,8,128]{2,1,0:T(8,128)S(1)} %bitcast.6), channel_id=1, replica_groups=mesh['groups'=2,'dp'=8,'layer'=2] {'dp','layer'}, dimensions={0} | all-to-all | bytes 131072 | tf_op jit(solution)/shard_map/all_to_all | solution.py:342
  40.5 0.0 copy-done.1
  40.5 1.2 %pick_tiles.1 = f32[4,8,128]{2,1,0:T(8,128)} custom-call(s32[1,4]{1,0:T(1,128)S(1)} %copy-done.1, f32[8,2,8,128]{3,2,1,0:T(8,128)S(1)} %bitcast.7), custom_call_target="tpu_custom_call" | custom-call | tf_op jit(solution)/shard_map/pick_tiles/pallas_call | solution.py:296
  (6 shorter events, 0.1 us)
Async XLA Ops:
  0.0 8.9 %collective-permute-start = (bf16[8,4096]{1,0:T(8,128)(2,1)}, bf16[8,4096]{1,0:T(8,128)(2,1)S(1)}, u32[]{:S(2)}, u32[]{:S(2)}) collective-permute-start(bf16[8,4096]{1,0:T(8,128)(2,1)} %bitcast.8), channel_id=1, source_target_pairs={{0,8},{2,10},{4,12},{6,14},{8,0},{10,2},{12,4},{14,6},{1,9},{3,11}... | collective-permute-start | bytes 196616 | tf_op jit(solution)/shard_map/ppermute | solution.py:307
  6.7 2.2 %copy-start.2 = (bf16[8,1,4096]{2,0,1:T(8,128)(2,1)S(1)}, bf16[8,1,4096]{2,0,1:T(8,128)(2,1)}, u32[]{:S(2)}) copy-start(bf16[8,1,4096]{2,0,1:T(8,128)(2,1)} %param.5) | copy-start | bytes 196612
  6.8 10.7 %copy-start.3 = (s32[8]{0:T(128)S(1)}, s32[8]{0:T(128)}, u32[]{:S(2)}) copy-start(s32[8]{0:T(128)} %constant.8.clone) | copy-start | bytes 100
  9.0 5.6 %collective-permute-start.1 = (bf16[16,4096]{1,0:T(8,128)(2,1)S(1)}, bf16[16,4096]{1,0:T(8,128)(2,1)S(1)}, u32[]{:S(2)}, u32[]{:S(2)}) collective-permute-start(bf16[16,4096]{1,0:T(8,128)(2,1)S(1)} %pad_maximum_fusion.1), channel_id=1, source_target_pairs={{0,4},{2,6},{4,0},{6,2},{8,12},{10,14},{12,8},{14,10},{1,5},{3,7},... | collective-permute-start | bytes 393224 | tf_op jit(solution)/shard_map/ppermute | solution.py:307
  10.6 3.9 %collective-permute-start.2 = (f32[64,128]{1,0:T(8,128)S(1)}, f32[64,128]{1,0:T(8,128)S(1)}, u32[]{:S(2)}, u32[]{:S(2)}) collective-permute-start(f32[64,128]{1,0:T(8,128)S(1)} %covariance.1), channel_id=1, source_target_pairs={{0,2},{2,0},{4,6},{6,4},{8,10},{10,8},{12,14},{14,12},{1,3},{3,1},... | collective-permute-start | bytes 98312 | tf_op jit(solution)/shard_map/ppermute | solution.py:307
  14.6 10.4 %copy-start = (bf16[256,1,4096]{2,0,1:T(8,128)(2,1)S(1)}, bf16[256,1,4096]{2,0,1:T(8,128)(2,1)}, u32[]{:S(2)}) copy-start(bf16[256,1,4096]{2,0,1:T(8,128)(2,1)} %param.4) | copy-start | bytes 6291460
  14.6 7.4 %collective-permute-start.3 = (bf16[32,4096]{1,0:T(8,128)(2,1)S(1)}, bf16[32,4096]{1,0:T(8,128)(2,1)S(1)}, u32[]{:S(2)}, u32[]{:S(2)}) collective-permute-start(bf16[32,4096]{1,0:T(8,128)(2,1)S(1)} %pad_maximum_fusion.refs_0_), channel_id=1, source_target_pairs={{0,2},{2,0},{4,6},{6,4},{8,10},{10,8},{12,14},{14,12},{1,3},{3,1},... | collective-permute-start | bytes 786440 | tf_op jit(solution)/shard_map/ppermute | solution.py:307
  16.1 4.9 %collective-permute-start.4 = (f32[64,128]{1,0:T(8,128)S(1)}, f32[64,128]{1,0:T(8,128)S(1)}, u32[]{:S(2)}, u32[]{:S(2)}) collective-permute-start(f32[64,128]{1,0:T(8,128)S(1)} %add.9), channel_id=1, source_target_pairs={{0,8},{2,10},{4,12},{6,14},{8,0},{10,2},{12,4},{14,6},{1,9},{3,11}... | collective-permute-start | bytes 98312 | tf_op jit(solution)/shard_map/ppermute | solution.py:307
  21.1 3.9 %collective-permute-start.5 = (f32[64,128]{1,0:T(8,128)S(1)}, f32[64,128]{1,0:T(8,128)S(1)}, u32[]{:S(2)}, u32[]{:S(2)}) collective-permute-start(f32[64,128]{1,0:T(8,128)S(1)} %add.10), channel_id=1, source_target_pairs={{0,4},{2,6},{4,0},{6,2},{8,12},{10,14},{12,8},{14,10},{1,5},{3,7},... | collective-permute-start | bytes 98312 | tf_op jit(solution)/shard_map/ppermute | solution.py:307
  23.0 17.4 %copy-start.1 = (s32[1,4]{1,0:T(1,128)S(1)}, s32[1,4]{1,0:T(1,128)}, u32[]{:S(2)}) copy-start(s32[1,4]{1,0:T(1,128)} %listed_ref.1) | copy-start | bytes 52

commit v7 on v6

--- a/solution.py
+++ b/solution.py
@@ -48,11 +48,16 @@
         source = train_ref.at[:, pl.ds(g * chunk, chunk)]
         copies.append(pltpu.make_async_copy(source, held.at[g], arrived.at[g]))
         copies[-1].start()
+    row = lax.broadcasted_iota(jnp.int32, (pair, pair), 0)
+    lane = lax.broadcasted_iota(jnp.int32, (pair, pair), 1)
+    unit = jnp.where(row == lane, 1.0, 0.0).astype(BF16)
     for m in range(width // pair):
         if m * pair % chunk == 0:
             copies[m * pair // chunk].wait()
         begin = m * pair % chunk
-        block = held[m * pair // chunk, :, begin:begin + pair].astype(F32).T
+        block = lax.dot_general(
+            unit, held[m * pair // chunk, :, begin:begin + pair], NT, preferred_element_type=F32
+        )
         for k in range(4):
             start = (4 * m + k) * examples
             by_in[:, start:start + examples] = block[k * K_IN:(k + 1) * K_IN, :].astype(BF16)
@@ -66,17 +71,24 @@
 
 
 def gram_kernel(in_ref, rows_ref, cov_ref):
-    count = rows_ref.shape[0]
-    every = lax.dot_general(rows_ref[...], rows_ref[...], NT, preferred_element_type=F32)
+    count = rows_ref.shape[0] // 2
     row = lax.broadcasted_iota(jnp.int32, (count, count), 0)
     lane = lax.broadcasted_iota(jnp.int32, (count, count), 1)
-    every = jnp.where((row & 7) == (lane & 7), every, 0.0)
-    summed = jnp.sum(every.reshape(count // 8, 8, count), axis=1)
+    same = (row & 7) == (lane & 7)
     lane = lax.broadcasted_iota(jnp.int32, (count, count // 8), 0)
     column = lax.broadcasted_iota(jnp.int32, (count, count // 8), 1)
     merge = jnp.where(lane // 8 == column, 1.0, 0.0).astype(BF16)
-    out_sum = sum(jnp.dot(part, merge, preferred_element_type=F32) for part in reversed(split(summed, 3)))
-    cov_ref[...] = jnp.concatenate([in_ref[...], out_sum], axis=1)
+    blocks = []
+    for a, b in ((0, 0), (0, 1), (1, 1)):
+        left = rows_ref[a * count:(a + 1) * count, :]
+        right = rows_ref[b * count:(b + 1) * count, :]
+        every = jnp.where(same, lax.dot_general(left, right, NT, preferred_element_type=F32), 0.0)
+        summed = jnp.sum(every.reshape(count // 8, 8, count), axis=1)
+        parts = split(summed, 3)
+        blocks.append(sum(jnp.dot(part, merge, preferred_element_type=F32) for part in reversed(parts)))
+    top = jnp.concatenate([blocks[0], blocks[1]], axis=1)
+    bottom = jnp.concatenate([blocks[1].T, blocks[2]], axis=1)
+    cov_ref[...] = jnp.concatenate([in_ref[...], jnp.concatenate([top, bottom], axis=0)], axis=1)
 
 
 def staged_rows(train):
@@ -236,10 +248,11 @@
         once = jnp.concatenate([once[:, k * LANES:(k + 1) * LANES] for k in range(group)], axis=0)
         wide = jnp.concatenate(split(once, 2), axis=1)
         twice = jnp.dot(wide, right[...], preferred_element_type=F32)
-        solved[g * group * K_OUT:(g + 1) * group * K_OUT, :] = twice[:, :LANES] + twice[:, LANES:]
+        solved[g * group:(g + 1) * group, :, :] = (twice[:, :LANES] + twice[:, LANES:]).reshape(group, K_OUT, LANES)
+    by_row = [jnp.swapaxes(solved[:, 8 * k:8 * (k + 1), :], 0, 1) for k in range(K_OUT // 8)]
     for c in range(blocks):
-        first = solved[pl.ds(c, half, stride=K_OUT), :]
-        second = solved[pl.ds(c + blocks, half, stride=K_OUT), :]
+        first = by_row[c // 8][c % 8]
+        second = by_row[(c + blocks) // 8][c % 8]
         even, odd = swap_pair(first, second)
         ready[:half, c * LANES:(c + 1) * LANES] = even.astype(BF16)
         ready[half:, c * LANES:(c + 1) * LANES] = odd.astype(BF16)
@@ -272,7 +285,7 @@
         scratch_shapes=[
             pltpu.VMEM((K_OUT, 3 * K_OUT), BF16),
             pltpu.VMEM((2 * LANES, 2 * LANES), BF16),
-            pltpu.VMEM((CHUNK // 2 * K_OUT, LANES), F32),
+            pltpu.VMEM((CHUNK // 2, K_OUT, LANES), F32),
             pltpu.VMEM((CHUNK, width), BF16),
         ],
         compiler_params=pltpu.CompilerParams(vmem_limit_bytes=VMEM_LIMIT),
@@ -283,24 +296,10 @@
     )(route, cov, turned, train)
 
 
-def pick_kernel(listed_ref, received_ref, out_ref):
-    for r in range(out_ref.shape[0]):
-        shard = listed_ref[0, r]
-        total = received_ref[shard, 0]
-        for layer in range(1, received_ref.shape[1]):
-            total = total + received_ref[shard, layer]
-        out_ref[r] = total
-
-
 def picked(listed, received):
-    return pl.pallas_call(
-        pick_kernel,
-        out_shape=jax.ShapeDtypeStruct((listed.shape[1],) + received.shape[2:], F32),
-        in_specs=[pl.BlockSpec(memory_space=pltpu.SMEM), pl.BlockSpec(memory_space=pltpu.VMEM)],
-        out_specs=pl.BlockSpec(memory_space=pltpu.VMEM),
-        compiler_params=pltpu.CompilerParams(vmem_limit_bytes=VMEM_LIMIT),
-        name="pick_tiles",
-    )(listed, received)
+    shard = jnp.arange(received.shape[0], dtype=jnp.int32)
+    wanted = (listed[0][:, None] == shard[None, :])[:, :, None, None, None]
+    return jnp.sum(jnp.where(wanted, received[None], 0.0), axis=(1, 2))
 
 
 def exchange(values, distance, count):
@@ -320,7 +319,7 @@
     if shard_count == 8:
         far = exchange(own_queries, 4, shard_count)
         cov = covariance_sums(*staged_rows(train))
-        far, cov = lax.optimization_barrier((far, cov))
+        far, _ = lax.optimization_barrier((far, cov))
         column = jnp.concatenate([own_queries, far], axis=0)
         cov = cov + exchange(cov, 1, shard_count)
         near = exchange(column, 2, shard_count)

time: 41.8 us -> 44 us (1.053)
  blocking collectives: 9.87 us -> 0 us
  waiting for transfers between devices: 7.96 us -> 15.7 us
  starting transfers between devices: 11 us -> 13.5 us
  Pallas kernels: 12.7 us -> 13.6 us
  other arithmetic: 0.06 us -> 0.84 us
    all_to_all x1 -> x0, blocking collectives: 9.87 us -> none  [shards(): lax.all_to_all(outgoing, ('dp', 'layer'), split_axis=0, concat_axis=0, ti...]
    all_to_all x0 -> x1, waiting for transfers between devices: none -> 6.78 us  [shards(): lax.all_to_all(outgoing, ('dp', 'layer'), split_axis=0, concat_axis=0, ti...]
    all_to_all x0 -> x1, starting transfers between devices: none -> 3.49 us  [shards(): lax.all_to_all(outgoing, ('dp', 'layer'), split_axis=0, concat_axis=0, ti...]
    pallas_call x1, Pallas kernels: 2.7 us -> 4.46 us  [staged_rows(): pl.pallas_call(stage_kernel, out_shape=(jax.ShapeDtypeStruct((K_IN, K_IN)...]
    pallas_call x1 -> x0, Pallas kernels: 1.15 us -> none  [picked(): pl.pallas_call(pick_kernel, out_shape=jax.ShapeDtypeStruct((listed.shape[...]
    ppermute x6, starting transfers between devices: 11 us -> 9.99 us  [exchange(): return lax.ppermute(values, 'dp', [(k, k ^ distance) for k in range(count)])]
    ppermute x6, waiting for transfers between devices: 7.96 us -> 8.94 us  [exchange(): return lax.ppermute(values, 'dp', [(k, k ^ distance) for k in range(count)])]
    reduce_sum x0 -> x1, other arithmetic: none -> 0.72 us  [picked(): return jnp.sum(jnp.where(wanted, received[None], 0.0), axis=(1, 2))]
  transfers between devices with their start and end apart: 6 -> 7, of which waited for: 3 -> 4; matrix products, arithmetic and copies ran while one was open for 0% -> 0% of each run, Pallas kernels for 14% -> 18%
where the time goes in v7:
time: 44 us; the launch traced here: 43.8 us
  waiting for transfers between devices  15.7 us (36%)
  Pallas kernels  13.6 us (31%)
  starting transfers between devices  13.5 us (31%)
  other arithmetic  0.84 us (2%)
    ppermute x6, starting transfers between devices, exchange(): return lax.ppermute(values, 'dp', [(k, k ^ distance) for k in range(count)])  9.99 us
    ppermute x6, waiting for transfers between devices, exchange(): return lax.ppermute(values, 'dp', [(k, k ^ distance) for k in range(count)])  8.94 us
    all_to_all x1, waiting for transfers between devices, shards(): lax.all_to_all(outgoing, ('dp', 'layer'), split_axis=0, concat_axis=0, ti...  6.78 us
    pallas_call x1, Pallas kernels, all_scores(): pl.pallas_call(functools.partial(score_kernel, total_count), out_shape=ja...  5.84 us
    pallas_call x1, Pallas kernels, staged_rows(): pl.pallas_call(stage_kernel, out_shape=(jax.ShapeDtypeStruct((K_IN, K_IN)...  4.46 us
    all_to_all x1, starting transfers between devices, shards(): lax.all_to_all(outgoing, ('dp', 'layer'), split_axis=0, concat_axis=0, ti...  3.49 us
    pallas_call x1, Pallas kernels, covariance_sums(): pl.pallas_call(gram_kernel, out_shape=jax.ShapeDtypeStruct((K_OUT, 2 * K_...  2.28 us
    pallas_call x1, Pallas kernels, turned_queries(): pl.pallas_call(turn_kernel, out_shape=jax.ShapeDtypeStruct((K_OUT, total...  1.04 us
  transfers between devices with their start and end apart: 7, of which 4 were waited for; matrix products, arithmetic and copies ran while one was open for 0% of the time, Pallas kernels for 18%

profile of v7, /device:TPU:0, one launch (start us, length us, event | category | flops | bytes accessed | tf_op | source)
XLA Modules:
  0.0 43.8 jit_solution(17659807368631904150)
XLA Ops:
  0.0 4.0 %collective-permute-start = (bf16[8,4096]{1,0:T(8,128)(2,1)}, bf16[8,4096]{1,0:T(8,128)(2,1)S(1)}, u32[]{:S(2)}, u32[]{:S(2)}) collective-permute-start(bf16[8,4096]{1,0:T(8,128)(2,1)} %bitcast.8), channel_id=1, source_target_pairs={{0,8},{2,10},{4,12},{6,14},{8,0},{10,2},{12,4},{14,6},{1,9},{3,11}... | collective-permute-start | bytes 196616 | tf_op jit(solution)/shard_map/ppermute | solution.py:306
  4.0 4.5 %stage_rows.1 = (f32[64,64]{1,0:T(8,128)S(1)}, bf16[512,2048]{1,0:T(8,128)(2,1)S(1)}) custom-call(bf16[256,4096]{1,0:T(8,128)(2,1)} %bitcast.5), custom_call_target="tpu_custom_call" | custom-call | flops 2147483648 | bytes 2097152 | tf_op jit(solution)/shard_map/stage_rows/pallas_call | solution.py:97
  8.5 0.0 copy-start.1
  8.5 0.0 copy-start.3
  8.5 2.3 %covariance.1 = f32[64,128]{1,0:T(8,128)S(1)} custom-call(f32[64,64]{1,0:T(8,128)S(1)} %get-tuple-element.12.in_ref, bf16[512,2048]{1,0:T(8,128)(2,1)S(1)} %get-tuple-element.13.rows_ref), custom_call_target="tpu_custom_call" | custom-call | flops 1073741824 | bytes 2097152 | tf_op jit(solution)/shard_map/covariance/pallas_call | solution.py:117
  10.8 0.0 collective-permute-done
  10.8 0.0 copy-done.1
  10.8 1.6 %collective-permute-start.1 = (bf16[16,4096]{1,0:T(8,128)(2,1)S(1)}, bf16[16,4096]{1,0:T(8,128)(2,1)S(1)}, u32[]{:S(2)}, u32[]{:S(2)}) collective-permute-start(bf16[16,4096]{1,0:T(8,128)(2,1)S(1)} %pad_maximum_fusion.1), channel_id=1, source_target_pairs={{0,4},{2,6},{4,0},{6,2},{8,12},{10,14},{12,8},{14,10},{1,5},{3,7},... | collective-permute-start | bytes 393224 | tf_op jit(solution)/shard_map/ppermute | solution.py:306
  12.5 1.5 %collective-permute-start.2 = (f32[64,128]{1,0:T(8,128)S(1)}, f32[64,128]{1,0:T(8,128)S(1)}, u32[]{:S(2)}, u32[]{:S(2)}) collective-permute-start(f32[64,128]{1,0:T(8,128)S(1)} %covariance.1), channel_id=1, source_target_pairs={{0,2},{2,0},{4,6},{6,4},{8,10},{10,8},{12,14},{14,12},{1,3},{3,1},... | collective-permute-start | bytes 98312 | tf_op jit(solution)/shard_map/ppermute | solution.py:306
  14.0 2.4 %collective-permute-done.2 = f32[64,128]{1,0:T(8,128)S(1)} collective-permute-done((f32[64,128]{1,0:T(8,128)S(1)}, f32[64,128]{1,0:T(8,128)S(1)}, u32[]{:S(2)}, u32[]{:S(2)}) %collective-permute-start.2) | collective-permute-done | bytes 32800 | tf_op jit(solution)/shard_map/ppermute | solution.py:306
  16.4 0.0 collective-permute-done.1
  16.4 0.0 copy-start
  16.5 1.6 %collective-permute-start.3 = (bf16[32,4096]{1,0:T(8,128)(2,1)S(1)}, bf16[32,4096]{1,0:T(8,128)(2,1)S(1)}, u32[]{:S(2)}, u32[]{:S(2)}) collective-permute-start(bf16[32,4096]{1,0:T(8,128)(2,1)S(1)} %pad_maximum_fusion.refs_0_), channel_id=1, source_target_pairs={{0,2},{2,0},{4,6},{6,4},{8,10},{10,8},{12,14},{14,12},{1,3},{3,1},... | collective-permute-start | bytes 786440 | tf_op jit(solution)/shard_map/ppermute | solution.py:306
  18.0 0.3 collective-permute-start.4
  18.4 0.0 copy-done.3
  18.4 4.6 %collective-permute-done.4 = f32[64,128]{1,0:T(8,128)S(1)} collective-permute-done((f32[64,128]{1,0:T(8,128)S(1)}, f32[64,128]{1,0:T(8,128)S(1)}, u32[]{:S(2)}, u32[]{:S(2)}) %collective-permute-start.4) | collective-permute-done | bytes 32800 | tf_op jit(solution)/shard_map/ppermute | solution.py:306
  22.9 0.9 %collective-permute-start.5 = (f32[64,128]{1,0:T(8,128)S(1)}, f32[64,128]{1,0:T(8,128)S(1)}, u32[]{:S(2)}, u32[]{:S(2)}) collective-permute-start(f32[64,128]{1,0:T(8,128)S(1)} %add.10), channel_id=1, source_target_pairs={{0,4},{2,6},{4,0},{6,2},{8,12},{10,14},{12,8},{14,10},{1,5},{3,7},... | collective-permute-start | bytes 98312 | tf_op jit(solution)/shard_map/ppermute | solution.py:306
  23.9 0.0 collective-permute-done.3.refs_1_
  23.9 1.0 %turn_queries.1.turned_ref = bf16[64,4096]{1,0:T(8,128)(2,1)S(1)} custom-call(bf16[32,4096]{1,0:T(8,128)(2,1)S(1)} %pad_maximum_fusion.refs_0_, bf16[32,4096]{1,0:T(8,128)(2,1)S(1)} %collective-permute-done.3.refs_1_), custom_call_target="tpu_custom_call" | custom-call | flops 1073741824 | bytes 1048576 | tf_op jit(solution)/shard_map/turn_queries/pallas_call | solution.py:154
  24.9 0.0 copy-start.2
  24.9 1.9 %collective-permute-done.5 = f32[64,128]{1,0:T(8,128)S(1)} collective-permute-done((f32[64,128]{1,0:T(8,128)S(1)}, f32[64,128]{1,0:T(8,128)S(1)}, u32[]{:S(2)}, u32[]{:S(2)}) %collective-permute-start.5) | collective-permute-done | bytes 32800 | tf_op jit(solution)/shard_map/ppermute | solution.py:306
  26.9 0.0 copy-done
  26.9 5.8 %solve_and_score.1 = f32[8,2,8,128]{3,2,1,0:T(8,128)} custom-call(s32[8]{0:T(128)S(1)} %broadcast_xor_fusion.route_ref, f32[64,128]{1,0:T(8,128)S(1)} %add.11.cov_ref, bf16[64,4096]{1,0:T(8,128)(2,1)S(1)} %turn_queries.1.turned_ref, bf16[256,4096]{1,0:T(8,128)(2,1)S(1)} %bitcast.6), custom_call_target="tpu_custom_call" | custom-call | flops 201326592 | bytes 2097152 | tf_op jit(solution)/shard_map/solve_and_score/pallas_call | solution.py:274
  32.7 3.5 %all-to-all-start = ((f32[16,8,128]{2,1,0:T(8,128)}), f32[16,8,128]{2,1,0:T(8,128)S(1)}, u32[]{:S(2)}, u32[]{:S(2)}) async-start(f32[16,8,128]{2,1,0:T(8,128)} %bitcast.3), calls=%async_computation | async-start | bytes 131072 | tf_op jit(solution)/shard_map/all_to_all | solution.py:341
  36.2 0.0 copy-done.2
  36.2 0.1 iota_compare_fusion
  36.3 6.8 %all-to-all-done = f32[16,8,128]{2,1,0:T(8,128)S(1)} async-done(((f32[16,8,128]{2,1,0:T(8,128)}), f32[16,8,128]{2,1,0:T(8,128)S(1)}, u32[]{:S(2)}, u32[]{:S(2)}) %all-to-all-start) | async-done | bytes 65568 | tf_op jit(solution)/shard_map/all_to_all | solution.py:341
  43.1 0.7 %select_reduce_fusion = f32[4,8,128]{2,1,0:T(8,128)} fusion(f32[8,2,8,128]{3,2,1,0:T(8,128)S(1)} %bitcast.7, pred[4,8]{1,0:T(4,128)(4,1)S(1)} %iota_compare_fusion), kind=kLoop, calls=%fused_computation.1 | loop fusion | flops 126976 | bytes 81952 | tf_op jit(solution)/shard_map/reduce_sum | solution.py:302
  (6 shorter events, 0.0 us)
Async XLA Ops:
  0.0 10.8 %collective-permute-start = (bf16[8,4096]{1,0:T(8,128)(2,1)}, bf16[8,4096]{1,0:T(8,128)(2,1)S(1)}, u32[]{:S(2)}, u32[]{:S(2)}) collective-permute-start(bf16[8,4096]{1,0:T(8,128)(2,1)} %bitcast.8), channel_id=1, source_target_pairs={{0,8},{2,10},{4,12},{6,14},{8,0},{10,2},{12,4},{14,6},{1,9},{3,11}... | collective-permute-start | bytes 196616 | tf_op jit(solution)/shard_map/ppermute | solution.py:306
  8.5 2.3 %copy-start.1 = (bf16[8,1,4096]{2,0,1:T(8,128)(2,1)S(1)}, bf16[8,1,4096]{2,0,1:T(8,128)(2,1)}, u32[]{:S(2)}) copy-start(bf16[8,1,4096]{2,0,1:T(8,128)(2,1)} %param.5) | copy-start | bytes 196612
  8.5 9.8 %copy-start.3 = (s32[8]{0:T(128)S(1)}, s32[8]{0:T(128)}, u32[]{:S(2)}) copy-start(s32[8]{0:T(128)} %constant.10.clone) | copy-start | bytes 100
  10.8 5.6 %collective-permute-start.1 = (bf16[16,4096]{1,0:T(8,128)(2,1)S(1)}, bf16[16,4096]{1,0:T(8,128)(2,1)S(1)}, u32[]{:S(2)}, u32[]{:S(2)}) collective-permute-start(bf16[16,4096]{1,0:T(8,128)(2,1)S(1)} %pad_maximum_fusion.1), channel_id=1, source_target_pairs={{0,4},{2,6},{4,0},{6,2},{8,12},{10,14},{12,8},{14,10},{1,5},{3,7},... | collective-permute-start | bytes 393224 | tf_op jit(solution)/shard_map/ppermute | solution.py:306
  12.5 3.9 %collective-permute-start.2 = (f32[64,128]{1,0:T(8,128)S(1)}, f32[64,128]{1,0:T(8,128)S(1)}, u32[]{:S(2)}, u32[]{:S(2)}) collective-permute-start(f32[64,128]{1,0:T(8,128)S(1)} %covariance.1), channel_id=1, source_target_pairs={{0,2},{2,0},{4,6},{6,4},{8,10},{10,8},{12,14},{14,12},{1,3},{3,1},... | collective-permute-start | bytes 98312 | tf_op jit(solution)/shard_map/ppermute | solution.py:306
  16.4 10.4 %copy-start = (bf16[256,1,4096]{2,0,1:T(8,128)(2,1)S(1)}, bf16[256,1,4096]{2,0,1:T(8,128)(2,1)}, u32[]{:S(2)}) copy-start(bf16[256,1,4096]{2,0,1:T(8,128)(2,1)} %param.4) | copy-start | bytes 6291460
  16.5 7.4 %collective-permute-start.3 = (bf16[32,4096]{1,0:T(8,128)(2,1)S(1)}, bf16[32,4096]{1,0:T(8,128)(2,1)S(1)}, u32[]{:S(2)}, u32[]{:S(2)}) collective-permute-start(bf16[32,4096]{1,0:T(8,128)(2,1)S(1)} %pad_maximum_fusion.refs_0_), channel_id=1, source_target_pairs={{0,2},{2,0},{4,6},{6,4},{8,10},{10,8},{12,14},{14,12},{1,3},{3,1},... | collective-permute-start | bytes 786440 | tf_op jit(solution)/shard_map/ppermute | solution.py:306
  18.0 4.9 %collective-permute-start.4 = (f32[64,128]{1,0:T(8,128)S(1)}, f32[64,128]{1,0:T(8,128)S(1)}, u32[]{:S(2)}, u32[]{:S(2)}) collective-permute-start(f32[64,128]{1,0:T(8,128)S(1)} %add.9), channel_id=1, source_target_pairs={{0,8},{2,10},{4,12},{6,14},{8,0},{10,2},{12,4},{14,6},{1,9},{3,11}... | collective-permute-start | bytes 98312 | tf_op jit(solution)/shard_map/ppermute | solution.py:306
  22.9 3.9 %collective-permute-start.5 = (f32[64,128]{1,0:T(8,128)S(1)}, f32[64,128]{1,0:T(8,128)S(1)}, u32[]{:S(2)}, u32[]{:S(2)}) collective-permute-start(f32[64,128]{1,0:T(8,128)S(1)} %add.10), channel_id=1, source_target_pairs={{0,4},{2,6},{4,0},{6,2},{8,12},{10,14},{12,8},{14,10},{1,5},{3,7},... | collective-permute-start | bytes 98312 | tf_op jit(solution)/shard_map/ppermute | solution.py:306
  24.9 11.3 %copy-start.2 = (s32[1,4]{1,0:T(1,128)S(1)}, s32[1,4]{1,0:T(1,128)}, u32[]{:S(2)}) copy-start(s32[1,4]{1,0:T(1,128)} %param.6) | copy-start | bytes 52
  32.7 10.4 %all-to-all-start = ((f32[16,8,128]{2,1,0:T(8,128)}), f32[16,8,128]{2,1,0:T(8,128)S(1)}, u32[]{:S(2)}, u32[]{:S(2)}) async-start(f32[16,8,128]{2,1,0:T(8,128)} %bitcast.3), calls=%async_computation | async-start | bytes 131072 | tf_op jit(solution)/shard_map/all_to_all | solution.py:341

commit v8 on v6

--- a/solution.py
+++ b/solution.py
@@ -169,25 +169,28 @@
 
 def inverses(matrix):
     size = matrix.shape[0]
-    lanes = lax.broadcasted_iota(jnp.int32, (size, LANES), 1)
+    sub = 8
+    lanes = lax.broadcasted_iota(jnp.int32, (sub, LANES), 1)
     offset = jnp.where(lanes < size, 0, size)
-    rows = lax.broadcasted_iota(jnp.int32, (size, LANES), 0)
-    row_lanes = lax.broadcasted_iota(jnp.int32, (8, LANES), 1)
-    row_place = jnp.where(row_lanes < size, row_lanes, row_lanes - size)
     place = lanes - offset
-
-    def spread_row(values, row):
-        return jnp.broadcast_to(values[row:row + 1, :], (8, LANES))
+    row = lax.broadcasted_iota(jnp.int32, (sub, LANES), 0)
+    tiles = [matrix[k:k + sub, :] for k in range(0, size, sub)]
+
+    def spread_row(values, at):
+        return jnp.broadcast_to(values[at:at + 1, :], (sub, LANES))
+
+    def column(values, lane):
+        return jnp.take_along_axis(values, offset + lane, axis=1, mode="promise_in_bounds")
 
     for begin in range(0, size, PIVOT):
-        columns = [jnp.take_along_axis(matrix, offset + begin + a, axis=1) for a in range(PIVOT)]
-        p = [[spread_row(columns[b], begin + a) for b in range(PIVOT)] for a in range(PIVOT)]
+        owner, first_row = begin // sub, begin % sub
+        inside = (place >= begin) & (place < begin + PIVOT)
+        columns = [[column(tile, begin + a) for a in range(PIVOT)] for tile in tiles]
+        p = [[spread_row(columns[owner][b], first_row + a) for b in range(PIVOT)] for a in range(PIVOT)]
         r = []
         for a in range(PIVOT):
-            row = spread_row(matrix, begin + a)
-            inside = (row_place >= begin) & (row_place < begin + PIVOT)
-            unit = jnp.where(row_place == begin + a, 1.0, 0.0)
-            r.append(jnp.where(inside, unit, row))
+            unit = jnp.where(place == begin + a, 1.0, 0.0)
+            r.append(jnp.where(inside, unit, spread_row(tiles[owner], first_row + a)))
         det = 1.0 / (p[0][0] * p[1][1] - p[0][1] * p[1][0])
         e = [[p[1][1] * det, -p[0][1] * det], [-p[1][0] * det, p[0][0] * det]]
         u = [[e[a][0] * p[0][b] + e[a][1] * p[1][b] for b in (2, 3)] for a in (0, 1)]
@@ -199,18 +202,18 @@
         last = [f[a][0] * t[0] + f[a][1] * t[1] for a in (0, 1)]
         first = [w[a] - (u[a][0] * last[0] + u[a][1] * last[1]) for a in (0, 1)]
         solved = first + last
-        inside = (place >= begin) & (place < begin + PIVOT)
-        rest = jnp.where(inside, 0.0, matrix)
-        tall = [jnp.concatenate([row] * (size // 8), axis=0) for row in solved]
-        for a in range(PIVOT):
-            rest = rest - columns[a] * tall[a]
-        for a in range(PIVOT):
-            rest = jnp.where(rows == begin + a, tall[a], rest)
-        matrix = rest
-    return matrix
-
-
-def score_kernel(total_count, route_ref, cov_ref, turned_ref, train_ref, out_ref, left, right, solved, ready):
+        for k in range(len(tiles)):
+            rest = jnp.where(inside, 0.0, tiles[k])
+            part = [columns[k][a] * solved[a] for a in range(PIVOT)]
+            rest = (rest - (part[0] + part[1])) - (part[2] + part[3])
+            if k == owner:
+                for a in range(PIVOT):
+                    rest = jnp.where(row == first_row + a, solved[a], rest)
+            tiles[k] = rest
+    return jnp.concatenate(tiles, axis=0)
+
+
+def score_kernel(total_count, route_ref, cov_ref, turned_ref, train_ref, out_ref, left, right, solved, wide, ready):
     blocks = K_OUT // 2
     half = CHUNK // 2
     step = pl.program_id(0)
@@ -233,10 +236,13 @@
         block = turned_ref[:, g * group * LANES:(g + 1) * group * LANES]
         tall = jnp.concatenate([block, block, block], axis=0)
         once = jnp.dot(left[...], tall, preferred_element_type=F32)
-        once = jnp.concatenate([once[:, k * LANES:(k + 1) * LANES] for k in range(group)], axis=0)
-        wide = jnp.concatenate(split(once, 2), axis=1)
-        twice = jnp.dot(wide, right[...], preferred_element_type=F32)
-        solved[g * group * K_OUT:(g + 1) * group * K_OUT, :] = twice[:, :LANES] + twice[:, LANES:]
+        for k in range(group):
+            high, small = split(once[:, k * LANES:(k + 1) * LANES], 2)
+            at = (g * group + k) * K_OUT
+            wide[at:at + K_OUT, :LANES] = high
+            wide[at:at + K_OUT, LANES:] = small
+    twice = jnp.dot(wide[...], right[...], preferred_element_type=F32)
+    solved[...] = twice[:, :LANES] + twice[:, LANES:]
     for c in range(blocks):
         first = solved[pl.ds(c, half, stride=K_OUT), :]
         second = solved[pl.ds(c + blocks, half, stride=K_OUT), :]
@@ -273,6 +279,7 @@
             pltpu.VMEM((K_OUT, 3 * K_OUT), BF16),
             pltpu.VMEM((2 * LANES, 2 * LANES), BF16),
             pltpu.VMEM((CHUNK // 2 * K_OUT, LANES), F32),
+            pltpu.VMEM((CHUNK // 2 * K_OUT, 2 * LANES), BF16),
             pltpu.VMEM((CHUNK, width), BF16),
         ],
         compiler_params=pltpu.CompilerParams(vmem_limit_bytes=VMEM_LIMIT),
@@ -281,26 +288,6 @@
         ),
         name="solve_and_score",
     )(route, cov, turned, train)
-
-
-def pick_kernel(listed_ref, received_ref, out_ref):
-    for r in range(out_ref.shape[0]):
-        shard = listed_ref[0, r]
-        total = received_ref[shard, 0]
-        for layer in range(1, received_ref.shape[1]):
-            total = total + received_ref[shard, layer]
-        out_ref[r] = total
-
-
-def picked(listed, received):
-    return pl.pallas_call(
-        pick_kernel,
-        out_shape=jax.ShapeDtypeStruct((listed.shape[1],) + received.shape[2:], F32),
-        in_specs=[pl.BlockSpec(memory_space=pltpu.SMEM), pl.BlockSpec(memory_space=pltpu.VMEM)],
-        out_specs=pl.BlockSpec(memory_space=pltpu.VMEM),
-        compiler_params=pltpu.CompilerParams(vmem_limit_bytes=VMEM_LIMIT),
-        name="pick_tiles",
-    )(listed, received)
 
 
 def exchange(values, distance, count):
@@ -320,7 +307,7 @@
     if shard_count == 8:
         far = exchange(own_queries, 4, shard_count)
         cov = covariance_sums(*staged_rows(train))
-        far, cov = lax.optimization_barrier((far, cov))
+        far, _ = lax.optimization_barrier((far, cov))
         column = jnp.concatenate([own_queries, far], axis=0)
         cov = cov + exchange(cov, 1, shard_count)
         near = exchange(column, 2, shard_count)
@@ -339,9 +326,11 @@
         route = order
     scores = all_scores(route, cov, turned, train, per_query, total_count)
     outgoing = scores.reshape(shard_count * layers, per_query, examples // layers)
+    wanted = listed[0][:, None] == jnp.arange(shard_count, dtype=jnp.int32)[None, :]
+    wanted, outgoing = lax.optimization_barrier((wanted, outgoing))
     received = lax.all_to_all(outgoing, ("dp", "layer"), split_axis=0, concat_axis=0, tiled=True)
-    received = received.reshape(shard_count, layers, per_query, examples // layers)
-    return picked(listed, received)
+    received = received.reshape(1, shard_count, layers, per_query, examples // layers)
+    return jnp.sum(jnp.where(wanted[:, :, None, None, None], received, 0.0), axis=(1, 2))
 
 
 def solution(mesh):

time: 41.8 us -> 41.3 us (0.988)
  Pallas kernels: 12.7 us -> 11.3 us
  other arithmetic: 0.06 us -> 0.85 us
    pallas_call x1 -> x0, Pallas kernels: 1.15 us -> none  [picked(): pl.pallas_call(pick_kernel, out_shape=jax.ShapeDtypeStruct((listed.shape[...]
    reduce_sum x0 -> x1, other arithmetic: none -> 0.72 us  [shards(): jnp.sum(jnp.where(wanted[:, :, None, None, None], received, 0.0), axis=(1...]
where the time goes in v8:
time: 41.3 us; the launch traced here: 41.1 us
  Pallas kernels  11.3 us (27%)
  starting transfers between devices  11 us (27%)
  blocking collectives  9.85 us (24%)
  waiting for transfers between devices  7.98 us (19%)
  other arithmetic  0.85 us (2%)
    ppermute x6, starting transfers between devices, exchange(): return lax.ppermute(values, 'dp', [(k, k ^ distance) for k in range(count)])  11 us
    all_to_all x1, blocking collectives, shards(): lax.all_to_all(outgoing, ('dp', 'layer'), split_axis=0, concat_axis=0, ti...  9.85 us
    ppermute x6, waiting for transfers between devices, exchange(): return lax.ppermute(values, 'dp', [(k, k ^ distance) for k in range(count)])  7.98 us
    pallas_call x1, Pallas kernels, all_scores(): pl.pallas_call(functools.partial(score_kernel, total_count), out_shape=ja...  5.43 us
    pallas_call x1, Pallas kernels, staged_rows(): pl.pallas_call(stage_kernel, out_shape=(jax.ShapeDtypeStruct((K_IN, K_IN)...  2.7 us
    pallas_call x1, Pallas kernels, covariance_sums(): pl.pallas_call(gram_kernel, out_shape=jax.ShapeDtypeStruct((K_OUT, 2 * K_...  2.16 us
    pallas_call x1, Pallas kernels, turned_queries(): pl.pallas_call(turn_kernel, out_shape=jax.ShapeDtypeStruct((K_OUT, total...  1.04 us
  transfers between devices with their start and end apart: 6, of which 3 were waited for; matrix products, arithmetic and copies ran while one was open for 0% of the time, Pallas kernels for 14%

profile of v8, /device:TPU:0, one launch (start us, length us, event | category | flops | bytes accessed | tf_op | source)
XLA Modules:
  0.0 41.1 jit_solution(13414265132745602561)
XLA Ops:
  0.0 4.0 %collective-permute-start = (bf16[8,4096]{1,0:T(8,128)(2,1)}, bf16[8,4096]{1,0:T(8,128)(2,1)S(1)}, u32[]{:S(2)}, u32[]{:S(2)}) collective-permute-start(bf16[8,4096]{1,0:T(8,128)(2,1)} %bitcast.9), channel_id=1, source_target_pairs={{0,8},{2,10},{4,12},{6,14},{8,0},{10,2},{12,4},{14,6},{1,9},{3,11}... | collective-permute-start | bytes 196616 | tf_op jit(solution)/shard_map/ppermute | solution.py:294
  4.0 2.7 %stage_rows.1 = (f32[64,64]{1,0:T(8,128)S(1)}, bf16[512,2048]{1,0:T(8,128)(2,1)S(1)}) custom-call(bf16[256,4096]{1,0:T(8,128)(2,1)} %bitcast.5), custom_call_target="tpu_custom_call" | custom-call | flops 2147483648 | bytes 2097152 | tf_op jit(solution)/shard_map/stage_rows/pallas_call | solution.py:85
  6.7 0.0 copy-start.1
  6.8 0.0 copy-start.2
  6.8 0.0 copy-start.3
  6.8 2.2 %covariance.1 = f32[64,128]{1,0:T(8,128)S(1)} custom-call(f32[64,64]{1,0:T(8,128)S(1)} %get-tuple-element.14.in_ref, bf16[512,2048]{1,0:T(8,128)(2,1)S(1)} %get-tuple-element.15.rows_ref), custom_call_target="tpu_custom_call" | custom-call | flops 1073741824 | bytes 2097152 | tf_op jit(solution)/shard_map/covariance/pallas_call | solution.py:105
  8.9 0.0 collective-permute-done
  8.9 0.0 copy-done.1
  9.0 1.6 %collective-permute-start.1 = (bf16[16,4096]{1,0:T(8,128)(2,1)S(1)}, bf16[16,4096]{1,0:T(8,128)(2,1)S(1)}, u32[]{:S(2)}, u32[]{:S(2)}) collective-permute-start(bf16[16,4096]{1,0:T(8,128)(2,1)S(1)} %pad_maximum_fusion.1), channel_id=1, source_target_pairs={{0,4},{2,6},{4,0},{6,2},{8,12},{10,14},{12,8},{14,10},{1,5},{3,7},... | collective-permute-start | bytes 393224 | tf_op jit(solution)/shard_map/ppermute | solution.py:294
  10.6 1.5 %collective-permute-start.2 = (f32[64,128]{1,0:T(8,128)S(1)}, f32[64,128]{1,0:T(8,128)S(1)}, u32[]{:S(2)}, u32[]{:S(2)}) collective-permute-start(f32[64,128]{1,0:T(8,128)S(1)} %covariance.1), channel_id=1, source_target_pairs={{0,2},{2,0},{4,6},{6,4},{8,10},{10,8},{12,14},{14,12},{1,3},{3,1},... | collective-permute-start | bytes 98312 | tf_op jit(solution)/shard_map/ppermute | solution.py:294
  12.1 2.4 %collective-permute-done.2 = f32[64,128]{1,0:T(8,128)S(1)} collective-permute-done((f32[64,128]{1,0:T(8,128)S(1)}, f32[64,128]{1,0:T(8,128)S(1)}, u32[]{:S(2)}, u32[]{:S(2)}) %collective-permute-start.2) | collective-permute-done | bytes 32800 | tf_op jit(solution)/shard_map/ppermute | solution.py:294
  14.5 0.0 collective-permute-done.1
  14.6 0.0 copy-start
  14.6 1.6 %collective-permute-start.3 = (bf16[32,4096]{1,0:T(8,128)(2,1)S(1)}, bf16[32,4096]{1,0:T(8,128)(2,1)S(1)}, u32[]{:S(2)}, u32[]{:S(2)}) collective-permute-start(bf16[32,4096]{1,0:T(8,128)(2,1)S(1)} %pad_maximum_fusion.refs_0_), channel_id=1, source_target_pairs={{0,2},{2,0},{4,6},{6,4},{8,10},{10,8},{12,14},{14,12},{1,3},{3,1},... | collective-permute-start | bytes 786440 | tf_op jit(solution)/shard_map/ppermute | solution.py:294
  16.2 0.0 copy-done.2
  16.2 0.1 iota_compare_fusion
  16.2 1.3 %collective-permute-start.4 = (f32[64,128]{1,0:T(8,128)S(1)}, f32[64,128]{1,0:T(8,128)S(1)}, u32[]{:S(2)}, u32[]{:S(2)}) collective-permute-start(f32[64,128]{1,0:T(8,128)S(1)} %add.9), channel_id=1, source_target_pairs={{0,8},{2,10},{4,12},{6,14},{8,0},{10,2},{12,4},{14,6},{1,9},{3,11}... | collective-permute-start | bytes 98312 | tf_op jit(solution)/shard_map/ppermute | solution.py:294
  17.5 0.0 copy-done.3
  17.5 3.6 %collective-permute-done.4 = f32[64,128]{1,0:T(8,128)S(1)} collective-permute-done((f32[64,128]{1,0:T(8,128)S(1)}, f32[64,128]{1,0:T(8,128)S(1)}, u32[]{:S(2)}, u32[]{:S(2)}) %collective-permute-start.4) | collective-permute-done | bytes 32800 | tf_op jit(solution)/shard_map/ppermute | solution.py:294
  21.2 0.9 %collective-permute-start.5 = (f32[64,128]{1,0:T(8,128)S(1)}, f32[64,128]{1,0:T(8,128)S(1)}, u32[]{:S(2)}, u32[]{:S(2)}) collective-permute-start(f32[64,128]{1,0:T(8,128)S(1)} %add.10), channel_id=1, source_target_pairs={{0,4},{2,6},{4,0},{6,2},{8,12},{10,14},{12,8},{14,10},{1,5},{3,7},... | collective-permute-start | bytes 98312 | tf_op jit(solution)/shard_map/ppermute | solution.py:294
  22.1 0.0 collective-permute-done.3.refs_1_
  22.1 1.0 %turn_queries.1.turned_ref = bf16[64,4096]{1,0:T(8,128)(2,1)S(1)} custom-call(bf16[32,4096]{1,0:T(8,128)(2,1)S(1)} %pad_maximum_fusion.refs_0_, bf16[32,4096]{1,0:T(8,128)(2,1)S(1)} %collective-permute-done.3.refs_1_), custom_call_target="tpu_custom_call" | custom-call | flops 1073741824 | bytes 1048576 | tf_op jit(solution)/shard_map/turn_queries/pallas_call | solution.py:142
  23.1 1.9 %collective-permute-done.5 = f32[64,128]{1,0:T(8,128)S(1)} collective-permute-done((f32[64,128]{1,0:T(8,128)S(1)}, f32[64,128]{1,0:T(8,128)S(1)}, u32[]{:S(2)}, u32[]{:S(2)}) %collective-permute-start.5) | collective-permute-done | bytes 32800 | tf_op jit(solution)/shard_map/ppermute | solution.py:294
  25.1 0.0 copy-done
  25.1 5.4 %solve_and_score.1 = f32[8,2,8,128]{3,2,1,0:T(8,128)S(1)} custom-call(s32[8]{0:T(128)S(1)} %broadcast_xor_fusion.route_ref, f32[64,128]{1,0:T(8,128)S(1)} %add.11.cov_ref, bf16[64,4096]{1,0:T(8,128)(2,1)S(1)} %turn_queries.1.turned_ref, bf16[256,4096]{1,0:T(8,128)(2,1)S(1)} %bitcast.6), custom_call_target="tpu_custom_call" | custom-call | flops 201326592 | bytes 2097152 | tf_op jit(solution)/shard_map/solve_and_score/pallas_call | solution.py:267
  30.5 9.8 %all_to_all.5 = f32[16,8,128]{2,1,0:T(8,128)S(1)} all-to-all(f32[16,8,128]{2,1,0:T(8,128)S(1)} %bitcast.7), channel_id=1, replica_groups=mesh['groups'=2,'dp'=8,'layer'=2] {'dp','layer'}, dimensions={0} | all-to-all | bytes 131072 | tf_op jit(solution)/shard_map/all_to_all | solution.py:331
  40.4 0.7 %select_reduce_fusion = f32[4,8,128]{2,1,0:T(8,128)} fusion(f32[8,2,8,128]{3,2,1,0:T(8,128)S(1)} %bitcast.8, pred[4,8]{1,0:T(4,128)(4,1)S(1)} %iota_compare_fusion), kind=kLoop, calls=%fused_computation.1 | loop fusion | flops 126976 | bytes 81952 | tf_op jit(solution)/shard_map/reduce_sum | solution.py:333
  (6 shorter events, 0.1 us)
Async XLA Ops:
  0.0 8.9 %collective-permute-start = (bf16[8,4096]{1,0:T(8,128)(2,1)}, bf16[8,4096]{1,0:T(8,128)(2,1)S(1)}, u32[]{:S(2)}, u32[]{:S(2)}) collective-permute-start(bf16[8,4096]{1,0:T(8,128)(2,1)} %bitcast.9), channel_id=1, source_target_pairs={{0,8},{2,10},{4,12},{6,14},{8,0},{10,2},{12,4},{14,6},{1,9},{3,11}... | collective-permute-start | bytes 196616 | tf_op jit(solution)/shard_map/ppermute | solution.py:294
  6.7 2.2 %copy-start.1 = (bf16[8,1,4096]{2,0,1:T(8,128)(2,1)S(1)}, bf16[8,1,4096]{2,0,1:T(8,128)(2,1)}, u32[]{:S(2)}) copy-start(bf16[8,1,4096]{2,0,1:T(8,128)(2,1)} %param.5) | copy-start | bytes 196612
  6.8 9.4 %copy-start.2 = (s32[1,4]{1,0:T(1,128)S(1)}, s32[1,4]{1,0:T(1,128)}, u32[]{:S(2)}) copy-start(s32[1,4]{1,0:T(1,128)} %param.6) | copy-start | bytes 52
  6.8 10.8 %copy-start.3 = (s32[8]{0:T(128)S(1)}, s32[8]{0:T(128)}, u32[]{:S(2)}) copy-start(s32[8]{0:T(128)} %constant.10.clone) | copy-start | bytes 100
  9.0 5.6 %collective-permute-start.1 = (bf16[16,4096]{1,0:T(8,128)(2,1)S(1)}, bf16[16,4096]{1,0:T(8,128)(2,1)S(1)}, u32[]{:S(2)}, u32[]{:S(2)}) collective-permute-start(bf16[16,4096]{1,0:T(8,128)(2,1)S(1)} %pad_maximum_fusion.1), channel_id=1, source_target_pairs={{0,4},{2,6},{4,0},{6,2},{8,12},{10,14},{12,8},{14,10},{1,5},{3,7},... | collective-permute-start | bytes 393224 | tf_op jit(solution)/shard_map/ppermute | solution.py:294
  10.6 3.9 %collective-permute-start.2 = (f32[64,128]{1,0:T(8,128)S(1)}, f32[64,128]{1,0:T(8,128)S(1)}, u32[]{:S(2)}, u32[]{:S(2)}) collective-permute-start(f32[64,128]{1,0:T(8,128)S(1)} %covariance.1), channel_id=1, source_target_pairs={{0,2},{2,0},{4,6},{6,4},{8,10},{10,8},{12,14},{14,12},{1,3},{3,1},... | collective-permute-start | bytes 98312 | tf_op jit(solution)/shard_map/ppermute | solution.py:294
  14.6 10.5 %copy-start = (bf16[256,1,4096]{2,0,1:T(8,128)(2,1)S(1)}, bf16[256,1,4096]{2,0,1:T(8,128)(2,1)}, u32[]{:S(2)}) copy-start(bf16[256,1,4096]{2,0,1:T(8,128)(2,1)} %param.4) | copy-start | bytes 6291460
  14.6 7.5 %collective-permute-start.3 = (bf16[32,4096]{1,0:T(8,128)(2,1)S(1)}, bf16[32,4096]{1,0:T(8,128)(2,1)S(1)}, u32[]{:S(2)}, u32[]{:S(2)}) collective-permute-start(bf16[32,4096]{1,0:T(8,128)(2,1)S(1)} %pad_maximum_fusion.refs_0_), channel_id=1, source_target_pairs={{0,2},{2,0},{4,6},{6,4},{8,10},{10,8},{12,14},{14,12},{1,3},{3,1},... | collective-permute-start | bytes 786440 | tf_op jit(solution)/shard_map/ppermute | solution.py:294
  16.2 4.9 %collective-permute-start.4 = (f32[64,128]{1,0:T(8,128)S(1)}, f32[64,128]{1,0:T(8,128)S(1)}, u32[]{:S(2)}, u32[]{:S(2)}) collective-permute-start(f32[64,128]{1,0:T(8,128)S(1)} %add.9), channel_id=1, source_target_pairs={{0,8},{2,10},{4,12},{6,14},{8,0},{10,2},{12,4},{14,6},{1,9},{3,11}... | collective-permute-start | bytes 98312 | tf_op jit(solution)/shard_map/ppermute | solution.py:294
  21.2 3.9 %collective-permute-start.5 = (f32[64,128]{1,0:T(8,128)S(1)}, f32[64,128]{1,0:T(8,128)S(1)}, u32[]{:S(2)}, u32[]{:S(2)}) collective-permute-start(f32[64,128]{1,0:T(8,128)S(1)} %add.10), channel_id=1, source_target_pairs={{0,4},{2,6},{4,0},{6,2},{8,12},{10,14},{12,8},{14,10},{1,5},{3,7},... | collective-permute-start | bytes 98312 | tf_op jit(solution)/shard_map/ppermute | solution.py:294

commit v9 on v8

--- a/solution.py
+++ b/solution.py
@@ -256,7 +256,7 @@
         owner = route_ref[step * (CHUNK // per_query) + s]
         for part in range(parts):
             piece = scores[s * per_query:(s + 1) * per_query, part * LANES:(part + 1) * LANES]
-            out_ref[owner, part, :, :] = piece
+            out_ref[owner, part, :, :] = piece.astype(BF16)
 
 
 def all_scores(route, cov, turned, train, per_query, total_count):
@@ -266,7 +266,7 @@
     parts = examples // LANES
     return pl.pallas_call(
         functools.partial(score_kernel, total_count),
-        out_shape=jax.ShapeDtypeStruct((shard_count, parts, per_query, LANES), F32),
+        out_shape=jax.ShapeDtypeStruct((shard_count, parts, per_query, LANES), BF16),
         grid=(steps,),
         in_specs=[
             pl.BlockSpec(memory_space=pltpu.SMEM),
@@ -305,20 +305,17 @@
     total_count = float(examples * shard_count)
     order = jnp.arange(shard_count, dtype=jnp.int32)
     if shard_count == 8:
-        far = exchange(own_queries, 4, shard_count)
+        column = [exchange(own_queries, distance, shard_count) for distance in (4, 6, 2)]
         cov = covariance_sums(*staged_rows(train))
-        far, _ = lax.optimization_barrier((far, cov))
-        column = jnp.concatenate([own_queries, far], axis=0)
-        cov = cov + exchange(cov, 1, shard_count)
-        near = exchange(column, 2, shard_count)
-        near, cov = lax.optimization_barrier((near, cov))
-        cov = cov + exchange(cov, 4, shard_count)
-        column = jnp.concatenate([column, near], axis=0)
+        column, cov = lax.optimization_barrier((column, cov))
+        column = jnp.concatenate([own_queries] + column, axis=0)
         queries = [column, exchange(column, 1, shard_count)]
-        last = exchange(cov, 2, shard_count)
+        for distance in (4, 2):
+            cov = cov + exchange(cov, distance, shard_count)
+        last = exchange(cov, 1, shard_count)
         turned, cov = lax.optimization_barrier((turned_queries(queries), cov))
         cov = cov + last
-        order = jnp.array([0, 4, 2, 6, 1, 5, 3, 7], jnp.int32)
+        order = jnp.array([0, 4, 6, 2, 1, 5, 7, 3], jnp.int32)
         route = own_index ^ order
     else:
         turned = turned_queries([lax.all_gather(own_queries, "dp", axis=0, tiled=True)])
@@ -329,7 +326,7 @@
     wanted = listed[0][:, None] == jnp.arange(shard_count, dtype=jnp.int32)[None, :]
     wanted, outgoing = lax.optimization_barrier((wanted, outgoing))
     received = lax.all_to_all(outgoing, ("dp", "layer"), split_axis=0, concat_axis=0, tiled=True)
-    received = received.reshape(1, shard_count, layers, per_query, examples // layers)
+    received = received.reshape(1, shard_count, layers, per_query, examples // layers).astype(F32)
     return jnp.sum(jnp.where(wanted[:, :, None, None, None], received, 0.0), axis=(1, 2))
 
 

time: 41.3 us -> 41.4 us (level)
  waiting for transfers between devices: 7.98 us -> 3.88 us
  starting transfers between devices: 11 us -> 13.4 us
  blocking collectives: 9.85 us -> 11.7 us
    ppermute x6 -> x7, waiting for transfers between devices: 7.98 us -> 3.88 us  [exchange(): return lax.ppermute(values, 'dp', [(k, k ^ distance) for k in range(count)])]
    ppermute x6 -> x7, starting transfers between devices: 11 us -> 13.4 us  [exchange(): return lax.ppermute(values, 'dp', [(k, k ^ distance) for k in range(count)])]
    all_to_all x1, blocking collectives: 9.85 us -> 11.7 us  [shards(): lax.all_to_all(outgoing, ('dp', 'layer'), split_axis=0, concat_axis=0, ti...]
  transfers between devices with their start and end apart: 6 -> 7, of which waited for: 3 -> 4; matrix products, arithmetic and copies ran while one was open for 0% -> 0% of each run, Pallas kernels for 14% -> 14%
where the time goes in v9:
time: 41.4 us; the launch traced here: 41.2 us
  starting transfers between devices  13.4 us (32%)
  blocking collectives  11.7 us (28%)
  Pallas kernels  11.4 us (28%)
  waiting for transfers between devices  3.88 us (9%)
  other arithmetic  0.83 us (2%)
    ppermute x7, starting transfers between devices, exchange(): return lax.ppermute(values, 'dp', [(k, k ^ distance) for k in range(count)])  13.4 us
    all_to_all x1, blocking collectives, shards(): lax.all_to_all(outgoing, ('dp', 'layer'), split_axis=0, concat_axis=0, ti...  11.7 us
    pallas_call x1, Pallas kernels, all_scores(): pl.pallas_call(functools.partial(score_kernel, total_count), out_shape=ja...  5.46 us
    ppermute x7, waiting for transfers between devices, exchange(): return lax.ppermute(values, 'dp', [(k, k ^ distance) for k in range(count)])  3.88 us
    pallas_call x1, Pallas kernels, staged_rows(): pl.pallas_call(stage_kernel, out_shape=(jax.ShapeDtypeStruct((K_IN, K_IN)...  2.71 us
    pallas_call x1, Pallas kernels, covariance_sums(): pl.pallas_call(gram_kernel, out_shape=jax.ShapeDtypeStruct((K_OUT, 2 * K_...  2.16 us
    pallas_call x1, Pallas kernels, turned_queries(): pl.pallas_call(turn_kernel, out_shape=jax.ShapeDtypeStruct((K_OUT, total...  1.04 us
  transfers between devices with their start and end apart: 7, of which 4 were waited for; matrix products, arithmetic and copies ran while one was open for 0% of the time, Pallas kernels for 14%

profile of v9, /device:TPU:0, one launch (start us, length us, event | category | flops | bytes accessed | tf_op | source)
XLA Modules:
  0.0 41.2 jit_solution(5388289375273955946)
XLA Ops:
  0.0 4.0 %collective-permute-start = (bf16[8,4096]{1,0:T(8,128)(2,1)}, bf16[8,4096]{1,0:T(8,128)(2,1)S(1)}, u32[]{:S(2)}, u32[]{:S(2)}) collective-permute-start(bf16[8,4096]{1,0:T(8,128)(2,1)} %bitcast.10), channel_id=1, source_target_pairs={{0,8},{2,10},{4,12},{6,14},{8,0},{10,2},{12,4},{14,6},{1,9},{3,11}... | collective-permute-start | bytes 196616 | tf_op jit(solution)/shard_map/ppermute | solution.py:294
  4.0 1.3 %collective-permute-start.1 = (bf16[8,4096]{1,0:T(8,128)(2,1)}, bf16[8,4096]{1,0:T(8,128)(2,1)S(1)}, u32[]{:S(2)}, u32[]{:S(2)}) collective-permute-start(bf16[8,4096]{1,0:T(8,128)(2,1)} %bitcast.11), channel_id=1, source_target_pairs={{0,12},{2,14},{4,8},{6,10},{8,4},{10,6},{12,0},{14,2},{1,13},{3,15... | collective-permute-start | bytes 196616 | tf_op jit(solution)/shard_map/ppermute | solution.py:294
  5.4 0.2 collective-permute-start.2
  5.6 2.7 %stage_rows.1 = (f32[64,64]{1,0:T(8,128)S(1)}, bf16[512,2048]{1,0:T(8,128)(2,1)S(1)}) custom-call(bf16[256,4096]{1,0:T(8,128)(2,1)} %bitcast.7), custom_call_target="tpu_custom_call" | custom-call | flops 2147483648 | bytes 2097152 | tf_op jit(solution)/shard_map/stage_rows/pallas_call | solution.py:85
  8.3 0.0 copy-start.1
  8.3 0.0 copy-start.2
  8.4 0.0 copy-start.3
  8.4 2.2 %covariance.1 = f32[64,128]{1,0:T(8,128)S(1)} custom-call(f32[64,64]{1,0:T(8,128)S(1)} %get-tuple-element.15.in_ref, bf16[512,2048]{1,0:T(8,128)(2,1)S(1)} %get-tuple-element.16.rows_ref), custom_call_target="tpu_custom_call" | custom-call | flops 1073741824 | bytes 2097152 | tf_op jit(solution)/shard_map/covariance/pallas_call | solution.py:105
  10.5 0.0 collective-permute-done
  10.5 0.0 collective-permute-done.1
  10.5 0.0 collective-permute-done.2
  10.6 2.9 %collective-permute-start.4 = (f32[64,128]{1,0:T(8,128)S(1)}, f32[64,128]{1,0:T(8,128)S(1)}, u32[]{:S(2)}, u32[]{:S(2)}) collective-permute-start(f32[64,128]{1,0:T(8,128)S(1)} %covariance.1), channel_id=1, source_target_pairs={{0,8},{2,10},{4,12},{6,14},{8,0},{10,2},{12,4},{14,6},{1,9},{3,11}... | collective-permute-start | bytes 98312 | tf_op jit(solution)/shard_map/ppermute | solution.py:294
  13.4 0.0 copy-done.1
  13.5 1.6 %collective-permute-start.3 = (bf16[32,4096]{1,0:T(8,128)(2,1)S(1)}, bf16[32,4096]{1,0:T(8,128)(2,1)S(1)}, u32[]{:S(2)}, u32[]{:S(2)}) collective-permute-start(bf16[32,4096]{1,0:T(8,128)(2,1)S(1)} %pad_maximum_fusion.refs_0_), channel_id=1, source_target_pairs={{0,2},{2,0},{4,6},{6,4},{8,10},{10,8},{12,14},{14,12},{1,3},{3,1},... | collective-permute-start | bytes 786440 | tf_op jit(solution)/shard_map/ppermute | solution.py:294
  15.0 0.0 copy-done.2
  15.0 0.1 iota_compare_fusion
  15.1 0.3 collective-permute-done.4
  15.4 0.0 copy-start
  15.4 1.9 %collective-permute-start.5 = (f32[64,128]{1,0:T(8,128)S(1)}, f32[64,128]{1,0:T(8,128)S(1)}, u32[]{:S(2)}, u32[]{:S(2)}) collective-permute-start(f32[64,128]{1,0:T(8,128)S(1)} %add.9), channel_id=1, source_target_pairs={{0,4},{2,6},{4,0},{6,2},{8,12},{10,14},{12,8},{14,10},{1,5},{3,7},... | collective-permute-start | bytes 98312 | tf_op jit(solution)/shard_map/ppermute | solution.py:294
  17.3 0.0 copy-done.3
  17.3 2.1 %collective-permute-done.5 = f32[64,128]{1,0:T(8,128)S(1)} collective-permute-done((f32[64,128]{1,0:T(8,128)S(1)}, f32[64,128]{1,0:T(8,128)S(1)}, u32[]{:S(2)}, u32[]{:S(2)}) %collective-permute-start.5) | collective-permute-done | bytes 32800 | tf_op jit(solution)/shard_map/ppermute | solution.py:294
  19.4 1.5 %collective-permute-start.6 = (f32[64,128]{1,0:T(8,128)S(1)}, f32[64,128]{1,0:T(8,128)S(1)}, u32[]{:S(2)}, u32[]{:S(2)}) collective-permute-start(f32[64,128]{1,0:T(8,128)S(1)} %add.10), channel_id=1, source_target_pairs={{0,2},{2,0},{4,6},{6,4},{8,10},{10,8},{12,14},{14,12},{1,3},{3,1},... | collective-permute-start | bytes 98312 | tf_op jit(solution)/shard_map/ppermute | solution.py:294
  20.9 0.4 %collective-permute-done.3.refs_1_ = bf16[32,4096]{1,0:T(8,128)(2,1)S(1)} collective-permute-done((bf16[32,4096]{1,0:T(8,128)(2,1)S(1)}, bf16[32,4096]{1,0:T(8,128)(2,1)S(1)}, u32[]{:S(2)}, u32[]{:S(2)}) %collective-permute-start.3) | collective-permute-done | bytes 262176 | tf_op jit(solution)/shard_map/ppermute | solution.py:294
  21.3 1.0 %turn_queries.1.turned_ref = bf16[64,4096]{1,0:T(8,128)(2,1)S(1)} custom-call(bf16[32,4096]{1,0:T(8,128)(2,1)S(1)} %pad_maximum_fusion.refs_0_, bf16[32,4096]{1,0:T(8,128)(2,1)S(1)} %collective-permute-done.3.refs_1_), custom_call_target="tpu_custom_call" | custom-call | flops 1073741824 | bytes 1048576 | tf_op jit(solution)/shard_map/turn_queries/pallas_call | solution.py:142
  22.4 1.0 %collective-permute-done.6 = f32[64,128]{1,0:T(8,128)S(1)} collective-permute-done((f32[64,128]{1,0:T(8,128)S(1)}, f32[64,128]{1,0:T(8,128)S(1)}, u32[]{:S(2)}, u32[]{:S(2)}) %collective-permute-start.6) | collective-permute-done | bytes 32800 | tf_op jit(solution)/shard_map/ppermute | solution.py:294
  23.4 0.0 copy-done
  23.4 5.5 %solve_and_score.1 = bf16[8,2,8,128]{3,2,1,0:T(8,128)(2,1)S(1)} custom-call(s32[8]{0:T(128)S(1)} %broadcast_xor_fusion.route_ref, f32[64,128]{1,0:T(8,128)S(1)} %add.11.cov_ref, bf16[64,4096]{1,0:T(8,128)(2,1)S(1)} %turn_queries.1.turned_ref, bf16[256,4096]{1,0:T(8,128)(2,1)S(1)} %bitcast.8), custom_call_target="tpu_custom_call" | custom-call | flops 201326592 | bytes 2097152 | tf_op jit(solution)/shard_map/solve_and_score/pallas_call | solution.py:267
  28.8 11.7 %all_to_all.5 = bf16[16,8,128]{2,1,0:T(8,128)(2,1)S(1)} all-to-all(bf16[16,8,128]{2,1,0:T(8,128)(2,1)S(1)} %bitcast.9), channel_id=1, replica_groups=mesh['groups'=2,'dp'=8,'layer'=2] {'dp','layer'}, dimensions={0} | all-to-all | bytes 65536 | tf_op jit(solution)/shard_map/all_to_all | solution.py:328
  40.5 0.7 %select_reduce_fusion = f32[4,8,128]{2,1,0:T(8,128)} fusion(f32[8,2,8,128]{3,2,1,0:T(8,128)S(1)} %bitcast_convert_fusion, pred[4,8]{1,0:T(4,128)(4,1)S(1)} %iota_compare_fusion), kind=kLoop, calls=%fused_computation.1 | loop fusion | flops 126976 | bytes 81952 | tf_op jit(solution)/shard_map/reduce_sum | solution.py:330
  (6 shorter events, 0.0 us)
Async XLA Ops:
  0.0 10.5 %collective-permute-start = (bf16[8,4096]{1,0:T(8,128)(2,1)}, bf16[8,4096]{1,0:T(8,128)(2,1)S(1)}, u32[]{:S(2)}, u32[]{:S(2)}) collective-permute-start(bf16[8,4096]{1,0:T(8,128)(2,1)} %bitcast.10), channel_id=1, source_target_pairs={{0,8},{2,10},{4,12},{6,14},{8,0},{10,2},{12,4},{14,6},{1,9},{3,11}... | collective-permute-start | bytes 196616 | tf_op jit(solution)/shard_map/ppermute | solution.py:294
  4.0 6.5 %collective-permute-start.1 = (bf16[8,4096]{1,0:T(8,128)(2,1)}, bf16[8,4096]{1,0:T(8,128)(2,1)S(1)}, u32[]{:S(2)}, u32[]{:S(2)}) collective-permute-start(bf16[8,4096]{1,0:T(8,128)(2,1)} %bitcast.11), channel_id=1, source_target_pairs={{0,12},{2,14},{4,8},{6,10},{8,4},{10,6},{12,0},{14,2},{1,13},{3,15... | collective-permute-start | bytes 196616 | tf_op jit(solution)/shard_map/ppermute | solution.py:294
  5.4 5.2 %collective-permute-start.2 = (bf16[8,4096]{1,0:T(8,128)(2,1)}, bf16[8,4096]{1,0:T(8,128)(2,1)S(1)}, u32[]{:S(2)}, u32[]{:S(2)}) collective-permute-start(bf16[8,4096]{1,0:T(8,128)(2,1)} %bitcast.12), channel_id=1, source_target_pairs={{0,4},{2,6},{4,0},{6,2},{8,12},{10,14},{12,8},{14,10},{1,5},{3,7},... | collective-permute-start | bytes 196616 | tf_op jit(solution)/shard_map/ppermute | solution.py:294
  8.3 5.1 %copy-start.1 = (bf16[8,1,4096]{2,0,1:T(8,128)(2,1)S(1)}, bf16[8,1,4096]{2,0,1:T(8,128)(2,1)}, u32[]{:S(2)}) copy-start(bf16[8,1,4096]{2,0,1:T(8,128)(2,1)} %param.5) | copy-start | bytes 196612
  8.3 6.7 %copy-start.2 = (s32[1,4]{1,0:T(1,128)S(1)}, s32[1,4]{1,0:T(1,128)}, u32[]{:S(2)}) copy-start(s32[1,4]{1,0:T(1,128)} %param.6) | copy-start | bytes 52
  8.4 9.0 %copy-start.3 = (s32[8]{0:T(128)S(1)}, s32[8]{0:T(128)}, u32[]{:S(2)}) copy-start(s32[8]{0:T(128)} %constant.10.clone) | copy-start | bytes 100
  10.6 4.9 %collective-permute-start.4 = (f32[64,128]{1,0:T(8,128)S(1)}, f32[64,128]{1,0:T(8,128)S(1)}, u32[]{:S(2)}, u32[]{:S(2)}) collective-permute-start(f32[64,128]{1,0:T(8,128)S(1)} %covariance.1), channel_id=1, source_target_pairs={{0,8},{2,10},{4,12},{6,14},{8,0},{10,2},{12,4},{14,6},{1,9},{3,11}... | collective-permute-start | bytes 98312 | tf_op jit(solution)/shard_map/ppermute | solution.py:294
  13.5 7.9 %collective-permute-start.3 = (bf16[32,4096]{1,0:T(8,128)(2,1)S(1)}, bf16[32,4096]{1,0:T(8,128)(2,1)S(1)}, u32[]{:S(2)}, u32[]{:S(2)}) collective-permute-start(bf16[32,4096]{1,0:T(8,128)(2,1)S(1)} %pad_maximum_fusion.refs_0_), channel_id=1, source_target_pairs={{0,2},{2,0},{4,6},{6,4},{8,10},{10,8},{12,14},{14,12},{1,3},{3,1},... | collective-permute-start | bytes 786440 | tf_op jit(solution)/shard_map/ppermute | solution.py:294
  15.4 7.9 %copy-start = (bf16[256,1,4096]{2,0,1:T(8,128)(2,1)S(1)}, bf16[256,1,4096]{2,0,1:T(8,128)(2,1)}, u32[]{:S(2)}) copy-start(bf16[256,1,4096]{2,0,1:T(8,128)(2,1)} %param.4) | copy-start | bytes 6291460
  15.4 4.0 %collective-permute-start.5 = (f32[64,128]{1,0:T(8,128)S(1)}, f32[64,128]{1,0:T(8,128)S(1)}, u32[]{:S(2)}, u32[]{:S(2)}) collective-permute-start(f32[64,128]{1,0:T(8,128)S(1)} %add.9), channel_id=1, source_target_pairs={{0,4},{2,6},{4,0},{6,2},{8,12},{10,14},{12,8},{14,10},{1,5},{3,7},... | collective-permute-start | bytes 98312 | tf_op jit(solution)/shard_map/ppermute | solution.py:294
  19.4 3.9 %collective-permute-start.6 = (f32[64,128]{1,0:T(8,128)S(1)}, f32[64,128]{1,0:T(8,128)S(1)}, u32[]{:S(2)}, u32[]{:S(2)}) collective-permute-start(f32[64,128]{1,0:T(8,128)S(1)} %add.10), channel_id=1, source_target_pairs={{0,2},{2,0},{4,6},{6,4},{8,10},{10,8},{12,14},{14,12},{1,3},{3,1},... | collective-permute-start | bytes 98312 | tf_op jit(solution)/shard_map/ppermute | solution.py:294

commit v10 on v8

--- a/solution.py
+++ b/solution.py
@@ -10,10 +10,12 @@
 K_IN = 64
 LANES = 128
 CHUNK = 64
+HALF = CHUNK // 2
 PIVOT = 4
 F32 = jnp.float32
 BF16 = jnp.bfloat16
 VMEM_LIMIT = 48 * 1024 * 1024
+INVERSE_COST = 2 * 10**9
 STAGE_VMEM_LIMIT = 50 * 1024 * 1024
 
 NT = (((1,), (1,)), ((), ()))
@@ -113,43 +115,33 @@
     )(in_sum, rows)
 
 
-def turn_kernel(*refs):
-    query_refs, out_ref, spread = refs[:-2], refs[-2], refs[-1]
-    blocks = out_ref.shape[0] // 2
-    half = CHUNK // 2
+def turn_kernel(query_ref, out_ref, spread):
+    count, width = query_ref.shape
+    blocks = width // LANES
+    pairs = count // 2
     for c in range(blocks):
-        at = c * CHUNK
-        for ref in query_refs:
-            count = ref.shape[0]
-            spread[at:at + count, :] = ref[:, c * LANES:(c + 1) * LANES].astype(F32)
-            at = at + count
-    for p in range(half):
-        first = spread[pl.ds(p, blocks, stride=CHUNK), :]
-        second = spread[pl.ds(p + half, blocks, stride=CHUNK), :]
+        spread[c * count:(c + 1) * count, :] = query_ref[:, c * LANES:(c + 1) * LANES].astype(F32)
+    for p in range(pairs):
+        first = spread[pl.ds(p, blocks, stride=count), :]
+        second = spread[pl.ds(p + pairs, blocks, stride=count), :]
         even, odd = swap_pair(first, second)
         out_ref[:blocks, p * LANES:(p + 1) * LANES] = even.astype(BF16)
         out_ref[blocks:, p * LANES:(p + 1) * LANES] = odd.astype(BF16)
 
 
 def turned_queries(queries):
-    width = queries[0].shape[1]
-    total = sum(part.shape[0] for part in queries)
-    steps = total // CHUNK
-    if steps == 1:
-        in_specs = [pl.BlockSpec(part.shape, lambda step: (0, 0)) for part in queries]
-    else:
-        in_specs = [pl.BlockSpec((CHUNK, width), lambda step: (step, 0))]
+    total, width = queries.shape
     return pl.pallas_call(
         turn_kernel,
         out_shape=jax.ShapeDtypeStruct((K_OUT, total * K_IN), BF16),
-        grid=(steps,),
-        in_specs=in_specs,
-        out_specs=pl.BlockSpec((K_OUT, CHUNK * K_IN), lambda step: (0, step)),
-        scratch_shapes=[pltpu.VMEM((width // LANES * CHUNK, LANES), F32)],
+        grid=(total // HALF,),
+        in_specs=[pl.BlockSpec((HALF, width), lambda step: (step, 0))],
+        out_specs=pl.BlockSpec((K_OUT, HALF * K_IN), lambda step: (0, step)),
+        scratch_shapes=[pltpu.VMEM((width // LANES * HALF, LANES), F32)],
         compiler_params=pltpu.CompilerParams(vmem_limit_bytes=VMEM_LIMIT),
         cost_estimate=pl.CostEstimate(flops=4096 * total * width, bytes_accessed=4 * total * width, transcendentals=0),
         name="turn_queries",
-    )(*queries)
+    )(queries)
 
 
 def damped(cov, total_count):
@@ -213,42 +205,60 @@
     return jnp.concatenate(tiles, axis=0)
 
 
-def score_kernel(total_count, route_ref, cov_ref, turned_ref, train_ref, out_ref, left, right, solved, wide, ready):
+def inverse_kernel(total_count, cov_ref, left_ref, right_ref):
+    inverse = inverses(damped(cov_ref[...], total_count))
+    turned = pltpu.roll(inverse, LANES // 2, 1)
+    low = low_half(K_OUT)
+    left_ref[...] = jnp.concatenate(split(turned[:, :K_OUT], 3), axis=1)
+    double = jnp.concatenate([jnp.where(low, inverse, 0.0), jnp.where(low, 0.0, turned)], axis=0)
+    high, small = split(double, 2)
+    right_ref[:LANES, :LANES] = high
+    right_ref[:LANES, LANES:] = small
+    right_ref[LANES:, :LANES] = high
+    right_ref[LANES:, LANES:] = jnp.zeros_like(small)
+
+
+def inverse_factors(cov, total_count):
+    return pl.pallas_call(
+        functools.partial(inverse_kernel, total_count),
+        out_shape=(
+            jax.ShapeDtypeStruct((K_OUT, 3 * K_OUT), BF16),
+            jax.ShapeDtypeStruct((2 * LANES, 2 * LANES), BF16),
+        ),
+        in_specs=[pl.BlockSpec(memory_space=pltpu.VMEM)],
+        out_specs=(pl.BlockSpec(memory_space=pltpu.VMEM), pl.BlockSpec(memory_space=pltpu.VMEM)),
+        compiler_params=pltpu.CompilerParams(vmem_limit_bytes=VMEM_LIMIT),
+        cost_estimate=pl.CostEstimate(flops=INVERSE_COST, bytes_accessed=0, transcendentals=0),
+        name="inverses",
+    )(cov)
+
+
+def score_kernel(route_ref, left_ref, right_ref, first_ref, second_ref, train_ref, out_ref, solved, wide, ready):
     blocks = K_OUT // 2
-    half = CHUNK // 2
+    pairs = HALF // 2
     step = pl.program_id(0)
-
-    @pl.when(step == 0)
-    def _():
-        inverse = inverses(damped(cov_ref[...], total_count))
-        turned = pltpu.roll(inverse, LANES // 2, 1)
-        low = low_half(K_OUT)
-        left[...] = jnp.concatenate(split(turned[:, :K_OUT], 3), axis=1)
-        double = jnp.concatenate([jnp.where(low, inverse, 0.0), jnp.where(low, 0.0, turned)], axis=0)
-        high, small = split(double, 2)
-        right[:LANES, :LANES] = high
-        right[:LANES, LANES:] = small
-        right[LANES:, :LANES] = high
-        right[LANES:, LANES:] = jnp.zeros_like(small)
-
     group = 4
-    for g in range(half // group):
-        block = turned_ref[:, g * group * LANES:(g + 1) * group * LANES]
-        tall = jnp.concatenate([block, block, block], axis=0)
-        once = jnp.dot(left[...], tall, preferred_element_type=F32)
-        for k in range(group):
-            high, small = split(once[:, k * LANES:(k + 1) * LANES], 2)
-            at = (g * group + k) * K_OUT
-            wide[at:at + K_OUT, :LANES] = high
-            wide[at:at + K_OUT, LANES:] = small
-    twice = jnp.dot(wide[...], right[...], preferred_element_type=F32)
+    for side, turned_ref in enumerate((first_ref, second_ref)):
+        for g in range(pairs // group):
+            block = turned_ref[:, g * group * LANES:(g + 1) * group * LANES]
+            tall = jnp.concatenate([block, block, block], axis=0)
+            once = jnp.dot(left_ref[...], tall, preferred_element_type=F32)
+            for k in range(group):
+                high, small = split(once[:, k * LANES:(k + 1) * LANES], 2)
+                at = (side * pairs + g * group + k) * K_OUT
+                wide[at:at + K_OUT, :LANES] = high
+                wide[at:at + K_OUT, LANES:] = small
+    twice = jnp.dot(wide[...], right_ref[...], preferred_element_type=F32)
     solved[...] = twice[:, :LANES] + twice[:, LANES:]
     for c in range(blocks):
-        first = solved[pl.ds(c, half, stride=K_OUT), :]
-        second = solved[pl.ds(c + blocks, half, stride=K_OUT), :]
+        first = solved[pl.ds(c, 2 * pairs, stride=K_OUT), :]
+        second = solved[pl.ds(c + blocks, 2 * pairs, stride=K_OUT), :]
         even, odd = swap_pair(first, second)
-        ready[:half, c * LANES:(c + 1) * LANES] = even.astype(BF16)
-        ready[half:, c * LANES:(c + 1) * LANES] = odd.astype(BF16)
+        columns = slice(c * LANES, (c + 1) * LANES)
+        for side in range(2):
+            at = side * HALF
+            ready[at:at + pairs, columns] = even[side * pairs:(side + 1) * pairs, :].astype(BF16)
+            ready[at + pairs:at + HALF, columns] = odd[side * pairs:(side + 1) * pairs, :].astype(BF16)
     scores = lax.dot_general(ready[...], train_ref[...], NT, preferred_element_type=F32)
     per_query = out_ref.shape[2]
     parts = out_ref.shape[1]
@@ -259,35 +269,40 @@
             out_ref[owner, part, :, :] = piece
 
 
-def all_scores(route, cov, turned, train, per_query, total_count):
+def all_scores(route, factors, turned, train, per_query):
     shard_count = route.shape[0]
     examples, width = train.shape
     steps = shard_count * per_query // CHUNK
     parts = examples // LANES
-    return pl.pallas_call(
-        functools.partial(score_kernel, total_count),
+    if len(turned) == 2:
+        places = [lambda step: (0, 0), lambda step: (0, 0)]
+    else:
+        turned = turned * 2
+        places = [lambda step: (0, 2 * step), lambda step: (0, 2 * step + 1)]
+    return pl.pallas_call(
+        score_kernel,
         out_shape=jax.ShapeDtypeStruct((shard_count, parts, per_query, LANES), F32),
         grid=(steps,),
         in_specs=[
             pl.BlockSpec(memory_space=pltpu.SMEM),
-            pl.BlockSpec((K_OUT, 2 * K_IN), lambda step: (0, 0)),
-            pl.BlockSpec((K_OUT, CHUNK * K_IN), lambda step: (0, step)),
+            pl.BlockSpec((K_OUT, 3 * K_OUT), lambda step: (0, 0)),
+            pl.BlockSpec((2 * LANES, 2 * LANES), lambda step: (0, 0)),
+            pl.BlockSpec((K_OUT, HALF * K_IN), places[0]),
+            pl.BlockSpec((K_OUT, HALF * K_IN), places[1]),
             pl.BlockSpec((examples, width), lambda step: (0, 0)),
         ],
         out_specs=pl.BlockSpec((shard_count, parts, per_query, LANES), lambda step: (0, 0, 0, 0)),
         scratch_shapes=[
-            pltpu.VMEM((K_OUT, 3 * K_OUT), BF16),
-            pltpu.VMEM((2 * LANES, 2 * LANES), BF16),
-            pltpu.VMEM((CHUNK // 2 * K_OUT, LANES), F32),
-            pltpu.VMEM((CHUNK // 2 * K_OUT, 2 * LANES), BF16),
+            pltpu.VMEM((HALF * K_OUT, LANES), F32),
+            pltpu.VMEM((HALF * K_OUT, 2 * LANES), BF16),
             pltpu.VMEM((CHUNK, width), BF16),
         ],
         compiler_params=pltpu.CompilerParams(vmem_limit_bytes=VMEM_LIMIT),
         cost_estimate=pl.CostEstimate(
             flops=2 * shard_count * per_query * width * (examples + 128), bytes_accessed=2 * examples * width, transcendentals=0
         ),
-        name="solve_and_score",
-    )(route, cov, turned, train)
+        name="products_and_scores",
+    )(route, *factors, *turned, train)
 
 
 def exchange(values, distance, count):
@@ -311,20 +326,22 @@
         column = jnp.concatenate([own_queries, far], axis=0)
         cov = cov + exchange(cov, 1, shard_count)
         near = exchange(column, 2, shard_count)
-        near, cov = lax.optimization_barrier((near, cov))
+        column = jnp.concatenate([column, near], axis=0)
         cov = cov + exchange(cov, 4, shard_count)
-        column = jnp.concatenate([column, near], axis=0)
-        queries = [column, exchange(column, 1, shard_count)]
+        beside = exchange(column, 1, shard_count)
         last = exchange(cov, 2, shard_count)
-        turned, cov = lax.optimization_barrier((turned_queries(queries), cov))
-        cov = cov + last
+        here, cov = lax.optimization_barrier((turned_queries(column), cov))
+        factors = inverse_factors(cov + last, total_count)
+        beside, _ = lax.optimization_barrier((beside, factors[0]))
+        turned = [here, turned_queries(beside)]
         order = jnp.array([0, 4, 2, 6, 1, 5, 3, 7], jnp.int32)
         route = own_index ^ order
     else:
-        turned = turned_queries([lax.all_gather(own_queries, "dp", axis=0, tiled=True)])
+        turned = [turned_queries(lax.all_gather(own_queries, "dp", axis=0, tiled=True))]
         cov = lax.psum(covariance_sums(*staged_rows(train)), "dp")
+        factors = inverse_factors(cov, total_count)
         route = order
-    scores = all_scores(route, cov, turned, train, per_query, total_count)
+    scores = all_scores(route, factors, turned, train, per_query)
     outgoing = scores.reshape(shard_count * layers, per_query, examples // layers)
     wanted = listed[0][:, None] == jnp.arange(shard_count, dtype=jnp.int32)[None, :]
     wanted, outgoing = lax.optimization_barrier((wanted, outgoing))

time: 41.3 us -> 39 us (0.944)
  starting transfers between devices: 11 us -> 9.26 us
  waiting for transfers between devices: 7.98 us -> 6.9 us
  blocking collectives: 9.85 us -> 10.6 us
    ppermute x6, starting transfers between devices: 11 us -> 9.26 us  [exchange(): return lax.ppermute(values, 'dp', [(k, k ^ distance) for k in range(count)])]
    ppermute x6, waiting for transfers between devices: 7.98 us -> 6.9 us  [exchange(): return lax.ppermute(values, 'dp', [(k, k ^ distance) for k in range(count)])]
    all_to_all x1, blocking collectives: 9.85 us -> 10.6 us  [shards(): lax.all_to_all(outgoing, ('dp', 'layer'), split_axis=0, concat_axis=0, ti...]
    pallas_call x1 -> x2, Pallas kernels: 1.04 us -> 0.87 us  [turned_queries(): pl.pallas_call(turn_kernel, out_shape=jax.ShapeDtypeStruct((K_OUT, total...]
    pallas_call x1 -> x2, Pallas kernels: 5.43 us -> 5.45 us  [the longest x1 2.9 us: all_scores(): pl.pallas_call(score_kernel, out_shape=jax.ShapeDtypeStruct((shard_count,...]
  transfers between devices with their start and end apart: 6 -> 6, of which waited for: 3 -> 4; matrix products, arithmetic and copies ran while one was open for 0% -> 0% of each run, Pallas kernels for 14% -> 20%
where the time goes in v10:
time: 39 us; the launch traced here: 38.9 us
  Pallas kernels  11.2 us (29%)
  blocking collectives  10.6 us (27%)
  starting transfers between devices  9.26 us (24%)
  waiting for transfers between devices  6.9 us (18%)
  other arithmetic  0.83 us (2%)
    all_to_all x1, blocking collectives, shards(): lax.all_to_all(outgoing, ('dp', 'layer'), split_axis=0, concat_axis=0, ti...  10.6 us
    ppermute x6, starting transfers between devices, exchange(): return lax.ppermute(values, 'dp', [(k, k ^ distance) for k in range(count)])  9.26 us
    ppermute x6, waiting for transfers between devices, exchange(): return lax.ppermute(values, 'dp', [(k, k ^ distance) for k in range(count)])  6.9 us
    pallas_call x1, Pallas kernels, all_scores(): pl.pallas_call(score_kernel, out_shape=jax.ShapeDtypeStruct((shard_count,...  2.9 us
    pallas_call x1, Pallas kernels, staged_rows(): pl.pallas_call(stage_kernel, out_shape=(jax.ShapeDtypeStruct((K_IN, K_IN)...  2.7 us
    pallas_call x1, Pallas kernels, inverse_factors(): pl.pallas_call(functools.partial(inverse_kernel, total_count), out_shape=...  2.56 us
    pallas_call x1, Pallas kernels, covariance_sums(): pl.pallas_call(gram_kernel, out_shape=jax.ShapeDtypeStruct((K_OUT, 2 * K_...  2.16 us
    pallas_call x2, Pallas kernels, turned_queries(): pl.pallas_call(turn_kernel, out_shape=jax.ShapeDtypeStruct((K_OUT, total...  0.87 us
  transfers between devices with their start and end apart: 6, of which 4 were waited for; matrix products, arithmetic and copies ran while one was open for 0% of the time, Pallas kernels for 20%

profile of v10, /device:TPU:0, one launch (start us, length us, event | category | flops | bytes accessed | tf_op | source)
XLA Modules:
  0.0 38.9 jit_solution(10649113631429336680)
XLA Ops:
  0.0 4.0 %collective-permute-start = (bf16[8,4096]{1,0:T(8,128)(2,1)}, bf16[8,4096]{1,0:T(8,128)(2,1)S(1)}, u32[]{:S(2)}, u32[]{:S(2)}) collective-permute-start(bf16[8,4096]{1,0:T(8,128)(2,1)} %bitcast.9), channel_id=1, source_target_pairs={{0,8},{2,10},{4,12},{6,14},{8,0},{10,2},{12,4},{14,6},{1,9},{3,11}... | collective-permute-start | bytes 196616 | tf_op jit(solution)/shard_map/ppermute | solution.py:309
  4.0 2.7 %stage_rows.1 = (f32[64,64]{1,0:T(8,128)S(1)}, bf16[512,2048]{1,0:T(8,128)(2,1)S(1)}) custom-call(bf16[256,4096]{1,0:T(8,128)(2,1)} %bitcast.5), custom_call_target="tpu_custom_call" | custom-call | flops 2147483648 | bytes 2097152 | tf_op jit(solution)/shard_map/stage_rows/pallas_call | solution.py:87
  6.7 0.0 copy-start.1
  6.8 0.0 copy-start.2
  6.8 0.0 copy-start.3
  6.8 2.2 %covariance.1 = f32[64,128]{1,0:T(8,128)S(1)} custom-call(f32[64,64]{1,0:T(8,128)S(1)} %get-tuple-element.15.in_ref, bf16[512,2048]{1,0:T(8,128)(2,1)S(1)} %get-tuple-element.16.rows_ref), custom_call_target="tpu_custom_call" | custom-call | flops 1073741824 | bytes 2097152 | tf_op jit(solution)/shard_map/covariance/pallas_call | solution.py:107
  8.9 1.5 %collective-permute-start.2 = (f32[64,128]{1,0:T(8,128)S(1)}, f32[64,128]{1,0:T(8,128)S(1)}, u32[]{:S(2)}, u32[]{:S(2)}) collective-permute-start(f32[64,128]{1,0:T(8,128)S(1)} %covariance.1), channel_id=1, source_target_pairs={{0,2},{2,0},{4,6},{6,4},{8,10},{10,8},{12,14},{14,12},{1,3},{3,1},... | collective-permute-start | bytes 98312 | tf_op jit(solution)/shard_map/ppermute | solution.py:309
  10.5 0.0 collective-permute-done
  10.5 0.0 copy-done.1
  10.5 1.6 %collective-permute-start.1 = (bf16[16,4096]{1,0:T(8,128)(2,1)S(1)}, bf16[16,4096]{1,0:T(8,128)(2,1)S(1)}, u32[]{:S(2)}, u32[]{:S(2)}) collective-permute-start(bf16[16,4096]{1,0:T(8,128)(2,1)S(1)} %pad_maximum_fusion.1), channel_id=1, source_target_pairs={{0,4},{2,6},{4,0},{6,2},{8,12},{10,14},{12,8},{14,10},{1,5},{3,7},... | collective-permute-start | bytes 393224 | tf_op jit(solution)/shard_map/ppermute | solution.py:309
  12.1 0.0 copy-done.2
  12.1 0.1 iota_compare_fusion
  12.2 0.7 %collective-permute-done.2 = f32[64,128]{1,0:T(8,128)S(1)} collective-permute-done((f32[64,128]{1,0:T(8,128)S(1)}, f32[64,128]{1,0:T(8,128)S(1)}, u32[]{:S(2)}, u32[]{:S(2)}) %collective-permute-start.2) | collective-permute-done | bytes 32800 | tf_op jit(solution)/shard_map/ppermute | solution.py:309
  12.9 0.0 collective-permute-start.3
  12.9 3.0 %collective-permute-done.1 = bf16[16,4096]{1,0:T(8,128)(2,1)S(1)} collective-permute-done((bf16[16,4096]{1,0:T(8,128)(2,1)S(1)}, bf16[16,4096]{1,0:T(8,128)(2,1)S(1)}, u32[]{:S(2)}, u32[]{:S(2)}) %collective-permute-start.1) | collective-permute-done | bytes 131104 | tf_op jit(solution)/shard_map/ppermute | solution.py:309
  15.9 0.2 collective-permute-start.5
  16.1 0.0 copy-done.3
  16.1 1.6 %collective-permute-done.3 = f32[64,128]{1,0:T(8,128)S(1)} collective-permute-done((f32[64,128]{1,0:T(8,128)S(1)}, f32[64,128]{1,0:T(8,128)S(1)}, u32[]{:S(2)}, u32[]{:S(2)}) %collective-permute-start.3) | collective-permute-done | bytes 32800 | tf_op jit(solution)/shard_map/ppermute | solution.py:309
  17.7 1.8 %collective-permute-start.4 = (f32[64,128]{1,0:T(8,128)S(1)}, f32[64,128]{1,0:T(8,128)S(1)}, u32[]{:S(2)}, u32[]{:S(2)}) collective-permute-start(f32[64,128]{1,0:T(8,128)S(1)} %add.10), channel_id=1, source_target_pairs={{0,4},{2,6},{4,0},{6,2},{8,12},{10,14},{12,8},{14,10},{1,5},{3,7},... | collective-permute-start | bytes 98312 | tf_op jit(solution)/shard_map/ppermute | solution.py:309
  19.5 0.4 %turn_queries.2.first_ref = bf16[64,2048]{1,0:T(8,128)(2,1)S(1)} custom-call(bf16[32,4096]{1,0:T(8,128)(2,1)S(1)} %pad_maximum_fusion.query_ref), custom_call_target="tpu_custom_call" | custom-call | flops 536870912 | bytes 524288 | tf_op jit(solution)/shard_map/turn_queries/pallas_call | solution.py:134
  19.9 1.7 %collective-permute-done.4 = f32[64,128]{1,0:T(8,128)S(1)} collective-permute-done((f32[64,128]{1,0:T(8,128)S(1)}, f32[64,128]{1,0:T(8,128)S(1)}, u32[]{:S(2)}, u32[]{:S(2)}) %collective-permute-start.4) | collective-permute-done | bytes 32800 | tf_op jit(solution)/shard_map/ppermute | solution.py:309
  21.6 0.0 copy-start
  21.6 2.6 %inverses.1 = (bf16[64,192]{1,0:T(8,128)(2,1)S(1)}, bf16[256,256]{1,0:T(8,128)(2,1)S(1)}) custom-call(f32[64,128]{1,0:T(8,128)S(1)} %add.11.cov_ref), custom_call_target="tpu_custom_call" | custom-call | flops 2000000000 | tf_op jit(solution)/shard_map/inverses/pallas_call | solution.py:222
  24.2 0.0 collective-permute-done.5.query_ref
  24.2 0.4 %turn_queries.3.second_ref = bf16[64,2048]{1,0:T(8,128)(2,1)S(1)} custom-call(bf16[32,4096]{1,0:T(8,128)(2,1)S(1)} %collective-permute-done.5.query_ref), custom_call_target="tpu_custom_call" | custom-call | flops 536870912 | bytes 524288 | tf_op jit(solution)/shard_map/turn_queries/pallas_call | solution.py:134
  24.6 0.0 copy-done
  24.6 2.9 %products_and_scores.1 = f32[8,2,8,128]{3,2,1,0:T(8,128)S(1)} custom-call(s32[8]{0:T(128)S(1)} %broadcast_xor_fusion.route_ref, bf16[64,192]{1,0:T(8,128)(2,1)S(1)} %get-tuple-element.19.left_ref, bf16[256,256]{1,0:T(8,128)(2,1)S(1)} %get-tuple-element.20.right_ref, bf16[64,2048]{1,0:T(8,128)(2,1)S(1)} %turn_queries.2.first_ref, ...), custom_call_target="tpu_custom_call" | custom-call | flops 201326592 | bytes 2097152 | tf_op jit(solution)/shard_map/products_and_scores/pallas_call | solution.py:282
  27.5 10.6 %all_to_all.5 = f32[16,8,128]{2,1,0:T(8,128)S(1)} all-to-all(f32[16,8,128]{2,1,0:T(8,128)S(1)} %bitcast.7), channel_id=1, replica_groups=mesh['groups'=2,'dp'=8,'layer'=2] {'dp','layer'}, dimensions={0} | all-to-all | bytes 131072 | tf_op jit(solution)/shard_map/all_to_all | solution.py:348
  38.1 0.7 %select_reduce_fusion = f32[4,8,128]{2,1,0:T(8,128)} fusion(f32[8,2,8,128]{3,2,1,0:T(8,128)S(1)} %bitcast.8, pred[4,8]{1,0:T(4,128)(4,1)S(1)} %iota_compare_fusion), kind=kLoop, calls=%fused_computation.1 | loop fusion | flops 126976 | bytes 81952 | tf_op jit(solution)/shard_map/reduce_sum | solution.py:350
  (6 shorter events, 0.0 us)
Async XLA Ops:
  0.0 10.5 %collective-permute-start = (bf16[8,4096]{1,0:T(8,128)(2,1)}, bf16[8,4096]{1,0:T(8,128)(2,1)S(1)}, u32[]{:S(2)}, u32[]{:S(2)}) collective-permute-start(bf16[8,4096]{1,0:T(8,128)(2,1)} %bitcast.9), channel_id=1, source_target_pairs={{0,8},{2,10},{4,12},{6,14},{8,0},{10,2},{12,4},{14,6},{1,9},{3,11}... | collective-permute-start | bytes 196616 | tf_op jit(solution)/shard_map/ppermute | solution.py:309
  6.7 3.7 %copy-start.1 = (bf16[8,1,4096]{2,0,1:T(8,128)(2,1)S(1)}, bf16[8,1,4096]{2,0,1:T(8,128)(2,1)}, u32[]{:S(2)}) copy-start(bf16[8,1,4096]{2,0,1:T(8,128)(2,1)} %param.5) | copy-start | bytes 196612
  6.8 5.4 %copy-start.2 = (s32[1,4]{1,0:T(1,128)S(1)}, s32[1,4]{1,0:T(1,128)}, u32[]{:S(2)}) copy-start(s32[1,4]{1,0:T(1,128)} %param.6) | copy-start | bytes 52
  6.8 9.4 %copy-start.3 = (s32[8]{0:T(128)S(1)}, s32[8]{0:T(128)}, u32[]{:S(2)}) copy-start(s32[8]{0:T(128)} %constant.10.clone) | copy-start | bytes 100
  8.9 3.9 %collective-permute-start.2 = (f32[64,128]{1,0:T(8,128)S(1)}, f32[64,128]{1,0:T(8,128)S(1)}, u32[]{:S(2)}, u32[]{:S(2)}) collective-permute-start(f32[64,128]{1,0:T(8,128)S(1)} %covariance.1), channel_id=1, source_target_pairs={{0,2},{2,0},{4,6},{6,4},{8,10},{10,8},{12,14},{14,12},{1,3},{3,1},... | collective-permute-start | bytes 98312 | tf_op jit(solution)/shard_map/ppermute | solution.py:309
  10.5 5.4 %collective-permute-start.1 = (bf16[16,4096]{1,0:T(8,128)(2,1)S(1)}, bf16[16,4096]{1,0:T(8,128)(2,1)S(1)}, u32[]{:S(2)}, u32[]{:S(2)}) collective-permute-start(bf16[16,4096]{1,0:T(8,128)(2,1)S(1)} %pad_maximum_fusion.1), channel_id=1, source_target_pairs={{0,4},{2,6},{4,0},{6,2},{8,12},{10,14},{12,8},{14,10},{1,5},{3,7},... | collective-permute-start | bytes 393224 | tf_op jit(solution)/shard_map/ppermute | solution.py:309
  12.9 4.8 %collective-permute-start.3 = (f32[64,128]{1,0:T(8,128)S(1)}, f32[64,128]{1,0:T(8,128)S(1)}, u32[]{:S(2)}, u32[]{:S(2)}) collective-permute-start(f32[64,128]{1,0:T(8,128)S(1)} %add.9), channel_id=1, source_target_pairs={{0,8},{2,10},{4,12},{6,14},{8,0},{10,2},{12,4},{14,6},{1,9},{3,11}... | collective-permute-start | bytes 98312 | tf_op jit(solution)/shard_map/ppermute | solution.py:309
  15.9 8.3 %collective-permute-start.5 = (bf16[32,4096]{1,0:T(8,128)(2,1)S(1)}, bf16[32,4096]{1,0:T(8,128)(2,1)S(1)}, u32[]{:S(2)}, u32[]{:S(2)}) collective-permute-start(bf16[32,4096]{1,0:T(8,128)(2,1)S(1)} %pad_maximum_fusion.query_ref), channel_id=1, source_target_pairs={{0,2},{2,0},{4,6},{6,4},{8,10},{10,8},{12,14},{14,12},{1,3},{3,1},... | collective-permute-start | bytes 786440 | tf_op jit(solution)/shard_map/ppermute | solution.py:309
  17.7 3.9 %collective-permute-start.4 = (f32[64,128]{1,0:T(8,128)S(1)}, f32[64,128]{1,0:T(8,128)S(1)}, u32[]{:S(2)}, u32[]{:S(2)}) collective-permute-start(f32[64,128]{1,0:T(8,128)S(1)} %add.10), channel_id=1, source_target_pairs={{0,4},{2,6},{4,0},{6,2},{8,12},{10,14},{12,8},{14,10},{1,5},{3,7},... | collective-permute-start | bytes 98312 | tf_op jit(solution)/shard_map/ppermute | solution.py:309
  21.6 3.0 %copy-start = (bf16[256,1,4096]{2,0,1:T(8,128)(2,1)S(1)}, bf16[256,1,4096]{2,0,1:T(8,128)(2,1)}, u32[]{:S(2)}) copy-start(bf16[256,1,4096]{2,0,1:T(8,128)(2,1)} %param.4) | copy-start | bytes 6291460

commit v11 on v10

--- a/solution.py
+++ b/solution.py
@@ -67,13 +67,27 @@
     in_ref[...] = lax.dot_general(by_in[...], by_in[...], NT, preferred_element_type=F32)
 
 
+def tile_sums(values):
+    count, width = values.shape
+    row = lax.broadcasted_iota(jnp.int32, (8, width), 0)
+    result = []
+    for begin in range(0, count, 64):
+        tiles = [values[begin + 8 * k:begin + 8 * k + 8, :] for k in range(8)]
+        for distance in (1, 2, 4):
+            low = (row & distance) == 0
+            pairs = zip(tiles[0::2], tiles[1::2])
+            tiles = [jnp.where(low, x, y) + pltpu.roll(jnp.where(low, y, x), distance, 0) for x, y in pairs]
+        result.append(tiles[0])
+    return jnp.concatenate(result, axis=0)
+
+
 def gram_kernel(in_ref, rows_ref, cov_ref):
     count = rows_ref.shape[0]
     every = lax.dot_general(rows_ref[...], rows_ref[...], NT, preferred_element_type=F32)
     row = lax.broadcasted_iota(jnp.int32, (count, count), 0)
     lane = lax.broadcasted_iota(jnp.int32, (count, count), 1)
     every = jnp.where((row & 7) == (lane & 7), every, 0.0)
-    summed = jnp.sum(every.reshape(count // 8, 8, count), axis=1)
+    summed = tile_sums(every)
     lane = lax.broadcasted_iota(jnp.int32, (count, count // 8), 0)
     column = lax.broadcasted_iota(jnp.int32, (count, count // 8), 1)
     merge = jnp.where(lane // 8 == column, 1.0, 0.0).astype(BF16)
@@ -83,7 +97,7 @@
 
 def staged_rows(train):
     examples, width = train.shape
-    chunks = 8 if width % (8 * 2 * LANES) == 0 else 1
+    chunks = 16 if width % (16 * 2 * LANES) == 0 else 1
     return pl.pallas_call(
         stage_kernel,
         out_shape=(
@@ -178,17 +192,22 @@
         owner, first_row = begin // sub, begin % sub
         inside = (place >= begin) & (place < begin + PIVOT)
         columns = [[column(tile, begin + a) for a in range(PIVOT)] for tile in tiles]
-        p = [[spread_row(columns[owner][b], first_row + a) for b in range(PIVOT)] for a in range(PIVOT)]
+        p = [[None] * PIVOT for _ in range(PIVOT)]
+        for a in range(PIVOT):
+            for b in range(a, PIVOT):
+                p[a][b] = p[b][a] = spread_row(columns[owner][b], first_row + a)
         r = []
         for a in range(PIVOT):
             unit = jnp.where(place == begin + a, 1.0, 0.0)
             r.append(jnp.where(inside, unit, spread_row(tiles[owner], first_row + a)))
         det = 1.0 / (p[0][0] * p[1][1] - p[0][1] * p[1][0])
-        e = [[p[1][1] * det, -p[0][1] * det], [-p[1][0] * det, p[0][0] * det]]
+        across = -p[0][1] * det
+        e = [[p[1][1] * det, across], [across, p[0][0] * det]]
         u = [[e[a][0] * p[0][b] + e[a][1] * p[1][b] for b in (2, 3)] for a in (0, 1)]
-        s = [[p[a][b + 2] - (p[a][0] * u[0][b] + p[a][1] * u[1][b]) for b in (0, 1)] for a in (2, 3)]
-        det = 1.0 / (s[0][0] * s[1][1] - s[0][1] * s[1][0])
-        f = [[s[1][1] * det, -s[0][1] * det], [-s[1][0] * det, s[0][0] * det]]
+        s = [p[a][b + 2] - (p[a][0] * u[0][b] + p[a][1] * u[1][b]) for a, b in ((2, 0), (2, 1), (3, 1))]
+        det = 1.0 / (s[0] * s[2] - s[1] * s[1])
+        across = -s[1] * det
+        f = [[s[2] * det, across], [across, s[0] * det]]
         w = [e[a][0] * r[0] + e[a][1] * r[1] for a in (0, 1)]
         t = [r[a] - (p[a][0] * w[0] + p[a][1] * w[1]) for a in (2, 3)]
         last = [f[a][0] * t[0] + f[a][1] * t[1] for a in (0, 1)]
@@ -259,7 +278,7 @@
             at = side * HALF
             ready[at:at + pairs, columns] = even[side * pairs:(side + 1) * pairs, :].astype(BF16)
             ready[at + pairs:at + HALF, columns] = odd[side * pairs:(side + 1) * pairs, :].astype(BF16)
-    scores = lax.dot_general(ready[...], train_ref[...], NT, preferred_element_type=F32)
+    scores = lax.dot_general(train_ref[...], ready[...], NT, preferred_element_type=F32).T
     per_query = out_ref.shape[2]
     parts = out_ref.shape[1]
     for s in range(CHUNK // per_query):

time: 39 us -> 39.3 us (level)
    pallas_call x1, Pallas kernels: 2.7 us -> 3.33 us  [staged_rows(): pl.pallas_call(stage_kernel, out_shape=(jax.ShapeDtypeStruct((K_IN, K_IN)...]
    pallas_call x1, Pallas kernels: 2.16 us -> 1.6 us  [covariance_sums(): pl.pallas_call(gram_kernel, out_shape=jax.ShapeDtypeStruct((K_OUT, 2 * K_...]
where the time goes in v11:
time: 39.3 us; the launch traced here: 39.1 us
  Pallas kernels  11.4 us (29%)
  blocking collectives  10.6 us (27%)
  starting transfers between devices  9.28 us (24%)
  waiting for transfers between devices  6.9 us (18%)
  other arithmetic  0.83 us (2%)
    all_to_all x1, blocking collectives, shards(): lax.all_to_all(outgoing, ('dp', 'layer'), split_axis=0, concat_axis=0, ti...  10.6 us
    ppermute x6, starting transfers between devices, exchange(): return lax.ppermute(values, 'dp', [(k, k ^ distance) for k in range(count)])  9.28 us
    ppermute x6, waiting for transfers between devices, exchange(): return lax.ppermute(values, 'dp', [(k, k ^ distance) for k in range(count)])  6.9 us
    pallas_call x1, Pallas kernels, staged_rows(): pl.pallas_call(stage_kernel, out_shape=(jax.ShapeDtypeStruct((K_IN, K_IN)...  3.33 us
    pallas_call x1, Pallas kernels, all_scores(): pl.pallas_call(score_kernel, out_shape=jax.ShapeDtypeStruct((shard_count,...  3.02 us
    pallas_call x1, Pallas kernels, inverse_factors(): pl.pallas_call(functools.partial(inverse_kernel, total_count), out_shape=...  2.56 us
    pallas_call x1, Pallas kernels, covariance_sums(): pl.pallas_call(gram_kernel, out_shape=jax.ShapeDtypeStruct((K_OUT, 2 * K_...  1.6 us
    pallas_call x2, Pallas kernels, turned_queries(): pl.pallas_call(turn_kernel, out_shape=jax.ShapeDtypeStruct((K_OUT, total...  0.87 us
  transfers between devices with their start and end apart: 6, of which 4 were waited for; matrix products, arithmetic and copies ran while one was open for 0% of the time, Pallas kernels for 20%

profile of v11, /device:TPU:0, one launch (start us, length us, event | category | flops | bytes accessed | tf_op | source)
XLA Modules:
  0.0 39.1 jit_solution(11256710436123420766)
XLA Ops:
  0.0 4.0 %collective-permute-start = (bf16[8,4096]{1,0:T(8,128)(2,1)}, bf16[8,4096]{1,0:T(8,128)(2,1)S(1)}, u32[]{:S(2)}, u32[]{:S(2)}) collective-permute-start(bf16[8,4096]{1,0:T(8,128)(2,1)} %bitcast.9), channel_id=1, source_target_pairs={{0,8},{2,10},{4,12},{6,14},{8,0},{10,2},{12,4},{14,6},{1,9},{3,11}... | collective-permute-start | bytes 196616 | tf_op jit(solution)/shard_map/ppermute | solution.py:328
  4.0 3.3 %stage_rows.1 = (f32[64,64]{1,0:T(8,128)S(1)}, bf16[512,2048]{1,0:T(8,128)(2,1)S(1)}) custom-call(bf16[256,4096]{1,0:T(8,128)(2,1)} %bitcast.5), custom_call_target="tpu_custom_call" | custom-call | flops 2147483648 | bytes 2097152 | tf_op jit(solution)/shard_map/stage_rows/pallas_call | solution.py:101
  7.4 0.0 copy-start.1
  7.4 0.0 copy-start.2
  7.4 0.0 copy-start.3
  7.4 1.6 %covariance.1 = f32[64,128]{1,0:T(8,128)S(1)} custom-call(f32[64,64]{1,0:T(8,128)S(1)} %get-tuple-element.15.in_ref, bf16[512,2048]{1,0:T(8,128)(2,1)S(1)} %get-tuple-element.16.rows_ref), custom_call_target="tpu_custom_call" | custom-call | flops 1073741824 | bytes 2097152 | tf_op jit(solution)/shard_map/covariance/pallas_call | solution.py:121
  9.0 1.6 %collective-permute-start.2 = (f32[64,128]{1,0:T(8,128)S(1)}, f32[64,128]{1,0:T(8,128)S(1)}, u32[]{:S(2)}, u32[]{:S(2)}) collective-permute-start(f32[64,128]{1,0:T(8,128)S(1)} %covariance.1), channel_id=1, source_target_pairs={{0,2},{2,0},{4,6},{6,4},{8,10},{10,8},{12,14},{14,12},{1,3},{3,1},... | collective-permute-start | bytes 98312 | tf_op jit(solution)/shard_map/ppermute | solution.py:328
  10.6 0.0 collective-permute-done
  10.6 0.0 copy-done.1
  10.6 1.6 %collective-permute-start.1 = (bf16[16,4096]{1,0:T(8,128)(2,1)S(1)}, bf16[16,4096]{1,0:T(8,128)(2,1)S(1)}, u32[]{:S(2)}, u32[]{:S(2)}) collective-permute-start(bf16[16,4096]{1,0:T(8,128)(2,1)S(1)} %pad_maximum_fusion.1), channel_id=1, source_target_pairs={{0,4},{2,6},{4,0},{6,2},{8,12},{10,14},{12,8},{14,10},{1,5},{3,7},... | collective-permute-start | bytes 393224 | tf_op jit(solution)/shard_map/ppermute | solution.py:328
  12.2 0.0 copy-done.2
  12.2 0.1 iota_compare_fusion
  12.3 0.7 %collective-permute-done.2 = f32[64,128]{1,0:T(8,128)S(1)} collective-permute-done((f32[64,128]{1,0:T(8,128)S(1)}, f32[64,128]{1,0:T(8,128)S(1)}, u32[]{:S(2)}, u32[]{:S(2)}) %collective-permute-start.2) | collective-permute-done | bytes 32800 | tf_op jit(solution)/shard_map/ppermute | solution.py:328
  13.0 0.0 collective-permute-start.3
  13.0 3.0 %collective-permute-done.1 = bf16[16,4096]{1,0:T(8,128)(2,1)S(1)} collective-permute-done((bf16[16,4096]{1,0:T(8,128)(2,1)S(1)}, bf16[16,4096]{1,0:T(8,128)(2,1)S(1)}, u32[]{:S(2)}, u32[]{:S(2)}) %collective-permute-start.1) | collective-permute-done | bytes 131104 | tf_op jit(solution)/shard_map/ppermute | solution.py:328
  16.0 0.2 collective-permute-start.5
  16.3 0.0 copy-done.3
  16.3 1.6 %collective-permute-done.3 = f32[64,128]{1,0:T(8,128)S(1)} collective-permute-done((f32[64,128]{1,0:T(8,128)S(1)}, f32[64,128]{1,0:T(8,128)S(1)}, u32[]{:S(2)}, u32[]{:S(2)}) %collective-permute-start.3) | collective-permute-done | bytes 32800 | tf_op jit(solution)/shard_map/ppermute | solution.py:328
  17.8 1.8 %collective-permute-start.4 = (f32[64,128]{1,0:T(8,128)S(1)}, f32[64,128]{1,0:T(8,128)S(1)}, u32[]{:S(2)}, u32[]{:S(2)}) collective-permute-start(f32[64,128]{1,0:T(8,128)S(1)} %add.10), channel_id=1, source_target_pairs={{0,4},{2,6},{4,0},{6,2},{8,12},{10,14},{12,8},{14,10},{1,5},{3,7},... | collective-permute-start | bytes 98312 | tf_op jit(solution)/shard_map/ppermute | solution.py:328
  19.6 0.4 %turn_queries.2.first_ref = bf16[64,2048]{1,0:T(8,128)(2,1)S(1)} custom-call(bf16[32,4096]{1,0:T(8,128)(2,1)S(1)} %pad_maximum_fusion.query_ref), custom_call_target="tpu_custom_call" | custom-call | flops 536870912 | bytes 524288 | tf_op jit(solution)/shard_map/turn_queries/pallas_call | solution.py:148
  20.1 1.7 %collective-permute-done.4 = f32[64,128]{1,0:T(8,128)S(1)} collective-permute-done((f32[64,128]{1,0:T(8,128)S(1)}, f32[64,128]{1,0:T(8,128)S(1)}, u32[]{:S(2)}, u32[]{:S(2)}) %collective-permute-start.4) | collective-permute-done | bytes 32800 | tf_op jit(solution)/shard_map/ppermute | solution.py:328
  21.7 0.0 copy-start
  21.8 2.6 %inverses.1 = (bf16[64,192]{1,0:T(8,128)(2,1)S(1)}, bf16[256,256]{1,0:T(8,128)(2,1)S(1)}) custom-call(f32[64,128]{1,0:T(8,128)S(1)} %add.11.cov_ref), custom_call_target="tpu_custom_call" | custom-call | flops 2000000000 | tf_op jit(solution)/shard_map/inverses/pallas_call | solution.py:241
  24.3 0.0 collective-permute-done.5.query_ref
  24.3 0.4 %turn_queries.3.second_ref = bf16[64,2048]{1,0:T(8,128)(2,1)S(1)} custom-call(bf16[32,4096]{1,0:T(8,128)(2,1)S(1)} %collective-permute-done.5.query_ref), custom_call_target="tpu_custom_call" | custom-call | flops 536870912 | bytes 524288 | tf_op jit(solution)/shard_map/turn_queries/pallas_call | solution.py:148
  24.7 0.0 copy-done
  24.8 3.0 %products_and_scores.1 = f32[8,2,8,128]{3,2,1,0:T(8,128)S(1)} custom-call(s32[8]{0:T(128)S(1)} %broadcast_xor_fusion.route_ref, bf16[64,192]{1,0:T(8,128)(2,1)S(1)} %get-tuple-element.19.left_ref, bf16[256,256]{1,0:T(8,128)(2,1)S(1)} %get-tuple-element.20.right_ref, bf16[64,2048]{1,0:T(8,128)(2,1)S(1)} %turn_queries.2.first_ref, ...), custom_call_target="tpu_custom_call" | custom-call | flops 201326592 | bytes 2097152 | tf_op jit(solution)/shard_map/products_and_scores/pallas_call | solution.py:301
  27.8 10.6 %all_to_all.5 = f32[16,8,128]{2,1,0:T(8,128)S(1)} all-to-all(f32[16,8,128]{2,1,0:T(8,128)S(1)} %bitcast.7), channel_id=1, replica_groups=mesh['groups'=2,'dp'=8,'layer'=2] {'dp','layer'}, dimensions={0} | all-to-all | bytes 131072 | tf_op jit(solution)/shard_map/all_to_all | solution.py:367
  38.4 0.7 %select_reduce_fusion = f32[4,8,128]{2,1,0:T(8,128)} fusion(f32[8,2,8,128]{3,2,1,0:T(8,128)S(1)} %bitcast.8, pred[4,8]{1,0:T(4,128)(4,1)S(1)} %iota_compare_fusion), kind=kLoop, calls=%fused_computation.1 | loop fusion | flops 126976 | bytes 81952 | tf_op jit(solution)/shard_map/reduce_sum | solution.py:369
  (6 shorter events, 0.0 us)
Async XLA Ops:
  0.0 10.6 %collective-permute-start = (bf16[8,4096]{1,0:T(8,128)(2,1)}, bf16[8,4096]{1,0:T(8,128)(2,1)S(1)}, u32[]{:S(2)}, u32[]{:S(2)}) collective-permute-start(bf16[8,4096]{1,0:T(8,128)(2,1)} %bitcast.9), channel_id=1, source_target_pairs={{0,8},{2,10},{4,12},{6,14},{8,0},{10,2},{12,4},{14,6},{1,9},{3,11}... | collective-permute-start | bytes 196616 | tf_op jit(solution)/shard_map/ppermute | solution.py:328
  7.4 3.2 %copy-start.1 = (bf16[8,1,4096]{2,0,1:T(8,128)(2,1)S(1)}, bf16[8,1,4096]{2,0,1:T(8,128)(2,1)}, u32[]{:S(2)}) copy-start(bf16[8,1,4096]{2,0,1:T(8,128)(2,1)} %param.5) | copy-start | bytes 196612
  7.4 4.9 %copy-start.2 = (s32[1,4]{1,0:T(1,128)S(1)}, s32[1,4]{1,0:T(1,128)}, u32[]{:S(2)}) copy-start(s32[1,4]{1,0:T(1,128)} %param.6) | copy-start | bytes 52
  7.4 8.9 %copy-start.3 = (s32[8]{0:T(128)S(1)}, s32[8]{0:T(128)}, u32[]{:S(2)}) copy-start(s32[8]{0:T(128)} %constant.10.clone) | copy-start | bytes 100
  9.0 4.0 %collective-permute-start.2 = (f32[64,128]{1,0:T(8,128)S(1)}, f32[64,128]{1,0:T(8,128)S(1)}, u32[]{:S(2)}, u32[]{:S(2)}) collective-permute-start(f32[64,128]{1,0:T(8,128)S(1)} %covariance.1), channel_id=1, source_target_pairs={{0,2},{2,0},{4,6},{6,4},{8,10},{10,8},{12,14},{14,12},{1,3},{3,1},... | collective-permute-start | bytes 98312 | tf_op jit(solution)/shard_map/ppermute | solution.py:328
  10.6 5.4 %collective-permute-start.1 = (bf16[16,4096]{1,0:T(8,128)(2,1)S(1)}, bf16[16,4096]{1,0:T(8,128)(2,1)S(1)}, u32[]{:S(2)}, u32[]{:S(2)}) collective-permute-start(bf16[16,4096]{1,0:T(8,128)(2,1)S(1)} %pad_maximum_fusion.1), channel_id=1, source_target_pairs={{0,4},{2,6},{4,0},{6,2},{8,12},{10,14},{12,8},{14,10},{1,5},{3,7},... | collective-permute-start | bytes 393224 | tf_op jit(solution)/shard_map/ppermute | solution.py:328
  13.0 4.8 %collective-permute-start.3 = (f32[64,128]{1,0:T(8,128)S(1)}, f32[64,128]{1,0:T(8,128)S(1)}, u32[]{:S(2)}, u32[]{:S(2)}) collective-permute-start(f32[64,128]{1,0:T(8,128)S(1)} %add.9), channel_id=1, source_target_pairs={{0,8},{2,10},{4,12},{6,14},{8,0},{10,2},{12,4},{14,6},{1,9},{3,11}... | collective-permute-start | bytes 98312 | tf_op jit(solution)/shard_map/ppermute | solution.py:328
  16.0 8.3 %collective-permute-start.5 = (bf16[32,4096]{1,0:T(8,128)(2,1)S(1)}, bf16[32,4096]{1,0:T(8,128)(2,1)S(1)}, u32[]{:S(2)}, u32[]{:S(2)}) collective-permute-start(bf16[32,4096]{1,0:T(8,128)(2,1)S(1)} %pad_maximum_fusion.query_ref), channel_id=1, source_target_pairs={{0,2},{2,0},{4,6},{6,4},{8,10},{10,8},{12,14},{14,12},{1,3},{3,1},... | collective-permute-start | bytes 786440 | tf_op jit(solution)/shard_map/ppermute | solution.py:328
  17.8 3.9 %collective-permute-start.4 = (f32[64,128]{1,0:T(8,128)S(1)}, f32[64,128]{1,0:T(8,128)S(1)}, u32[]{:S(2)}, u32[]{:S(2)}) collective-permute-start(f32[64,128]{1,0:T(8,128)S(1)} %add.10), channel_id=1, source_target_pairs={{0,4},{2,6},{4,0},{6,2},{8,12},{10,14},{12,8},{14,10},{1,5},{3,7},... | collective-permute-start | bytes 98312 | tf_op jit(solution)/shard_map/ppermute | solution.py:328
  21.7 3.0 %copy-start = (bf16[256,1,4096]{2,0,1:T(8,128)(2,1)S(1)}, bf16[256,1,4096]{2,0,1:T(8,128)(2,1)}, u32[]{:S(2)}) copy-start(bf16[256,1,4096]{2,0,1:T(8,128)(2,1)} %param.4) | copy-start | bytes 6291460

commit v12 on v11

--- a/solution.py
+++ b/solution.py
@@ -92,12 +92,30 @@
     column = lax.broadcasted_iota(jnp.int32, (count, count // 8), 1)
     merge = jnp.where(lane // 8 == column, 1.0, 0.0).astype(BF16)
     out_sum = sum(jnp.dot(part, merge, preferred_element_type=F32) for part in reversed(split(summed, 3)))
-    cov_ref[...] = jnp.concatenate([in_ref[...], out_sum], axis=1)
+    cov_ref[...] = packed(jnp.concatenate([in_ref[...], out_sum], axis=1))
+
+
+def packed(sums):
+    rows = K_OUT // 2
+    odd = (lax.broadcasted_iota(jnp.int32, (rows // 2, LANES), 1) // rows) % 2 == 1
+    corner = jnp.where(odd, sums[rows:rows + rows // 2, :], pltpu.roll(sums[rows + rows // 2:, :], LANES - rows, 1))
+    return jnp.concatenate([sums[:rows, :], corner], axis=0)
+
+
+def unpacked(sums):
+    rows = K_OUT // 2
+    top, corner = sums[:rows, :], sums[rows:, :]
+    right = jnp.concatenate([corner, pltpu.roll(corner, rows, 1)], axis=0)
+    turned = top.T
+    empty = jnp.zeros((rows, rows), F32)
+    left = jnp.concatenate([turned[rows:2 * rows, :], empty, turned[3 * rows:, :], empty], axis=1)
+    odd = (lax.broadcasted_iota(jnp.int32, (rows, LANES), 1) // rows) % 2 == 1
+    return jnp.concatenate([top, jnp.where(odd, right, left)], axis=0)
 
 
 def staged_rows(train):
     examples, width = train.shape
-    chunks = 16 if width % (16 * 2 * LANES) == 0 else 1
+    chunks = 4 if width % (4 * 2 * LANES) == 0 else 1
     return pl.pallas_call(
         stage_kernel,
         out_shape=(
@@ -120,7 +138,7 @@
 def covariance_sums(in_sum, rows):
     return pl.pallas_call(
         gram_kernel,
-        out_shape=jax.ShapeDtypeStruct((K_OUT, 2 * K_IN), F32),
+        out_shape=jax.ShapeDtypeStruct((K_OUT * 3 // 4, 2 * K_IN), F32),
         in_specs=[pl.BlockSpec(memory_space=pltpu.VMEM), pl.BlockSpec(memory_space=pltpu.VMEM)],
         out_specs=pl.BlockSpec(memory_space=pltpu.VMEM),
         compiler_params=pltpu.CompilerParams(vmem_limit_bytes=VMEM_LIMIT),
@@ -173,6 +191,13 @@
     return cov * scale + jnp.where(diagonal, added, 0.0)
 
 
+def reciprocal(values):
+    estimate = pl.reciprocal(values, approx=True)
+    for _ in range(2):
+        estimate = estimate * (2.0 - values * estimate)
+    return estimate
+
+
 def inverses(matrix):
     size = matrix.shape[0]
     sub = 8
@@ -200,12 +225,12 @@
         for a in range(PIVOT):
             unit = jnp.where(place == begin + a, 1.0, 0.0)
             r.append(jnp.where(inside, unit, spread_row(tiles[owner], first_row + a)))
-        det = 1.0 / (p[0][0] * p[1][1] - p[0][1] * p[1][0])
+        det = reciprocal(p[0][0] * p[1][1] - p[0][1] * p[1][0])
         across = -p[0][1] * det
         e = [[p[1][1] * det, across], [across, p[0][0] * det]]
         u = [[e[a][0] * p[0][b] + e[a][1] * p[1][b] for b in (2, 3)] for a in (0, 1)]
         s = [p[a][b + 2] - (p[a][0] * u[0][b] + p[a][1] * u[1][b]) for a, b in ((2, 0), (2, 1), (3, 1))]
-        det = 1.0 / (s[0] * s[2] - s[1] * s[1])
+        det = reciprocal(s[0] * s[2] - s[1] * s[1])
         across = -s[1] * det
         f = [[s[2] * det, across], [across, s[0] * det]]
         w = [e[a][0] * r[0] + e[a][1] * r[1] for a in (0, 1)]
@@ -225,7 +250,7 @@
 
 
 def inverse_kernel(total_count, cov_ref, left_ref, right_ref):
-    inverse = inverses(damped(cov_ref[...], total_count))
+    inverse = inverses(damped(unpacked(cov_ref[...]), total_count))
     turned = pltpu.roll(inverse, LANES // 2, 1)
     low = low_half(K_OUT)
     left_ref[...] = jnp.concatenate(split(turned[:, :K_OUT], 3), axis=1)
@@ -278,7 +303,7 @@
             at = side * HALF
             ready[at:at + pairs, columns] = even[side * pairs:(side + 1) * pairs, :].astype(BF16)
             ready[at + pairs:at + HALF, columns] = odd[side * pairs:(side + 1) * pairs, :].astype(BF16)
-    scores = lax.dot_general(train_ref[...], ready[...], NT, preferred_element_type=F32).T
+    scores = lax.dot_general(ready[...], train_ref[...], NT, preferred_element_type=F32)
     per_query = out_ref.shape[2]
     parts = out_ref.shape[1]
     for s in range(CHUNK // per_query):

time: 39.3 us -> 38.7 us (0.985)
  Pallas kernels: 11.4 us -> 11 us
    pallas_call x1, Pallas kernels: 3.33 us -> 2.41 us  [staged_rows(): pl.pallas_call(stage_kernel, out_shape=(jax.ShapeDtypeStruct((K_IN, K_IN)...]
    pallas_call x1, Pallas kernels: 2.56 us -> 3.19 us  [inverse_factors(): pl.pallas_call(functools.partial(inverse_kernel, total_count), out_shape=...]
where the time goes in v12:
time: 38.7 us; the launch traced here: 38.5 us
  Pallas kernels  11 us (28%)
  blocking collectives  10.7 us (28%)
  starting transfers between devices  9.18 us (24%)
  waiting for transfers between devices  6.7 us (17%)
  other arithmetic  0.83 us (2%)
    all_to_all x1, blocking collectives, shards(): lax.all_to_all(outgoing, ('dp', 'layer'), split_axis=0, concat_axis=0, ti...  10.7 us
    ppermute x6, starting transfers between devices, exchange(): return lax.ppermute(values, 'dp', [(k, k ^ distance) for k in range(count)])  9.18 us
    ppermute x6, waiting for transfers between devices, exchange(): return lax.ppermute(values, 'dp', [(k, k ^ distance) for k in range(count)])  6.7 us
    pallas_call x1, Pallas kernels, inverse_factors(): pl.pallas_call(functools.partial(inverse_kernel, total_count), out_shape=...  3.19 us
    pallas_call x1, Pallas kernels, all_scores(): pl.pallas_call(score_kernel, out_shape=jax.ShapeDtypeStruct((shard_count,...  2.9 us
    pallas_call x1, Pallas kernels, staged_rows(): pl.pallas_call(stage_kernel, out_shape=(jax.ShapeDtypeStruct((K_IN, K_IN)...  2.41 us
    pallas_call x1, Pallas kernels, covariance_sums(): pl.pallas_call(gram_kernel, out_shape=jax.ShapeDtypeStruct((K_OUT * 3 //...  1.67 us
    pallas_call x2, Pallas kernels, turned_queries(): pl.pallas_call(turn_kernel, out_shape=jax.ShapeDtypeStruct((K_OUT, total...  0.87 us
  transfers between devices with their start and end apart: 6, of which 4 were waited for; matrix products, arithmetic and copies ran while one was open for 0% of the time, Pallas kernels for 20%

profile of v12, /device:TPU:0, one launch (start us, length us, event | category | flops | bytes accessed | tf_op | source)
XLA Modules:
  0.0 38.5 jit_solution(15604790936103790179)
XLA Ops:
  0.0 4.0 %collective-permute-start = (bf16[8,4096]{1,0:T(8,128)(2,1)}, bf16[8,4096]{1,0:T(8,128)(2,1)S(1)}, u32[]{:S(2)}, u32[]{:S(2)}) collective-permute-start(bf16[8,4096]{1,0:T(8,128)(2,1)} %bitcast.9), channel_id=1, source_target_pairs={{0,8},{2,10},{4,12},{6,14},{8,0},{10,2},{12,4},{14,6},{1,9},{3,11}... | collective-permute-start | bytes 196616 | tf_op jit(solution)/shard_map/ppermute | solution.py:353
  4.0 2.4 %stage_rows.1 = (f32[64,64]{1,0:T(8,128)S(1)}, bf16[512,2048]{1,0:T(8,128)(2,1)S(1)}) custom-call(bf16[256,4096]{1,0:T(8,128)(2,1)} %bitcast.5), custom_call_target="tpu_custom_call" | custom-call | flops 2147483648 | bytes 2097152 | tf_op jit(solution)/shard_map/stage_rows/pallas_call | solution.py:119
  6.5 0.0 copy-start.1
  6.5 0.0 copy-start.2
  6.5 0.0 copy-start.3
  6.5 1.7 %covariance.1 = f32[48,128]{1,0:T(8,128)S(1)} custom-call(f32[64,64]{1,0:T(8,128)S(1)} %get-tuple-element.15.in_ref, bf16[512,2048]{1,0:T(8,128)(2,1)S(1)} %get-tuple-element.16.rows_ref), custom_call_target="tpu_custom_call" | custom-call | flops 1073741824 | bytes 2097152 | tf_op jit(solution)/shard_map/covariance/pallas_call | solution.py:139
  8.2 1.5 %collective-permute-start.2 = (f32[48,128]{1,0:T(8,128)S(1)}, f32[48,128]{1,0:T(8,128)S(1)}, u32[]{:S(2)}, u32[]{:S(2)}) collective-permute-start(f32[48,128]{1,0:T(8,128)S(1)} %covariance.1), channel_id=1, source_target_pairs={{0,2},{2,0},{4,6},{6,4},{8,10},{10,8},{12,14},{14,12},{1,3},{3,1},... | collective-permute-start | bytes 73736 | tf_op jit(solution)/shard_map/ppermute | solution.py:353
  9.7 0.0 collective-permute-done
  9.7 0.0 copy-done.1
  9.7 1.6 %collective-permute-start.1 = (bf16[16,4096]{1,0:T(8,128)(2,1)S(1)}, bf16[16,4096]{1,0:T(8,128)(2,1)S(1)}, u32[]{:S(2)}, u32[]{:S(2)}) collective-permute-start(bf16[16,4096]{1,0:T(8,128)(2,1)S(1)} %pad_maximum_fusion.1), channel_id=1, source_target_pairs={{0,4},{2,6},{4,0},{6,2},{8,12},{10,14},{12,8},{14,10},{1,5},{3,7},... | collective-permute-start | bytes 393224 | tf_op jit(solution)/shard_map/ppermute | solution.py:353
  11.3 0.0 copy-done.2
  11.3 0.1 iota_compare_fusion
  11.4 0.6 %collective-permute-done.2 = f32[48,128]{1,0:T(8,128)S(1)} collective-permute-done((f32[48,128]{1,0:T(8,128)S(1)}, f32[48,128]{1,0:T(8,128)S(1)}, u32[]{:S(2)}, u32[]{:S(2)}) %collective-permute-start.2) | collective-permute-done | bytes 24608 | tf_op jit(solution)/shard_map/ppermute | solution.py:353
  12.0 0.1 collective-permute-start.3
  12.1 2.9 %collective-permute-done.1 = bf16[16,4096]{1,0:T(8,128)(2,1)S(1)} collective-permute-done((bf16[16,4096]{1,0:T(8,128)(2,1)S(1)}, bf16[16,4096]{1,0:T(8,128)(2,1)S(1)}, u32[]{:S(2)}, u32[]{:S(2)}) %collective-permute-start.1) | collective-permute-done | bytes 131104 | tf_op jit(solution)/shard_map/ppermute | solution.py:353
  15.0 0.3 collective-permute-start.5
  15.3 0.0 copy-done.3
  15.3 1.4 %collective-permute-done.3 = f32[48,128]{1,0:T(8,128)S(1)} collective-permute-done((f32[48,128]{1,0:T(8,128)S(1)}, f32[48,128]{1,0:T(8,128)S(1)}, u32[]{:S(2)}, u32[]{:S(2)}) %collective-permute-start.3) | collective-permute-done | bytes 24608 | tf_op jit(solution)/shard_map/ppermute | solution.py:353
  16.7 1.6 %collective-permute-start.4 = (f32[48,128]{1,0:T(8,128)S(1)}, f32[48,128]{1,0:T(8,128)S(1)}, u32[]{:S(2)}, u32[]{:S(2)}) collective-permute-start(f32[48,128]{1,0:T(8,128)S(1)} %add.10), channel_id=1, source_target_pairs={{0,4},{2,6},{4,0},{6,2},{8,12},{10,14},{12,8},{14,10},{1,5},{3,7},... | collective-permute-start | bytes 73736 | tf_op jit(solution)/shard_map/ppermute | solution.py:353
  18.3 0.4 %turn_queries.2.first_ref = bf16[64,2048]{1,0:T(8,128)(2,1)S(1)} custom-call(bf16[32,4096]{1,0:T(8,128)(2,1)S(1)} %pad_maximum_fusion.query_ref), custom_call_target="tpu_custom_call" | custom-call | flops 536870912 | bytes 524288 | tf_op jit(solution)/shard_map/turn_queries/pallas_call | solution.py:166
  18.7 1.8 %collective-permute-done.4 = f32[48,128]{1,0:T(8,128)S(1)} collective-permute-done((f32[48,128]{1,0:T(8,128)S(1)}, f32[48,128]{1,0:T(8,128)S(1)}, u32[]{:S(2)}, u32[]{:S(2)}) %collective-permute-start.4) | collective-permute-done | bytes 24608 | tf_op jit(solution)/shard_map/ppermute | solution.py:353
  20.6 0.0 copy-start
  20.6 3.2 %inverses.1 = (bf16[64,192]{1,0:T(8,128)(2,1)S(1)}, bf16[256,256]{1,0:T(8,128)(2,1)S(1)}) custom-call(f32[48,128]{1,0:T(8,128)S(1)} %add.11.cov_ref), custom_call_target="tpu_custom_call" | custom-call | flops 2000000000 | tf_op jit(solution)/shard_map/inverses/pallas_call | solution.py:266
  23.8 0.0 collective-permute-done.5.query_ref
  23.8 0.4 %turn_queries.3.second_ref = bf16[64,2048]{1,0:T(8,128)(2,1)S(1)} custom-call(bf16[32,4096]{1,0:T(8,128)(2,1)S(1)} %collective-permute-done.5.query_ref), custom_call_target="tpu_custom_call" | custom-call | flops 536870912 | bytes 524288 | tf_op jit(solution)/shard_map/turn_queries/pallas_call | solution.py:166
  24.2 0.0 copy-done
  24.2 2.9 %products_and_scores.1 = f32[8,2,8,128]{3,2,1,0:T(8,128)S(1)} custom-call(s32[8]{0:T(128)S(1)} %broadcast_xor_fusion.route_ref, bf16[64,192]{1,0:T(8,128)(2,1)S(1)} %get-tuple-element.19.left_ref, bf16[256,256]{1,0:T(8,128)(2,1)S(1)} %get-tuple-element.20.right_ref, bf16[64,2048]{1,0:T(8,128)(2,1)S(1)} %turn_queries.2.first_ref, ...), custom_call_target="tpu_custom_call" | custom-call | flops 201326592 | bytes 2097152 | tf_op jit(solution)/shard_map/products_and_scores/pallas_call | solution.py:326
  27.1 10.7 %all_to_all.5 = f32[16,8,128]{2,1,0:T(8,128)S(1)} all-to-all(f32[16,8,128]{2,1,0:T(8,128)S(1)} %bitcast.7), channel_id=1, replica_groups=mesh['groups'=2,'dp'=8,'layer'=2] {'dp','layer'}, dimensions={0} | all-to-all | bytes 131072 | tf_op jit(solution)/shard_map/all_to_all | solution.py:392
  37.8 0.7 %select_reduce_fusion = f32[4,8,128]{2,1,0:T(8,128)} fusion(f32[8,2,8,128]{3,2,1,0:T(8,128)S(1)} %bitcast.8, pred[4,8]{1,0:T(4,128)(4,1)S(1)} %iota_compare_fusion), kind=kLoop, calls=%fused_computation.1 | loop fusion | flops 126976 | bytes 81952 | tf_op jit(solution)/shard_map/reduce_sum | solution.py:394
  (6 shorter events, 0.0 us)
Async XLA Ops:
  0.0 9.7 %collective-permute-start = (bf16[8,4096]{1,0:T(8,128)(2,1)}, bf16[8,4096]{1,0:T(8,128)(2,1)S(1)}, u32[]{:S(2)}, u32[]{:S(2)}) collective-permute-start(bf16[8,4096]{1,0:T(8,128)(2,1)} %bitcast.9), channel_id=1, source_target_pairs={{0,8},{2,10},{4,12},{6,14},{8,0},{10,2},{12,4},{14,6},{1,9},{3,11}... | collective-permute-start | bytes 196616 | tf_op jit(solution)/shard_map/ppermute | solution.py:353
  6.5 3.2 %copy-start.1 = (bf16[8,1,4096]{2,0,1:T(8,128)(2,1)S(1)}, bf16[8,1,4096]{2,0,1:T(8,128)(2,1)}, u32[]{:S(2)}) copy-start(bf16[8,1,4096]{2,0,1:T(8,128)(2,1)} %param.5) | copy-start | bytes 196612
  6.5 4.9 %copy-start.2 = (s32[1,4]{1,0:T(1,128)S(1)}, s32[1,4]{1,0:T(1,128)}, u32[]{:S(2)}) copy-start(s32[1,4]{1,0:T(1,128)} %param.6) | copy-start | bytes 52
  6.5 8.9 %copy-start.3 = (s32[8]{0:T(128)S(1)}, s32[8]{0:T(128)}, u32[]{:S(2)}) copy-start(s32[8]{0:T(128)} %constant.10.clone) | copy-start | bytes 100
  8.2 3.8 %collective-permute-start.2 = (f32[48,128]{1,0:T(8,128)S(1)}, f32[48,128]{1,0:T(8,128)S(1)}, u32[]{:S(2)}, u32[]{:S(2)}) collective-permute-start(f32[48,128]{1,0:T(8,128)S(1)} %covariance.1), channel_id=1, source_target_pairs={{0,2},{2,0},{4,6},{6,4},{8,10},{10,8},{12,14},{14,12},{1,3},{3,1},... | collective-permute-start | bytes 73736 | tf_op jit(solution)/shard_map/ppermute | solution.py:353
  9.7 5.3 %collective-permute-start.1 = (bf16[16,4096]{1,0:T(8,128)(2,1)S(1)}, bf16[16,4096]{1,0:T(8,128)(2,1)S(1)}, u32[]{:S(2)}, u32[]{:S(2)}) collective-permute-start(bf16[16,4096]{1,0:T(8,128)(2,1)S(1)} %pad_maximum_fusion.1), channel_id=1, source_target_pairs={{0,4},{2,6},{4,0},{6,2},{8,12},{10,14},{12,8},{14,10},{1,5},{3,7},... | collective-permute-start | bytes 393224 | tf_op jit(solution)/shard_map/ppermute | solution.py:353
  12.0 4.7 %collective-permute-start.3 = (f32[48,128]{1,0:T(8,128)S(1)}, f32[48,128]{1,0:T(8,128)S(1)}, u32[]{:S(2)}, u32[]{:S(2)}) collective-permute-start(f32[48,128]{1,0:T(8,128)S(1)} %add.9), channel_id=1, source_target_pairs={{0,8},{2,10},{4,12},{6,14},{8,0},{10,2},{12,4},{14,6},{1,9},{3,11}... | collective-permute-start | bytes 73736 | tf_op jit(solution)/shard_map/ppermute | solution.py:353
  15.0 8.8 %collective-permute-start.5 = (bf16[32,4096]{1,0:T(8,128)(2,1)S(1)}, bf16[32,4096]{1,0:T(8,128)(2,1)S(1)}, u32[]{:S(2)}, u32[]{:S(2)}) collective-permute-start(bf16[32,4096]{1,0:T(8,128)(2,1)S(1)} %pad_maximum_fusion.query_ref), channel_id=1, source_target_pairs={{0,2},{2,0},{4,6},{6,4},{8,10},{10,8},{12,14},{14,12},{1,3},{3,1},... | collective-permute-start | bytes 786440 | tf_op jit(solution)/shard_map/ppermute | solution.py:353
  16.7 3.8 %collective-permute-start.4 = (f32[48,128]{1,0:T(8,128)S(1)}, f32[48,128]{1,0:T(8,128)S(1)}, u32[]{:S(2)}, u32[]{:S(2)}) collective-permute-start(f32[48,128]{1,0:T(8,128)S(1)} %add.10), channel_id=1, source_target_pairs={{0,4},{2,6},{4,0},{6,2},{8,12},{10,14},{12,8},{14,10},{1,5},{3,7},... | collective-permute-start | bytes 73736 | tf_op jit(solution)/shard_map/ppermute | solution.py:353
  20.6 3.6 %copy-start = (bf16[256,1,4096]{2,0,1:T(8,128)(2,1)S(1)}, bf16[256,1,4096]{2,0,1:T(8,128)(2,1)}, u32[]{:S(2)}) copy-start(bf16[256,1,4096]{2,0,1:T(8,128)(2,1)} %param.4) | copy-start | bytes 6291460

commit v13 on v11

--- a/solution.py
+++ b/solution.py
@@ -97,7 +97,7 @@
 
 def staged_rows(train):
     examples, width = train.shape
-    chunks = 16 if width % (16 * 2 * LANES) == 0 else 1
+    chunks = 4 if width % (4 * 2 * LANES) == 0 else 1
     return pl.pallas_call(
         stage_kernel,
         out_shape=(
@@ -133,11 +133,12 @@
     count, width = query_ref.shape
     blocks = width // LANES
     pairs = count // 2
+    pitch = spread.shape[0] // blocks
     for c in range(blocks):
-        spread[c * count:(c + 1) * count, :] = query_ref[:, c * LANES:(c + 1) * LANES].astype(F32)
+        spread[c * pitch:c * pitch + count, :] = query_ref[:, c * LANES:(c + 1) * LANES].astype(F32)
     for p in range(pairs):
-        first = spread[pl.ds(p, blocks, stride=count), :]
-        second = spread[pl.ds(p + pairs, blocks, stride=count), :]
+        first = spread[pl.ds(p, blocks, stride=pitch), :]
+        second = spread[pl.ds(p + pairs, blocks, stride=pitch), :]
         even, odd = swap_pair(first, second)
         out_ref[:blocks, p * LANES:(p + 1) * LANES] = even.astype(BF16)
         out_ref[blocks:, p * LANES:(p + 1) * LANES] = odd.astype(BF16)
@@ -151,7 +152,7 @@
         grid=(total // HALF,),
         in_specs=[pl.BlockSpec((HALF, width), lambda step: (step, 0))],
         out_specs=pl.BlockSpec((K_OUT, HALF * K_IN), lambda step: (0, step)),
-        scratch_shapes=[pltpu.VMEM((width // LANES * HALF, LANES), F32)],
+        scratch_shapes=[pltpu.VMEM((width // LANES * (HALF + 8), LANES), F32)],
         compiler_params=pltpu.CompilerParams(vmem_limit_bytes=VMEM_LIMIT),
         cost_estimate=pl.CostEstimate(flops=4096 * total * width, bytes_accessed=4 * total * width, transcendentals=0),
         name="turn_queries",
@@ -228,7 +229,7 @@
     inverse = inverses(damped(cov_ref[...], total_count))
     turned = pltpu.roll(inverse, LANES // 2, 1)
     low = low_half(K_OUT)
-    left_ref[...] = jnp.concatenate(split(turned[:, :K_OUT], 3), axis=1)
+    left_ref[...] = jnp.concatenate(split(turned[:, :K_OUT], 3), axis=0)
     double = jnp.concatenate([jnp.where(low, inverse, 0.0), jnp.where(low, 0.0, turned)], axis=0)
     high, small = split(double, 2)
     right_ref[:LANES, :LANES] = high
@@ -241,7 +242,7 @@
     return pl.pallas_call(
         functools.partial(inverse_kernel, total_count),
         out_shape=(
-            jax.ShapeDtypeStruct((K_OUT, 3 * K_OUT), BF16),
+            jax.ShapeDtypeStruct((3 * K_OUT, K_OUT), BF16),
             jax.ShapeDtypeStruct((2 * LANES, 2 * LANES), BF16),
         ),
         in_specs=[pl.BlockSpec(memory_space=pltpu.VMEM)],
@@ -255,30 +256,33 @@
 def score_kernel(route_ref, left_ref, right_ref, first_ref, second_ref, train_ref, out_ref, solved, wide, ready):
     blocks = K_OUT // 2
     pairs = HALF // 2
+    pitch = solved.shape[0] // (2 * pairs)
     step = pl.program_id(0)
     group = 4
     for side, turned_ref in enumerate((first_ref, second_ref)):
         for g in range(pairs // group):
             block = turned_ref[:, g * group * LANES:(g + 1) * group * LANES]
-            tall = jnp.concatenate([block, block, block], axis=0)
-            once = jnp.dot(left_ref[...], tall, preferred_element_type=F32)
+            terms = jnp.dot(left_ref[...], block, preferred_element_type=F32)
+            once = terms[:K_OUT, :] + (terms[K_OUT:2 * K_OUT, :] + terms[2 * K_OUT:, :])
             for k in range(group):
                 high, small = split(once[:, k * LANES:(k + 1) * LANES], 2)
                 at = (side * pairs + g * group + k) * K_OUT
                 wide[at:at + K_OUT, :LANES] = high
                 wide[at:at + K_OUT, LANES:] = small
     twice = jnp.dot(wide[...], right_ref[...], preferred_element_type=F32)
-    solved[...] = twice[:, :LANES] + twice[:, LANES:]
+    for p in range(2 * pairs):
+        part = twice[p * K_OUT:(p + 1) * K_OUT, :]
+        solved[p * pitch:p * pitch + K_OUT, :] = part[:, :LANES] + part[:, LANES:]
     for c in range(blocks):
-        first = solved[pl.ds(c, 2 * pairs, stride=K_OUT), :]
-        second = solved[pl.ds(c + blocks, 2 * pairs, stride=K_OUT), :]
+        first = solved[pl.ds(c, 2 * pairs, stride=pitch), :]
+        second = solved[pl.ds(c + blocks, 2 * pairs, stride=pitch), :]
         even, odd = swap_pair(first, second)
         columns = slice(c * LANES, (c + 1) * LANES)
         for side in range(2):
             at = side * HALF
             ready[at:at + pairs, columns] = even[side * pairs:(side + 1) * pairs, :].astype(BF16)
             ready[at + pairs:at + HALF, columns] = odd[side * pairs:(side + 1) * pairs, :].astype(BF16)
-    scores = lax.dot_general(train_ref[...], ready[...], NT, preferred_element_type=F32).T
+    scores = lax.dot_general(ready[...], train_ref[...], NT, preferred_element_type=F32)
     per_query = out_ref.shape[2]
     parts = out_ref.shape[1]
     for s in range(CHUNK // per_query):
@@ -304,7 +308,7 @@
         grid=(steps,),
         in_specs=[
             pl.BlockSpec(memory_space=pltpu.SMEM),
-            pl.BlockSpec((K_OUT, 3 * K_OUT), lambda step: (0, 0)),
+            pl.BlockSpec((3 * K_OUT, K_OUT), lambda step: (0, 0)),
             pl.BlockSpec((2 * LANES, 2 * LANES), lambda step: (0, 0)),
             pl.BlockSpec((K_OUT, HALF * K_IN), places[0]),
             pl.BlockSpec((K_OUT, HALF * K_IN), places[1]),
@@ -312,7 +316,7 @@
         ],
         out_specs=pl.BlockSpec((shard_count, parts, per_query, LANES), lambda step: (0, 0, 0, 0)),
         scratch_shapes=[
-            pltpu.VMEM((HALF * K_OUT, LANES), F32),
+            pltpu.VMEM((HALF * (K_OUT + 8), LANES), F32),
             pltpu.VMEM((HALF * K_OUT, 2 * LANES), BF16),
             pltpu.VMEM((CHUNK, width), BF16),
         ],

time: 39.3 us -> 37.9 us (0.964)
  Pallas kernels: 11.4 us -> 9.44 us
    pallas_call x1, Pallas kernels: 3.33 us -> 2.41 us  [staged_rows(): pl.pallas_call(stage_kernel, out_shape=(jax.ShapeDtypeStruct((K_IN, K_IN)...]
    pallas_call x2, Pallas kernels: 0.87 us -> 0.4 us  [turned_queries(): pl.pallas_call(turn_kernel, out_shape=jax.ShapeDtypeStruct((K_OUT, total...]
  transfers between devices with their start and end apart: 6 -> 6, of which waited for: 4 -> 4; matrix products, arithmetic and copies ran while one was open for 0% -> 0% of each run, Pallas kernels for 20% -> 17%
where the time goes in v13:
time: 37.9 us; the launch traced here: 37.7 us
  blocking collectives  10.9 us (29%)
  Pallas kernels  9.44 us (25%)
  starting transfers between devices  9.22 us (24%)
  waiting for transfers between devices  7.21 us (19%)
  other arithmetic  0.83 us (2%)
    all_to_all x1, blocking collectives, shards(): lax.all_to_all(outgoing, ('dp', 'layer'), split_axis=0, concat_axis=0, ti...  10.9 us
    ppermute x6, starting transfers between devices, exchange(): return lax.ppermute(values, 'dp', [(k, k ^ distance) for k in range(count)])  9.22 us
    ppermute x6, waiting for transfers between devices, exchange(): return lax.ppermute(values, 'dp', [(k, k ^ distance) for k in range(count)])  7.21 us
    pallas_call x1, Pallas kernels, all_scores(): pl.pallas_call(score_kernel, out_shape=jax.ShapeDtypeStruct((shard_count,...  2.68 us
    pallas_call x1, Pallas kernels, staged_rows(): pl.pallas_call(stage_kernel, out_shape=(jax.ShapeDtypeStruct((K_IN, K_IN)...  2.41 us
    pallas_call x1, Pallas kernels, inverse_factors(): pl.pallas_call(functools.partial(inverse_kernel, total_count), out_shape=...  2.36 us
    pallas_call x1, Pallas kernels, covariance_sums(): pl.pallas_call(gram_kernel, out_shape=jax.ShapeDtypeStruct((K_OUT, 2 * K_...  1.6 us
  transfers between devices with their start and end apart: 6, of which 4 were waited for; matrix products, arithmetic and copies ran while one was open for 0% of the time, Pallas kernels for 17%

profile of v13, /device:TPU:0, one launch (start us, length us, event | category | flops | bytes accessed | tf_op | source)
XLA Modules:
  0.0 37.7 jit_solution(14727111901761474717)
XLA Ops:
  0.0 4.0 %collective-permute-start = (bf16[8,4096]{1,0:T(8,128)(2,1)}, bf16[8,4096]{1,0:T(8,128)(2,1)S(1)}, u32[]{:S(2)}, u32[]{:S(2)}) collective-permute-start(bf16[8,4096]{1,0:T(8,128)(2,1)} %bitcast.9), channel_id=1, source_target_pairs={{0,8},{2,10},{4,12},{6,14},{8,0},{10,2},{12,4},{14,6},{1,9},{3,11}... | collective-permute-start | bytes 196616 | tf_op jit(solution)/shard_map/ppermute | solution.py:332
  4.0 2.4 %stage_rows.1 = (f32[64,64]{1,0:T(8,128)S(1)}, bf16[512,2048]{1,0:T(8,128)(2,1)S(1)}) custom-call(bf16[256,4096]{1,0:T(8,128)(2,1)} %bitcast.5), custom_call_target="tpu_custom_call" | custom-call | flops 2147483648 | bytes 2097152 | tf_op jit(solution)/shard_map/stage_rows/pallas_call | solution.py:101
  6.5 0.0 copy-start.1
  6.5 0.0 copy-start.2
  6.5 0.0 copy-start.3
  6.5 1.6 %covariance.1 = f32[64,128]{1,0:T(8,128)S(1)} custom-call(f32[64,64]{1,0:T(8,128)S(1)} %get-tuple-element.15.in_ref, bf16[512,2048]{1,0:T(8,128)(2,1)S(1)} %get-tuple-element.16.rows_ref), custom_call_target="tpu_custom_call" | custom-call | flops 1073741824 | bytes 2097152 | tf_op jit(solution)/shard_map/covariance/pallas_call | solution.py:121
  8.1 1.5 %collective-permute-start.2 = (f32[64,128]{1,0:T(8,128)S(1)}, f32[64,128]{1,0:T(8,128)S(1)}, u32[]{:S(2)}, u32[]{:S(2)}) collective-permute-start(f32[64,128]{1,0:T(8,128)S(1)} %covariance.1), channel_id=1, source_target_pairs={{0,2},{2,0},{4,6},{6,4},{8,10},{10,8},{12,14},{14,12},{1,3},{3,1},... | collective-permute-start | bytes 98312 | tf_op jit(solution)/shard_map/ppermute | solution.py:332
  9.6 0.0 collective-permute-done
  9.6 0.0 copy-done.1
  9.7 1.6 %collective-permute-start.1 = (bf16[16,4096]{1,0:T(8,128)(2,1)S(1)}, bf16[16,4096]{1,0:T(8,128)(2,1)S(1)}, u32[]{:S(2)}, u32[]{:S(2)}) collective-permute-start(bf16[16,4096]{1,0:T(8,128)(2,1)S(1)} %pad_maximum_fusion.1), channel_id=1, source_target_pairs={{0,4},{2,6},{4,0},{6,2},{8,12},{10,14},{12,8},{14,10},{1,5},{3,7},... | collective-permute-start | bytes 393224 | tf_op jit(solution)/shard_map/ppermute | solution.py:332
  11.3 0.0 copy-done.2
  11.3 0.1 iota_compare_fusion
  11.4 0.7 %collective-permute-done.2 = f32[64,128]{1,0:T(8,128)S(1)} collective-permute-done((f32[64,128]{1,0:T(8,128)S(1)}, f32[64,128]{1,0:T(8,128)S(1)}, u32[]{:S(2)}, u32[]{:S(2)}) %collective-permute-start.2) | collective-permute-done | bytes 32800 | tf_op jit(solution)/shard_map/ppermute | solution.py:332
  12.1 0.0 collective-permute-start.3
  12.1 2.9 %collective-permute-done.1 = bf16[16,4096]{1,0:T(8,128)(2,1)S(1)} collective-permute-done((bf16[16,4096]{1,0:T(8,128)(2,1)S(1)}, bf16[16,4096]{1,0:T(8,128)(2,1)S(1)}, u32[]{:S(2)}, u32[]{:S(2)}) %collective-permute-start.1) | collective-permute-done | bytes 131104 | tf_op jit(solution)/shard_map/ppermute | solution.py:332
  15.1 0.3 collective-permute-start.5
  15.3 0.0 copy-done.3
  15.3 1.6 %collective-permute-done.3 = f32[64,128]{1,0:T(8,128)S(1)} collective-permute-done((f32[64,128]{1,0:T(8,128)S(1)}, f32[64,128]{1,0:T(8,128)S(1)}, u32[]{:S(2)}, u32[]{:S(2)}) %collective-permute-start.3) | collective-permute-done | bytes 32800 | tf_op jit(solution)/shard_map/ppermute | solution.py:332
  16.9 1.7 %collective-permute-start.4 = (f32[64,128]{1,0:T(8,128)S(1)}, f32[64,128]{1,0:T(8,128)S(1)}, u32[]{:S(2)}, u32[]{:S(2)}) collective-permute-start(f32[64,128]{1,0:T(8,128)S(1)} %add.10), channel_id=1, source_target_pairs={{0,4},{2,6},{4,0},{6,2},{8,12},{10,14},{12,8},{14,10},{1,5},{3,7},... | collective-permute-start | bytes 98312 | tf_op jit(solution)/shard_map/ppermute | solution.py:332
  18.6 0.2 turn_queries.2.first_ref
  18.8 2.0 %collective-permute-done.4 = f32[64,128]{1,0:T(8,128)S(1)} collective-permute-done((f32[64,128]{1,0:T(8,128)S(1)}, f32[64,128]{1,0:T(8,128)S(1)}, u32[]{:S(2)}, u32[]{:S(2)}) %collective-permute-start.4) | collective-permute-done | bytes 32800 | tf_op jit(solution)/shard_map/ppermute | solution.py:332
  20.8 0.0 copy-start
  20.8 2.4 %inverses.1 = (bf16[192,64]{1,0:T(8,128)(2,1)S(1)}, bf16[256,256]{1,0:T(8,128)(2,1)S(1)}) custom-call(f32[64,128]{1,0:T(8,128)S(1)} %add.11.cov_ref), custom_call_target="tpu_custom_call" | custom-call | flops 2000000000 | tf_op jit(solution)/shard_map/inverses/pallas_call | solution.py:242
  23.2 0.0 collective-permute-done.5.query_ref
  23.2 0.2 turn_queries.3.second_ref
  23.4 0.0 copy-done
  23.4 2.7 %products_and_scores.1 = f32[8,2,8,128]{3,2,1,0:T(8,128)S(1)} custom-call(s32[8]{0:T(128)S(1)} %broadcast_xor_fusion.route_ref, bf16[192,64]{1,0:T(8,128)(2,1)S(1)} %get-tuple-element.19.left_ref, bf16[256,256]{1,0:T(8,128)(2,1)S(1)} %get-tuple-element.20.right_ref, bf16[64,2048]{1,0:T(8,128)(2,1)S(1)} %turn_queries.2.first_ref, ...), custom_call_target="tpu_custom_call" | custom-call | flops 201326592 | bytes 2097152 | tf_op jit(solution)/shard_map/products_and_scores/pallas_call | solution.py:305
  26.1 10.9 %all_to_all.5 = f32[16,8,128]{2,1,0:T(8,128)S(1)} all-to-all(f32[16,8,128]{2,1,0:T(8,128)S(1)} %bitcast.7), channel_id=1, replica_groups=mesh['groups'=2,'dp'=8,'layer'=2] {'dp','layer'}, dimensions={0} | all-to-all | bytes 131072 | tf_op jit(solution)/shard_map/all_to_all | solution.py:371
  37.0 0.7 %select_reduce_fusion = f32[4,8,128]{2,1,0:T(8,128)} fusion(f32[8,2,8,128]{3,2,1,0:T(8,128)S(1)} %bitcast.8, pred[4,8]{1,0:T(4,128)(4,1)S(1)} %iota_compare_fusion), kind=kLoop, calls=%fused_computation.1 | loop fusion | flops 126976 | bytes 81952 | tf_op jit(solution)/shard_map/reduce_sum | solution.py:373
  (6 shorter events, 0.0 us)
Async XLA Ops:
  0.0 9.6 %collective-permute-start = (bf16[8,4096]{1,0:T(8,128)(2,1)}, bf16[8,4096]{1,0:T(8,128)(2,1)S(1)}, u32[]{:S(2)}, u32[]{:S(2)}) collective-permute-start(bf16[8,4096]{1,0:T(8,128)(2,1)} %bitcast.9), channel_id=1, source_target_pairs={{0,8},{2,10},{4,12},{6,14},{8,0},{10,2},{12,4},{14,6},{1,9},{3,11}... | collective-permute-start | bytes 196616 | tf_op jit(solution)/shard_map/ppermute | solution.py:332
  6.5 3.2 %copy-start.1 = (bf16[8,1,4096]{2,0,1:T(8,128)(2,1)S(1)}, bf16[8,1,4096]{2,0,1:T(8,128)(2,1)}, u32[]{:S(2)}) copy-start(bf16[8,1,4096]{2,0,1:T(8,128)(2,1)} %param.5) | copy-start | bytes 196612
  6.5 4.8 %copy-start.2 = (s32[1,4]{1,0:T(1,128)S(1)}, s32[1,4]{1,0:T(1,128)}, u32[]{:S(2)}) copy-start(s32[1,4]{1,0:T(1,128)} %param.6) | copy-start | bytes 52
  6.5 8.9 %copy-start.3 = (s32[8]{0:T(128)S(1)}, s32[8]{0:T(128)}, u32[]{:S(2)}) copy-start(s32[8]{0:T(128)} %constant.10.clone) | copy-start | bytes 100
  8.1 4.0 %collective-permute-start.2 = (f32[64,128]{1,0:T(8,128)S(1)}, f32[64,128]{1,0:T(8,128)S(1)}, u32[]{:S(2)}, u32[]{:S(2)}) collective-permute-start(f32[64,128]{1,0:T(8,128)S(1)} %covariance.1), channel_id=1, source_target_pairs={{0,2},{2,0},{4,6},{6,4},{8,10},{10,8},{12,14},{14,12},{1,3},{3,1},... | collective-permute-start | bytes 98312 | tf_op jit(solution)/shard_map/ppermute | solution.py:332
  9.7 5.4 %collective-permute-start.1 = (bf16[16,4096]{1,0:T(8,128)(2,1)S(1)}, bf16[16,4096]{1,0:T(8,128)(2,1)S(1)}, u32[]{:S(2)}, u32[]{:S(2)}) collective-permute-start(bf16[16,4096]{1,0:T(8,128)(2,1)S(1)} %pad_maximum_fusion.1), channel_id=1, source_target_pairs={{0,4},{2,6},{4,0},{6,2},{8,12},{10,14},{12,8},{14,10},{1,5},{3,7},... | collective-permute-start | bytes 393224 | tf_op jit(solution)/shard_map/ppermute | solution.py:332
  12.1 4.8 %collective-permute-start.3 = (f32[64,128]{1,0:T(8,128)S(1)}, f32[64,128]{1,0:T(8,128)S(1)}, u32[]{:S(2)}, u32[]{:S(2)}) collective-permute-start(f32[64,128]{1,0:T(8,128)S(1)} %add.9), channel_id=1, source_target_pairs={{0,8},{2,10},{4,12},{6,14},{8,0},{10,2},{12,4},{14,6},{1,9},{3,11}... | collective-permute-start | bytes 98312 | tf_op jit(solution)/shard_map/ppermute | solution.py:332
  15.1 8.1 %collective-permute-start.5 = (bf16[32,4096]{1,0:T(8,128)(2,1)S(1)}, bf16[32,4096]{1,0:T(8,128)(2,1)S(1)}, u32[]{:S(2)}, u32[]{:S(2)}) collective-permute-start(bf16[32,4096]{1,0:T(8,128)(2,1)S(1)} %pad_maximum_fusion.query_ref), channel_id=1, source_target_pairs={{0,2},{2,0},{4,6},{6,4},{8,10},{10,8},{12,14},{14,12},{1,3},{3,1},... | collective-permute-start | bytes 786440 | tf_op jit(solution)/shard_map/ppermute | solution.py:332
  16.9 3.9 %collective-permute-start.4 = (f32[64,128]{1,0:T(8,128)S(1)}, f32[64,128]{1,0:T(8,128)S(1)}, u32[]{:S(2)}, u32[]{:S(2)}) collective-permute-start(f32[64,128]{1,0:T(8,128)S(1)} %add.10), channel_id=1, source_target_pairs={{0,4},{2,6},{4,0},{6,2},{8,12},{10,14},{12,8},{14,10},{1,5},{3,7},... | collective-permute-start | bytes 98312 | tf_op jit(solution)/shard_map/ppermute | solution.py:332
  20.8 2.6 %copy-start = (bf16[256,1,4096]{2,0,1:T(8,128)(2,1)S(1)}, bf16[256,1,4096]{2,0,1:T(8,128)(2,1)}, u32[]{:S(2)}) copy-start(bf16[256,1,4096]{2,0,1:T(8,128)(2,1)} %param.4) | copy-start | bytes 6291460

commit v14 on v13

--- a/solution.py
+++ b/solution.py
@@ -41,92 +41,57 @@
     return parts
 
 
-def stage_kernel(train_ref, in_ref, rows_ref, held, by_in, arrived):
+def covariance_kernel(train_ref, cov_ref, held, turned, by_in, by_out, arrived):
     examples, width = train_ref.shape
-    pair = 2 * LANES
+    blocks = width // LANES
+    parts = examples // LANES
+    pitch = turned.shape[1] // blocks
     chunks, _, chunk = held.shape
     copies = []
     for g in range(chunks):
         source = train_ref.at[:, pl.ds(g * chunk, chunk)]
         copies.append(pltpu.make_async_copy(source, held.at[g], arrived.at[g]))
         copies[-1].start()
-    for m in range(width // pair):
-        if m * pair % chunk == 0:
-            copies[m * pair // chunk].wait()
-        begin = m * pair % chunk
-        block = held[m * pair // chunk, :, begin:begin + pair].astype(F32).T
-        for k in range(4):
-            start = (4 * m + k) * examples
-            by_in[:, start:start + examples] = block[k * K_IN:(k + 1) * K_IN, :].astype(BF16)
+    for c in range(blocks):
+        if c * LANES % chunk == 0:
+            copies[c * LANES // chunk].wait()
+        begin = c * LANES % chunk
+        block = held[c * LANES // chunk, :, begin:begin + LANES].astype(F32).T
+        for part in range(parts):
+            turned[part, c * pitch:c * pitch + LANES, :] = block[:, part * LANES:(part + 1) * LANES]
         for half in range(2):
-            for j in range(K_IN // 8):
-                first = half * K_IN + j * 8
-                both = jnp.concatenate([block[first:first + 8, :], block[first + LANES:first + LANES + 8, :]], axis=0)
-                at = half * K_OUT // 2 * 8 + m * 16
-                rows_ref[at:at + 16, j * examples:(j + 1) * examples] = both.astype(BF16)
-    in_ref[...] = lax.dot_general(by_in[...], by_in[...], NT, preferred_element_type=F32)
-
-
-def tile_sums(values):
-    count, width = values.shape
-    row = lax.broadcasted_iota(jnp.int32, (8, width), 0)
-    result = []
-    for begin in range(0, count, 64):
-        tiles = [values[begin + 8 * k:begin + 8 * k + 8, :] for k in range(8)]
-        for distance in (1, 2, 4):
-            low = (row & distance) == 0
-            pairs = zip(tiles[0::2], tiles[1::2])
-            tiles = [jnp.where(low, x, y) + pltpu.roll(jnp.where(low, y, x), distance, 0) for x, y in pairs]
-        result.append(tiles[0])
-    return jnp.concatenate(result, axis=0)
-
-
-def gram_kernel(in_ref, rows_ref, cov_ref):
-    count = rows_ref.shape[0]
-    every = lax.dot_general(rows_ref[...], rows_ref[...], NT, preferred_element_type=F32)
-    row = lax.broadcasted_iota(jnp.int32, (count, count), 0)
-    lane = lax.broadcasted_iota(jnp.int32, (count, count), 1)
-    every = jnp.where((row & 7) == (lane & 7), every, 0.0)
-    summed = tile_sums(every)
-    lane = lax.broadcasted_iota(jnp.int32, (count, count // 8), 0)
-    column = lax.broadcasted_iota(jnp.int32, (count, count // 8), 1)
-    merge = jnp.where(lane // 8 == column, 1.0, 0.0).astype(BF16)
-    out_sum = sum(jnp.dot(part, merge, preferred_element_type=F32) for part in reversed(split(summed, 3)))
-    cov_ref[...] = jnp.concatenate([in_ref[...], out_sum], axis=1)
-
-
-def staged_rows(train):
+            start = (2 * c + half) * examples
+            by_in[:, start:start + examples] = block[half * K_IN:(half + 1) * K_IN, :].astype(BF16)
+    for j in range(K_IN):
+        for part in range(parts):
+            start = j * examples + part * LANES
+            for half in range(2):
+                rows = turned[part, pl.ds(half * K_IN + j, blocks, stride=pitch), :]
+                by_out[half * blocks:(half + 1) * blocks, start:start + LANES] = rows.astype(BF16)
+    in_sum = lax.dot_general(by_in[...], by_in[...], NT, preferred_element_type=F32)
+    out_sum = lax.dot_general(by_out[...], by_out[...], NT, preferred_element_type=F32)
+    cov_ref[...] = jnp.concatenate([in_sum, out_sum], axis=1)
+
+
+def covariance_sums(train):
     examples, width = train.shape
-    chunks = 4 if width % (4 * 2 * LANES) == 0 else 1
+    chunks = 4 if width % (4 * LANES) == 0 else 1
     return pl.pallas_call(
-        stage_kernel,
-        out_shape=(
-            jax.ShapeDtypeStruct((K_IN, K_IN), F32),
-            jax.ShapeDtypeStruct((8 * K_OUT, K_IN // 8 * examples), BF16),
-        ),
+        covariance_kernel,
+        out_shape=jax.ShapeDtypeStruct((K_OUT, 2 * K_IN), F32),
         in_specs=[pl.BlockSpec(memory_space=pltpu.HBM)],
-        out_specs=(pl.BlockSpec(memory_space=pltpu.VMEM), pl.BlockSpec(memory_space=pltpu.VMEM)),
+        out_specs=pl.BlockSpec(memory_space=pltpu.VMEM),
         scratch_shapes=[
             pltpu.VMEM((chunks, examples, width // chunks), BF16),
+            pltpu.VMEM((examples // LANES, width // LANES * (LANES + 8), LANES), F32),
             pltpu.VMEM((K_IN, K_OUT * examples), BF16),
+            pltpu.VMEM((K_OUT, K_IN * examples), BF16),
             pltpu.SemaphoreType.DMA((chunks,)),
         ],
         compiler_params=pltpu.CompilerParams(vmem_limit_bytes=STAGE_VMEM_LIMIT),
-        cost_estimate=pl.CostEstimate(flops=32 * examples * 64**3, bytes_accessed=2 * examples * width, transcendentals=0),
-        name="stage_rows",
+        cost_estimate=pl.CostEstimate(flops=64 * examples * 64**3, bytes_accessed=2 * examples * width, transcendentals=0),
+        name="covariance",
     )(train)
-
-
-def covariance_sums(in_sum, rows):
-    return pl.pallas_call(
-        gram_kernel,
-        out_shape=jax.ShapeDtypeStruct((K_OUT, 2 * K_IN), F32),
-        in_specs=[pl.BlockSpec(memory_space=pltpu.VMEM), pl.BlockSpec(memory_space=pltpu.VMEM)],
-        out_specs=pl.BlockSpec(memory_space=pltpu.VMEM),
-        compiler_params=pltpu.CompilerParams(vmem_limit_bytes=VMEM_LIMIT),
-        cost_estimate=pl.CostEstimate(flops=2 * rows.shape[0] * rows.size, bytes_accessed=2 * rows.size, transcendentals=0),
-        name="covariance",
-    )(in_sum, rows)
 
 
 def turn_kernel(query_ref, out_ref, spread):
@@ -344,7 +309,7 @@
     order = jnp.arange(shard_count, dtype=jnp.int32)
     if shard_count == 8:
         far = exchange(own_queries, 4, shard_count)
-        cov = covariance_sums(*staged_rows(train))
+        cov = covariance_sums(train)
         far, _ = lax.optimization_barrier((far, cov))
         column = jnp.concatenate([own_queries, far], axis=0)
         cov = cov + exchange(cov, 1, shard_count)
@@ -361,7 +326,7 @@
         route = own_index ^ order
     else:
         turned = [turned_queries(lax.all_gather(own_queries, "dp", axis=0, tiled=True))]
-        cov = lax.psum(covariance_sums(*staged_rows(train)), "dp")
+        cov = lax.psum(covariance_sums(train), "dp")
         factors = inverse_factors(cov, total_count)
         route = order
     scores = all_scores(route, factors, turned, train, per_query)

time: 37.9 us -> 37.9 us (level)
  local copies, waits for them, and re-layouts: 0.02 us -> 1.61 us
  Pallas kernels: 9.44 us -> 8.19 us
    unnamed x8 -> x10, local copies, waits for them, and re-layouts: 0.02 us -> 1.61 us
    pallas_call x2 -> x1, Pallas kernels: 4.01 us -> 2.76 us  [covariance_sums(): pl.pallas_call(covariance_kernel, out_shape=jax.ShapeDtypeStruct((K_OUT,...]
  transfers between devices with their start and end apart: 6 -> 6, of which waited for: 4 -> 4; matrix products, arithmetic and copies ran while one was open for 0% -> 0% of each run, Pallas kernels for 17% -> 14%
where the time goes in v14:
time: 37.9 us; the launch traced here: 37.7 us
  blocking collectives  10.6 us (28%)
  starting transfers between devices  9.27 us (24%)
  Pallas kernels  8.19 us (22%)
  waiting for transfers between devices  7.15 us (19%)
  local copies, waits for them, and re-layouts  1.61 us (4%)
  other arithmetic  0.83 us (2%)
    all_to_all x1, blocking collectives, shards(): lax.all_to_all(outgoing, ('dp', 'layer'), split_axis=0, concat_axis=0, ti...  10.6 us
    ppermute x6, starting transfers between devices, exchange(): return lax.ppermute(values, 'dp', [(k, k ^ distance) for k in range(count)])  9.27 us
    ppermute x6, waiting for transfers between devices, exchange(): return lax.ppermute(values, 'dp', [(k, k ^ distance) for k in range(count)])  7.15 us
    pallas_call x1, Pallas kernels, covariance_sums(): pl.pallas_call(covariance_kernel, out_shape=jax.ShapeDtypeStruct((K_OUT,...  2.76 us
    pallas_call x1, Pallas kernels, all_scores(): pl.pallas_call(score_kernel, out_shape=jax.ShapeDtypeStruct((shard_count,...  2.68 us
    pallas_call x1, Pallas kernels, inverse_factors(): pl.pallas_call(functools.partial(inverse_kernel, total_count), out_shape=...  2.36 us
    unnamed x10, local copies, waits for them, and re-layouts  1.61 us
  transfers between devices with their start and end apart: 6, of which 4 were waited for; matrix products, arithmetic and copies ran while one was open for 0% of the time, Pallas kernels for 14%

profile of v14, /device:TPU:0, one launch (start us, length us, event | category | flops | bytes accessed | tf_op | source)
XLA Modules:
  0.0 37.7 jit_solution(12756828939294822039)
XLA Ops:
  0.0 4.0 %collective-permute-start = (bf16[8,4096]{1,0:T(8,128)(2,1)}, bf16[8,4096]{1,0:T(8,128)(2,1)S(1)}, u32[]{:S(2)}, u32[]{:S(2)}) collective-permute-start(bf16[8,4096]{1,0:T(8,128)(2,1)} %bitcast.9), channel_id=1, source_target_pairs={{0,8},{2,10},{4,12},{6,14},{8,0},{10,2},{12,4},{14,6},{1,9},{3,11}... | collective-permute-start | bytes 196616 | tf_op jit(solution)/shard_map/ppermute | solution.py:297
  4.0 0.0 copy-start
  4.0 1.6 %copy-done = bf16[256,1,4096]{2,0,1:T(8,128)(2,1)S(1)} copy-done((bf16[256,1,4096]{2,0,1:T(8,128)(2,1)S(1)}, bf16[256,1,4096]{2,0,1:T(8,128)(2,1)}, u32[]{:S(2)}) %copy-start) | copy-done | bytes 2097176
  5.6 0.0 copy-start.2
  5.6 0.0 copy-start.3
  5.6 0.0 copy-start.4
  5.6 2.8 %covariance.1 = f32[64,128]{1,0:T(8,128)S(1)} custom-call(bf16[256,4096]{1,0:T(8,128)(2,1)S(1)} %bitcast.5), custom_call_target="tpu_custom_call" | custom-call | flops 4294967296 | bytes 2097152 | tf_op jit(solution)/shard_map/covariance/pallas_call | solution.py:79
  8.4 1.6 %collective-permute-start.2 = (f32[64,128]{1,0:T(8,128)S(1)}, f32[64,128]{1,0:T(8,128)S(1)}, u32[]{:S(2)}, u32[]{:S(2)}) collective-permute-start(f32[64,128]{1,0:T(8,128)S(1)} %covariance.1), channel_id=1, source_target_pairs={{0,2},{2,0},{4,6},{6,4},{8,10},{10,8},{12,14},{14,12},{1,3},{3,1},... | collective-permute-start | bytes 98312 | tf_op jit(solution)/shard_map/ppermute | solution.py:297
  10.0 0.0 collective-permute-done
  10.0 0.0 copy-done.2
  10.0 1.6 %collective-permute-start.1 = (bf16[16,4096]{1,0:T(8,128)(2,1)S(1)}, bf16[16,4096]{1,0:T(8,128)(2,1)S(1)}, u32[]{:S(2)}, u32[]{:S(2)}) collective-permute-start(bf16[16,4096]{1,0:T(8,128)(2,1)S(1)} %pad_maximum_fusion.1), channel_id=1, source_target_pairs={{0,4},{2,6},{4,0},{6,2},{8,12},{10,14},{12,8},{14,10},{1,5},{3,7},... | collective-permute-start | bytes 393224 | tf_op jit(solution)/shard_map/ppermute | solution.py:297
  11.6 0.0 copy-done.3
  11.6 0.1 iota_compare_fusion
  11.7 0.7 %collective-permute-done.2 = f32[64,128]{1,0:T(8,128)S(1)} collective-permute-done((f32[64,128]{1,0:T(8,128)S(1)}, f32[64,128]{1,0:T(8,128)S(1)}, u32[]{:S(2)}, u32[]{:S(2)}) %collective-permute-start.2) | collective-permute-done | bytes 32800 | tf_op jit(solution)/shard_map/ppermute | solution.py:297
  12.4 0.0 collective-permute-start.3
  12.4 3.0 %collective-permute-done.1 = bf16[16,4096]{1,0:T(8,128)(2,1)S(1)} collective-permute-done((bf16[16,4096]{1,0:T(8,128)(2,1)S(1)}, bf16[16,4096]{1,0:T(8,128)(2,1)S(1)}, u32[]{:S(2)}, u32[]{:S(2)}) %collective-permute-start.1) | collective-permute-done | bytes 131104 | tf_op jit(solution)/shard_map/ppermute | solution.py:297
  15.4 0.2 collective-permute-start.5
  15.6 0.0 copy-done.4
  15.6 1.6 %collective-permute-done.3 = f32[64,128]{1,0:T(8,128)S(1)} collective-permute-done((f32[64,128]{1,0:T(8,128)S(1)}, f32[64,128]{1,0:T(8,128)S(1)}, u32[]{:S(2)}, u32[]{:S(2)}) %collective-permute-start.3) | collective-permute-done | bytes 32800 | tf_op jit(solution)/shard_map/ppermute | solution.py:297
  17.2 1.8 %collective-permute-start.4 = (f32[64,128]{1,0:T(8,128)S(1)}, f32[64,128]{1,0:T(8,128)S(1)}, u32[]{:S(2)}, u32[]{:S(2)}) collective-permute-start(f32[64,128]{1,0:T(8,128)S(1)} %add.10), channel_id=1, source_target_pairs={{0,4},{2,6},{4,0},{6,2},{8,12},{10,14},{12,8},{14,10},{1,5},{3,7},... | collective-permute-start | bytes 98312 | tf_op jit(solution)/shard_map/ppermute | solution.py:297
  19.0 0.2 turn_queries.2.first_ref
  19.2 1.9 %collective-permute-done.4 = f32[64,128]{1,0:T(8,128)S(1)} collective-permute-done((f32[64,128]{1,0:T(8,128)S(1)}, f32[64,128]{1,0:T(8,128)S(1)}, u32[]{:S(2)}, u32[]{:S(2)}) %collective-permute-start.4) | collective-permute-done | bytes 32800 | tf_op jit(solution)/shard_map/ppermute | solution.py:297
  21.1 0.0 copy-start.1
  21.1 2.4 %inverses.1 = (bf16[192,64]{1,0:T(8,128)(2,1)S(1)}, bf16[256,256]{1,0:T(8,128)(2,1)S(1)}) custom-call(f32[64,128]{1,0:T(8,128)S(1)} %add.11.cov_ref), custom_call_target="tpu_custom_call" | custom-call | flops 2000000000 | tf_op jit(solution)/shard_map/inverses/pallas_call | solution.py:207
  23.5 0.0 collective-permute-done.5.query_ref
  23.5 0.2 turn_queries.3.second_ref
  23.7 0.0 copy-done.1
  23.7 2.7 %products_and_scores.1 = f32[8,2,8,128]{3,2,1,0:T(8,128)S(1)} custom-call(s32[8]{0:T(128)S(1)} %broadcast_xor_fusion.route_ref, bf16[192,64]{1,0:T(8,128)(2,1)S(1)} %get-tuple-element.15.left_ref, bf16[256,256]{1,0:T(8,128)(2,1)S(1)} %get-tuple-element.16.right_ref, bf16[64,2048]{1,0:T(8,128)(2,1)S(1)} %turn_queries.2.first_ref, ...), custom_call_target="tpu_custom_call" | custom-call | flops 201326592 | bytes 2097152 | tf_op jit(solution)/shard_map/products_and_scores/pallas_call | solution.py:270
  26.4 10.6 %all_to_all.5 = f32[16,8,128]{2,1,0:T(8,128)S(1)} all-to-all(f32[16,8,128]{2,1,0:T(8,128)S(1)} %bitcast.7), channel_id=1, replica_groups=mesh['groups'=2,'dp'=8,'layer'=2] {'dp','layer'}, dimensions={0} | all-to-all | bytes 131072 | tf_op jit(solution)/shard_map/all_to_all | solution.py:336
  37.0 0.7 %select_reduce_fusion = f32[4,8,128]{2,1,0:T(8,128)} fusion(f32[8,2,8,128]{3,2,1,0:T(8,128)S(1)} %bitcast.8, pred[4,8]{1,0:T(4,128)(4,1)S(1)} %iota_compare_fusion), kind=kLoop, calls=%fused_computation.1 | loop fusion | flops 126976 | bytes 81952 | tf_op jit(solution)/shard_map/reduce_sum | solution.py:338
  (6 shorter events, 0.0 us)
Async XLA Ops:
  0.0 10.0 %collective-permute-start = (bf16[8,4096]{1,0:T(8,128)(2,1)}, bf16[8,4096]{1,0:T(8,128)(2,1)S(1)}, u32[]{:S(2)}, u32[]{:S(2)}) collective-permute-start(bf16[8,4096]{1,0:T(8,128)(2,1)} %bitcast.9), channel_id=1, source_target_pairs={{0,8},{2,10},{4,12},{6,14},{8,0},{10,2},{12,4},{14,6},{1,9},{3,11}... | collective-permute-start | bytes 196616 | tf_op jit(solution)/shard_map/ppermute | solution.py:297
  4.0 1.6 %copy-start = (bf16[256,1,4096]{2,0,1:T(8,128)(2,1)S(1)}, bf16[256,1,4096]{2,0,1:T(8,128)(2,1)}, u32[]{:S(2)}) copy-start(bf16[256,1,4096]{2,0,1:T(8,128)(2,1)} %param.4) | copy-start | bytes 6291460
  5.6 4.3 %copy-start.2 = (bf16[8,1,4096]{2,0,1:T(8,128)(2,1)S(1)}, bf16[8,1,4096]{2,0,1:T(8,128)(2,1)}, u32[]{:S(2)}) copy-start(bf16[8,1,4096]{2,0,1:T(8,128)(2,1)} %param.5) | copy-start | bytes 196612
  5.6 6.0 %copy-start.3 = (s32[1,4]{1,0:T(1,128)S(1)}, s32[1,4]{1,0:T(1,128)}, u32[]{:S(2)}) copy-start(s32[1,4]{1,0:T(1,128)} %param.6) | copy-start | bytes 52
  5.6 10.0 %copy-start.4 = (s32[8]{0:T(128)S(1)}, s32[8]{0:T(128)}, u32[]{:S(2)}) copy-start(s32[8]{0:T(128)} %constant.10.clone) | copy-start | bytes 100
  8.4 4.0 %collective-permute-start.2 = (f32[64,128]{1,0:T(8,128)S(1)}, f32[64,128]{1,0:T(8,128)S(1)}, u32[]{:S(2)}, u32[]{:S(2)}) collective-permute-start(f32[64,128]{1,0:T(8,128)S(1)} %covariance.1), channel_id=1, source_target_pairs={{0,2},{2,0},{4,6},{6,4},{8,10},{10,8},{12,14},{14,12},{1,3},{3,1},... | collective-permute-start | bytes 98312 | tf_op jit(solution)/shard_map/ppermute | solution.py:297
  10.0 5.4 %collective-permute-start.1 = (bf16[16,4096]{1,0:T(8,128)(2,1)S(1)}, bf16[16,4096]{1,0:T(8,128)(2,1)S(1)}, u32[]{:S(2)}, u32[]{:S(2)}) collective-permute-start(bf16[16,4096]{1,0:T(8,128)(2,1)S(1)} %pad_maximum_fusion.1), channel_id=1, source_target_pairs={{0,4},{2,6},{4,0},{6,2},{8,12},{10,14},{12,8},{14,10},{1,5},{3,7},... | collective-permute-start | bytes 393224 | tf_op jit(solution)/shard_map/ppermute | solution.py:297
  12.4 4.8 %collective-permute-start.3 = (f32[64,128]{1,0:T(8,128)S(1)}, f32[64,128]{1,0:T(8,128)S(1)}, u32[]{:S(2)}, u32[]{:S(2)}) collective-permute-start(f32[64,128]{1,0:T(8,128)S(1)} %add.9), channel_id=1, source_target_pairs={{0,8},{2,10},{4,12},{6,14},{8,0},{10,2},{12,4},{14,6},{1,9},{3,11}... | collective-permute-start | bytes 98312 | tf_op jit(solution)/shard_map/ppermute | solution.py:297
  15.4 8.1 %collective-permute-start.5 = (bf16[32,4096]{1,0:T(8,128)(2,1)S(1)}, bf16[32,4096]{1,0:T(8,128)(2,1)S(1)}, u32[]{:S(2)}, u32[]{:S(2)}) collective-permute-start(bf16[32,4096]{1,0:T(8,128)(2,1)S(1)} %pad_maximum_fusion.query_ref), channel_id=1, source_target_pairs={{0,2},{2,0},{4,6},{6,4},{8,10},{10,8},{12,14},{14,12},{1,3},{3,1},... | collective-permute-start | bytes 786440 | tf_op jit(solution)/shard_map/ppermute | solution.py:297
  17.2 3.9 %collective-permute-start.4 = (f32[64,128]{1,0:T(8,128)S(1)}, f32[64,128]{1,0:T(8,128)S(1)}, u32[]{:S(2)}, u32[]{:S(2)}) collective-permute-start(f32[64,128]{1,0:T(8,128)S(1)} %add.10), channel_id=1, source_target_pairs={{0,4},{2,6},{4,0},{6,2},{8,12},{10,14},{12,8},{14,10},{1,5},{3,7},... | collective-permute-start | bytes 98312 | tf_op jit(solution)/shard_map/ppermute | solution.py:297
  21.1 2.6 %copy-start.1 = (bf16[256,1,4096]{2,0,1:T(8,128)(2,1)S(1)}, bf16[256,1,4096]{2,0,1:T(8,128)(2,1)}, u32[]{:S(2)}) copy-start(bf16[256,1,4096]{2,0,1:T(8,128)(2,1)} %param.4) | copy-start | bytes 6291460

commit v15 on v14

--- a/solution.py
+++ b/solution.py
@@ -16,7 +16,7 @@
 BF16 = jnp.bfloat16
 VMEM_LIMIT = 48 * 1024 * 1024
 INVERSE_COST = 2 * 10**9
-STAGE_VMEM_LIMIT = 50 * 1024 * 1024
+STAGE_VMEM_LIMIT = 105 * 512 * 1024
 
 NT = (((1,), (1,)), ((), ()))
 
@@ -197,10 +197,9 @@
     left_ref[...] = jnp.concatenate(split(turned[:, :K_OUT], 3), axis=0)
     double = jnp.concatenate([jnp.where(low, inverse, 0.0), jnp.where(low, 0.0, turned)], axis=0)
     high, small = split(double, 2)
-    right_ref[:LANES, :LANES] = high
-    right_ref[:LANES, LANES:] = small
-    right_ref[LANES:, :LANES] = high
-    right_ref[LANES:, LANES:] = jnp.zeros_like(small)
+    right_ref[:LANES, :] = high
+    right_ref[LANES:2 * LANES, :] = high
+    right_ref[2 * LANES:, :] = small
 
 
 def inverse_factors(cov, total_count):
@@ -208,7 +207,7 @@
         functools.partial(inverse_kernel, total_count),
         out_shape=(
             jax.ShapeDtypeStruct((3 * K_OUT, K_OUT), BF16),
-            jax.ShapeDtypeStruct((2 * LANES, 2 * LANES), BF16),
+            jax.ShapeDtypeStruct((3 * LANES, LANES), BF16),
         ),
         in_specs=[pl.BlockSpec(memory_space=pltpu.VMEM)],
         out_specs=(pl.BlockSpec(memory_space=pltpu.VMEM), pl.BlockSpec(memory_space=pltpu.VMEM)),
@@ -233,11 +232,11 @@
                 high, small = split(once[:, k * LANES:(k + 1) * LANES], 2)
                 at = (side * pairs + g * group + k) * K_OUT
                 wide[at:at + K_OUT, :LANES] = high
-                wide[at:at + K_OUT, LANES:] = small
+                wide[at:at + K_OUT, LANES:2 * LANES] = small
+                wide[at:at + K_OUT, 2 * LANES:] = high
     twice = jnp.dot(wide[...], right_ref[...], preferred_element_type=F32)
     for p in range(2 * pairs):
-        part = twice[p * K_OUT:(p + 1) * K_OUT, :]
-        solved[p * pitch:p * pitch + K_OUT, :] = part[:, :LANES] + part[:, LANES:]
+        solved[p * pitch:p * pitch + K_OUT, :] = twice[p * K_OUT:(p + 1) * K_OUT, :]
     for c in range(blocks):
         first = solved[pl.ds(c, 2 * pairs, stride=pitch), :]
         second = solved[pl.ds(c + blocks, 2 * pairs, stride=pitch), :]
@@ -274,7 +273,7 @@
         in_specs=[
             pl.BlockSpec(memory_space=pltpu.SMEM),
             pl.BlockSpec((3 * K_OUT, K_OUT), lambda step: (0, 0)),
-            pl.BlockSpec((2 * LANES, 2 * LANES), lambda step: (0, 0)),
+            pl.BlockSpec((3 * LANES, LANES), lambda step: (0, 0)),
             pl.BlockSpec((K_OUT, HALF * K_IN), places[0]),
             pl.BlockSpec((K_OUT, HALF * K_IN), places[1]),
             pl.BlockSpec((examples, width), lambda step: (0, 0)),
@@ -282,7 +281,7 @@
         out_specs=pl.BlockSpec((shard_count, parts, per_query, LANES), lambda step: (0, 0, 0, 0)),
         scratch_shapes=[
             pltpu.VMEM((HALF * (K_OUT + 8), LANES), F32),
-            pltpu.VMEM((HALF * K_OUT, 2 * LANES), BF16),
+            pltpu.VMEM((HALF * K_OUT, 3 * LANES), BF16),
             pltpu.VMEM((CHUNK, width), BF16),
         ],
         compiler_params=pltpu.CompilerParams(vmem_limit_bytes=VMEM_LIMIT),

time: 37.9 us -> 37.7 us (level)
  local copies, waits for them, and re-layouts: 1.61 us -> 0.01 us
  Pallas kernels: 8.19 us -> 9.49 us
    unnamed x10 -> x8, local copies, waits for them, and re-layouts: 1.61 us -> 0.01 us
    pallas_call x1, Pallas kernels: 2.76 us -> 3.65 us  [covariance_sums(): pl.pallas_call(covariance_kernel, out_shape=jax.ShapeDtypeStruct((K_OUT,...]
    pallas_call x1, Pallas kernels: 2.68 us -> 3.09 us  [all_scores(): pl.pallas_call(score_kernel, out_shape=jax.ShapeDtypeStruct((shard_count,...]
  transfers between devices with their start and end apart: 6 -> 6, of which waited for: 4 -> 4; matrix products, arithmetic and copies ran while one was open for 0% -> 0% of each run, Pallas kernels for 14% -> 17%
where the time goes in v15:
time: 37.7 us; the launch traced here: 37.5 us
  blocking collectives  10.7 us (28%)
  Pallas kernels  9.49 us (25%)
  starting transfers between devices  9.46 us (25%)
  waiting for transfers between devices  6.96 us (18%)
  other arithmetic  0.83 us (2%)
    all_to_all x1, blocking collectives, shards(): lax.all_to_all(outgoing, ('dp', 'layer'), split_axis=0, concat_axis=0, ti...  10.7 us
    ppermute x6, starting transfers between devices, exchange(): return lax.ppermute(values, 'dp', [(k, k ^ distance) for k in range(count)])  9.46 us
    ppermute x6, waiting for transfers between devices, exchange(): return lax.ppermute(values, 'dp', [(k, k ^ distance) for k in range(count)])  6.96 us
    pallas_call x1, Pallas kernels, covariance_sums(): pl.pallas_call(covariance_kernel, out_shape=jax.ShapeDtypeStruct((K_OUT,...  3.65 us
    pallas_call x1, Pallas kernels, all_scores(): pl.pallas_call(score_kernel, out_shape=jax.ShapeDtypeStruct((shard_count,...  3.09 us
    pallas_call x1, Pallas kernels, inverse_factors(): pl.pallas_call(functools.partial(inverse_kernel, total_count), out_shape=...  2.36 us
  transfers between devices with their start and end apart: 6, of which 4 were waited for; matrix products, arithmetic and copies ran while one was open for 0% of the time, Pallas kernels for 17%

profile of v15, /device:TPU:0, one launch (start us, length us, event | category | flops | bytes accessed | tf_op | source)
XLA Modules:
  0.0 37.5 jit_solution(9775714319362415093)
XLA Ops:
  0.0 4.0 %collective-permute-start = (bf16[8,4096]{1,0:T(8,128)(2,1)}, bf16[8,4096]{1,0:T(8,128)(2,1)S(1)}, u32[]{:S(2)}, u32[]{:S(2)}) collective-permute-start(bf16[8,4096]{1,0:T(8,128)(2,1)} %bitcast.9), channel_id=1, source_target_pairs={{0,8},{2,10},{4,12},{6,14},{8,0},{10,2},{12,4},{14,6},{1,9},{3,11}... | collective-permute-start | bytes 196616 | tf_op jit(solution)/shard_map/ppermute | solution.py:296
  4.0 0.0 copy-start.1
  4.0 0.0 copy-start.2
  4.0 0.0 copy-start.3
  4.0 3.6 %covariance.1 = f32[64,128]{1,0:T(8,128)S(1)} custom-call(bf16[256,4096]{1,0:T(8,128)(2,1)} %bitcast.5), custom_call_target="tpu_custom_call" | custom-call | flops 4294967296 | bytes 2097152 | tf_op jit(solution)/shard_map/covariance/pallas_call | solution.py:79
  7.7 1.6 %collective-permute-start.2 = (f32[64,128]{1,0:T(8,128)S(1)}, f32[64,128]{1,0:T(8,128)S(1)}, u32[]{:S(2)}, u32[]{:S(2)}) collective-permute-start(f32[64,128]{1,0:T(8,128)S(1)} %covariance.1), channel_id=1, source_target_pairs={{0,2},{2,0},{4,6},{6,4},{8,10},{10,8},{12,14},{14,12},{1,3},{3,1},... | collective-permute-start | bytes 98312 | tf_op jit(solution)/shard_map/ppermute | solution.py:296
  9.3 0.0 collective-permute-done
  9.3 0.0 copy-done.1
  9.3 1.6 %collective-permute-start.1 = (bf16[16,4096]{1,0:T(8,128)(2,1)S(1)}, bf16[16,4096]{1,0:T(8,128)(2,1)S(1)}, u32[]{:S(2)}, u32[]{:S(2)}) collective-permute-start(bf16[16,4096]{1,0:T(8,128)(2,1)S(1)} %pad_maximum_fusion.1), channel_id=1, source_target_pairs={{0,4},{2,6},{4,0},{6,2},{8,12},{10,14},{12,8},{14,10},{1,5},{3,7},... | collective-permute-start | bytes 393224 | tf_op jit(solution)/shard_map/ppermute | solution.py:296
  10.9 0.0 copy-done.2
  10.9 0.1 iota_compare_fusion
  11.0 0.7 %collective-permute-done.2 = f32[64,128]{1,0:T(8,128)S(1)} collective-permute-done((f32[64,128]{1,0:T(8,128)S(1)}, f32[64,128]{1,0:T(8,128)S(1)}, u32[]{:S(2)}, u32[]{:S(2)}) %collective-permute-start.2) | collective-permute-done | bytes 32800 | tf_op jit(solution)/shard_map/ppermute | solution.py:296
  11.7 0.4 %collective-permute-start.3 = (f32[64,128]{1,0:T(8,128)S(1)}, f32[64,128]{1,0:T(8,128)S(1)}, u32[]{:S(2)}, u32[]{:S(2)}) collective-permute-start(f32[64,128]{1,0:T(8,128)S(1)} %add.9), channel_id=1, source_target_pairs={{0,8},{2,10},{4,12},{6,14},{8,0},{10,2},{12,4},{14,6},{1,9},{3,11}... | collective-permute-start | bytes 98312 | tf_op jit(solution)/shard_map/ppermute | solution.py:296
  12.1 2.6 %collective-permute-done.1 = bf16[16,4096]{1,0:T(8,128)(2,1)S(1)} collective-permute-done((bf16[16,4096]{1,0:T(8,128)(2,1)S(1)}, bf16[16,4096]{1,0:T(8,128)(2,1)S(1)}, u32[]{:S(2)}, u32[]{:S(2)}) %collective-permute-start.1) | collective-permute-done | bytes 131104 | tf_op jit(solution)/shard_map/ppermute | solution.py:296
  14.7 0.3 collective-permute-start.5
  14.9 0.0 copy-done.3
  14.9 1.6 %collective-permute-done.3 = f32[64,128]{1,0:T(8,128)S(1)} collective-permute-done((f32[64,128]{1,0:T(8,128)S(1)}, f32[64,128]{1,0:T(8,128)S(1)}, u32[]{:S(2)}, u32[]{:S(2)}) %collective-permute-start.3) | collective-permute-done | bytes 32800 | tf_op jit(solution)/shard_map/ppermute | solution.py:296
  16.5 1.6 %collective-permute-start.4 = (f32[64,128]{1,0:T(8,128)S(1)}, f32[64,128]{1,0:T(8,128)S(1)}, u32[]{:S(2)}, u32[]{:S(2)}) collective-permute-start(f32[64,128]{1,0:T(8,128)S(1)} %add.10), channel_id=1, source_target_pairs={{0,4},{2,6},{4,0},{6,2},{8,12},{10,14},{12,8},{14,10},{1,5},{3,7},... | collective-permute-start | bytes 98312 | tf_op jit(solution)/shard_map/ppermute | solution.py:296
  18.1 0.2 turn_queries.2.first_ref
  18.3 2.1 %collective-permute-done.4 = f32[64,128]{1,0:T(8,128)S(1)} collective-permute-done((f32[64,128]{1,0:T(8,128)S(1)}, f32[64,128]{1,0:T(8,128)S(1)}, u32[]{:S(2)}, u32[]{:S(2)}) %collective-permute-start.4) | collective-permute-done | bytes 32800 | tf_op jit(solution)/shard_map/ppermute | solution.py:296
  20.4 0.0 copy-start
  20.4 2.4 %inverses.1 = (bf16[192,64]{1,0:T(8,128)(2,1)S(1)}, bf16[384,128]{1,0:T(8,128)(2,1)S(1)}) custom-call(f32[64,128]{1,0:T(8,128)S(1)} %add.11.cov_ref), custom_call_target="tpu_custom_call" | custom-call | flops 2000000000 | tf_op jit(solution)/shard_map/inverses/pallas_call | solution.py:206
  22.8 0.0 collective-permute-done.5.query_ref
  22.8 0.2 turn_queries.3.second_ref
  23.0 0.0 copy-done
  23.0 3.1 %products_and_scores.1 = f32[8,2,8,128]{3,2,1,0:T(8,128)S(1)} custom-call(s32[8]{0:T(128)S(1)} %broadcast_xor_fusion.route_ref, bf16[192,64]{1,0:T(8,128)(2,1)S(1)} %get-tuple-element.15.left_ref, bf16[384,128]{1,0:T(8,128)(2,1)S(1)} %get-tuple-element.16.right_ref, bf16[64,2048]{1,0:T(8,128)(2,1)S(1)} %turn_queries.2.first_ref, ...), custom_call_target="tpu_custom_call" | custom-call | flops 201326592 | bytes 2097152 | tf_op jit(solution)/shard_map/products_and_scores/pallas_call | solution.py:269
  26.1 10.7 %all_to_all.5 = f32[16,8,128]{2,1,0:T(8,128)S(1)} all-to-all(f32[16,8,128]{2,1,0:T(8,128)S(1)} %bitcast.7), channel_id=1, replica_groups=mesh['groups'=2,'dp'=8,'layer'=2] {'dp','layer'}, dimensions={0} | all-to-all | bytes 131072 | tf_op jit(solution)/shard_map/all_to_all | solution.py:335
  36.8 0.7 %select_reduce_fusion = f32[4,8,128]{2,1,0:T(8,128)} fusion(f32[8,2,8,128]{3,2,1,0:T(8,128)S(1)} %bitcast.8, pred[4,8]{1,0:T(4,128)(4,1)S(1)} %iota_compare_fusion), kind=kLoop, calls=%fused_computation.1 | loop fusion | flops 126976 | bytes 81952 | tf_op jit(solution)/shard_map/reduce_sum | solution.py:337
  (6 shorter events, 0.0 us)
Async XLA Ops:
  0.0 9.3 %collective-permute-start = (bf16[8,4096]{1,0:T(8,128)(2,1)}, bf16[8,4096]{1,0:T(8,128)(2,1)S(1)}, u32[]{:S(2)}, u32[]{:S(2)}) collective-permute-start(bf16[8,4096]{1,0:T(8,128)(2,1)} %bitcast.9), channel_id=1, source_target_pairs={{0,8},{2,10},{4,12},{6,14},{8,0},{10,2},{12,4},{14,6},{1,9},{3,11}... | collective-permute-start | bytes 196616 | tf_op jit(solution)/shard_map/ppermute | solution.py:296
  4.0 5.2 %copy-start.1 = (bf16[8,1,4096]{2,0,1:T(8,128)(2,1)S(1)}, bf16[8,1,4096]{2,0,1:T(8,128)(2,1)}, u32[]{:S(2)}) copy-start(bf16[8,1,4096]{2,0,1:T(8,128)(2,1)} %param.5) | copy-start | bytes 196612
  4.0 6.9 %copy-start.2 = (s32[1,4]{1,0:T(1,128)S(1)}, s32[1,4]{1,0:T(1,128)}, u32[]{:S(2)}) copy-start(s32[1,4]{1,0:T(1,128)} %param.6) | copy-start | bytes 52
  4.0 10.9 %copy-start.3 = (s32[8]{0:T(128)S(1)}, s32[8]{0:T(128)}, u32[]{:S(2)}) copy-start(s32[8]{0:T(128)} %constant.10.clone) | copy-start | bytes 100
  7.7 4.0 %collective-permute-start.2 = (f32[64,128]{1,0:T(8,128)S(1)}, f32[64,128]{1,0:T(8,128)S(1)}, u32[]{:S(2)}, u32[]{:S(2)}) collective-permute-start(f32[64,128]{1,0:T(8,128)S(1)} %covariance.1), channel_id=1, source_target_pairs={{0,2},{2,0},{4,6},{6,4},{8,10},{10,8},{12,14},{14,12},{1,3},{3,1},... | collective-permute-start | bytes 98312 | tf_op jit(solution)/shard_map/ppermute | solution.py:296
  9.3 5.4 %collective-permute-start.1 = (bf16[16,4096]{1,0:T(8,128)(2,1)S(1)}, bf16[16,4096]{1,0:T(8,128)(2,1)S(1)}, u32[]{:S(2)}, u32[]{:S(2)}) collective-permute-start(bf16[16,4096]{1,0:T(8,128)(2,1)S(1)} %pad_maximum_fusion.1), channel_id=1, source_target_pairs={{0,4},{2,6},{4,0},{6,2},{8,12},{10,14},{12,8},{14,10},{1,5},{3,7},... | collective-permute-start | bytes 393224 | tf_op jit(solution)/shard_map/ppermute | solution.py:296
  11.7 4.8 %collective-permute-start.3 = (f32[64,128]{1,0:T(8,128)S(1)}, f32[64,128]{1,0:T(8,128)S(1)}, u32[]{:S(2)}, u32[]{:S(2)}) collective-permute-start(f32[64,128]{1,0:T(8,128)S(1)} %add.9), channel_id=1, source_target_pairs={{0,8},{2,10},{4,12},{6,14},{8,0},{10,2},{12,4},{14,6},{1,9},{3,11}... | collective-permute-start | bytes 98312 | tf_op jit(solution)/shard_map/ppermute | solution.py:296
  14.7 8.1 %collective-permute-start.5 = (bf16[32,4096]{1,0:T(8,128)(2,1)S(1)}, bf16[32,4096]{1,0:T(8,128)(2,1)S(1)}, u32[]{:S(2)}, u32[]{:S(2)}) collective-permute-start(bf16[32,4096]{1,0:T(8,128)(2,1)S(1)} %pad_maximum_fusion.query_ref), channel_id=1, source_target_pairs={{0,2},{2,0},{4,6},{6,4},{8,10},{10,8},{12,14},{14,12},{1,3},{3,1},... | collective-permute-start | bytes 786440 | tf_op jit(solution)/shard_map/ppermute | solution.py:296
  16.5 3.9 %collective-permute-start.4 = (f32[64,128]{1,0:T(8,128)S(1)}, f32[64,128]{1,0:T(8,128)S(1)}, u32[]{:S(2)}, u32[]{:S(2)}) collective-permute-start(f32[64,128]{1,0:T(8,128)S(1)} %add.10), channel_id=1, source_target_pairs={{0,4},{2,6},{4,0},{6,2},{8,12},{10,14},{12,8},{14,10},{1,5},{3,7},... | collective-permute-start | bytes 98312 | tf_op jit(solution)/shard_map/ppermute | solution.py:296
  20.4 2.6 %copy-start = (bf16[256,1,4096]{2,0,1:T(8,128)(2,1)S(1)}, bf16[256,1,4096]{2,0,1:T(8,128)(2,1)}, u32[]{:S(2)}) copy-start(bf16[256,1,4096]{2,0,1:T(8,128)(2,1)} %param.4) | copy-start | bytes 6291460

commit v16 on v14

--- a/solution.py
+++ b/solution.py
@@ -16,7 +16,7 @@
 BF16 = jnp.bfloat16
 VMEM_LIMIT = 48 * 1024 * 1024
 INVERSE_COST = 2 * 10**9
-STAGE_VMEM_LIMIT = 50 * 1024 * 1024
+STAGE_VMEM_LIMIT = 105 * 512 * 1024
 
 NT = (((1,), (1,)), ((), ()))
 

time: 37.9 us -> 37.2 us (0.982)
  local copies, waits for them, and re-layouts: 1.61 us -> 0.01 us
  Pallas kernels: 8.19 us -> 9.08 us
    unnamed x10 -> x8, local copies, waits for them, and re-layouts: 1.61 us -> 0.01 us
    pallas_call x1, Pallas kernels: 2.76 us -> 3.65 us  [covariance_sums(): pl.pallas_call(covariance_kernel, out_shape=jax.ShapeDtypeStruct((K_OUT,...]
  transfers between devices with their start and end apart: 6 -> 6, of which waited for: 4 -> 4; matrix products, arithmetic and copies ran while one was open for 0% -> 0% of each run, Pallas kernels for 14% -> 17%
where the time goes in v16:
time: 37.2 us; the launch traced here: 37.1 us
  blocking collectives  10.7 us (29%)
  starting transfers between devices  9.46 us (25%)
  Pallas kernels  9.08 us (24%)
  waiting for transfers between devices  6.96 us (19%)
  other arithmetic  0.83 us (2%)
    all_to_all x1, blocking collectives, shards(): lax.all_to_all(outgoing, ('dp', 'layer'), split_axis=0, concat_axis=0, ti...  10.7 us
    ppermute x6, starting transfers between devices, exchange(): return lax.ppermute(values, 'dp', [(k, k ^ distance) for k in range(count)])  9.46 us
    ppermute x6, waiting for transfers between devices, exchange(): return lax.ppermute(values, 'dp', [(k, k ^ distance) for k in range(count)])  6.96 us
    pallas_call x1, Pallas kernels, covariance_sums(): pl.pallas_call(covariance_kernel, out_shape=jax.ShapeDtypeStruct((K_OUT,...  3.65 us
    pallas_call x1, Pallas kernels, all_scores(): pl.pallas_call(score_kernel, out_shape=jax.ShapeDtypeStruct((shard_count,...  2.68 us
    pallas_call x1, Pallas kernels, inverse_factors(): pl.pallas_call(functools.partial(inverse_kernel, total_count), out_shape=...  2.36 us
  transfers between devices with their start and end apart: 6, of which 4 were waited for; matrix products, arithmetic and copies ran while one was open for 0% of the time, Pallas kernels for 17%

profile of v16, /device:TPU:0, one launch (start us, length us, event | category | flops | bytes accessed | tf_op | source)
XLA Modules:
  0.0 37.1 jit_solution(13277624504552928461)
XLA Ops:
  0.0 4.0 %collective-permute-start = (bf16[8,4096]{1,0:T(8,128)(2,1)}, bf16[8,4096]{1,0:T(8,128)(2,1)S(1)}, u32[]{:S(2)}, u32[]{:S(2)}) collective-permute-start(bf16[8,4096]{1,0:T(8,128)(2,1)} %bitcast.9), channel_id=1, source_target_pairs={{0,8},{2,10},{4,12},{6,14},{8,0},{10,2},{12,4},{14,6},{1,9},{3,11}... | collective-permute-start | bytes 196616 | tf_op jit(solution)/shard_map/ppermute | solution.py:297
  4.0 0.0 copy-start.1
  4.0 0.0 copy-start.2
  4.0 0.0 copy-start.3
  4.0 3.6 %covariance.1 = f32[64,128]{1,0:T(8,128)S(1)} custom-call(bf16[256,4096]{1,0:T(8,128)(2,1)} %bitcast.5), custom_call_target="tpu_custom_call" | custom-call | flops 4294967296 | bytes 2097152 | tf_op jit(solution)/shard_map/covariance/pallas_call | solution.py:79
  7.7 1.6 %collective-permute-start.2 = (f32[64,128]{1,0:T(8,128)S(1)}, f32[64,128]{1,0:T(8,128)S(1)}, u32[]{:S(2)}, u32[]{:S(2)}) collective-permute-start(f32[64,128]{1,0:T(8,128)S(1)} %covariance.1), channel_id=1, source_target_pairs={{0,2},{2,0},{4,6},{6,4},{8,10},{10,8},{12,14},{14,12},{1,3},{3,1},... | collective-permute-start | bytes 98312 | tf_op jit(solution)/shard_map/ppermute | solution.py:297
  9.3 0.0 collective-permute-done
  9.3 0.0 copy-done.1
  9.3 1.6 %collective-permute-start.1 = (bf16[16,4096]{1,0:T(8,128)(2,1)S(1)}, bf16[16,4096]{1,0:T(8,128)(2,1)S(1)}, u32[]{:S(2)}, u32[]{:S(2)}) collective-permute-start(bf16[16,4096]{1,0:T(8,128)(2,1)S(1)} %pad_maximum_fusion.1), channel_id=1, source_target_pairs={{0,4},{2,6},{4,0},{6,2},{8,12},{10,14},{12,8},{14,10},{1,5},{3,7},... | collective-permute-start | bytes 393224 | tf_op jit(solution)/shard_map/ppermute | solution.py:297
  10.9 0.0 copy-done.2
  10.9 0.1 iota_compare_fusion
  11.0 0.7 %collective-permute-done.2 = f32[64,128]{1,0:T(8,128)S(1)} collective-permute-done((f32[64,128]{1,0:T(8,128)S(1)}, f32[64,128]{1,0:T(8,128)S(1)}, u32[]{:S(2)}, u32[]{:S(2)}) %collective-permute-start.2) | collective-permute-done | bytes 32800 | tf_op jit(solution)/shard_map/ppermute | solution.py:297
  11.7 0.4 %collective-permute-start.3 = (f32[64,128]{1,0:T(8,128)S(1)}, f32[64,128]{1,0:T(8,128)S(1)}, u32[]{:S(2)}, u32[]{:S(2)}) collective-permute-start(f32[64,128]{1,0:T(8,128)S(1)} %add.9), channel_id=1, source_target_pairs={{0,8},{2,10},{4,12},{6,14},{8,0},{10,2},{12,4},{14,6},{1,9},{3,11}... | collective-permute-start | bytes 98312 | tf_op jit(solution)/shard_map/ppermute | solution.py:297
  12.1 2.6 %collective-permute-done.1 = bf16[16,4096]{1,0:T(8,128)(2,1)S(1)} collective-permute-done((bf16[16,4096]{1,0:T(8,128)(2,1)S(1)}, bf16[16,4096]{1,0:T(8,128)(2,1)S(1)}, u32[]{:S(2)}, u32[]{:S(2)}) %collective-permute-start.1) | collective-permute-done | bytes 131104 | tf_op jit(solution)/shard_map/ppermute | solution.py:297
  14.7 0.3 collective-permute-start.5
  14.9 0.0 copy-done.3
  14.9 1.6 %collective-permute-done.3 = f32[64,128]{1,0:T(8,128)S(1)} collective-permute-done((f32[64,128]{1,0:T(8,128)S(1)}, f32[64,128]{1,0:T(8,128)S(1)}, u32[]{:S(2)}, u32[]{:S(2)}) %collective-permute-start.3) | collective-permute-done | bytes 32800 | tf_op jit(solution)/shard_map/ppermute | solution.py:297
  16.5 1.6 %collective-permute-start.4 = (f32[64,128]{1,0:T(8,128)S(1)}, f32[64,128]{1,0:T(8,128)S(1)}, u32[]{:S(2)}, u32[]{:S(2)}) collective-permute-start(f32[64,128]{1,0:T(8,128)S(1)} %add.10), channel_id=1, source_target_pairs={{0,4},{2,6},{4,0},{6,2},{8,12},{10,14},{12,8},{14,10},{1,5},{3,7},... | collective-permute-start | bytes 98312 | tf_op jit(solution)/shard_map/ppermute | solution.py:297
  18.1 0.2 turn_queries.2.first_ref
  18.3 2.1 %collective-permute-done.4 = f32[64,128]{1,0:T(8,128)S(1)} collective-permute-done((f32[64,128]{1,0:T(8,128)S(1)}, f32[64,128]{1,0:T(8,128)S(1)}, u32[]{:S(2)}, u32[]{:S(2)}) %collective-permute-start.4) | collective-permute-done | bytes 32800 | tf_op jit(solution)/shard_map/ppermute | solution.py:297
  20.4 0.0 copy-start
  20.4 2.4 %inverses.1 = (bf16[192,64]{1,0:T(8,128)(2,1)S(1)}, bf16[256,256]{1,0:T(8,128)(2,1)S(1)}) custom-call(f32[64,128]{1,0:T(8,128)S(1)} %add.11.cov_ref), custom_call_target="tpu_custom_call" | custom-call | flops 2000000000 | tf_op jit(solution)/shard_map/inverses/pallas_call | solution.py:207
  22.8 0.0 collective-permute-done.5.query_ref
  22.8 0.2 turn_queries.3.second_ref
  23.0 0.0 copy-done
  23.0 2.7 %products_and_scores.1 = f32[8,2,8,128]{3,2,1,0:T(8,128)S(1)} custom-call(s32[8]{0:T(128)S(1)} %broadcast_xor_fusion.route_ref, bf16[192,64]{1,0:T(8,128)(2,1)S(1)} %get-tuple-element.15.left_ref, bf16[256,256]{1,0:T(8,128)(2,1)S(1)} %get-tuple-element.16.right_ref, bf16[64,2048]{1,0:T(8,128)(2,1)S(1)} %turn_queries.2.first_ref, ...), custom_call_target="tpu_custom_call" | custom-call | flops 201326592 | bytes 2097152 | tf_op jit(solution)/shard_map/products_and_scores/pallas_call | solution.py:270
  25.7 10.7 %all_to_all.5 = f32[16,8,128]{2,1,0:T(8,128)S(1)} all-to-all(f32[16,8,128]{2,1,0:T(8,128)S(1)} %bitcast.7), channel_id=1, replica_groups=mesh['groups'=2,'dp'=8,'layer'=2] {'dp','layer'}, dimensions={0} | all-to-all | bytes 131072 | tf_op jit(solution)/shard_map/all_to_all | solution.py:336
  36.4 0.7 %select_reduce_fusion = f32[4,8,128]{2,1,0:T(8,128)} fusion(f32[8,2,8,128]{3,2,1,0:T(8,128)S(1)} %bitcast.8, pred[4,8]{1,0:T(4,128)(4,1)S(1)} %iota_compare_fusion), kind=kLoop, calls=%fused_computation.1 | loop fusion | flops 126976 | bytes 81952 | tf_op jit(solution)/shard_map/reduce_sum | solution.py:338
  (6 shorter events, 0.0 us)
Async XLA Ops:
  0.0 9.3 %collective-permute-start = (bf16[8,4096]{1,0:T(8,128)(2,1)}, bf16[8,4096]{1,0:T(8,128)(2,1)S(1)}, u32[]{:S(2)}, u32[]{:S(2)}) collective-permute-start(bf16[8,4096]{1,0:T(8,128)(2,1)} %bitcast.9), channel_id=1, source_target_pairs={{0,8},{2,10},{4,12},{6,14},{8,0},{10,2},{12,4},{14,6},{1,9},{3,11}... | collective-permute-start | bytes 196616 | tf_op jit(solution)/shard_map/ppermute | solution.py:297
  4.0 5.2 %copy-start.1 = (bf16[8,1,4096]{2,0,1:T(8,128)(2,1)S(1)}, bf16[8,1,4096]{2,0,1:T(8,128)(2,1)}, u32[]{:S(2)}) copy-start(bf16[8,1,4096]{2,0,1:T(8,128)(2,1)} %param.5) | copy-start | bytes 196612
  4.0 6.9 %copy-start.2 = (s32[1,4]{1,0:T(1,128)S(1)}, s32[1,4]{1,0:T(1,128)}, u32[]{:S(2)}) copy-start(s32[1,4]{1,0:T(1,128)} %param.6) | copy-start | bytes 52
  4.0 10.9 %copy-start.3 = (s32[8]{0:T(128)S(1)}, s32[8]{0:T(128)}, u32[]{:S(2)}) copy-start(s32[8]{0:T(128)} %constant.10.clone) | copy-start | bytes 100
  7.7 4.0 %collective-permute-start.2 = (f32[64,128]{1,0:T(8,128)S(1)}, f32[64,128]{1,0:T(8,128)S(1)}, u32[]{:S(2)}, u32[]{:S(2)}) collective-permute-start(f32[64,128]{1,0:T(8,128)S(1)} %covariance.1), channel_id=1, source_target_pairs={{0,2},{2,0},{4,6},{6,4},{8,10},{10,8},{12,14},{14,12},{1,3},{3,1},... | collective-permute-start | bytes 98312 | tf_op jit(solution)/shard_map/ppermute | solution.py:297
  9.3 5.4 %collective-permute-start.1 = (bf16[16,4096]{1,0:T(8,128)(2,1)S(1)}, bf16[16,4096]{1,0:T(8,128)(2,1)S(1)}, u32[]{:S(2)}, u32[]{:S(2)}) collective-permute-start(bf16[16,4096]{1,0:T(8,128)(2,1)S(1)} %pad_maximum_fusion.1), channel_id=1, source_target_pairs={{0,4},{2,6},{4,0},{6,2},{8,12},{10,14},{12,8},{14,10},{1,5},{3,7},... | collective-permute-start | bytes 393224 | tf_op jit(solution)/shard_map/ppermute | solution.py:297
  11.7 4.8 %collective-permute-start.3 = (f32[64,128]{1,0:T(8,128)S(1)}, f32[64,128]{1,0:T(8,128)S(1)}, u32[]{:S(2)}, u32[]{:S(2)}) collective-permute-start(f32[64,128]{1,0:T(8,128)S(1)} %add.9), channel_id=1, source_target_pairs={{0,8},{2,10},{4,12},{6,14},{8,0},{10,2},{12,4},{14,6},{1,9},{3,11}... | collective-permute-start | bytes 98312 | tf_op jit(solution)/shard_map/ppermute | solution.py:297
  14.7 8.1 %collective-permute-start.5 = (bf16[32,4096]{1,0:T(8,128)(2,1)S(1)}, bf16[32,4096]{1,0:T(8,128)(2,1)S(1)}, u32[]{:S(2)}, u32[]{:S(2)}) collective-permute-start(bf16[32,4096]{1,0:T(8,128)(2,1)S(1)} %pad_maximum_fusion.query_ref), channel_id=1, source_target_pairs={{0,2},{2,0},{4,6},{6,4},{8,10},{10,8},{12,14},{14,12},{1,3},{3,1},... | collective-permute-start | bytes 786440 | tf_op jit(solution)/shard_map/ppermute | solution.py:297
  16.5 3.9 %collective-permute-start.4 = (f32[64,128]{1,0:T(8,128)S(1)}, f32[64,128]{1,0:T(8,128)S(1)}, u32[]{:S(2)}, u32[]{:S(2)}) collective-permute-start(f32[64,128]{1,0:T(8,128)S(1)} %add.10), channel_id=1, source_target_pairs={{0,4},{2,6},{4,0},{6,2},{8,12},{10,14},{12,8},{14,10},{1,5},{3,7},... | collective-permute-start | bytes 98312 | tf_op jit(solution)/shard_map/ppermute | solution.py:297
  20.4 2.6 %copy-start = (bf16[256,1,4096]{2,0,1:T(8,128)(2,1)S(1)}, bf16[256,1,4096]{2,0,1:T(8,128)(2,1)}, u32[]{:S(2)}) copy-start(bf16[256,1,4096]{2,0,1:T(8,128)(2,1)} %param.4) | copy-start | bytes 6291460

commit v17 on v16

--- a/solution.py
+++ b/solution.py
@@ -75,7 +75,7 @@
 
 def covariance_sums(train):
     examples, width = train.shape
-    chunks = 4 if width % (4 * LANES) == 0 else 1
+    chunks = 2 if width % (2 * LANES) == 0 else 1
     return pl.pallas_call(
         covariance_kernel,
         out_shape=jax.ShapeDtypeStruct((K_OUT, 2 * K_IN), F32),
@@ -223,7 +223,7 @@
     pairs = HALF // 2
     pitch = solved.shape[0] // (2 * pairs)
     step = pl.program_id(0)
-    group = 4
+    group = 8
     for side, turned_ref in enumerate((first_ref, second_ref)):
         for g in range(pairs // group):
             block = turned_ref[:, g * group * LANES:(g + 1) * group * LANES]

time: 37.2 us -> 37.3 us (level)
  no operation moved by 1% of the time
where the time goes in v17:
time: 37.3 us; the launch traced here: 37.1 us
  blocking collectives  10.6 us (28%)
  starting transfers between devices  9.44 us (25%)
  Pallas kernels  9.1 us (24%)
  waiting for transfers between devices  6.98 us (19%)
  other arithmetic  0.83 us (2%)
    all_to_all x1, blocking collectives, shards(): lax.all_to_all(outgoing, ('dp', 'layer'), split_axis=0, concat_axis=0, ti...  10.6 us
    ppermute x6, starting transfers between devices, exchange(): return lax.ppermute(values, 'dp', [(k, k ^ distance) for k in range(count)])  9.44 us
    ppermute x6, waiting for transfers between devices, exchange(): return lax.ppermute(values, 'dp', [(k, k ^ distance) for k in range(count)])  6.98 us
    pallas_call x1, Pallas kernels, covariance_sums(): pl.pallas_call(covariance_kernel, out_shape=jax.ShapeDtypeStruct((K_OUT,...  3.66 us
    pallas_call x1, Pallas kernels, all_scores(): pl.pallas_call(score_kernel, out_shape=jax.ShapeDtypeStruct((shard_count,...  2.68 us
    pallas_call x1, Pallas kernels, inverse_factors(): pl.pallas_call(functools.partial(inverse_kernel, total_count), out_shape=...  2.36 us
  transfers between devices with their start and end apart: 6, of which 4 were waited for; matrix products, arithmetic and copies ran while one was open for 0% of the time, Pallas kernels for 17%

profile of v17, /device:TPU:0, one launch (start us, length us, event | category | flops | bytes accessed | tf_op | source)
XLA Modules:
  0.0 37.1 jit_solution(11562596485672523440)
XLA Ops:
  0.0 4.0 %collective-permute-start = (bf16[8,4096]{1,0:T(8,128)(2,1)}, bf16[8,4096]{1,0:T(8,128)(2,1)S(1)}, u32[]{:S(2)}, u32[]{:S(2)}) collective-permute-start(bf16[8,4096]{1,0:T(8,128)(2,1)} %bitcast.9), channel_id=1, source_target_pairs={{0,8},{2,10},{4,12},{6,14},{8,0},{10,2},{12,4},{14,6},{1,9},{3,11}... | collective-permute-start | bytes 196616 | tf_op jit(solution)/shard_map/ppermute | solution.py:297
  4.0 0.0 copy-start.1
  4.0 0.0 copy-start.2
  4.0 0.0 copy-start.3
  4.0 3.7 %covariance.1 = f32[64,128]{1,0:T(8,128)S(1)} custom-call(bf16[256,4096]{1,0:T(8,128)(2,1)} %bitcast.5), custom_call_target="tpu_custom_call" | custom-call | flops 4294967296 | bytes 2097152 | tf_op jit(solution)/shard_map/covariance/pallas_call | solution.py:79
  7.7 1.6 %collective-permute-start.2 = (f32[64,128]{1,0:T(8,128)S(1)}, f32[64,128]{1,0:T(8,128)S(1)}, u32[]{:S(2)}, u32[]{:S(2)}) collective-permute-start(f32[64,128]{1,0:T(8,128)S(1)} %covariance.1), channel_id=1, source_target_pairs={{0,2},{2,0},{4,6},{6,4},{8,10},{10,8},{12,14},{14,12},{1,3},{3,1},... | collective-permute-start | bytes 98312 | tf_op jit(solution)/shard_map/ppermute | solution.py:297
  9.3 0.0 collective-permute-done
  9.3 0.0 copy-done.1
  9.3 1.6 %collective-permute-start.1 = (bf16[16,4096]{1,0:T(8,128)(2,1)S(1)}, bf16[16,4096]{1,0:T(8,128)(2,1)S(1)}, u32[]{:S(2)}, u32[]{:S(2)}) collective-permute-start(bf16[16,4096]{1,0:T(8,128)(2,1)S(1)} %pad_maximum_fusion.1), channel_id=1, source_target_pairs={{0,4},{2,6},{4,0},{6,2},{8,12},{10,14},{12,8},{14,10},{1,5},{3,7},... | collective-permute-start | bytes 393224 | tf_op jit(solution)/shard_map/ppermute | solution.py:297
  10.9 0.0 copy-done.2
  10.9 0.1 iota_compare_fusion
  11.0 0.7 %collective-permute-done.2 = f32[64,128]{1,0:T(8,128)S(1)} collective-permute-done((f32[64,128]{1,0:T(8,128)S(1)}, f32[64,128]{1,0:T(8,128)S(1)}, u32[]{:S(2)}, u32[]{:S(2)}) %collective-permute-start.2) | collective-permute-done | bytes 32800 | tf_op jit(solution)/shard_map/ppermute | solution.py:297
  11.7 0.4 %collective-permute-start.3 = (f32[64,128]{1,0:T(8,128)S(1)}, f32[64,128]{1,0:T(8,128)S(1)}, u32[]{:S(2)}, u32[]{:S(2)}) collective-permute-start(f32[64,128]{1,0:T(8,128)S(1)} %add.9), channel_id=1, source_target_pairs={{0,8},{2,10},{4,12},{6,14},{8,0},{10,2},{12,4},{14,6},{1,9},{3,11}... | collective-permute-start | bytes 98312 | tf_op jit(solution)/shard_map/ppermute | solution.py:297
  12.1 2.6 %collective-permute-done.1 = bf16[16,4096]{1,0:T(8,128)(2,1)S(1)} collective-permute-done((bf16[16,4096]{1,0:T(8,128)(2,1)S(1)}, bf16[16,4096]{1,0:T(8,128)(2,1)S(1)}, u32[]{:S(2)}, u32[]{:S(2)}) %collective-permute-start.1) | collective-permute-done | bytes 131104 | tf_op jit(solution)/shard_map/ppermute | solution.py:297
  14.7 0.2 collective-permute-start.5
  14.9 0.0 copy-done.3
  14.9 1.6 %collective-permute-done.3 = f32[64,128]{1,0:T(8,128)S(1)} collective-permute-done((f32[64,128]{1,0:T(8,128)S(1)}, f32[64,128]{1,0:T(8,128)S(1)}, u32[]{:S(2)}, u32[]{:S(2)}) %collective-permute-start.3) | collective-permute-done | bytes 32800 | tf_op jit(solution)/shard_map/ppermute | solution.py:297
  16.5 1.6 %collective-permute-start.4 = (f32[64,128]{1,0:T(8,128)S(1)}, f32[64,128]{1,0:T(8,128)S(1)}, u32[]{:S(2)}, u32[]{:S(2)}) collective-permute-start(f32[64,128]{1,0:T(8,128)S(1)} %add.10), channel_id=1, source_target_pairs={{0,4},{2,6},{4,0},{6,2},{8,12},{10,14},{12,8},{14,10},{1,5},{3,7},... | collective-permute-start | bytes 98312 | tf_op jit(solution)/shard_map/ppermute | solution.py:297
  18.1 0.2 turn_queries.2.first_ref
  18.3 2.1 %collective-permute-done.4 = f32[64,128]{1,0:T(8,128)S(1)} collective-permute-done((f32[64,128]{1,0:T(8,128)S(1)}, f32[64,128]{1,0:T(8,128)S(1)}, u32[]{:S(2)}, u32[]{:S(2)}) %collective-permute-start.4) | collective-permute-done | bytes 32800 | tf_op jit(solution)/shard_map/ppermute | solution.py:297
  20.4 0.0 copy-start
  20.4 2.4 %inverses.1 = (bf16[192,64]{1,0:T(8,128)(2,1)S(1)}, bf16[256,256]{1,0:T(8,128)(2,1)S(1)}) custom-call(f32[64,128]{1,0:T(8,128)S(1)} %add.11.cov_ref), custom_call_target="tpu_custom_call" | custom-call | flops 2000000000 | tf_op jit(solution)/shard_map/inverses/pallas_call | solution.py:207
  22.8 0.0 collective-permute-done.5.query_ref
  22.8 0.2 turn_queries.3.second_ref
  23.0 0.0 copy-done
  23.0 2.7 %products_and_scores.1 = f32[8,2,8,128]{3,2,1,0:T(8,128)S(1)} custom-call(s32[8]{0:T(128)S(1)} %broadcast_xor_fusion.route_ref, bf16[192,64]{1,0:T(8,128)(2,1)S(1)} %get-tuple-element.15.left_ref, bf16[256,256]{1,0:T(8,128)(2,1)S(1)} %get-tuple-element.16.right_ref, bf16[64,2048]{1,0:T(8,128)(2,1)S(1)} %turn_queries.2.first_ref, ...), custom_call_target="tpu_custom_call" | custom-call | flops 201326592 | bytes 2097152 | tf_op jit(solution)/shard_map/products_and_scores/pallas_call | solution.py:270
  25.7 10.6 %all_to_all.5 = f32[16,8,128]{2,1,0:T(8,128)S(1)} all-to-all(f32[16,8,128]{2,1,0:T(8,128)S(1)} %bitcast.7), channel_id=1, replica_groups=mesh['groups'=2,'dp'=8,'layer'=2] {'dp','layer'}, dimensions={0} | all-to-all | bytes 131072 | tf_op jit(solution)/shard_map/all_to_all | solution.py:336
  36.4 0.7 %select_reduce_fusion = f32[4,8,128]{2,1,0:T(8,128)} fusion(f32[8,2,8,128]{3,2,1,0:T(8,128)S(1)} %bitcast.8, pred[4,8]{1,0:T(4,128)(4,1)S(1)} %iota_compare_fusion), kind=kLoop, calls=%fused_computation.1 | loop fusion | flops 126976 | bytes 81952 | tf_op jit(solution)/shard_map/reduce_sum | solution.py:338
  (6 shorter events, 0.0 us)
Async XLA Ops:
  0.0 9.3 %collective-permute-start = (bf16[8,4096]{1,0:T(8,128)(2,1)}, bf16[8,4096]{1,0:T(8,128)(2,1)S(1)}, u32[]{:S(2)}, u32[]{:S(2)}) collective-permute-start(bf16[8,4096]{1,0:T(8,128)(2,1)} %bitcast.9), channel_id=1, source_target_pairs={{0,8},{2,10},{4,12},{6,14},{8,0},{10,2},{12,4},{14,6},{1,9},{3,11}... | collective-permute-start | bytes 196616 | tf_op jit(solution)/shard_map/ppermute | solution.py:297
  4.0 5.2 %copy-start.1 = (bf16[8,1,4096]{2,0,1:T(8,128)(2,1)S(1)}, bf16[8,1,4096]{2,0,1:T(8,128)(2,1)}, u32[]{:S(2)}) copy-start(bf16[8,1,4096]{2,0,1:T(8,128)(2,1)} %param.5) | copy-start | bytes 196612
  4.0 6.9 %copy-start.2 = (s32[1,4]{1,0:T(1,128)S(1)}, s32[1,4]{1,0:T(1,128)}, u32[]{:S(2)}) copy-start(s32[1,4]{1,0:T(1,128)} %param.6) | copy-start | bytes 52
  4.0 10.9 %copy-start.3 = (s32[8]{0:T(128)S(1)}, s32[8]{0:T(128)}, u32[]{:S(2)}) copy-start(s32[8]{0:T(128)} %constant.10.clone) | copy-start | bytes 100
  7.7 4.0 %collective-permute-start.2 = (f32[64,128]{1,0:T(8,128)S(1)}, f32[64,128]{1,0:T(8,128)S(1)}, u32[]{:S(2)}, u32[]{:S(2)}) collective-permute-start(f32[64,128]{1,0:T(8,128)S(1)} %covariance.1), channel_id=1, source_target_pairs={{0,2},{2,0},{4,6},{6,4},{8,10},{10,8},{12,14},{14,12},{1,3},{3,1},... | collective-permute-start | bytes 98312 | tf_op jit(solution)/shard_map/ppermute | solution.py:297
  9.3 5.4 %collective-permute-start.1 = (bf16[16,4096]{1,0:T(8,128)(2,1)S(1)}, bf16[16,4096]{1,0:T(8,128)(2,1)S(1)}, u32[]{:S(2)}, u32[]{:S(2)}) collective-permute-start(bf16[16,4096]{1,0:T(8,128)(2,1)S(1)} %pad_maximum_fusion.1), channel_id=1, source_target_pairs={{0,4},{2,6},{4,0},{6,2},{8,12},{10,14},{12,8},{14,10},{1,5},{3,7},... | collective-permute-start | bytes 393224 | tf_op jit(solution)/shard_map/ppermute | solution.py:297
  11.7 4.8 %collective-permute-start.3 = (f32[64,128]{1,0:T(8,128)S(1)}, f32[64,128]{1,0:T(8,128)S(1)}, u32[]{:S(2)}, u32[]{:S(2)}) collective-permute-start(f32[64,128]{1,0:T(8,128)S(1)} %add.9), channel_id=1, source_target_pairs={{0,8},{2,10},{4,12},{6,14},{8,0},{10,2},{12,4},{14,6},{1,9},{3,11}... | collective-permute-start | bytes 98312 | tf_op jit(solution)/shard_map/ppermute | solution.py:297
  14.7 8.1 %collective-permute-start.5 = (bf16[32,4096]{1,0:T(8,128)(2,1)S(1)}, bf16[32,4096]{1,0:T(8,128)(2,1)S(1)}, u32[]{:S(2)}, u32[]{:S(2)}) collective-permute-start(bf16[32,4096]{1,0:T(8,128)(2,1)S(1)} %pad_maximum_fusion.query_ref), channel_id=1, source_target_pairs={{0,2},{2,0},{4,6},{6,4},{8,10},{10,8},{12,14},{14,12},{1,3},{3,1},... | collective-permute-start | bytes 786440 | tf_op jit(solution)/shard_map/ppermute | solution.py:297
  16.5 3.9 %collective-permute-start.4 = (f32[64,128]{1,0:T(8,128)S(1)}, f32[64,128]{1,0:T(8,128)S(1)}, u32[]{:S(2)}, u32[]{:S(2)}) collective-permute-start(f32[64,128]{1,0:T(8,128)S(1)} %add.10), channel_id=1, source_target_pairs={{0,4},{2,6},{4,0},{6,2},{8,12},{10,14},{12,8},{14,10},{1,5},{3,7},... | collective-permute-start | bytes 98312 | tf_op jit(solution)/shard_map/ppermute | solution.py:297
  20.4 2.6 %copy-start = (bf16[256,1,4096]{2,0,1:T(8,128)(2,1)S(1)}, bf16[256,1,4096]{2,0,1:T(8,128)(2,1)}, u32[]{:S(2)}) copy-start(bf16[256,1,4096]{2,0,1:T(8,128)(2,1)} %param.4) | copy-start | bytes 6291460

commit v18 on v16

--- a/solution.py
+++ b/solution.py
@@ -139,6 +139,13 @@
     return cov * scale + jnp.where(diagonal, added, 0.0)
 
 
+def reciprocal(values):
+    estimate = pl.reciprocal(values, approx=True)
+    for _ in range(2):
+        estimate = estimate * (2.0 - values * estimate)
+    return estimate
+
+
 def inverses(matrix):
     size = matrix.shape[0]
     sub = 8
@@ -166,12 +173,12 @@
         for a in range(PIVOT):
             unit = jnp.where(place == begin + a, 1.0, 0.0)
             r.append(jnp.where(inside, unit, spread_row(tiles[owner], first_row + a)))
-        det = 1.0 / (p[0][0] * p[1][1] - p[0][1] * p[1][0])
+        det = reciprocal(p[0][0] * p[1][1] - p[0][1] * p[1][0])
         across = -p[0][1] * det
         e = [[p[1][1] * det, across], [across, p[0][0] * det]]
         u = [[e[a][0] * p[0][b] + e[a][1] * p[1][b] for b in (2, 3)] for a in (0, 1)]
         s = [p[a][b + 2] - (p[a][0] * u[0][b] + p[a][1] * u[1][b]) for a, b in ((2, 0), (2, 1), (3, 1))]
-        det = 1.0 / (s[0] * s[2] - s[1] * s[1])
+        det = reciprocal(s[0] * s[2] - s[1] * s[1])
         across = -s[1] * det
         f = [[s[2] * det, across], [across, s[0] * det]]
         w = [e[a][0] * r[0] + e[a][1] * r[1] for a in (0, 1)]

time: 37.2 us -> 37.8 us (1.016)
  Pallas kernels: 9.08 us -> 9.64 us
    pallas_call x1, Pallas kernels: 2.36 us -> 2.92 us  [inverse_factors(): pl.pallas_call(functools.partial(inverse_kernel, total_count), out_shape=...]
  transfers between devices with their start and end apart: 6 -> 6, of which waited for: 4 -> 4; matrix products, arithmetic and copies ran while one was open for 0% -> 0% of each run, Pallas kernels for 17% -> 18%
where the time goes in v18:
time: 37.8 us; the launch traced here: 37.6 us
  blocking collectives  10.7 us (28%)
  Pallas kernels  9.64 us (26%)
  starting transfers between devices  9.46 us (25%)
  waiting for transfers between devices  6.96 us (18%)
  other arithmetic  0.83 us (2%)
    all_to_all x1, blocking collectives, shards(): lax.all_to_all(outgoing, ('dp', 'layer'), split_axis=0, concat_axis=0, ti...  10.7 us
    ppermute x6, starting transfers between devices, exchange(): return lax.ppermute(values, 'dp', [(k, k ^ distance) for k in range(count)])  9.46 us
    ppermute x6, waiting for transfers between devices, exchange(): return lax.ppermute(values, 'dp', [(k, k ^ distance) for k in range(count)])  6.96 us
    pallas_call x1, Pallas kernels, covariance_sums(): pl.pallas_call(covariance_kernel, out_shape=jax.ShapeDtypeStruct((K_OUT,...  3.65 us
    pallas_call x1, Pallas kernels, inverse_factors(): pl.pallas_call(functools.partial(inverse_kernel, total_count), out_shape=...  2.92 us
    pallas_call x1, Pallas kernels, all_scores(): pl.pallas_call(score_kernel, out_shape=jax.ShapeDtypeStruct((shard_count,...  2.68 us
  transfers between devices with their start and end apart: 6, of which 4 were waited for; matrix products, arithmetic and copies ran while one was open for 0% of the time, Pallas kernels for 18%

profile of v18, /device:TPU:0, one launch (start us, length us, event | category | flops | bytes accessed | tf_op | source)
XLA Modules:
  0.0 37.6 jit_solution(3173904785946824404)
XLA Ops:
  0.0 4.0 %collective-permute-start = (bf16[8,4096]{1,0:T(8,128)(2,1)}, bf16[8,4096]{1,0:T(8,128)(2,1)S(1)}, u32[]{:S(2)}, u32[]{:S(2)}) collective-permute-start(bf16[8,4096]{1,0:T(8,128)(2,1)} %bitcast.9), channel_id=1, source_target_pairs={{0,8},{2,10},{4,12},{6,14},{8,0},{10,2},{12,4},{14,6},{1,9},{3,11}... | collective-permute-start | bytes 196616 | tf_op jit(solution)/shard_map/ppermute | solution.py:304
  4.0 0.0 copy-start.1
  4.0 0.0 copy-start.2
  4.0 0.0 copy-start.3
  4.0 3.6 %covariance.1 = f32[64,128]{1,0:T(8,128)S(1)} custom-call(bf16[256,4096]{1,0:T(8,128)(2,1)} %bitcast.5), custom_call_target="tpu_custom_call" | custom-call | flops 4294967296 | bytes 2097152 | tf_op jit(solution)/shard_map/covariance/pallas_call | solution.py:79
  7.7 1.6 %collective-permute-start.2 = (f32[64,128]{1,0:T(8,128)S(1)}, f32[64,128]{1,0:T(8,128)S(1)}, u32[]{:S(2)}, u32[]{:S(2)}) collective-permute-start(f32[64,128]{1,0:T(8,128)S(1)} %covariance.1), channel_id=1, source_target_pairs={{0,2},{2,0},{4,6},{6,4},{8,10},{10,8},{12,14},{14,12},{1,3},{3,1},... | collective-permute-start | bytes 98312 | tf_op jit(solution)/shard_map/ppermute | solution.py:304
  9.3 0.0 collective-permute-done
  9.3 0.0 copy-done.1
  9.3 1.6 %collective-permute-start.1 = (bf16[16,4096]{1,0:T(8,128)(2,1)S(1)}, bf16[16,4096]{1,0:T(8,128)(2,1)S(1)}, u32[]{:S(2)}, u32[]{:S(2)}) collective-permute-start(bf16[16,4096]{1,0:T(8,128)(2,1)S(1)} %pad_maximum_fusion.1), channel_id=1, source_target_pairs={{0,4},{2,6},{4,0},{6,2},{8,12},{10,14},{12,8},{14,10},{1,5},{3,7},... | collective-permute-start | bytes 393224 | tf_op jit(solution)/shard_map/ppermute | solution.py:304
  10.9 0.0 copy-done.2
  10.9 0.1 iota_compare_fusion
  11.0 0.7 %collective-permute-done.2 = f32[64,128]{1,0:T(8,128)S(1)} collective-permute-done((f32[64,128]{1,0:T(8,128)S(1)}, f32[64,128]{1,0:T(8,128)S(1)}, u32[]{:S(2)}, u32[]{:S(2)}) %collective-permute-start.2) | collective-permute-done | bytes 32800 | tf_op jit(solution)/shard_map/ppermute | solution.py:304
  11.7 0.4 %collective-permute-start.3 = (f32[64,128]{1,0:T(8,128)S(1)}, f32[64,128]{1,0:T(8,128)S(1)}, u32[]{:S(2)}, u32[]{:S(2)}) collective-permute-start(f32[64,128]{1,0:T(8,128)S(1)} %add.9), channel_id=1, source_target_pairs={{0,8},{2,10},{4,12},{6,14},{8,0},{10,2},{12,4},{14,6},{1,9},{3,11}... | collective-permute-start | bytes 98312 | tf_op jit(solution)/shard_map/ppermute | solution.py:304
  12.1 2.6 %collective-permute-done.1 = bf16[16,4096]{1,0:T(8,128)(2,1)S(1)} collective-permute-done((bf16[16,4096]{1,0:T(8,128)(2,1)S(1)}, bf16[16,4096]{1,0:T(8,128)(2,1)S(1)}, u32[]{:S(2)}, u32[]{:S(2)}) %collective-permute-start.1) | collective-permute-done | bytes 131104 | tf_op jit(solution)/shard_map/ppermute | solution.py:304
  14.7 0.3 collective-permute-start.5
  14.9 0.0 copy-done.3
  14.9 1.6 %collective-permute-done.3 = f32[64,128]{1,0:T(8,128)S(1)} collective-permute-done((f32[64,128]{1,0:T(8,128)S(1)}, f32[64,128]{1,0:T(8,128)S(1)}, u32[]{:S(2)}, u32[]{:S(2)}) %collective-permute-start.3) | collective-permute-done | bytes 32800 | tf_op jit(solution)/shard_map/ppermute | solution.py:304
  16.5 1.6 %collective-permute-start.4 = (f32[64,128]{1,0:T(8,128)S(1)}, f32[64,128]{1,0:T(8,128)S(1)}, u32[]{:S(2)}, u32[]{:S(2)}) collective-permute-start(f32[64,128]{1,0:T(8,128)S(1)} %add.10), channel_id=1, source_target_pairs={{0,4},{2,6},{4,0},{6,2},{8,12},{10,14},{12,8},{14,10},{1,5},{3,7},... | collective-permute-start | bytes 98312 | tf_op jit(solution)/shard_map/ppermute | solution.py:304
  18.1 0.2 turn_queries.2.first_ref
  18.3 2.1 %collective-permute-done.4 = f32[64,128]{1,0:T(8,128)S(1)} collective-permute-done((f32[64,128]{1,0:T(8,128)S(1)}, f32[64,128]{1,0:T(8,128)S(1)}, u32[]{:S(2)}, u32[]{:S(2)}) %collective-permute-start.4) | collective-permute-done | bytes 32800 | tf_op jit(solution)/shard_map/ppermute | solution.py:304
  20.4 0.0 copy-start
  20.4 2.9 %inverses.1 = (bf16[192,64]{1,0:T(8,128)(2,1)S(1)}, bf16[256,256]{1,0:T(8,128)(2,1)S(1)}) custom-call(f32[64,128]{1,0:T(8,128)S(1)} %add.11.cov_ref), custom_call_target="tpu_custom_call" | custom-call | flops 2000000000 | tf_op jit(solution)/shard_map/inverses/pallas_call | solution.py:214
  23.4 0.0 collective-permute-done.5.query_ref
  23.4 0.2 turn_queries.3.second_ref
  23.6 0.0 copy-done
  23.6 2.7 %products_and_scores.1 = f32[8,2,8,128]{3,2,1,0:T(8,128)S(1)} custom-call(s32[8]{0:T(128)S(1)} %broadcast_xor_fusion.route_ref, bf16[192,64]{1,0:T(8,128)(2,1)S(1)} %get-tuple-element.15.left_ref, bf16[256,256]{1,0:T(8,128)(2,1)S(1)} %get-tuple-element.16.right_ref, bf16[64,2048]{1,0:T(8,128)(2,1)S(1)} %turn_queries.2.first_ref, ...), custom_call_target="tpu_custom_call" | custom-call | flops 201326592 | bytes 2097152 | tf_op jit(solution)/shard_map/products_and_scores/pallas_call | solution.py:277
  26.3 10.7 %all_to_all.5 = f32[16,8,128]{2,1,0:T(8,128)S(1)} all-to-all(f32[16,8,128]{2,1,0:T(8,128)S(1)} %bitcast.7), channel_id=1, replica_groups=mesh['groups'=2,'dp'=8,'layer'=2] {'dp','layer'}, dimensions={0} | all-to-all | bytes 131072 | tf_op jit(solution)/shard_map/all_to_all | solution.py:343
  36.9 0.7 %select_reduce_fusion = f32[4,8,128]{2,1,0:T(8,128)} fusion(f32[8,2,8,128]{3,2,1,0:T(8,128)S(1)} %bitcast.8, pred[4,8]{1,0:T(4,128)(4,1)S(1)} %iota_compare_fusion), kind=kLoop, calls=%fused_computation.1 | loop fusion | flops 126976 | bytes 81952 | tf_op jit(solution)/shard_map/reduce_sum | solution.py:345
  (6 shorter events, 0.0 us)
Async XLA Ops:
  0.0 9.3 %collective-permute-start = (bf16[8,4096]{1,0:T(8,128)(2,1)}, bf16[8,4096]{1,0:T(8,128)(2,1)S(1)}, u32[]{:S(2)}, u32[]{:S(2)}) collective-permute-start(bf16[8,4096]{1,0:T(8,128)(2,1)} %bitcast.9), channel_id=1, source_target_pairs={{0,8},{2,10},{4,12},{6,14},{8,0},{10,2},{12,4},{14,6},{1,9},{3,11}... | collective-permute-start | bytes 196616 | tf_op jit(solution)/shard_map/ppermute | solution.py:304
  4.0 5.2 %copy-start.1 = (bf16[8,1,4096]{2,0,1:T(8,128)(2,1)S(1)}, bf16[8,1,4096]{2,0,1:T(8,128)(2,1)}, u32[]{:S(2)}) copy-start(bf16[8,1,4096]{2,0,1:T(8,128)(2,1)} %param.5) | copy-start | bytes 196612
  4.0 6.9 %copy-start.2 = (s32[1,4]{1,0:T(1,128)S(1)}, s32[1,4]{1,0:T(1,128)}, u32[]{:S(2)}) copy-start(s32[1,4]{1,0:T(1,128)} %param.6) | copy-start | bytes 52
  4.0 10.9 %copy-start.3 = (s32[8]{0:T(128)S(1)}, s32[8]{0:T(128)}, u32[]{:S(2)}) copy-start(s32[8]{0:T(128)} %constant.10.clone) | copy-start | bytes 100
  7.7 4.0 %collective-permute-start.2 = (f32[64,128]{1,0:T(8,128)S(1)}, f32[64,128]{1,0:T(8,128)S(1)}, u32[]{:S(2)}, u32[]{:S(2)}) collective-permute-start(f32[64,128]{1,0:T(8,128)S(1)} %covariance.1), channel_id=1, source_target_pairs={{0,2},{2,0},{4,6},{6,4},{8,10},{10,8},{12,14},{14,12},{1,3},{3,1},... | collective-permute-start | bytes 98312 | tf_op jit(solution)/shard_map/ppermute | solution.py:304
  9.3 5.4 %collective-permute-start.1 = (bf16[16,4096]{1,0:T(8,128)(2,1)S(1)}, bf16[16,4096]{1,0:T(8,128)(2,1)S(1)}, u32[]{:S(2)}, u32[]{:S(2)}) collective-permute-start(bf16[16,4096]{1,0:T(8,128)(2,1)S(1)} %pad_maximum_fusion.1), channel_id=1, source_target_pairs={{0,4},{2,6},{4,0},{6,2},{8,12},{10,14},{12,8},{14,10},{1,5},{3,7},... | collective-permute-start | bytes 393224 | tf_op jit(solution)/shard_map/ppermute | solution.py:304
  11.7 4.8 %collective-permute-start.3 = (f32[64,128]{1,0:T(8,128)S(1)}, f32[64,128]{1,0:T(8,128)S(1)}, u32[]{:S(2)}, u32[]{:S(2)}) collective-permute-start(f32[64,128]{1,0:T(8,128)S(1)} %add.9), channel_id=1, source_target_pairs={{0,8},{2,10},{4,12},{6,14},{8,0},{10,2},{12,4},{14,6},{1,9},{3,11}... | collective-permute-start | bytes 98312 | tf_op jit(solution)/shard_map/ppermute | solution.py:304
  14.7 8.7 %collective-permute-start.5 = (bf16[32,4096]{1,0:T(8,128)(2,1)S(1)}, bf16[32,4096]{1,0:T(8,128)(2,1)S(1)}, u32[]{:S(2)}, u32[]{:S(2)}) collective-permute-start(bf16[32,4096]{1,0:T(8,128)(2,1)S(1)} %pad_maximum_fusion.query_ref), channel_id=1, source_target_pairs={{0,2},{2,0},{4,6},{6,4},{8,10},{10,8},{12,14},{14,12},{1,3},{3,1},... | collective-permute-start | bytes 786440 | tf_op jit(solution)/shard_map/ppermute | solution.py:304
  16.5 3.9 %collective-permute-start.4 = (f32[64,128]{1,0:T(8,128)S(1)}, f32[64,128]{1,0:T(8,128)S(1)}, u32[]{:S(2)}, u32[]{:S(2)}) collective-permute-start(f32[64,128]{1,0:T(8,128)S(1)} %add.10), channel_id=1, source_target_pairs={{0,4},{2,6},{4,0},{6,2},{8,12},{10,14},{12,8},{14,10},{1,5},{3,7},... | collective-permute-start | bytes 98312 | tf_op jit(solution)/shard_map/ppermute | solution.py:304
  20.4 3.1 %copy-start = (bf16[256,1,4096]{2,0,1:T(8,128)(2,1)S(1)}, bf16[256,1,4096]{2,0,1:T(8,128)(2,1)}, u32[]{:S(2)}) copy-start(bf16[256,1,4096]{2,0,1:T(8,128)(2,1)} %param.4) | copy-start | bytes 6291460

commit v19 on v16

--- a/solution.py
+++ b/solution.py
@@ -179,14 +179,15 @@
         last = [f[a][0] * t[0] + f[a][1] * t[1] for a in (0, 1)]
         first = [w[a] - (u[a][0] * last[0] + u[a][1] * last[1]) for a in (0, 1)]
         solved = first + last
+        even = (row & 1) == 0
+        upper = (row & 2) == 0
+        stored = jnp.where(upper, jnp.where(even, solved[0], solved[1]), jnp.where(even, solved[2], solved[3]))
+        mine = (row >= first_row) & (row < first_row + PIVOT)
         for k in range(len(tiles)):
-            rest = jnp.where(inside, 0.0, tiles[k])
             part = [columns[k][a] * solved[a] for a in range(PIVOT)]
-            rest = (rest - (part[0] + part[1])) - (part[2] + part[3])
-            if k == owner:
-                for a in range(PIVOT):
-                    rest = jnp.where(row == first_row + a, solved[a], rest)
-            tiles[k] = rest
+            rest = jnp.where(inside, 0.0, tiles[k]) - (part[2] + part[3])
+            rest = rest - (part[0] + part[1])
+            tiles[k] = jnp.where(mine, stored, rest) if k == owner else rest
     return jnp.concatenate(tiles, axis=0)
 
 

time: 37.2 us -> 37.2 us (level)
  no operation moved by 1% of the time
where the time goes in v19:
time: 37.2 us; the launch traced here: 37 us
  blocking collectives  10.6 us (28%)
  starting transfers between devices  9.46 us (25%)
  Pallas kernels  9.06 us (24%)
  waiting for transfers between devices  6.96 us (19%)
  other arithmetic  0.83 us (2%)
    all_to_all x1, blocking collectives, shards(): lax.all_to_all(outgoing, ('dp', 'layer'), split_axis=0, concat_axis=0, ti...  10.6 us
    ppermute x6, starting transfers between devices, exchange(): return lax.ppermute(values, 'dp', [(k, k ^ distance) for k in range(count)])  9.46 us
    ppermute x6, waiting for transfers between devices, exchange(): return lax.ppermute(values, 'dp', [(k, k ^ distance) for k in range(count)])  6.96 us
    pallas_call x1, Pallas kernels, covariance_sums(): pl.pallas_call(covariance_kernel, out_shape=jax.ShapeDtypeStruct((K_OUT,...  3.65 us
    pallas_call x1, Pallas kernels, all_scores(): pl.pallas_call(score_kernel, out_shape=jax.ShapeDtypeStruct((shard_count,...  2.68 us
    pallas_call x1, Pallas kernels, inverse_factors(): pl.pallas_call(functools.partial(inverse_kernel, total_count), out_shape=...  2.34 us
  transfers between devices with their start and end apart: 6, of which 4 were waited for; matrix products, arithmetic and copies ran while one was open for 0% of the time, Pallas kernels for 17%

profile of v19, /device:TPU:0, one launch (start us, length us, event | category | flops | bytes accessed | tf_op | source)
XLA Modules:
  0.0 37.0 jit_solution(11895304697549565842)
XLA Ops:
  0.0 4.0 %collective-permute-start = (bf16[8,4096]{1,0:T(8,128)(2,1)}, bf16[8,4096]{1,0:T(8,128)(2,1)S(1)}, u32[]{:S(2)}, u32[]{:S(2)}) collective-permute-start(bf16[8,4096]{1,0:T(8,128)(2,1)} %bitcast.9), channel_id=1, source_target_pairs={{0,8},{2,10},{4,12},{6,14},{8,0},{10,2},{12,4},{14,6},{1,9},{3,11}... | collective-permute-start | bytes 196616 | tf_op jit(solution)/shard_map/ppermute | solution.py:298
  4.0 0.0 copy-start.1
  4.0 0.0 copy-start.2
  4.0 0.0 copy-start.3
  4.0 3.6 %covariance.1 = f32[64,128]{1,0:T(8,128)S(1)} custom-call(bf16[256,4096]{1,0:T(8,128)(2,1)} %bitcast.5), custom_call_target="tpu_custom_call" | custom-call | flops 4294967296 | bytes 2097152 | tf_op jit(solution)/shard_map/covariance/pallas_call | solution.py:79
  7.7 1.6 %collective-permute-start.2 = (f32[64,128]{1,0:T(8,128)S(1)}, f32[64,128]{1,0:T(8,128)S(1)}, u32[]{:S(2)}, u32[]{:S(2)}) collective-permute-start(f32[64,128]{1,0:T(8,128)S(1)} %covariance.1), channel_id=1, source_target_pairs={{0,2},{2,0},{4,6},{6,4},{8,10},{10,8},{12,14},{14,12},{1,3},{3,1},... | collective-permute-start | bytes 98312 | tf_op jit(solution)/shard_map/ppermute | solution.py:298
  9.3 0.0 collective-permute-done
  9.3 0.0 copy-done.1
  9.3 1.6 %collective-permute-start.1 = (bf16[16,4096]{1,0:T(8,128)(2,1)S(1)}, bf16[16,4096]{1,0:T(8,128)(2,1)S(1)}, u32[]{:S(2)}, u32[]{:S(2)}) collective-permute-start(bf16[16,4096]{1,0:T(8,128)(2,1)S(1)} %pad_maximum_fusion.1), channel_id=1, source_target_pairs={{0,4},{2,6},{4,0},{6,2},{8,12},{10,14},{12,8},{14,10},{1,5},{3,7},... | collective-permute-start | bytes 393224 | tf_op jit(solution)/shard_map/ppermute | solution.py:298
  10.9 0.0 copy-done.2
  10.9 0.1 iota_compare_fusion
  11.0 0.7 %collective-permute-done.2 = f32[64,128]{1,0:T(8,128)S(1)} collective-permute-done((f32[64,128]{1,0:T(8,128)S(1)}, f32[64,128]{1,0:T(8,128)S(1)}, u32[]{:S(2)}, u32[]{:S(2)}) %collective-permute-start.2) | collective-permute-done | bytes 32800 | tf_op jit(solution)/shard_map/ppermute | solution.py:298
  11.7 0.4 %collective-permute-start.3 = (f32[64,128]{1,0:T(8,128)S(1)}, f32[64,128]{1,0:T(8,128)S(1)}, u32[]{:S(2)}, u32[]{:S(2)}) collective-permute-start(f32[64,128]{1,0:T(8,128)S(1)} %add.9), channel_id=1, source_target_pairs={{0,8},{2,10},{4,12},{6,14},{8,0},{10,2},{12,4},{14,6},{1,9},{3,11}... | collective-permute-start | bytes 98312 | tf_op jit(solution)/shard_map/ppermute | solution.py:298
  12.1 2.6 %collective-permute-done.1 = bf16[16,4096]{1,0:T(8,128)(2,1)S(1)} collective-permute-done((bf16[16,4096]{1,0:T(8,128)(2,1)S(1)}, bf16[16,4096]{1,0:T(8,128)(2,1)S(1)}, u32[]{:S(2)}, u32[]{:S(2)}) %collective-permute-start.1) | collective-permute-done | bytes 131104 | tf_op jit(solution)/shard_map/ppermute | solution.py:298
  14.7 0.3 collective-permute-start.5
  14.9 0.0 copy-done.3
  14.9 1.6 %collective-permute-done.3 = f32[64,128]{1,0:T(8,128)S(1)} collective-permute-done((f32[64,128]{1,0:T(8,128)S(1)}, f32[64,128]{1,0:T(8,128)S(1)}, u32[]{:S(2)}, u32[]{:S(2)}) %collective-permute-start.3) | collective-permute-done | bytes 32800 | tf_op jit(solution)/shard_map/ppermute | solution.py:298
  16.5 1.6 %collective-permute-start.4 = (f32[64,128]{1,0:T(8,128)S(1)}, f32[64,128]{1,0:T(8,128)S(1)}, u32[]{:S(2)}, u32[]{:S(2)}) collective-permute-start(f32[64,128]{1,0:T(8,128)S(1)} %add.10), channel_id=1, source_target_pairs={{0,4},{2,6},{4,0},{6,2},{8,12},{10,14},{12,8},{14,10},{1,5},{3,7},... | collective-permute-start | bytes 98312 | tf_op jit(solution)/shard_map/ppermute | solution.py:298
  18.1 0.2 turn_queries.2.first_ref
  18.3 2.1 %collective-permute-done.4 = f32[64,128]{1,0:T(8,128)S(1)} collective-permute-done((f32[64,128]{1,0:T(8,128)S(1)}, f32[64,128]{1,0:T(8,128)S(1)}, u32[]{:S(2)}, u32[]{:S(2)}) %collective-permute-start.4) | collective-permute-done | bytes 32800 | tf_op jit(solution)/shard_map/ppermute | solution.py:298
  20.4 0.0 copy-start
  20.4 2.3 %inverses.1 = (bf16[192,64]{1,0:T(8,128)(2,1)S(1)}, bf16[256,256]{1,0:T(8,128)(2,1)S(1)}) custom-call(f32[64,128]{1,0:T(8,128)S(1)} %add.11.cov_ref), custom_call_target="tpu_custom_call" | custom-call | flops 2000000000 | tf_op jit(solution)/shard_map/inverses/pallas_call | solution.py:208
  22.8 0.0 collective-permute-done.5.query_ref
  22.8 0.2 turn_queries.3.second_ref
  23.0 0.0 copy-done
  23.0 2.7 %products_and_scores.1 = f32[8,2,8,128]{3,2,1,0:T(8,128)S(1)} custom-call(s32[8]{0:T(128)S(1)} %broadcast_xor_fusion.route_ref, bf16[192,64]{1,0:T(8,128)(2,1)S(1)} %get-tuple-element.15.left_ref, bf16[256,256]{1,0:T(8,128)(2,1)S(1)} %get-tuple-element.16.right_ref, bf16[64,2048]{1,0:T(8,128)(2,1)S(1)} %turn_queries.2.first_ref, ...), custom_call_target="tpu_custom_call" | custom-call | flops 201326592 | bytes 2097152 | tf_op jit(solution)/shard_map/products_and_scores/pallas_call | solution.py:271
  25.7 10.6 %all_to_all.5 = f32[16,8,128]{2,1,0:T(8,128)S(1)} all-to-all(f32[16,8,128]{2,1,0:T(8,128)S(1)} %bitcast.7), channel_id=1, replica_groups=mesh['groups'=2,'dp'=8,'layer'=2] {'dp','layer'}, dimensions={0} | all-to-all | bytes 131072 | tf_op jit(solution)/shard_map/all_to_all | solution.py:337
  36.3 0.7 %select_reduce_fusion = f32[4,8,128]{2,1,0:T(8,128)} fusion(f32[8,2,8,128]{3,2,1,0:T(8,128)S(1)} %bitcast.8, pred[4,8]{1,0:T(4,128)(4,1)S(1)} %iota_compare_fusion), kind=kLoop, calls=%fused_computation.1 | loop fusion | flops 126976 | bytes 81952 | tf_op jit(solution)/shard_map/reduce_sum | solution.py:339
  (6 shorter events, 0.0 us)
Async XLA Ops:
  0.0 9.3 %collective-permute-start = (bf16[8,4096]{1,0:T(8,128)(2,1)}, bf16[8,4096]{1,0:T(8,128)(2,1)S(1)}, u32[]{:S(2)}, u32[]{:S(2)}) collective-permute-start(bf16[8,4096]{1,0:T(8,128)(2,1)} %bitcast.9), channel_id=1, source_target_pairs={{0,8},{2,10},{4,12},{6,14},{8,0},{10,2},{12,4},{14,6},{1,9},{3,11}... | collective-permute-start | bytes 196616 | tf_op jit(solution)/shard_map/ppermute | solution.py:298
  4.0 5.2 %copy-start.1 = (bf16[8,1,4096]{2,0,1:T(8,128)(2,1)S(1)}, bf16[8,1,4096]{2,0,1:T(8,128)(2,1)}, u32[]{:S(2)}) copy-start(bf16[8,1,4096]{2,0,1:T(8,128)(2,1)} %param.5) | copy-start | bytes 196612
  4.0 6.9 %copy-start.2 = (s32[1,4]{1,0:T(1,128)S(1)}, s32[1,4]{1,0:T(1,128)}, u32[]{:S(2)}) copy-start(s32[1,4]{1,0:T(1,128)} %param.6) | copy-start | bytes 52
  4.0 10.9 %copy-start.3 = (s32[8]{0:T(128)S(1)}, s32[8]{0:T(128)}, u32[]{:S(2)}) copy-start(s32[8]{0:T(128)} %constant.10.clone) | copy-start | bytes 100
  7.7 4.0 %collective-permute-start.2 = (f32[64,128]{1,0:T(8,128)S(1)}, f32[64,128]{1,0:T(8,128)S(1)}, u32[]{:S(2)}, u32[]{:S(2)}) collective-permute-start(f32[64,128]{1,0:T(8,128)S(1)} %covariance.1), channel_id=1, source_target_pairs={{0,2},{2,0},{4,6},{6,4},{8,10},{10,8},{12,14},{14,12},{1,3},{3,1},... | collective-permute-start | bytes 98312 | tf_op jit(solution)/shard_map/ppermute | solution.py:298
  9.3 5.4 %collective-permute-start.1 = (bf16[16,4096]{1,0:T(8,128)(2,1)S(1)}, bf16[16,4096]{1,0:T(8,128)(2,1)S(1)}, u32[]{:S(2)}, u32[]{:S(2)}) collective-permute-start(bf16[16,4096]{1,0:T(8,128)(2,1)S(1)} %pad_maximum_fusion.1), channel_id=1, source_target_pairs={{0,4},{2,6},{4,0},{6,2},{8,12},{10,14},{12,8},{14,10},{1,5},{3,7},... | collective-permute-start | bytes 393224 | tf_op jit(solution)/shard_map/ppermute | solution.py:298
  11.7 4.8 %collective-permute-start.3 = (f32[64,128]{1,0:T(8,128)S(1)}, f32[64,128]{1,0:T(8,128)S(1)}, u32[]{:S(2)}, u32[]{:S(2)}) collective-permute-start(f32[64,128]{1,0:T(8,128)S(1)} %add.9), channel_id=1, source_target_pairs={{0,8},{2,10},{4,12},{6,14},{8,0},{10,2},{12,4},{14,6},{1,9},{3,11}... | collective-permute-start | bytes 98312 | tf_op jit(solution)/shard_map/ppermute | solution.py:298
  14.7 8.1 %collective-permute-start.5 = (bf16[32,4096]{1,0:T(8,128)(2,1)S(1)}, bf16[32,4096]{1,0:T(8,128)(2,1)S(1)}, u32[]{:S(2)}, u32[]{:S(2)}) collective-permute-start(bf16[32,4096]{1,0:T(8,128)(2,1)S(1)} %pad_maximum_fusion.query_ref), channel_id=1, source_target_pairs={{0,2},{2,0},{4,6},{6,4},{8,10},{10,8},{12,14},{14,12},{1,3},{3,1},... | collective-permute-start | bytes 786440 | tf_op jit(solution)/shard_map/ppermute | solution.py:298
  16.5 3.9 %collective-permute-start.4 = (f32[64,128]{1,0:T(8,128)S(1)}, f32[64,128]{1,0:T(8,128)S(1)}, u32[]{:S(2)}, u32[]{:S(2)}) collective-permute-start(f32[64,128]{1,0:T(8,128)S(1)} %add.10), channel_id=1, source_target_pairs={{0,4},{2,6},{4,0},{6,2},{8,12},{10,14},{12,8},{14,10},{1,5},{3,7},... | collective-permute-start | bytes 98312 | tf_op jit(solution)/shard_map/ppermute | solution.py:298
  20.4 2.6 %copy-start = (bf16[256,1,4096]{2,0,1:T(8,128)(2,1)S(1)}, bf16[256,1,4096]{2,0,1:T(8,128)(2,1)}, u32[]{:S(2)}) copy-start(bf16[256,1,4096]{2,0,1:T(8,128)(2,1)} %param.4) | copy-start | bytes 6291460
